TPU v7x, 32 devices: a whole 2x2x4 slice. The times are simulated.
32 devices in a mesh: dp: 8 (over z, x), ctx: 2 (over y), tensor: 2 (over core).
Axes of the slice: x: 2, y: 2, z: 4, core: 2. Of those that a mesh axis runs over, the one named last changes fastest.
Arguments:
- tokens: bfloat16 [16384, 768], P(('dp', 'ctx')), may hold values from -6 to 6
- lengths: int32 [8, 4], P('dp'), may hold values from 1 to 2045, as said below
- gain_one: bfloat16 [768], P('dp'), may hold values from 0.5 to 1.5
- w_qkv: bfloat16 [3, 768, 768], P(None, 'dp', 'tensor'), may hold values from -0.21875 to 0.21875
- w_out: bfloat16 [768, 768], P('tensor', 'dp'), may hold values from -0.625 to 0.625
- gain_two: bfloat16 [768], P('dp'), may hold values from 0.5 to 1.5
- w_in: bfloat16 [2, 768, 1152], P(None, 'dp', 'tensor'), may hold values from -0.21875 to 0.21875
- w_down: bfloat16 [1152, 768], P('tensor', 'dp'), may hold values from -0.25 to 0.25
- cotangent: bfloat16 [16384, 768], P(('dp', 'ctx')), may hold values from -6 to 6
Outputs:
- mixed: bfloat16 [16384, 768], P(('dp', 'ctx'))
- token_grad: float32 [16384, 768], P(('dp', 'ctx'))
- grad_gain_one: float32 [768], P('dp')
- grad_qkv: float32 [3, 768, 768], P(None, 'dp', 'tensor')
- grad_out: float32 [768, 768], P('tensor', 'dp')
- grad_gain_two: float32 [768], P('dp')
- grad_in: float32 [2, 768, 1152], P(None, 'dp', 'tensor')
- grad_down: float32 [1152, 768], P('tensor', 'dp')
Inputs may be any that keep to these rules, and one draw needn't show every extreme that they name: Each group's 4 lengths sum to 2048; one of them, at a place drawn from the seed, is 1025 or more; in one group, drawn from the seed, all other lengths are 1.
All inputs are finite; a program needn't handle non-finite values.
Results may differ from a plain program's by a relative error of at most 0.02.
Values may be sent and summed in bfloat16 or wider, within the bound.
No kernel may reach another device: no remote copies, remote signals or barrier semaphores. Data moves between devices by JAX's collectives and lax.ppermute only.
A program may use at most 256 MiB of HBM per device.

v0:
```python
import math

import jax
import jax.numpy as jnp
from jax import lax
from jax.sharding import PartitionSpec as P

HEAD = 64
WINDOW = 128
NSEQ = 4


norm_eps = 1e-05


def with_halo(array, sides, width):
    for axis, dim in sides:
        devices, length = (lax.axis_size(axis), array.shape[dim])
        up = [(i, (i + 1) % devices) for i in range(devices - 1)]
        down = [(j, i) for i, j in up]
        last = lax.slice_in_dim(array, length - width, length, axis=dim)
        initial = lax.slice_in_dim(array, 0, width, axis=dim)
        before = lax.ppermute(last, axis, up)
        after = lax.ppermute(initial, axis, down)
        array = jnp.concatenate([before, array, after], axis=dim)
    return array


def from_behind(array, axis, by):
    devices = lax.axis_size(axis)
    pairs = [(i, i + by) for i in range(devices) if 0 <= i + by < devices]
    return lax.ppermute(array, axis, pairs)


def layer_norm(values, gain):
    centered = values - jnp.mean(values, axis=-1, keepdims=True)
    spread = jnp.mean(centered * centered, axis=-1, keepdims=True)
    return centered * lax.rsqrt(spread + norm_eps) * gain


def turn_half(values):
    middle = values.shape[-1] // 2
    return jnp.concatenate([-values[..., middle:], values[..., :middle]], axis=-1)


def rotate(values, cosine, sine):
    return values * cosine + turn_half(values) * sine


def unrotate(values, cosine, sine):
    return values * cosine - turn_half(values) * sine


def angle_tables(position):
    number = (jnp.arange(HEAD, dtype=jnp.int32) % (HEAD // 2)).astype(jnp.float32)
    freq = jnp.exp(number * (-2.0 * math.log(10000.0) / HEAD))
    angle = position.astype(jnp.float32)[:, None] * freq[None, :]
    return (jnp.cos(angle)[:, None, :], jnp.sin(angle)[:, None, :])


def geglu(gate, upper):
    return jax.nn.gelu(gate, approximate=False) * upper


def block_scores(query_blk, key_blk, allowed, scale):
    raw = jnp.einsum("qhd,khd->hqk", query_blk, key_blk, preferred_element_type=jnp.float32) * scale
    return jnp.where(allowed[None], raw, -1e30)


def body(tokens, lengths, gain_one, w_qkv, w_out, gain_two, w_in, w_down, cotangent):
    fetched = (
        lax.all_gather(gain_one, "dp", axis=0, tiled=True),
        lax.all_gather(w_qkv, "dp", axis=1, tiled=True),
        lax.all_gather(w_out, "dp", axis=1, tiled=True),
        lax.all_gather(gain_two, "dp", axis=0, tiled=True),
        lax.all_gather(w_in, "dp", axis=1, tiled=True),
        lax.all_gather(w_down, "dp", axis=1, tiled=True),
    )
    norm_one, qkv_full, out_full, norm_two, in_full, down_full = fetched
    rows = tokens.shape[0]
    local = out_full.shape[0]
    heads = local // HEAD
    half = WINDOW // 2
    scale = HEAD ** (-0.5)
    split = (rows, heads, HEAD)
    place = lax.axis_index("ctx") * rows
    span = place + jnp.arange(-half, rows + half, dtype=jnp.int32)
    ends = jnp.cumsum(lengths[0])
    starts = ends - lengths[0]
    inside = (span[:, None] >= starts[None, :]) & (span[:, None] < ends[None, :])
    labels = jnp.arange(1, NSEQ + 1, dtype=jnp.int32)
    owner = jnp.sum(jnp.where(inside, labels[None, :], 0), axis=1) - 1
    begin = jnp.sum(jnp.where(inside, starts[None, :], 0), axis=1)
    position = (span - begin)[half : half + rows]
    cosine, sine = angle_tables(position)
    near = (
        jnp.abs(
            jnp.arange(rows, dtype=jnp.int32)[:, None]
            + half
            - jnp.arange(rows + 2 * half, dtype=jnp.int32)[None, :]
        )
        <= half
    )
    base = tokens.astype(jnp.float32)
    normed_one, norm_one_back = jax.vjp(layer_norm, base, norm_one.astype(jnp.float32))
    first = normed_one.astype(jnp.bfloat16)
    proj = jnp.einsum("rd,jde->jre", first, qkv_full, preferred_element_type=jnp.float32)
    query = rotate(proj[0].reshape(split), cosine, sine).astype(jnp.bfloat16)
    key = rotate(proj[1].reshape(split), cosine, sine).astype(jnp.bfloat16)
    value = proj[2].astype(jnp.bfloat16)
    pair = jnp.stack([key.reshape(rows, local), value])
    padded = with_halo(pair, (("ctx", 1),), half)
    key_pad = padded[0].reshape(rows + 2 * half, heads, HEAD)
    value_pad = padded[1].reshape(rows + 2 * half, heads, HEAD)
    starts_list = list(range(0, rows, rows))
    masks = []
    outputs = []
    totals = []
    for start in starts_list:
        query_blk = query
        key_blk = key_pad
        value_blk = value_pad
        allowed = near & (owner[start + half : start + half + rows][:, None] == owner[None, :])
        masks.append(allowed)
        scores = block_scores(query_blk, key_blk, allowed, scale)
        peak = jnp.max(scores, axis=-1, keepdims=True)
        weights = jnp.exp(scores - peak)
        total = jnp.sum(weights, axis=-1, keepdims=True)
        shares = (weights / total).astype(jnp.bfloat16)
        outputs.append(
            jnp.einsum("hqk,khd->qhd", shares, value_blk, preferred_element_type=jnp.float32)
        )
        totals.append(peak + jnp.log(total))
    attended = outputs[0].reshape(rows, local).astype(jnp.bfloat16)
    branch = lax.psum(jnp.dot(attended, out_full, preferred_element_type=jnp.float32), "tensor")
    middle = base + branch
    normed_two, norm_two_back = jax.vjp(layer_norm, middle, norm_two.astype(jnp.float32))
    second = normed_two.astype(jnp.bfloat16)
    gate_up = jnp.einsum("rd,jdf->jrf", second, in_full, preferred_element_type=jnp.float32)
    activated, geglu_back = jax.vjp(geglu, gate_up[0], gate_up[1])
    hidden = activated.astype(jnp.bfloat16)
    feed = lax.psum(
        jnp.dot(hidden, down_full, preferred_element_type=jnp.float32).astype(jnp.bfloat16),
        "tensor",
    ).astype(jnp.float32)
    mixed = (middle + feed).astype(jnp.bfloat16)
    grad_top = cotangent.astype(jnp.float32)
    grad_down = jnp.einsum("rf,rd->fd", hidden, cotangent, preferred_element_type=jnp.float32)
    grad_hidden = jnp.einsum("rd,fd->rf", cotangent, down_full, preferred_element_type=jnp.float32)
    grad_gate, grad_upper = geglu_back(grad_hidden)
    grad_pair = jnp.stack([grad_gate, grad_upper]).astype(jnp.bfloat16)
    grad_in = jnp.einsum("rd,jrf->jdf", second, grad_pair, preferred_element_type=jnp.float32)
    grad_second = lax.psum(
        jnp.einsum("jrf,jdf->rd", grad_pair, in_full, preferred_element_type=jnp.float32), "tensor"
    )
    grad_from_norm, grad_norm_two = norm_two_back(grad_second)
    grad_middle = grad_top + grad_from_norm
    middle_low = grad_middle.astype(jnp.bfloat16)
    grad_out = jnp.einsum("rc,rd->cd", attended, middle_low, preferred_element_type=jnp.float32)
    grad_attended = (
        jnp.einsum("rd,cd->rc", middle_low, out_full, preferred_element_type=jnp.float32)
        .astype(jnp.bfloat16)
        .reshape(split)
    )
    grad_pad = jnp.zeros((2, rows + 2 * half, heads, HEAD), jnp.float32)
    query_parts = []
    for number, start in enumerate(starts_list):
        query_blk = query
        key_blk = key_pad
        value_blk = value_pad
        scores = block_scores(query_blk, key_blk, masks[number], scale)
        shares = jnp.exp(scores - totals[number])
        grad_shares = jnp.einsum(
            "qhd,khd->hqk", grad_attended, value_blk, preferred_element_type=jnp.float32
        )
        grad_raw = (
            shares * (grad_shares - jnp.sum(shares * grad_shares, axis=-1, keepdims=True))
        ).astype(jnp.bfloat16)
        query_parts.append(
            jnp.einsum("hqk,khd->qhd", grad_raw, key_blk, preferred_element_type=jnp.float32)
            * scale
        )
        grad_key_blk = (
            jnp.einsum("hqk,qhd->khd", grad_raw, query_blk, preferred_element_type=jnp.float32)
            * scale
        )
        grad_value_blk = jnp.einsum(
            "hqk,qhd->khd",
            shares.astype(jnp.bfloat16),
            grad_attended,
            preferred_element_type=jnp.float32,
        )
        grad_pad = grad_pad.at[:, start : start + rows + 2 * half].add(
            jnp.stack([grad_key_blk, grad_value_blk])
        )
    grad_query = query_parts[0]
    flat = grad_pad.reshape(2, rows + 2 * half, local)
    from_after = from_behind(flat[:, :half].astype(jnp.bfloat16), "ctx", -1).astype(jnp.float32)
    from_before = from_behind(flat[:, rows + half :].astype(jnp.bfloat16), "ctx", 1).astype(
        jnp.float32
    )
    owned = flat[:, half : half + rows]
    owned = owned.at[:, rows - half :].add(from_after)
    owned = owned.at[:, :half].add(from_before)
    grad_proj = jnp.stack(
        [
            unrotate(grad_query, cosine, sine).reshape(rows, local),
            unrotate(owned[0].reshape(split), cosine, sine).reshape(rows, local),
            owned[1],
        ]
    ).astype(jnp.bfloat16)
    grad_qkv = jnp.einsum("rd,jre->jde", first, grad_proj, preferred_element_type=jnp.float32)
    grad_first = lax.psum(
        jnp.einsum("jre,jde->rd", grad_proj, qkv_full, preferred_element_type=jnp.float32).astype(
            jnp.bfloat16
        ),
        "tensor",
    ).astype(jnp.float32)
    grad_base, grad_norm_one = norm_one_back(grad_first)
    token_grad = grad_middle + grad_base
    grads = (grad_norm_one, grad_qkv, grad_out, grad_norm_two, grad_in, grad_down)
    summed = (
        lax.psum_scatter(
            grads[0].astype(jnp.bfloat16), "dp", scatter_dimension=0, tiled=True
        ).astype(jnp.float32),
        lax.psum_scatter(
            grads[1].astype(jnp.bfloat16), "dp", scatter_dimension=1, tiled=True
        ).astype(jnp.float32),
        lax.psum_scatter(
            grads[2].astype(jnp.bfloat16), "dp", scatter_dimension=1, tiled=True
        ).astype(jnp.float32),
        lax.psum_scatter(
            grads[3].astype(jnp.bfloat16), "dp", scatter_dimension=0, tiled=True
        ).astype(jnp.float32),
        lax.psum_scatter(
            grads[4].astype(jnp.bfloat16), "dp", scatter_dimension=1, tiled=True
        ).astype(jnp.float32),
        lax.psum_scatter(
            grads[5].astype(jnp.bfloat16), "dp", scatter_dimension=1, tiled=True
        ).astype(jnp.float32),
    )
    shards = (
        lax.psum(summed[0].astype(jnp.bfloat16), "ctx").astype(jnp.float32),
        lax.psum(summed[1].astype(jnp.bfloat16), "ctx").astype(jnp.float32),
        lax.psum(summed[2].astype(jnp.bfloat16), "ctx").astype(jnp.float32),
        lax.psum(summed[3].astype(jnp.bfloat16), "ctx").astype(jnp.float32),
        lax.psum(summed[4].astype(jnp.bfloat16), "ctx").astype(jnp.float32),
        lax.psum(summed[5].astype(jnp.bfloat16), "ctx").astype(jnp.float32),
    )
    return (mixed, token_grad, shards[0], shards[1], shards[2], shards[3], shards[4], shards[5])


def solution(mesh):
    in_specs = (
        P(("dp", "ctx"), None),
        P("dp", None),
        P("dp"),
        P(None, "dp", "tensor"),
        P("tensor", "dp"),
        P("dp"),
        P(None, "dp", "tensor"),
        P("tensor", "dp"),
        P(("dp", "ctx"), None),
    )
    out_specs = (
        P(("dp", "ctx"), None),
        P(("dp", "ctx"), None),
        P("dp"),
        P(None, "dp", "tensor"),
        P("tensor", "dp"),
        P("dp"),
        P(None, "dp", "tensor"),
        P("tensor", "dp"),
    )
    return jax.shard_map(body, mesh=mesh, in_specs=in_specs, out_specs=out_specs, check_vma=False)
```

profile of v0, /device:TPU:0, one launch (start us, length us, event | category | flops | bytes accessed | tf_op | source)
XLA Modules:
  0.0 662.2 jit_solution(9245362513522619992)
XLA Ops:
  11.7 23.1 %all-reduce.6 = (bf16[768]{0:T(1024)(128)(2,1)S(1)}, bf16[768]{0:T(1024)(128)(2,1)S(1)}) all-reduce(bf16[768]{0:T(1024)(128)(2,1)S(1)} %dynamic-update-slice.8, bf16[768]{0:T(1024)(128)(2,1)S(1)} %dynamic-update-slice.9), channel_id=1, replica_groups=mesh['dp'=8,'ctx'=2,'tensor'=2] {'dp'}, use_global_device_ids=true, to_apply=%add | all-reduce | flops 1536 | bytes 6144
  42.5 34.4 %all_gather.20 = bf16[384,768]{0,1:T(8,128)(2,1)} all-gather(bf16[384,96]{0,1:T(8,128)(2,1)S(1)} %copy-done.46), channel_id=1, replica_groups=mesh['dp'=8,'ctx'=2,'tensor'=2] {'dp'}, dimensions={1}, use_global_device_ids=true | all-gather | bytes 663552 | tf_op jit(solution)/shard_map/all_gather | solution.py:74
  113.2 12.1 %fusion.76 = (f32[6,1024]{1,0:T(8,128)S(1)}, f32[6,1024,1152]{2,1,0:T(8,128)}) fusion(bf16[1024,6,64]{0,2,1:T(8,128)(2,1)S(1)} %fusion.44, bf16[1152,6,64]{0,2,1:T(8,128)(2,1)S(1)} %bitcast.179, pred[1024,1152]{1,0:T(8,128)(4,1)S(1)} %copy-done.11), kind=kOutput, calls=%fused_computation.162 | convolution fusion | flops 927197184 | bytes 31186944 | tf_op jit(solution)/shard_map/qhd,khd->hqk/dot_general | solution.py:66
  125.4 10.1 %fusion = f32[6,1024]{1,0:T(8,128)S(1)} fusion(f32[6,1024,1152]{2,1,0:T(8,128)} %get-tuple-element.134, f32[6,1024]{1,0:T(8,128)S(1)} %get-tuple-element.133), kind=kLoop, calls=%fused_computation.6 | loop fusion | flops 14149632 | bytes 28360704 | tf_op jit(solution)/shard_map/reduce_sum | solution.py:128
  135.5 11.5 %fusion.47 = bf16[6,64,1024]{2,1,0:T(8,128)(2,1)S(1)} fusion(bf16[1152,6,64]{0,2,1:T(8,128)(2,1)S(1)} %bitcast.192, f32[6,1024,1152]{2,1,0:T(8,128)} %get-tuple-element.134, f32[6,1024]{1,0:T(8,128)S(1)} %fusion, f32[6,1024]{1,0:T(8,128)S(1)} %get-tuple-element.133), kind=kOutput, calls=%fused_computation.107 | convolution fusion | flops 927596544 | bytes 30031872 | tf_op jit(solution)/shard_map/hqk,khd->qhd/dot_general | solution.py:131
  151.5 32.7 %all_gather.23 = bf16[576,768]{0,1:T(8,128)(2,1)S(1)} all-gather(bf16[576,96]{0,1:T(8,128)(2,1)S(1)} %copy-done.43), channel_id=1, replica_groups=mesh['dp'=8,'ctx'=2,'tensor'=2] {'dp'}, dimensions={1}, use_global_device_ids=true | all-gather | bytes 995328 | tf_op jit(solution)/shard_map/all_gather | solution.py:77
  191.0 30.4 %all-gather.5.cloned.1.call-done = bf16[2,768,576]{2,1,0:T(8,128)(2,1)} async-done(((bf16[2,96,576]{2,1,0:T(8,128)(2,1)}), bf16[2,768,576]{2,1,0:T(8,128)(2,1)}) %all-gather.5.cloned.1.call-update) | async-done | bytes 1769488 | tf_op jit(solution)/shard_map/all_gather | solution.py:76
  225.5 5.6 fusion.49
  238.7 5.1 convert_bitcast_fusion
  243.7 6.7 %copy.81 = bf16[2,768,576]{2,0,1:T(2,128)(2,1)} copy(bf16[2,768,576]{1,2,0:T(8,128)(2,1)} %convert_bitcast_fusion) | data formatting | bytes 3538944 | tf_op jit(solution)/shard_map/convert_element_type | solution.py:236
  254.7 6.4 all-reduce.18.cloned.1.call-done
  269.5 13.2 %fusion.2 = f32[6,64,1152]{2,1,0:T(8,128)} fusion(bf16[1024,6,64]{0,2,1:T(8,128)(2,1)S(1)} %bitcast.182, f32[6,1024,1152]{2,1,0:T(8,128)} %get-tuple-element.134, f32[6,1024]{1,0:T(8,128)S(1)} %log_add_fusion), kind=kOutput, calls=%fused_computation.8 | convolution fusion | flops 920125440 | bytes 30892032 | tf_op jit(solution)/shard_map/hqk,qhd->khd/dot_general | solution.py:187
  282.7 18.2 %multiply_reduce_fusion = (f32[6,1024]{1,0:T(8,128)S(1)}, f32[6,1024,1152]{2,1,0:T(8,128)}) fusion(f32[6,1024,1152]{2,1,0:T(8,128)} %get-tuple-element.134, f32[6,1024]{1,0:T(8,128)S(1)} %log_add_fusion, bf16[1024,6,64]{0,2,1:T(8,128)(2,1)} %bitcast.183, bf16[1152,6,64]{0,2,1:T(8,128)(2,1)} %bitcast.191), kind=kOutput, calls=%fused_computation.1 | convolution fusion | flops 927197184 | bytes 58343424 | tf_op jit(solution)/shard_map/qhd,khd->hqk/dot_general | solution.py:173
  301.0 24.1 %multiply_convert_fusion = bf16[6,1024,1152]{2,1,0:T(8,128)(2,1)} fusion(f32[6,1024,1152]{2,1,0:T(8,128)} %get-tuple-element.136, f32[6,1024,1152]{2,1,0:T(8,128)} %get-tuple-element.134, f32[6,1024]{1,0:T(8,128)S(1)} %get-tuple-element.135, f32[6,1024]{1,0:T(8,128)S(1)} %log_add_fusion), kind=kLoop, calls=%fused_computation | loop fusion | flops 28311552 | bytes 70828032 | tf_op jit(solution)/shard_map/convert_element_type | solution.py:178
  325.1 8.9 %convolution_multiply_fusion = f32[6,64,1152]{2,1,0:T(8,128)} fusion(bf16[1024,6,64]{0,2,1:T(8,128)(2,1)S(1)} %copy-done.16, bf16[6,1024,1152]{2,1,0:T(8,128)(2,1)} %multiply_convert_fusion), kind=kOutput, calls=%fused_computation.33 | convolution fusion | flops 906412032 | bytes 16711680 | tf_op jit(solution)/shard_map/hqk,qhd->khd/dot_general | solution.py:184
  334.0 11.1 %bitcast_multiply_fusion.4 = (f32[1024,6,64]{0,2,1:T(8,128)}, f32[6,64,1024]{2,1,0:T(8,128)}) fusion(bf16[1152,6,64]{0,2,1:T(8,128)(2,1)S(1)} %bitcast.180, bf16[6,1024,1152]{2,1,0:T(8,128)(2,1)} %multiply_convert_fusion), kind=kOutput, calls=%fused_computation.101 | convolution fusion | flops 906362880 | bytes 18186240 | tf_op jit(solution)/shard_map/hqk,khd->qhd/dot_general | solution.py:180
  358.4 5.2 collective-permute-done.2
  387.9 5.7 convert_bitcast_fusion.1
  393.6 5.3 copy.85
  420.3 61.0 %reduce-scatter.10.cloned.1.call-done = bf16[96,1152]{1,0:T(8,128)(2,1)} async-done(((bf16[768,1152]{1,0:T(8,128)(2,1)}), bf16[96,1152]{1,0:T(8,128)(2,1)}) %reduce-scatter.10.cloned.1.call-update) | async-done | bytes 221200
  483.2 64.6 %reduce-scatter.8.cloned.1.call-done = bf16[576,96]{0,1:T(8,128)(2,1)} async-done(((bf16[576,768]{0,1:T(8,128)(2,1)}), bf16[576,96]{0,1:T(8,128)(2,1)}) %reduce-scatter.8.cloned.1.call-update) | async-done | bytes 110608 | tf_op jit(solution)/shard_map/reduce_scatter | solution.py:238
  547.9 64.4 %reduce-scatter.6.cloned.1.call-done = bf16[384,96]{0,1:T(8,128)(2,1)} async-done(((bf16[384,768]{0,1:T(8,128)(2,1)}), bf16[384,96]{0,1:T(8,128)(2,1)}) %reduce-scatter.6.cloned.1.call-update) | async-done | bytes 73744 | tf_op jit(solution)/shard_map/reduce_scatter | solution.py:229
  612.3 19.5 %all-reduce.5 = (bf16[768]{0:T(1024)(128)(2,1)S(1)}, bf16[768]{0:T(1024)(128)(2,1)S(1)}) all-reduce(bf16[768]{0:T(1024)(128)(2,1)S(1)} %get-tuple-element.86, bf16[768]{0:T(1024)(128)(2,1)S(1)} %get-tuple-element.84), channel_id=2, replica_groups=mesh['dp'=8,'ctx'=2,'tensor'=2] {'dp'}, use_global_device_ids=true, to_apply=%region_19.20.clone | all-reduce | flops 1536 | bytes 6144
  642.3 5.9 all-reduce.24.cloned.1.call-done
  (236 shorter events, 160.3 us)
Async XLA Ops:
  7.2 72.4 %all-gather.3.cloned.1.call-start = ((), (), s32[]{:S(2)}) async-start(), calls=%async_computation.3 | async-start | bytes 1990656 | tf_op jit(solution)/shard_map/all_gather | solution.py:73
  7.9 179.8 %all-reduce.16.cloned.1.call-start = ((), (), s32[]{:S(2)}) async-start(), calls=%async_computation.4 | async-start | bytes 6291456 | tf_op jit(solution)/shard_map/psum | solution.py:135
  34.8 44.8 %copy-start.47 = (f32[768]{0:T(1024)}, f32[768]{0:T(1024)S(1)}, u32[]{:S(2)}) copy-start(f32[768]{0:T(1024)S(1)} %convert_element_type.144) | copy-start | bytes 9220
  38.3 64.5 %copy-start.27 = (f32[1024,64]{0,1:T(8,128)}, f32[1024,64]{0,1:T(8,128)S(1)}, u32[]{:S(2)}) copy-start(f32[1024,64]{0,1:T(8,128)S(1)} %get-tuple-element.129) | copy-start | bytes 786436
  41.5 49.6 %copy-start.9 = (f32[1,1024,384]{2,1,0:T(8,128)}, f32[1,1024,384]{2,1,0:T(8,128)S(1)}, u32[]{:S(2)}) copy-start(f32[1,1024,384]{2,1,0:T(8,128)S(1)} %copy.68) | copy-start | bytes 4718596
  41.8 41.6 %copy-start.44 = (f32[1024]{0:T(1024)}, f32[1024]{0:T(1024)S(1)}, u32[]{:S(2)}) copy-start(f32[1024]{0:T(1024)S(1)} %broadcast_multiply_fusion.2) | copy-start | bytes 12292
  42.5 34.4 %copy-start.51 = (f32[1024]{0:T(1024)}, f32[1024]{0:T(1024)S(1)}, u32[]{:S(2)}) copy-start(f32[1024]{0:T(1024)S(1)} %fusion.16) | copy-start | bytes 12292
  42.5 41.0 %copy-start.49 = (f32[1024]{0:T(1024)}, f32[1024]{0:T(1024)S(1)}, u32[]{:S(2)}) copy-start(f32[1024]{0:T(1024)S(1)} %fusion.57) | copy-start | bytes 12292
  97.2 6.0 collective-permute-start
  100.8 6.5 collective-permute-start.1
  150.6 34.6 %copy-start.23 = (bf16[1024,768]{1,0:T(8,128)(2,1)S(1)}, bf16[1024,768]{1,0:T(8,128)(2,1)}, u32[]{:S(2)}) copy-start(bf16[1024,768]{1,0:T(8,128)(2,1)} %param.25) | copy-start | bytes 4718596
  150.6 70.8 %all-gather.5.cloned.1.call-start = ((), (), s32[]{:S(2)}) async-start(), calls=%async_computation.5 | async-start | bytes 2211840 | tf_op jit(solution)/shard_map/all_gather | solution.py:76
  151.3 109.7 %all-reduce.18.cloned.1.call-start = ((), (), s32[]{:S(2)}) async-start(), calls=%async_computation.6 | async-start | bytes 6291456 | tf_op jit(solution)/shard_map/psum | solution.py:153
  238.6 168.5 %all-reduce.20.cloned.1.call-start = ((), (), s32[]{:S(2)}) async-start(), calls=%async_computation.10 | async-start | bytes 3932160
  254.6 158.3 %all-reduce.22.cloned.1.call-start = ((), (), s32[]{:S(2)}) async-start(), calls=%async_computation.11 | async-start | bytes 6291456 | tf_op jit(solution)/shard_map/psum | solution.py:142
  301.0 24.1 %copy-start.16 = (bf16[1024,6,64]{0,2,1:T(8,128)(2,1)S(1)}, bf16[1024,6,64]{0,2,1:T(8,128)(2,1)}, u32[]{:S(2)}) copy-start(bf16[1024,6,64]{0,2,1:T(8,128)(2,1)} %copy-done.15) | copy-start | bytes 2359300
  353.3 10.4 %collective-permute-start.3 = (bf16[2,64,384]{2,1,0:T(8,128)(2,1)S(1)}, bf16[2,64,384]{2,1,0:T(8,128)(2,1)S(1)}, u32[]{:S(2)}, u32[]{:S(2)}) collective-permute-start(bf16[2,64,384]{2,1,0:T(8,128)(2,1)S(1)} %get-tuple-element.112), channel_id=1, source_target_pairs={{0,2},{1,3},{4,6},{5,7},{8,10},{9,11},{12,14},{13,15},{16,18},{17,... | collective-permute-start | bytes 294920 | tf_op jit(solution)/shard_map/ppermute | solution.py:32
  356.9 6.7 %collective-permute-start.2 = (bf16[2,64,384]{2,1,0:T(8,128)(2,1)S(1)}, bf16[2,64,384]{2,1,0:T(8,128)(2,1)S(1)}, u32[]{:S(2)}, u32[]{:S(2)}) collective-permute-start(bf16[2,64,384]{2,1,0:T(8,128)(2,1)S(1)} %get-tuple-element.113), channel_id=1, source_target_pairs={{2,0},{3,1},{6,4},{7,5},{10,8},{11,9},{14,12},{15,13},{18,16},{19,... | collective-permute-start | bytes 294920 | tf_op jit(solution)/shard_map/ppermute | solution.py:32
  387.2 94.0 %reduce-scatter.10.cloned.1.call-start = ((), (), s32[]{:S(2)}) async-start(), calls=%async_computation.9 | async-start | bytes 1990656
  402.2 145.7 %reduce-scatter.8.cloned.1.call-start = ((), (), s32[]{:S(2)}) async-start(), calls=%async_computation.8 | async-start | bytes 1105920 | tf_op jit(solution)/shard_map/reduce_scatter | solution.py:238
  406.4 205.9 %reduce-scatter.6.cloned.1.call-start = ((), (), s32[]{:S(2)}) async-start(), calls=%async_computation.7 | async-start | bytes 663552 | tf_op jit(solution)/shard_map/reduce_scatter | solution.py:229
  412.7 235.6 %all-reduce.24.cloned.1.call-start = ((), (), s32[]{:S(2)}) async-start(), calls=%async_computation.12 | async-start | bytes 1474560 | tf_op jit(solution)/shard_map/psum | solution.py:244
  418.3 219.7 %copy-start.2 = (bf16[1024,768]{1,0:T(8,128)(2,1)S(1)}, bf16[1024,768]{1,0:T(8,128)(2,1)}, u32[]{:S(2)}) copy-start(bf16[1024,768]{1,0:T(8,128)(2,1)} %param.17) | copy-start | bytes 4718596
  418.3 219.7 %copy-start.8 = (bf16[1024,768]{1,0:T(8,128)(2,1)S(1)}, bf16[1024,768]{1,0:T(8,128)(2,1)}, u32[]{:S(2)}) copy-start(bf16[1024,768]{1,0:T(8,128)(2,1)} %get-tuple-element.95) | copy-start | bytes 4718596
  (45 other events, 159.2 us)
Sparse Core Ops, SparseCore 0:
  10.2 55.1 all-gather.2
  150.7 19.5 all-reduce.15
  172.7 48.6 all-gather.4
  238.7 22.2 all-reduce.17
  264.5 99.4 all-reduce.19
  387.4 23.1 all-reduce.21
  414.1 67.1 reduce-scatter.9
  485.6 62.2 reduce-scatter.7
  551.2 61.0 reduce-scatter.5
  615.3 32.9 all-reduce.23
where the time goes:
time: 670 us; the launch traced here: 662 us
  waiting for transfers between devices  244 us (36%)
  matrix products  119 us (18%)
  blocking collectives  115 us (17%)
  other arithmetic  87.9 us (13%)
  local copies, waits for them, and re-layouts  69.4 us (10%)
  between operations  16.5 us (2%)
  starting transfers between devices  10.9 us (2%)
    reduce_scatter x1, waiting for transfers between devices, body(): lax.psum_scatter(grads[5].astype(jnp.bfloat16), 'dp', scatter_dimension=1...  64.6 us
    reduce_scatter x1, waiting for transfers between devices, body(): lax.psum_scatter(grads[2].astype(jnp.bfloat16), 'dp', scatter_dimension=1...  64.4 us
    unnamed x12, waiting for transfers between devices  62.5 us
    unnamed x2, blocking collectives  42.6 us
    all_gather x1, blocking collectives, body(): lax.all_gather(w_out, 'dp', axis=1, tiled=True)  34.4 us
    all_gather x1, blocking collectives, body(): lax.all_gather(w_down, 'dp', axis=1, tiled=True)  32.7 us
    all_gather x1, waiting for transfers between devices, body(): lax.all_gather(w_in, 'dp', axis=1, tiled=True)  30.4 us
    unnamed x124, local copies, waits for them, and re-layouts  29.2 us
  transfers between devices with their start and end apart: 14, of which 8 were waited for; matrix products, arithmetic and copies ran while one was open for 28% of the time, Pallas kernels for 0%

commit v1 on v0

v1 whole, which is shorter than its diff:
```python
import functools
import math

import jax
import jax.numpy as jnp
from jax import lax
from jax.experimental import pallas as pl
from jax.experimental.pallas import tpu as pltpu
from jax.sharding import PartitionSpec as P

HEAD = 64
WINDOW = 128
NSEQ = 4
HALF = WINDOW // 2
BLOCK = 128
LANES = 128
KEYS = BLOCK + WINDOW

norm_eps = 1e-05
f32 = jnp.float32
bf16 = jnp.bfloat16

NN = (((1,), (0,)), ((), ()))
NT = (((1,), (1,)), ((), ()))
TN = (((0,), (0,)), ((), ()))


def dot(a, b, dims=NN):
    return lax.dot_general(a, b, dims, preferred_element_type=f32)


def step_of(rows, most):
    best = LANES
    for size in range(LANES, most + 1, LANES):
        if rows % size == 0:
            best = size
    return best


def call(kernel, out_shape, args, flops, name, scalars=()):
    vmem = pl.BlockSpec(memory_space=pltpu.VMEM)
    smem = pl.BlockSpec(memory_space=pltpu.SMEM)
    moved = sum(x.size * x.dtype.itemsize for x in (*args, *out_shape))
    return pl.pallas_call(
        kernel[0],
        out_shape=out_shape,
        in_specs=[smem] * len(scalars) + [vmem] * len(args),
        out_specs=[vmem] * len(out_shape),
        scratch_shapes=kernel[1],
        compiler_params=pltpu.CompilerParams(vmem_limit_bytes=56 * 2**20),
        cost_estimate=pl.CostEstimate(flops=flops, bytes_accessed=moved, transcendentals=0),
        name=name,
    )(*scalars, *args)


def shape(dims, dtype):
    return jax.ShapeDtypeStruct(dims, dtype)


def normed(values):
    centered = values - jnp.mean(values, axis=-1, keepdims=True)
    spread = jnp.mean(centered * centered, axis=-1, keepdims=True)
    scale = lax.rsqrt(spread + norm_eps)
    return centered * scale, scale


def norm_back(grad, gain, hat, scale):
    inner = grad * gain
    one = jnp.mean(inner, axis=-1, keepdims=True)
    two = jnp.mean(inner * hat, axis=-1, keepdims=True)
    return scale * (inner - one - hat * two)


def turned(values, low):
    return jnp.where(low, pltpu.roll(values, LANES - HEAD // 2, 1), pltpu.roll(values, HEAD // 2, 1))


def halves(values):
    even = (lax.broadcasted_iota(jnp.int32, (1, LANES), 1) < HEAD).astype(f32).astype(bf16)
    return jnp.concatenate([values * even, values * (1 - even)], axis=0)


def joined(values):
    return jnp.concatenate([values[:HEAD, :BLOCK], values[HEAD:, BLOCK:]], axis=0).T


def stack_weight(src, index, dst):
    parts, _, depth, _ = src.shape
    for part in range(parts):
        dst[part * depth : (part + 1) * depth, :] = src[part, index]


def loop(count, body):
    def run(index, carry):
        body(index)
        return carry

    lax.fori_loop(0, count, run, 0)


def attend_kernel(
    bounds, tokens, before, after, gain, weights, cosine, sine,
    first, query, key, value, shares, attended, branch,
    wide, out_t,
):
    rows, width = tokens.shape
    extent, local = key.shape
    pairs = local // LANES
    for number in range(3):
        stack_weight(weights, number, wide.at[number])
    stack_weight(weights, 3, out_t)
    gains = gain[...]

    def norm_rows(src, dst, size):
        hat, _ = normed(src.astype(f32))
        first[pl.ds(dst, size), :] = (hat * gains).astype(bf16)

    norm_rows(before[...], 0, HALF)
    norm_rows(after[...], rows + HALF, HALF)

    def norm_step(index):
        at = pl.multiple_of(index * BLOCK, BLOCK)
        norm_rows(tokens[pl.ds(at, BLOCK), :], at + HALF, BLOCK)

    loop(rows // BLOCK, norm_step)
    low = lax.broadcasted_iota(jnp.int32, (1, LANES), 1) % HEAD < HEAD // 2

    def rotated(src, at, size, dst, place, scale):
        co, si = cosine[pl.ds(at, size), :], sine[pl.ds(at, size), :]
        for pair in range(pairs):
            lanes = slice(pair * LANES, (pair + 1) * LANES)
            part = src[:, lanes]
            dst[pl.ds(place, size), lanes] = ((part * co + turned(part, low) * si) * scale).astype(bf16)

    chunk = step_of(extent, 384)

    def key_step(index):
        at = pl.multiple_of(index * chunk, chunk)
        part = first[pl.ds(at, chunk), :]
        rotated(dot(part, wide[1]), at, chunk, key, at, 1.0)
        value[pl.ds(at, chunk), :] = dot(part, wide[2]).astype(bf16)

    loop(extent // chunk, key_step)
    size = step_of(rows, 256)

    def query_step(index):
        at = pl.multiple_of(index * size, size)
        start = pl.multiple_of(at + HALF, HALF)
        rotated(dot(first[pl.ds(start, size), :], wide[0]), start, size, query, at, HEAD**-0.5)

    loop(rows // size, query_step)
    key_at = lax.broadcasted_iota(jnp.int32, (KEYS, KEYS), 0)
    lane_at = lax.broadcasted_iota(jnp.int32, (1, KEYS), 1) % BLOCK

    def attend_step(index):
        at = pl.multiple_of(index * BLOCK, BLOCK)
        origin = bounds[NSEQ] + at - HALF
        own = lane_at + (origin + HALF)
        begin = jnp.zeros_like(own)
        end = jnp.zeros_like(own) + bounds[NSEQ - 1]
        for number in range(NSEQ - 1):
            begin = jnp.where(own >= bounds[number], bounds[number], begin)
        for number in reversed(range(NSEQ - 1)):
            end = jnp.where(own < bounds[number], bounds[number], end)
        least = jnp.maximum(lane_at, begin - origin)
        most = jnp.minimum(lane_at + WINDOW, end - 1 - origin)
        bias = jnp.where((key_at >= least) & (key_at <= most), 0.0, -1e30)
        for pair in range(pairs):
            lanes = slice(pair * LANES, (pair + 1) * LANES)
            both = halves(query[pl.ds(at, BLOCK), lanes])
            scores = dot(key[pl.ds(at, KEYS), lanes], both, NT) + bias
            weight = jnp.exp(scores - jnp.max(scores, axis=0, keepdims=True))
            part = (weight * (1.0 / jnp.sum(weight, axis=0, keepdims=True))).astype(bf16)
            shares[index * pairs + pair] = part
            mixed = dot(value[pl.ds(at, KEYS), lanes], part, TN)
            attended[pl.ds(at, BLOCK), lanes] = joined(mixed).astype(bf16)

    loop(rows // BLOCK, attend_step)

    def out_step(index):
        at = pl.multiple_of(index * size, size)
        branch[pl.ds(at, size), :] = dot(attended[pl.ds(at, size), :], out_t[...], NT).astype(bf16)

    loop(rows // size, out_step)


def feed_kernel(
    tokens, own, other, gain, weights, cotangent,
    middle, second, hidden, grad_gate, grad_upper, partial,
    gate_w, upper_w, down_t,
):
    rows, width = tokens.shape
    stack_weight(weights, 0, gate_w)
    stack_weight(weights, 1, upper_w)
    stack_weight(weights, 2, down_t)
    gains = gain[...]
    size = step_of(rows, 256)

    def step(index):
        at = pl.multiple_of(index * size, size)
        here = pl.ds(at, size)
        mid = tokens[here, :].astype(f32) + (own[here, :].astype(f32) + other[here, :].astype(f32))
        middle[here, :] = mid
        hat, _ = normed(mid)
        low = (hat * gains).astype(bf16)
        second[here, :] = low
        gate = dot(low, gate_w[...])
        upper = dot(low, upper_w[...])
        grad = dot(cotangent[here, :], down_t[...])
        share = 0.5 * (1.0 + lax.erf(gate * (0.5**0.5)))
        smooth = gate * share
        slope = share + gate * (jnp.exp(gate * gate * -0.5) * ((2.0 * math.pi) ** -0.5))
        hidden[here, :] = (smooth * upper).astype(bf16)
        gate_low = (grad * upper * slope).astype(bf16)
        upper_low = (grad * smooth).astype(bf16)
        grad_gate[here, :] = gate_low
        grad_upper[here, :] = upper_low
        partial[here, :] = (dot(gate_low, gate_w[...], NT) + dot(upper_low, upper_w[...], NT)).astype(bf16)

    loop(rows // size, step)


def weight_kernel(second, hidden, grad_gate, grad_upper, cotangent, weights, feed, grads, down_t, total):
    rows, width = second.shape
    stack_weight(weights, 2, down_t)
    size = step_of(rows, 256)

    def step(index):
        here = pl.ds(pl.multiple_of(index * size, size), size)
        feed[here, :] = dot(hidden[here, :], down_t[...], NT).astype(bf16)

    loop(rows // size, step)
    scatter_grads(second, grad_gate, grads, 0, total)
    scatter_grads(second, grad_upper, grads, 1, total)
    scatter_grads(cotangent, hidden, grads, 2, total)


def scatter_grads(left, right, grads, number, total):
    width = left.shape[-1]
    parts, _, depth, _ = grads.shape
    for start in range(0, width, 2 * LANES):
        total[start : start + 2 * LANES, :] = dot(left[:, start : start + 2 * LANES], right[...], TN).astype(bf16)
    for part in range(parts):
        grads[part, number] = total[part * depth : (part + 1) * depth, :]


def back_kernel(
    middle, own, other, gain, cotangent, weights, first, query, key, value, shares, attended, cosine, sine,
    grad_middle, grad_proj, grads, gain_grad,
    out_t, low_mid, grad_att, grad_key, grad_value, total,
):
    rows, width = middle.shape
    extent, local = key.shape
    pairs = local // LANES
    stack_weight(weights, 3, out_t)
    gains = gain[...]
    size = step_of(rows, 256)
    gain_grad[...] = jnp.zeros_like(gain_grad)

    def norm_step(index):
        here = pl.ds(pl.multiple_of(index * size, size), size)
        hat, scale = normed(middle[here, :])
        grad = own[here, :].astype(f32) + other[here, :].astype(f32)
        gain_grad[...] += jnp.sum(grad * hat, axis=0, keepdims=True)
        mid = cotangent[here, :].astype(f32) + norm_back(grad, gains, hat, scale)
        grad_middle[here, :] = mid
        mid_low = mid.astype(bf16)
        low_mid[here, :] = mid_low
        grad_att[here, :] = dot(mid_low, out_t[...]).astype(bf16)

    loop(rows // size, norm_step)
    grad_key[...] = jnp.zeros_like(grad_key)
    grad_value[...] = jnp.zeros_like(grad_value)
    low = lax.broadcasted_iota(jnp.int32, (1, LANES), 1) % HEAD < HEAD // 2
    zero = jnp.zeros((HALF, local), bf16)
    grad_proj[:HALF, :local] = zero
    grad_proj[rows + HALF :, :local] = zero

    def attend_step(index):
        at = pl.multiple_of(index * BLOCK, BLOCK)
        start = pl.multiple_of(at + HALF, HALF)
        co, si = cosine[pl.ds(start, BLOCK), :], sine[pl.ds(start, BLOCK), :]
        for pair in range(pairs):
            lanes = slice(pair * LANES, (pair + 1) * LANES)
            both = halves(query[pl.ds(at, BLOCK), lanes])
            grad = halves(grad_att[pl.ds(at, BLOCK), lanes])
            keys = key[pl.ds(at, KEYS), lanes]
            part = shares[index * pairs + pair]
            wide = part.astype(f32)
            grad_shares = dot(value[pl.ds(at, KEYS), lanes], grad, NT)
            delta = jnp.sum(wide * grad_shares, axis=0, keepdims=True)
            raw = (wide * (grad_shares - delta)).astype(bf16)
            grad_key[pl.ds(at, KEYS), lanes] += dot(raw, both)
            grad_value[pl.ds(at, KEYS), lanes] += dot(part, grad)
            grad_query = joined(dot(keys, raw, TN)) * HEAD**-0.5
            grad_proj[pl.ds(start, BLOCK), lanes] = (grad_query * co - turned(grad_query, low) * si).astype(bf16)

    loop(rows // BLOCK, attend_step)

    def turn_step(index):
        at = pl.multiple_of(index * BLOCK, BLOCK)
        here = pl.ds(at, BLOCK)
        co, si = cosine[here, :], sine[here, :]
        for pair in range(pairs):
            lanes = slice(pair * LANES, (pair + 1) * LANES)
            part = grad_key[here, lanes]
            turn = slice(local + pair * LANES, local + (pair + 1) * LANES)
            grad_proj[here, turn] = (part * co - turned(part, low) * si).astype(bf16)
        grad_proj[here, 2 * local :] = grad_value[here, :].astype(bf16)

    loop(extent // BLOCK, turn_step)
    for number in range(3):
        scatter_grads(first, grad_proj.at[:, number * local : (number + 1) * local], grads, number, total)
    scatter_grads(low_mid, attended, grads, 3, total)


def first_kernel(grad_proj, weights, tokens, before, after, partial, front, behind, gain_grad, wide):
    rows, width = tokens.shape
    extent = grad_proj.shape[0]
    local = weights.shape[-1]
    for number in range(3):
        stack_weight(weights, number, wide.at[:, number * local : (number + 1) * local])
    gain_grad[...] = jnp.zeros_like(gain_grad)

    def part(at, values, size):
        grad = dot(grad_proj[pl.ds(at, size), :], wide[...], NT)
        hat, _ = normed(values.astype(f32))
        gain_grad[...] += jnp.sum(grad * hat, axis=0, keepdims=True)
        return grad.astype(bf16)

    front[...] = part(0, before[...], HALF)
    behind[...] = part(rows + HALF, after[...], HALF)
    size = step_of(rows, 256)

    def step(index):
        at = pl.multiple_of(index * size, size)
        here = pl.ds(at, size)
        partial[here, :] = part(pl.multiple_of(at + HALF, HALF), tokens[here, :], size)

    loop(rows // size, step)


def final_kernel(tokens, gain, grad_middle, own, other, middle, feed_own, feed_other, *rest):
    edges, (mixed, token_grad) = rest[:4], rest[4:]
    rows, width = tokens.shape
    gains = gain[...]
    size = BLOCK

    def back(here, values, grad):
        hat, scale = normed(values)
        return norm_back(grad, gains, hat, scale)

    def step(index):
        here = pl.ds(pl.multiple_of(index * size, size), size)
        grad = own[here, :].astype(f32) + other[here, :].astype(f32)
        token_grad[here, :] = grad_middle[here, :] + back(here, tokens[here, :].astype(f32), grad)
        feed = feed_own[here, :].astype(f32) + feed_other[here, :].astype(f32)
        mixed[here, :] = (middle[here, :] + feed).astype(bf16)

    loop(rows // size, step)
    for start, one, two in ((0, edges[0], edges[1]), (rows - HALF, edges[2], edges[3])):
        here = pl.ds(start, HALF)
        grad = one[...].astype(f32) + two[...].astype(f32)
        token_grad[here, :] += back(here, tokens[here, :].astype(f32), grad)


def edge(array, by, cross):
    devices, cores = lax.axis_size("ctx"), lax.axis_size("tensor")
    pairs = []
    for i in range(devices):
        if 0 <= i + by < devices:
            for c in range(cores):
                pairs.append((i * cores + c, (i + by) * cores + (c + cross) % cores))
    return lax.ppermute(array, ("ctx", "tensor"), pairs)


def swap(array):
    return lax.ppermute(array, "tensor", [(0, 1), (1, 0)])


def tables(lengths, rows):
    place = lax.axis_index("ctx") * rows
    ends = jnp.cumsum(lengths[0])
    starts = ends - lengths[0]
    span = place + jnp.arange(-HALF, rows + HALF, dtype=jnp.int32)
    inside = (span[:, None] >= starts[None, :]) & (span[:, None] < ends[None, :])
    position = span - jnp.sum(jnp.where(inside, starts[None, :], 0), axis=1)
    number = (jnp.arange(HEAD, dtype=jnp.int32) % (HEAD // 2)).astype(f32)
    freq = jnp.exp(number * (-2.0 * math.log(10000.0) / HEAD))
    angle = position.astype(f32)[:, None] * freq[None, :]
    cosine, sine = jnp.cos(angle), jnp.sin(angle)
    sine = jnp.where(jnp.arange(HEAD)[None, :] < HEAD // 2, -sine, sine)
    bounds = jnp.concatenate([ends, place[None]]).astype(jnp.int32)
    return jnp.tile(cosine, (1, 2)), jnp.tile(sine, (1, 2)), bounds


def body(tokens, lengths, gain_one, w_qkv, w_out, gain_two, w_in, w_down, cotangent):
    rows, width = tokens.shape
    local, units = w_out.shape[0], w_down.shape[0]
    pairs, blocks, extent = local // LANES, rows // BLOCK, rows + WINDOW
    groups = lax.axis_size("dp")
    gains = lax.all_gather(jnp.stack([gain_one, gain_two]), "dp", axis=0, tiled=False)
    mine_one = jnp.concatenate([w_qkv, w_out.T[None]])
    mine_two = jnp.concatenate([w_in, w_down.T[None]])
    weights_one = lax.all_gather(mine_one, "dp", axis=0, tiled=False)
    weights_two = lax.all_gather(mine_two, "dp", axis=0, tiled=False)
    norm_one = gains[:, 0].reshape(1, width).astype(f32)
    norm_two = gains[:, 1].reshape(1, width).astype(f32)
    before = edge(tokens[rows - HALF :], 1, 0)
    after = edge(tokens[:HALF], -1, 0)
    cosine, sine, bounds = tables(lengths, rows)

    first, query, key, value, shares, attended, branch = call(
        (attend_kernel, [pltpu.VMEM((3, width, local), bf16), pltpu.VMEM((width, local), bf16)]),
        [
            shape((extent, width), bf16),
            shape((rows, local), bf16),
            shape((extent, local), bf16),
            shape((extent, local), bf16),
            shape((blocks * pairs, KEYS, KEYS), bf16),
            shape((rows, local), bf16),
            shape((rows, width), bf16),
        ],
        (tokens, before, after, norm_one, weights_one, cosine, sine),
        2 * rows * width * local * 5,
        "project_and_attend",
        (bounds,),
    )
    branch_other = swap(branch)
    plain = [pltpu.VMEM((width, units), bf16)] * 3
    middle, second, hidden, grad_gate, grad_upper, partial = call(
        (feed_kernel, plain),
        [
            shape((rows, width), f32),
            shape((rows, width), bf16),
            shape((rows, units), bf16),
            shape((rows, units), bf16),
            shape((rows, units), bf16),
            shape((rows, width), bf16),
        ],
        (tokens, branch, branch_other, norm_two, weights_two, cotangent),
        2 * rows * width * units * 5,
        "feed_forward_and_back",
    )
    partial_other = swap(partial)
    feed, grads_two = call(
        (weight_kernel, [pltpu.VMEM((width, units), bf16)] * 2),
        [shape((rows, width), bf16), shape((groups, 3, width // groups, units), bf16)],
        (second, hidden, grad_gate, grad_upper, cotangent, weights_two),
        2 * rows * width * units * 4,
        "feed_weight_grads",
    )
    feed_other = swap(feed)
    grad_middle, grad_proj, grads_one, grad_gain_two = call(
        (
            back_kernel,
            [
                pltpu.VMEM((width, local), bf16),
                pltpu.VMEM((rows, width), bf16),
                pltpu.VMEM((rows, local), bf16),
                pltpu.VMEM((extent, local), f32),
                pltpu.VMEM((extent, local), f32),
                pltpu.VMEM((width, local), bf16),
            ],
        ),
        [
            shape((rows, width), f32),
            shape((extent, 3 * local), bf16),
            shape((groups, 4, width // groups, local), bf16),
            shape((1, width), f32),
        ],
        (
            middle, partial, partial_other, norm_two, cotangent, weights_one, first, query, key, value, shares,
            attended, cosine, sine,
        ),
        2 * rows * width * local * 6,
        "attention_back",
    )
    first_part, front, behind, grad_gain_one = call(
        (first_kernel, [pltpu.VMEM((width, 3 * local), bf16)]),
        [
            shape((rows, width), bf16),
            shape((HALF, width), bf16),
            shape((HALF, width), bf16),
            shape((1, width), f32),
        ],
        (grad_proj, weights_one, tokens, before, after),
        2 * rows * width * local * 3,
        "first_grad",
    )
    first_other = swap(first_part)
    edges = [edge(behind, 1, 0), edge(behind, 1, 1), edge(front, -1, 0), edge(front, -1, 1)]
    mixed, token_grad = call(
        (final_kernel, []),
        [shape((rows, width), bf16), shape((rows, width), f32)],
        (tokens, norm_one, grad_middle, first_part, first_other, middle, feed, feed_other, *edges),
        rows * width * 20,
        "token_grad",
    )

    def reduced(grads):
        part = lax.psum_scatter(grads, "dp", scatter_dimension=0, tiled=False)
        return lax.psum(part, "ctx")

    two = reduced(grads_two).astype(f32)
    one = reduced(grads_one).astype(f32)
    gain_grads = jnp.stack([grad_gain_one.reshape(groups, -1), grad_gain_two.reshape(groups, -1)], axis=1)
    both = lax.psum_scatter(gain_grads, "dp", scatter_dimension=0, tiled=False)
    gain_one_grad = lax.psum(both[0], ("ctx", "tensor"))
    gain_two_grad = lax.psum(both[1], "ctx")
    return (mixed, token_grad, gain_one_grad, one[:3], one[3].T, gain_two_grad, two[:2], two[2].T)


def solution(mesh):
    in_specs = (
        P(("dp", "ctx"), None),
        P("dp", None),
        P("dp"),
        P(None, "dp", "tensor"),
        P("tensor", "dp"),
        P("dp"),
        P(None, "dp", "tensor"),
        P("tensor", "dp"),
        P(("dp", "ctx"), None),
    )
    out_specs = (
        P(("dp", "ctx"), None),
        P(("dp", "ctx"), None),
        P("dp"),
        P(None, "dp", "tensor"),
        P("tensor", "dp"),
        P("dp"),
        P(None, "dp", "tensor"),
        P("tensor", "dp"),
    )
    return jax.shard_map(body, mesh=mesh, in_specs=in_specs, out_specs=out_specs, check_vma=False)
```

time: 670 us -> 365 us (0.54); the launches traced: 662 us -> 364 us
  matrix products: 119 us -> 0 us
  Pallas kernels: 0 us -> 98.1 us
  waiting for transfers between devices: 244 us -> 159 us
  other arithmetic: 87.9 us -> 7.42 us
  blocking collectives: 115 us -> 55.5 us
  local copies, waits for them, and re-layouts: 69.4 us -> 15.4 us
    dot_general x18 -> x0, matrix products: 119 us -> none  [the longest x1 18.2 us: body(): jnp.einsum('qhd,khd->hqk', grad_attended, value_blk, preferred_element_ty...]
    pallas_call x0 -> x6, Pallas kernels: none -> 98.1 us  [call(): pl.pallas_call(kernel[0], out_shape=out_shape, in_specs=[smem] * len(scal...]
    unnamed x12 -> x5, waiting for transfers between devices: 62.5 us -> 0.08 us
    all_gather x2 -> x1, blocking collectives: 67.1 us -> 20.7 us  [body(): lax.all_gather(jnp.stack([gain_one, gain_two]), 'dp', axis=0, tiled=False)]
    reduce_scatter x2, waiting for transfers between devices: 129 us -> 99.1 us  [reduced(): part = lax.psum_scatter(grads, 'dp', scatter_dimension=0, tiled=False)]
    convert_element_type x11 -> x4, other arithmetic: 30.8 us -> 1.16 us  [the longest x1 1.08 us: body(): two = reduced(grads_two).astype(f32)]
    all_gather x2, waiting for transfers between devices: 30.4 us -> 56.6 us  [the longest x1 35 us: body(): weights_two = lax.all_gather(mine_two, 'dp', axis=0, tiled=False)]
    reduce_sum x10 -> x1, other arithmetic: 23.8 us -> 0.09 us  [tables(): position = span - jnp.sum(jnp.where(inside, starts[None, :], 0), axis=1)]
  transfers between devices with their start and end apart: 14 -> 15, of which waited for: 8 -> 5; matrix products, arithmetic and copies ran while one was open for 28% -> 3% of each run, Pallas kernels for 0% -> 19%
where the time goes in v1:
time: 365 us; the launch traced here: 364 us
  waiting for transfers between devices  159 us (44%)
  Pallas kernels  98.1 us (27%)
  blocking collectives  55.5 us (15%)
  local copies, waits for them, and re-layouts  15.4 us (4%)
  starting transfers between devices  14.4 us (4%)
  between operations  14.1 us (4%)
  other arithmetic  7.42 us (2%)
    reduce_scatter x2, waiting for transfers between devices, reduced(): part = lax.psum_scatter(grads, 'dp', scatter_dimension=0, tiled=False)  99.1 us
    pallas_call x6, Pallas kernels, call(): pl.pallas_call(kernel[0], out_shape=out_shape, in_specs=[smem] * len(scal...  98.1 us
    all_gather x1, waiting for transfers between devices, body(): weights_two = lax.all_gather(mine_two, 'dp', axis=0, tiled=False)  35 us
    all_gather x1, waiting for transfers between devices, body(): weights_one = lax.all_gather(mine_one, 'dp', axis=0, tiled=False)  21.6 us
    all_gather x1, blocking collectives, body(): lax.all_gather(jnp.stack([gain_one, gain_two]), 'dp', axis=0, tiled=False)  20.7 us
    unnamed x1, blocking collectives  19.4 us
    ppermute x6, starting transfers between devices, edge(): return lax.ppermute(array, ('ctx', 'tensor'), pairs)  13.4 us
    psum x1, blocking collectives, body(): gain_one_grad = lax.psum(both[0], ('ctx', 'tensor'))  9.3 us
  transfers between devices with their start and end apart: 15, of which 5 were waited for; matrix products, arithmetic and copies ran while one was open for 3% of the time, Pallas kernels for 19%

profile of v1, /device:TPU:0, one launch (start us, length us, event | category | flops | bytes accessed | tf_op | source)
XLA Modules:
  0.0 364.1 jit_solution(17565271295074228045)
XLA Ops:
  7.2 1.7 pad_maximum_fusion.1
  9.0 1.8 pad_maximum_fusion
  11.8 4.9 %collective-permute-start = (bf16[64,768]{1,0:T(8,128)(2,1)S(1)}, bf16[64,768]{1,0:T(8,128)(2,1)S(1)}, u32[]{:S(2)}, u32[]{:S(2)}) collective-permute-start(bf16[64,768]{1,0:T(8,128)(2,1)S(1)} %get-tuple-element.63), channel_id=1, source_target_pairs={{0,2},{1,3},{4,6},{5,7},{8,10},{9,11},{12,14},{13,15},{16,18},{17,... | collective-permute-start | bytes 294920 | tf_op jit(solution)/shard_map/ppermute | solution.py:374
  16.7 1.3 collective-permute-start.1
  21.8 20.7 %all-gather.3 = bf16[8,2,96]{2,1,0:T(2,128)(2,1)S(1)} all-gather(bf16[1,2,96]{2,1,0:T(2,128)(2,1)S(1)} %maximum_bitcast_fusion), channel_id=2, replica_groups=mesh['dp'=8,'ctx'=2,'tensor'=2] {'dp'}, dimensions={0}, use_global_device_ids=true | all-gather | bytes 3456 | tf_op jit(solution)/shard_map/all_gather | solution.py:402
  43.8 21.6 %all-gather.7.cloned.1.call-done = bf16[32,96,384]{2,1,0:T(8,128)(2,1)} async-done(((bf16[4,96,384]{2,1,0:T(8,128)(2,1)}), bf16[32,96,384]{2,1,0:T(8,128)(2,1)}) %all-gather.7.cloned.1.call-update) | async-done | bytes 2359312 | tf_op jit(solution)/shard_map/all_gather | solution.py:405
  65.4 24.1 %project_and_attend.1 = (bf16[1152,768]{1,0:T(8,128)(2,1)}, bf16[1024,384]{1,0:T(8,128)(2,1)}, bf16[1152,384]{1,0:T(8,128)(2,1)}, bf16[1152,384]{1,0:T(8,128)(2,...) custom-call(s32[5]{0:T(128)} %pad_add_fusion.bounds, ...), custom_call_target="tpu_custom_call" | custom-call | flops 3019898880 | bytes 15141888 | tf_op jit(solution)/shard_map/project_and_attend/pallas_call | solution.py:44
  90.2 35.0 %all-gather.9.cloned.1.call-done = bf16[24,96,576]{2,1,0:T(8,128)(2,1)} async-done(((bf16[3,96,576]{2,1,0:T(8,128)(2,1)}), bf16[24,96,576]{2,1,0:T(8,128)(2,1)}) %all-gather.9.cloned.1.call-update) | async-done | bytes 2654224 | tf_op jit(solution)/shard_map/all_gather | solution.py:406
  126.3 15.3 %feed_forward_and_back.1 = (f32[1024,768]{1,0:T(8,128)}, bf16[1024,768]{1,0:T(8,128)(2,1)}, bf16[1024,576]{1,0:T(8,128)(2,1)}, bf16[1024,576]{1,0:T(8,128)(2,1)}...) custom-call(bf16[1024,768]{1,0:T(8,128)(2,1)} %tokens.7, bf16[1024,768]{1,0:T(8,128)(2,1)} %get-tuple-element.33.own, ...), custom_call_target="tpu_custom_call" | custom-call | flops 4529848320 | bytes 18779136 | tf_op jit(solution)/shard_map/feed_forward_and_back/pallas_call | solution.py:44
  141.6 11.8 %feed_weight_grads.1 = (bf16[1024,768]{1,0:T(8,128)(2,1)}, bf16[8,3,96,576]{3,2,1,0:T(8,128)(2,1)}) custom-call(bf16[1024,768]{1,0:T(8,128)(2,1)} %get-tuple-element.45.second, bf16[1024,576]{1,0:T(8,128)(2,1)} %get-tuple-element.46.hidden, bf16[1024,576]{1,0:T(8,128)(2,1)} %get-tuple-element.47.grad_gate, bf16[1024,576]{1,0:T(8,128)(2,1)} %get-tuple-element.48.grad_upper, ...), custom_call_target="tpu_custom_call" | custom-call | flops 3623878656 | bytes 13565952 | tf_op jit(solution)/shard_map/feed_weight_grads/pallas_call | solution.py:44
  154.8 3.4 collective-permute-done.3.other
  159.4 27.8 %attention_back.1 = (f32[1024,768]{1,0:T(8,128)}, bf16[1152,1152]{1,0:T(8,128)(2,1)}, bf16[8,4,96,384]{3,2,1,0:T(8,128)(2,1)}, f32[1,768]{1,0:T(1,128)}) custom-call(f32[1024,768]{1,0:T(8,128)} %get-tuple-element.34.middle, bf16[1024,768]{1,0:T(8,128)(2,1)} %get-tuple-element.35.own, bf16[1024,768]{1,0:T(8,128)(2,1)} %copy-done.4, f32[1,768]{1,0:T(1,128)} %reshape.167.gain, ...), custom_call_target="tpu_custom_call" | custom-call | flops 3623878656 | bytes 27826176 | tf_op jit(solution)/shard_map/attention_back/pallas_call | solution.py:44
  187.3 1.4 copy-done.1
  188.8 8.3 %first_grad.1 = (bf16[1024,768]{1,0:T(8,128)(2,1)}, bf16[64,768]{1,0:T(8,128)(2,1)}, bf16[64,768]{1,0:T(8,128)(2,1)}, f32[1,768]{1,0:T(1,128)}) custom-call(bf16[1152,1152]{1,0:T(8,128)(2,1)} %get-tuple-element.43.grad_proj, bf16[8,4,96,384]{3,2,1,0:T(8,128)(2,1)} %bitcast.42, bf16[1024,768]{1,0:T(8,128)(2,1)} %tokens.7, bf16[64,768]{1,0:T(8,128)(2,1)} %copy-done.9, ...), custom_call_target="tpu_custom_call" | custom-call | flops 1811939328 | bytes 8555520 | tf_op jit(solution)/shard_map/first_grad/pallas_call | solution.py:44
  197.5 27.2 %reduce-scatter.5.cloned.1.call-done = bf16[1,3,96,576]{3,2,1,0:T(8,128)(2,1)} async-done(((bf16[8,3,96,576]{3,2,1,0:T(8,128)(2,1)}), bf16[1,3,96,576]{3,2,1,0:T(8,128)(2,1)}) %reduce-scatter.5.cloned.1.call-update) | async-done | bytes 331792 | tf_op jit(solution)/shard_map/reduce_scatter | solution.py:502
  224.8 71.9 %reduce-scatter.3.cloned.1.call-done = bf16[1,4,96,384]{3,2,1,0:T(8,128)(2,1)} async-done(((bf16[8,4,96,384]{3,2,1,0:T(8,128)(2,1)}), bf16[1,4,96,384]{3,2,1,0:T(8,128)(2,1)}) %reduce-scatter.3.cloned.1.call-update) | async-done | bytes 294928 | tf_op jit(solution)/shard_map/reduce_scatter | solution.py:502
  297.3 3.4 collective-permute-start.6
  300.7 1.3 collective-permute-start.7
  304.2 19.4 %all-reduce = f32[8,2,96]{2,1,0:T(2,128)S(1)} all-reduce(f32[8,2,96]{2,1,0:T(2,128)S(1)} %pad_maximum_fusion.2), channel_id=5, replica_groups=mesh['dp'=8,'ctx'=2,'tensor'=2] {'dp'}, use_global_device_ids=true, to_apply=%region_2.3.clone | all-reduce | flops 1536 | bytes 12288
  324.3 1.3 collective-permute-start.9
  325.6 9.3 %psum.28 = f32[96]{0:T(128)} all-reduce(f32[96]{0:T(128)S(1)} %get-tuple-element.67), channel_id=1, replica_groups=mesh['dp'=8,'ctx'=2,'tensor'=2] {'ctx','tensor'}, use_global_device_ids=true, to_apply=%region_3.4 | all-reduce | flops 96 | bytes 768 | tf_op jit(solution)/shard_map/psum | solution.py:509
  334.9 6.1 %psum.30 = f32[96]{0:T(128)} all-reduce(f32[96]{0:T(128)S(1)} %get-tuple-element.66), channel_id=1, replica_groups=mesh['dp'=8,'ctx'=2,'tensor'=2] {'ctx'}, use_global_device_ids=true, to_apply=%region_6.7 | all-reduce | flops 96 | bytes 768 | tf_op jit(solution)/shard_map/psum | solution.py:510
  341.8 10.7 %token_grad.1 = (bf16[1024,768]{1,0:T(8,128)(2,1)}, f32[1024,768]{1,0:T(8,128)}) custom-call(bf16[1024,768]{1,0:T(8,128)(2,1)} %tokens.7, f32[1,768]{1,0:T(1,128)} %reshape.166.gain, f32[1024,768]{1,0:T(8,128)} %get-tuple-element.42.grad_middle, bf16[1024,768]{1,0:T(8,128)(2,1)} %get-tuple-element.44.own, bf16[1024,768]{1,0:T(8,128)(2,1)} %collective-permute-done.4.other, ...), custom_call_target="tpu_custom_call" | custom-call | flops 15728640 | bytes 19270656 | tf_op jit(solution)/shard_map/token_grad/pallas_call | solution.py:44
  353.6 1.8 slice.46
  (89 shorter events, 18.5 us)
Async XLA Ops:
  7.2 10.9 %copy-start.13 = (s32[1,4]{1,0:T(1,128)S(1)}, s32[1,4]{1,0:T(1,128)}, u32[]{:S(2)}) copy-start(s32[1,4]{1,0:T(1,128)} %param.10) | copy-start | bytes 52
  7.2 58.3 %all-gather.7.cloned.1.call-start = ((), (), s32[]{:S(2)}) async-start(), calls=%async_computation.4 | async-start | bytes 2654208 | tf_op jit(solution)/shard_map/all_gather | solution.py:405
  9.0 116.2 %all-gather.9.cloned.1.call-start = ((), (), s32[]{:S(2)}) async-start(), calls=%async_computation.5 | async-start | bytes 3317760 | tf_op jit(solution)/shard_map/all_gather | solution.py:406
  10.8 213.9 %reduce-scatter.5.cloned.1.call-start = ((), (), s32[]{:S(2)}) async-start(), calls=%async_computation.3 | async-start | bytes 3317760 | tf_op jit(solution)/shard_map/reduce_scatter | solution.py:502
  11.8 31.9 %collective-permute-start = (bf16[64,768]{1,0:T(8,128)(2,1)S(1)}, bf16[64,768]{1,0:T(8,128)(2,1)S(1)}, u32[]{:S(2)}, u32[]{:S(2)}) collective-permute-start(bf16[64,768]{1,0:T(8,128)(2,1)S(1)} %get-tuple-element.63), channel_id=1, source_target_pairs={{0,2},{1,3},{4,6},{5,7},{8,10},{9,11},{12,14},{13,15},{16,18},{17,... | collective-permute-start | bytes 294920 | tf_op jit(solution)/shard_map/ppermute | solution.py:374
  16.7 27.1 %collective-permute-start.1 = (bf16[64,768]{1,0:T(8,128)(2,1)S(1)}, bf16[64,768]{1,0:T(8,128)(2,1)S(1)}, u32[]{:S(2)}, u32[]{:S(2)}) collective-permute-start(bf16[64,768]{1,0:T(8,128)(2,1)S(1)} %get-tuple-element.62), channel_id=1, source_target_pairs={{2,0},{3,1},{6,4},{7,5},{10,8},{11,9},{14,12},{15,13},{18,16},{19,... | collective-permute-start | bytes 294920 | tf_op jit(solution)/shard_map/ppermute | solution.py:374
  19.5 2.2 copy-start.14
  19.6 2.2 copy-start.15
  43.8 21.6 %copy-start.9 = (bf16[64,768]{1,0:T(8,128)(2,1)}, bf16[64,768]{1,0:T(8,128)(2,1)S(1)}, u32[]{:S(2)}) copy-start(bf16[64,768]{1,0:T(8,128)(2,1)S(1)} %collective-permute-done.before) | copy-start | bytes 294916
  43.8 21.6 %copy-start.10 = (bf16[64,768]{1,0:T(8,128)(2,1)}, bf16[64,768]{1,0:T(8,128)(2,1)S(1)}, u32[]{:S(2)}) copy-start(bf16[64,768]{1,0:T(8,128)(2,1)S(1)} %collective-permute-done.1.after) | copy-start | bytes 294916
  89.5 35.6 %collective-permute-start.2 = (bf16[1024,768]{1,0:T(8,128)(2,1)}, bf16[1024,768]{1,0:T(8,128)(2,1)S(1)}, u32[]{:S(2)}, u32[]{:S(2)}) collective-permute-start(bf16[1024,768]{1,0:T(8,128)(2,1)} %get-tuple-element.33.own), channel_id=1, source_target_pairs={{0,1},{1,0},{2,3},{3,2},{4,5},{5,4},{6,7},{7,6},{8,9},{9,8},{10,11... | collective-permute-start | bytes 4718600 | tf_op jit(solution)/shard_map/ppermute | solution.py:378
  153.4 143.3 %reduce-scatter.3.cloned.1.call-start = ((), (), s32[]{:S(2)}) async-start(), calls=%async_computation.2 | async-start | bytes 2654208 | tf_op jit(solution)/shard_map/reduce_scatter | solution.py:502
  154.8 3.4 collective-permute-start.3
  187.2 165.3 %all-reduce.4.cloned.1.call-start = ((), (), s32[]{:S(2)}) async-start(), calls=%async_computation.6 | async-start | bytes 1327104 | tf_op jit(solution)/shard_map/psum | solution.py:503
  188.7 135.6 %collective-permute-start.5 = (bf16[1024,768]{1,0:T(8,128)(2,1)S(1)}, bf16[1024,768]{1,0:T(8,128)(2,1)S(1)}, u32[]{:S(2)}, u32[]{:S(2)}) collective-permute-start(bf16[1024,768]{1,0:T(8,128)(2,1)S(1)} %copy-done.1), channel_id=1, source_target_pairs={{0,1},{1,0},{2,3},{3,2},{4,5},{5,4},{6,7},{7,6},{8,9},{9,8},{10,11... | collective-permute-start | bytes 4718600 | tf_op jit(solution)/shard_map/ppermute | solution.py:378
  188.8 107.9 %copy-start.16 = (u32[32]{0:T(128)S(1)}, u32[32]{0:T(128)}, u32[]{:S(2)}) copy-start(u32[32]{0:T(128)} %constant.34) | copy-start | bytes 388
  188.8 114.0 %copy-start.11 = (f32[1,768]{1,0:T(1,128)S(1)}, f32[1,768]{1,0:T(1,128)}, u32[]{:S(2)}) copy-start(f32[1,768]{1,0:T(1,128)} %get-tuple-element.55) | copy-start | bytes 9220
  197.1 144.0 %collective-permute-start.4 = (bf16[1024,768]{1,0:T(8,128)(2,1)}, bf16[1024,768]{1,0:T(8,128)(2,1)}, u32[]{:S(2)}, u32[]{:S(2)}) collective-permute-start(bf16[1024,768]{1,0:T(8,128)(2,1)} %get-tuple-element.44.own), channel_id=1, source_target_pairs={{0,1},{1,0},{2,3},{3,2},{4,5},{5,4},{6,7},{7,6},{8,9},{9,8},{10,11... | collective-permute-start | bytes 4718600 | tf_op jit(solution)/shard_map/ppermute | solution.py:378
  297.3 43.7 %collective-permute-start.6 = (bf16[64,768]{1,0:T(8,128)(2,1)}, bf16[64,768]{1,0:T(8,128)(2,1)S(1)}, u32[]{:S(2)}, u32[]{:S(2)}) collective-permute-start(bf16[64,768]{1,0:T(8,128)(2,1)} %get-tuple-element.50), channel_id=1, source_target_pairs={{0,2},{1,3},{4,6},{5,7},{8,10},{9,11},{12,14},{13,15},{16,18},{17,... | collective-permute-start | bytes 294920 | tf_op jit(solution)/shard_map/ppermute | solution.py:374
  300.7 40.3 %collective-permute-start.7 = (bf16[64,768]{1,0:T(8,128)(2,1)}, bf16[64,768]{1,0:T(8,128)(2,1)S(1)}, u32[]{:S(2)}, u32[]{:S(2)}) collective-permute-start(bf16[64,768]{1,0:T(8,128)(2,1)} %get-tuple-element.50), channel_id=1, source_target_pairs={{0,3},{1,2},{4,7},{5,6},{8,11},{9,10},{12,15},{13,14},{16,19},{17,... | collective-permute-start | bytes 294920 | tf_op jit(solution)/shard_map/ppermute | solution.py:374
  302.9 38.1 %collective-permute-start.8 = (bf16[64,768]{1,0:T(8,128)(2,1)}, bf16[64,768]{1,0:T(8,128)(2,1)S(1)}, u32[]{:S(2)}, u32[]{:S(2)}) collective-permute-start(bf16[64,768]{1,0:T(8,128)(2,1)} %get-tuple-element.51), channel_id=1, source_target_pairs={{2,0},{3,1},{6,4},{7,5},{10,8},{11,9},{14,12},{15,13},{18,16},{19,... | collective-permute-start | bytes 294920 | tf_op jit(solution)/shard_map/ppermute | solution.py:374
  324.3 16.8 %copy-start.2 = (bf16[1024,768]{1,0:T(8,128)(2,1)}, bf16[1024,768]{1,0:T(8,128)(2,1)S(1)}, u32[]{:S(2)}) copy-start(bf16[1024,768]{1,0:T(8,128)(2,1)S(1)} %collective-permute-done.5.feed_other) | copy-start | bytes 4718596
  324.3 16.8 %collective-permute-start.9 = (bf16[64,768]{1,0:T(8,128)(2,1)}, bf16[64,768]{1,0:T(8,128)(2,1)S(1)}, u32[]{:S(2)}, u32[]{:S(2)}) collective-permute-start(bf16[64,768]{1,0:T(8,128)(2,1)} %get-tuple-element.51), channel_id=1, source_target_pairs={{2,1},{3,0},{6,5},{7,4},{10,9},{11,8},{14,13},{15,12},{18,17},{19,... | collective-permute-start | bytes 294920 | tf_op jit(solution)/shard_map/ppermute | solution.py:374
  352.5 2.8 copy-start
  (8 other events, 7.9 us)
Sparse Core Ops, SparseCore 0:
  10.8 54.6 all-gather.6
  68.2 56.8 all-gather.8
  153.5 71.1 reduce-scatter.4
  228.5 68.1 reduce-scatter.2
  299.1 35.1 all-reduce.3

commit v2 on v1

--- a/solution.py
+++ b/solution.py
@@ -12,6 +12,7 @@
 WINDOW = 128
 NSEQ = 4
 HALF = WINDOW // 2
+PAD = 16
 BLOCK = 128
 LANES = 128
 KEYS = BLOCK + WINDOW
@@ -41,13 +42,15 @@
     vmem = pl.BlockSpec(memory_space=pltpu.VMEM)
     smem = pl.BlockSpec(memory_space=pltpu.SMEM)
     moved = sum(x.size * x.dtype.itemsize for x in (*args, *out_shape))
+    held = sum(math.prod(x.shape) * jnp.dtype(x.dtype).itemsize for x in kernel[1])
+    limit = min(56 * 2**20, (moved + held) * 9 // 8 + 8 * 2**20)
     return pl.pallas_call(
         kernel[0],
         out_shape=out_shape,
         in_specs=[smem] * len(scalars) + [vmem] * len(args),
         out_specs=[vmem] * len(out_shape),
         scratch_shapes=kernel[1],
-        compiler_params=pltpu.CompilerParams(vmem_limit_bytes=56 * 2**20),
+        compiler_params=pltpu.CompilerParams(vmem_limit_bytes=limit),
         cost_estimate=pl.CostEstimate(flops=flops, bytes_accessed=moved, transcendentals=0),
         name=name,
     )(*scalars, *args)
@@ -99,17 +102,25 @@
 
 
 def attend_kernel(
-    bounds, tokens, before, after, gain, weights, cosine, sine,
-    first, query, key, value, shares, attended, branch,
-    wide, out_t,
+    bounds, slots, tokens, before, after, cosine, sine, *rest
 ):
+    pieces, (wide, gain, first, query, key, value, shares, attended, branch) = rest[:-9], rest[-9:]
     rows, width = tokens.shape
     extent, local = key.shape
     pairs = local // LANES
-    for number in range(3):
-        stack_weight(weights, number, wide.at[number])
-    stack_weight(weights, 3, out_t)
-    gains = gain[...]
+    groups = len(pieces)
+    depth = width // groups
+    lane = lax.broadcasted_iota(jnp.int32, (LANES, width), 1) - lax.broadcasted_iota(jnp.int32, (LANES, width), 0)
+    gain_sum = jnp.zeros((PAD, width), f32)
+    for number, piece in enumerate(pieces):
+        place = pl.multiple_of(slots[number] * depth, depth)
+        for part in range(4):
+            wide[pl.ds(place, depth), part * local : (part + 1) * local] = piece[part * depth : (part + 1) * depth, :]
+        spread = jnp.where(lane == place, 1.0, 0.0).astype(bf16)
+        gain_sum += dot(piece[4 * depth :, :LANES], spread)
+    gain[...] = gain_sum
+    gains = gain_sum[:1]
+    query_w, key_w, value_w, out_t = (wide.at[:, part * local : (part + 1) * local] for part in range(4))
 
     def norm_rows(src, dst, size):
         hat, _ = normed(src.astype(f32))
@@ -137,8 +148,8 @@
     def key_step(index):
         at = pl.multiple_of(index * chunk, chunk)
         part = first[pl.ds(at, chunk), :]
-        rotated(dot(part, wide[1]), at, chunk, key, at, 1.0)
-        value[pl.ds(at, chunk), :] = dot(part, wide[2]).astype(bf16)
+        rotated(dot(part, key_w[...]), at, chunk, key, at, 1.0)
+        value[pl.ds(at, chunk), :] = dot(part, value_w[...]).astype(bf16)
 
     loop(extent // chunk, key_step)
     size = step_of(rows, 256)
@@ -146,7 +157,7 @@
     def query_step(index):
         at = pl.multiple_of(index * size, size)
         start = pl.multiple_of(at + HALF, HALF)
-        rotated(dot(first[pl.ds(start, size), :], wide[0]), start, size, query, at, HEAD**-0.5)
+        rotated(dot(first[pl.ds(start, size), :], query_w[...]), start, size, query, at, HEAD**-0.5)
 
     loop(rows // size, query_step)
     key_at = lax.broadcasted_iota(jnp.int32, (KEYS, KEYS), 0)
@@ -193,7 +204,7 @@
     stack_weight(weights, 0, gate_w)
     stack_weight(weights, 1, upper_w)
     stack_weight(weights, 2, down_t)
-    gains = gain[...]
+    gains = gain[1:2, :]
     size = step_of(rows, 256)
 
     def step(index):
@@ -235,33 +246,32 @@
     scatter_grads(cotangent, hidden, grads, 2, total)
 
 
-def scatter_grads(left, right, grads, number, total):
+def scatter_grads(left, right, grads, number, total, slots=None):
     width = left.shape[-1]
     parts, _, depth, _ = grads.shape
     for start in range(0, width, 2 * LANES):
         total[start : start + 2 * LANES, :] = dot(left[:, start : start + 2 * LANES], right[...], TN).astype(bf16)
     for part in range(parts):
-        grads[part, number] = total[part * depth : (part + 1) * depth, :]
+        place = part * depth if slots is None else pl.multiple_of(slots[part] * depth, depth)
+        grads[part, number] = total[pl.ds(place, depth), :]
 
 
 def back_kernel(
-    middle, own, other, gain, cotangent, weights, first, query, key, value, shares, attended, cosine, sine,
-    grad_middle, grad_proj, grads, gain_grad,
-    out_t, low_mid, grad_att, grad_key, grad_value, total,
+    slots, middle, own, other, gain, cotangent, wide, first, query, key, value, shares, attended, cosine, sine,
+    grad_middle, grad_proj, grads,
+    low_mid, grad_att, grad_key, grad_value, total,
 ):
     rows, width = middle.shape
     extent, local = key.shape
     pairs = local // LANES
-    stack_weight(weights, 3, out_t)
-    gains = gain[...]
+    out_t = wide.at[:, 3 * local :]
+    gains = gain[1:2, :]
     size = step_of(rows, 256)
-    gain_grad[...] = jnp.zeros_like(gain_grad)
 
     def norm_step(index):
         here = pl.ds(pl.multiple_of(index * size, size), size)
         hat, scale = normed(middle[here, :])
         grad = own[here, :].astype(f32) + other[here, :].astype(f32)
-        gain_grad[...] += jnp.sum(grad * hat, axis=0, keepdims=True)
         mid = cotangent[here, :].astype(f32) + norm_back(grad, gains, hat, scale)
         grad_middle[here, :] = mid
         mid_low = mid.astype(bf16)
@@ -310,72 +320,104 @@
 
     loop(extent // BLOCK, turn_step)
     for number in range(3):
-        scatter_grads(first, grad_proj.at[:, number * local : (number + 1) * local], grads, number, total)
-    scatter_grads(low_mid, attended, grads, 3, total)
-
-
-def first_kernel(grad_proj, weights, tokens, before, after, partial, front, behind, gain_grad, wide):
+        part = grad_proj.at[:, number * local : (number + 1) * local]
+        scatter_grads(first, part, grads, number, total, slots)
+    scatter_grads(low_mid, attended, grads, 3, total, slots)
+
+
+def first_kernel(grad_proj, wide, partial):
+    extent, inner = grad_proj.shape
+    size = step_of(extent, 384)
+
+    def step(index):
+        here = pl.ds(pl.multiple_of(index * size, size), size)
+        partial[here, :] = dot(grad_proj[here, :], wide[:, :inner], NT).astype(bf16)
+
+    loop(extent // size, step)
+
+
+def final_kernel(tokens, gain, grad_middle, own, other, before, after, middle, feed_own, feed_other, mixed, token_grad):
     rows, width = tokens.shape
-    extent = grad_proj.shape[0]
-    local = weights.shape[-1]
-    for number in range(3):
-        stack_weight(weights, number, wide.at[:, number * local : (number + 1) * local])
-    gain_grad[...] = jnp.zeros_like(gain_grad)
-
-    def part(at, values, size):
-        grad = dot(grad_proj[pl.ds(at, size), :], wide[...], NT)
-        hat, _ = normed(values.astype(f32))
-        gain_grad[...] += jnp.sum(grad * hat, axis=0, keepdims=True)
-        return grad.astype(bf16)
-
-    front[...] = part(0, before[...], HALF)
-    behind[...] = part(rows + HALF, after[...], HALF)
-    size = step_of(rows, 256)
+    gains = gain[:1, :]
+    size = BLOCK
+
+    def back(here, grad):
+        hat, scale = normed(tokens[here, :].astype(f32))
+        return norm_back(grad, gains, hat, scale)
 
     def step(index):
         at = pl.multiple_of(index * size, size)
-        here = pl.ds(at, size)
-        partial[here, :] = part(pl.multiple_of(at + HALF, HALF), tokens[here, :], size)
-
-    loop(rows // size, step)
-
-
-def final_kernel(tokens, gain, grad_middle, own, other, middle, feed_own, feed_other, *rest):
-    edges, (mixed, token_grad) = rest[:4], rest[4:]
-    rows, width = tokens.shape
-    gains = gain[...]
-    size = BLOCK
-
-    def back(here, values, grad):
-        hat, scale = normed(values)
-        return norm_back(grad, gains, hat, scale)
-
-    def step(index):
-        here = pl.ds(pl.multiple_of(index * size, size), size)
-        grad = own[here, :].astype(f32) + other[here, :].astype(f32)
-        token_grad[here, :] = grad_middle[here, :] + back(here, tokens[here, :].astype(f32), grad)
+        here, wider = pl.ds(at, size), pl.ds(pl.multiple_of(at + HALF, HALF), size)
+        grad = own[wider, :].astype(f32) + other[wider, :].astype(f32)
+        token_grad[here, :] = grad_middle[here, :] + back(here, grad)
         feed = feed_own[here, :].astype(f32) + feed_other[here, :].astype(f32)
         mixed[here, :] = (middle[here, :] + feed).astype(bf16)
 
     loop(rows // size, step)
-    for start, one, two in ((0, edges[0], edges[1]), (rows - HALF, edges[2], edges[3])):
+    for start, edge in ((0, before), (rows - HALF, after)):
         here = pl.ds(start, HALF)
-        grad = one[...].astype(f32) + two[...].astype(f32)
-        token_grad[here, :] += back(here, tokens[here, :].astype(f32), grad)
-
-
-def edge(array, by, cross):
-    devices, cores = lax.axis_size("ctx"), lax.axis_size("tensor")
-    pairs = []
-    for i in range(devices):
-        if 0 <= i + by < devices:
-            for c in range(cores):
-                pairs.append((i * cores + c, (i + by) * cores + (c + cross) % cores))
-    return lax.ppermute(array, ("ctx", "tensor"), pairs)
-
-
-def swap(array):
-    return lax.ppermute(array, "tensor", [(0, 1), (1, 0)])
+        token_grad[here, :] += back(here, edge[...].astype(f32))
+
+
+def exchange(initial, last):
+    devices, spot = lax.axis_size("ctx"), lax.axis_index("ctx")
+    if devices == 2:
+        got = lax.ppermute(jnp.where(spot == 0, last, initial), "ctx", [(0, 1), (1, 0)])
+        none = jnp.zeros_like(got)
+        return jnp.where(spot == 1, got, none), jnp.where(spot == 0, got, none)
+    up = [(i, i + 1) for i in range(devices - 1)]
+    return lax.ppermute(last, "ctx", up), lax.ppermute(initial, "ctx", [(j, i) for i, j in up])
+
+
+def swap(array, axis="tensor"):
+    return lax.ppermute(array, axis, [(0, 1), (1, 0)])
+
+
+def over_ctx(array):
+    if lax.axis_size("ctx") == 2:
+        return array.astype(f32) + swap(array, "ctx").astype(f32)
+    return lax.psum(array, "ctx").astype(f32)
+
+
+def ring():
+    count = lax.axis_size("dp")
+    order = [2 * i for i in range(count // 2)] + [2 * i + 1 for i in reversed(range(count // 2))]
+    ahead = [(order[i], order[(i + 1) % count]) for i in range(count)]
+    back = [(j, i) for i, j in ahead]
+    index = lax.axis_index("dp")
+    spot = jnp.where(index % 2 == 0, index // 2, count - 1 - index // 2)
+    place = (spot + jnp.arange(count, dtype=jnp.int32)) % count
+    slots = jnp.where(place < count // 2, 2 * place, 2 * (count - 1 - place) + 1)
+    return count, ahead, back, slots.astype(jnp.int32)
+
+
+def ring_gather(mine):
+    count, ahead, back, _ = ring()
+    middle = count // 2
+    half = mine.shape[0] // 2
+    pieces = {0: mine}
+    one = two = mine
+    for hop in range(1, middle):
+        one, two = lax.ppermute(one, "dp", ahead), lax.ppermute(two, "dp", back)
+        pieces[count - hop], pieces[hop] = one, two
+    pieces[middle] = jnp.concatenate(
+        [lax.ppermute(one[:half], "dp", ahead), lax.ppermute(two[half:], "dp", back)]
+    )
+    return [pieces[i] for i in range(count)]
+
+
+def ring_scatter(parts):
+    count, ahead, back, _ = ring()
+    middle = count // 2
+    half = parts.shape[1] // 2
+    one = lax.ppermute(parts[middle, :half], "dp", ahead)
+    two = lax.ppermute(parts[middle, half:], "dp", back)
+    none = jnp.zeros_like(one)
+    one, two = jnp.concatenate([one, none]), jnp.concatenate([none, two])
+    for hop in range(middle - 1, 0, -1):
+        one = lax.ppermute(parts[hop] + one, "dp", ahead)
+        two = lax.ppermute(parts[count - hop] + two, "dp", back)
+    return (parts[0].astype(f32) + one.astype(f32) + two.astype(f32)).astype(bf16)
 
 
 def tables(lengths, rows):
@@ -399,20 +441,21 @@
     local, units = w_out.shape[0], w_down.shape[0]
     pairs, blocks, extent = local // LANES, rows // BLOCK, rows + WINDOW
     groups = lax.axis_size("dp")
-    gains = lax.all_gather(jnp.stack([gain_one, gain_two]), "dp", axis=0, tiled=False)
-    mine_one = jnp.concatenate([w_qkv, w_out.T[None]])
+    depth = width // groups
+    gains = jnp.pad(jnp.stack([gain_one, gain_two]), ((0, PAD - 2), (0, local - depth)))
+    mine_one = jnp.concatenate([w_qkv.reshape(3 * depth, local), w_out.T, gains])
     mine_two = jnp.concatenate([w_in, w_down.T[None]])
-    weights_one = lax.all_gather(mine_one, "dp", axis=0, tiled=False)
+    pieces = ring_gather(mine_one)
+    slots = ring()[-1]
     weights_two = lax.all_gather(mine_two, "dp", axis=0, tiled=False)
-    norm_one = gains[:, 0].reshape(1, width).astype(f32)
-    norm_two = gains[:, 1].reshape(1, width).astype(f32)
-    before = edge(tokens[rows - HALF :], 1, 0)
-    after = edge(tokens[:HALF], -1, 0)
+    before, after = exchange(tokens[:HALF], tokens[rows - HALF :])
     cosine, sine, bounds = tables(lengths, rows)
 
-    first, query, key, value, shares, attended, branch = call(
-        (attend_kernel, [pltpu.VMEM((3, width, local), bf16), pltpu.VMEM((width, local), bf16)]),
+    wide, gain, first, query, key, value, shares, attended, branch = call(
+        (attend_kernel, []),
         [
+            shape((width, 4 * local), bf16),
+            shape((PAD, width), f32),
             shape((extent, width), bf16),
             shape((rows, local), bf16),
             shape((extent, local), bf16),
@@ -421,10 +464,10 @@
             shape((rows, local), bf16),
             shape((rows, width), bf16),
         ],
-        (tokens, before, after, norm_one, weights_one, cosine, sine),
+        (tokens, before, after, cosine, sine, *pieces),
         2 * rows * width * local * 5,
         "project_and_attend",
-        (bounds,),
+        (bounds, slots),
     )
     branch_other = swap(branch)
     plain = [pltpu.VMEM((width, units), bf16)] * 3
@@ -438,7 +481,7 @@
             shape((rows, units), bf16),
             shape((rows, width), bf16),
         ],
-        (tokens, branch, branch_other, norm_two, weights_two, cotangent),
+        (tokens, branch, branch_other, gain, weights_two, cotangent),
         2 * rows * width * units * 5,
         "feed_forward_and_back",
     )
@@ -451,11 +494,10 @@
         "feed_weight_grads",
     )
     feed_other = swap(feed)
-    grad_middle, grad_proj, grads_one, grad_gain_two = call(
+    grad_middle, grad_proj, grads_one = call(
         (
             back_kernel,
             [
-                pltpu.VMEM((width, local), bf16),
                 pltpu.VMEM((rows, width), bf16),
                 pltpu.VMEM((rows, local), bf16),
                 pltpu.VMEM((extent, local), f32),
@@ -466,49 +508,46 @@
         [
             shape((rows, width), f32),
             shape((extent, 3 * local), bf16),
-            shape((groups, 4, width // groups, local), bf16),
-            shape((1, width), f32),
+            shape((groups, 4, depth, local), bf16),
         ],
         (
-            middle, partial, partial_other, norm_two, cotangent, weights_one, first, query, key, value, shares,
-            attended, cosine, sine,
+            middle, partial, partial_other, gain, cotangent, wide, first, query, key, value, shares, attended,
+            cosine, sine,
         ),
         2 * rows * width * local * 6,
         "attention_back",
-    )
-    first_part, front, behind, grad_gain_one = call(
-        (first_kernel, [pltpu.VMEM((width, 3 * local), bf16)]),
-        [
-            shape((rows, width), bf16),
-            shape((HALF, width), bf16),
-            shape((HALF, width), bf16),
-            shape((1, width), f32),
-        ],
-        (grad_proj, weights_one, tokens, before, after),
+        (slots,),
+    )
+    one = over_ctx(ring_scatter(grads_one.reshape(groups, 4 * depth, local))).reshape(4, depth, local)
+    two = over_ctx(lax.psum_scatter(grads_two, "dp", scatter_dimension=0, tiled=False))
+    first_part, = call(
+        (first_kernel, []),
+        [shape((extent, width), bf16)],
+        (grad_proj, wide),
         2 * rows * width * local * 3,
         "first_grad",
     )
     first_other = swap(first_part)
-    edges = [edge(behind, 1, 0), edge(behind, 1, 1), edge(front, -1, 0), edge(front, -1, 1)]
+
+    def edge_sum(at):
+        here = slice(at, at + HALF)
+        return (first_part[here].astype(f32) + first_other[here].astype(f32)).astype(bf16)
+
+    from_before, from_after = exchange(edge_sum(0), edge_sum(rows + HALF))
     mixed, token_grad = call(
         (final_kernel, []),
         [shape((rows, width), bf16), shape((rows, width), f32)],
-        (tokens, norm_one, grad_middle, first_part, first_other, middle, feed, feed_other, *edges),
+        (
+            tokens, gain, grad_middle, first_part, first_other, from_before, from_after, middle, feed, feed_other,
+        ),
         rows * width * 20,
         "token_grad",
     )
-
-    def reduced(grads):
-        part = lax.psum_scatter(grads, "dp", scatter_dimension=0, tiled=False)
-        return lax.psum(part, "ctx")
-
-    two = reduced(grads_two).astype(f32)
-    one = reduced(grads_one).astype(f32)
-    gain_grads = jnp.stack([grad_gain_one.reshape(groups, -1), grad_gain_two.reshape(groups, -1)], axis=1)
-    both = lax.psum_scatter(gain_grads, "dp", scatter_dimension=0, tiled=False)
-    gain_one_grad = lax.psum(both[0], ("ctx", "tensor"))
-    gain_two_grad = lax.psum(both[1], "ctx")
-    return (mixed, token_grad, gain_one_grad, one[:3], one[3].T, gain_two_grad, two[:2], two[2].T)
+    gain_one_grad = jnp.sum(one[:3] * w_qkv.astype(f32), axis=(0, 2)) / gain_one.astype(f32)
+    gain_two_grad = jnp.sum(two[:2] * w_in.astype(f32), axis=(0, 2)) / gain_two.astype(f32)
+    both = jnp.stack([gain_one_grad, gain_two_grad])
+    both = both + swap(both)
+    return (mixed, token_grad, both[0], one[:3], one[3].T, both[1], two[:2], two[2].T)
 
 
 def solution(mesh):

time: 365 us -> 252 us (0.69)
  waiting for transfers between devices: 159 us -> 76.4 us
  blocking collectives: 55.5 us -> 0 us
  local copies, waits for them, and re-layouts: 15.4 us -> 46.6 us
  Pallas kernels: 98.1 us -> 76.3 us
  starting transfers between devices: 14.4 us -> 25.8 us
  other arithmetic: 7.42 us -> 11.1 us
    reduce_scatter x2 -> x1, waiting for transfers between devices: 99.1 us -> 0.01 us  [body(): lax.psum_scatter(grads_two, 'dp', scatter_dimension=0, tiled=False)]
    ppermute x10 -> x25, waiting for transfers between devices: 3.43 us -> 76.4 us  [the longest x3 23.9 us: ring_scatter(): one = lax.ppermute(parts[hop] + one, 'dp', ahead)]
    all_gather x1, waiting for transfers between devices: 35 us -> 0.01 us  [body(): weights_two = lax.all_gather(mine_two, 'dp', axis=0, tiled=False)]
    unnamed x36 -> x98, local copies, waits for them, and re-layouts: 6.81 us -> 34.8 us
    pallas_call x6, Pallas kernels: 98.1 us -> 76.3 us  [call(): pl.pallas_call(kernel[0], out_shape=out_shape, in_specs=[smem] * len(scal...]
    all_gather x1 -> x0, waiting for transfers between devices: 21.6 us -> none  [body(): weights_one = lax.all_gather(mine_one, 'dp', axis=0, tiled=False)]
    all_gather x1 -> x0, blocking collectives: 20.7 us -> none  [body(): lax.all_gather(jnp.stack([gain_one, gain_two]), 'dp', axis=0, tiled=False)]
    unnamed x1 -> x0, blocking collectives: 19.4 us -> none
  transfers between devices with their start and end apart: 15 -> 27, of which waited for: 5 -> 14; matrix products, arithmetic and copies ran while one was open for 3% -> 8% of each run, Pallas kernels for 19% -> 26%
where the time goes in v2:
time: 252 us; the launch traced here: 251 us
  waiting for transfers between devices  76.4 us (30%)
  Pallas kernels  76.3 us (30%)
  local copies, waits for them, and re-layouts  46.6 us (18%)
  starting transfers between devices  25.8 us (10%)
  between operations  14.5 us (6%)
  other arithmetic  11.1 us (4%)
    pallas_call x6, Pallas kernels, call(): pl.pallas_call(kernel[0], out_shape=out_shape, in_specs=[smem] * len(scal...  76.3 us
    unnamed x98, local copies, waits for them, and re-layouts  34.8 us
    ppermute x3, waiting for transfers between devices, ring_scatter(): one = lax.ppermute(parts[hop] + one, 'dp', ahead)  23.9 us
    ppermute x6, waiting for transfers between devices, ring_gather(): one, two = (lax.ppermute(one, 'dp', ahead), lax.ppermute(two, 'dp', back))  18.5 us
    ppermute x6, starting transfers between devices, ring_gather(): one, two = (lax.ppermute(one, 'dp', ahead), lax.ppermute(two, 'dp', back))  8.98 us
    ppermute x7, waiting for transfers between devices, swap(): return lax.ppermute(array, axis, [(0, 1), (1, 0)])  8.22 us
    ppermute x1, waiting for transfers between devices, ring_gather(): lax.ppermute(two[half:], 'dp', back)  7.63 us
    ppermute x3, waiting for transfers between devices, ring_scatter(): two = lax.ppermute(parts[count - hop] + two, 'dp', back)  6.37 us
  transfers between devices with their start and end apart: 27, of which 14 were waited for; matrix products, arithmetic and copies ran while one was open for 8% of the time, Pallas kernels for 26%

profile of v2, /device:TPU:0, one launch (start us, length us, event | category | flops | bytes accessed | tf_op | source)
XLA Modules:
  0.0 250.8 jit_solution(11173387224660446454)
XLA Ops:
  10.9 3.1 %collective-permute-start.4 = (bf16[400,384]{1,0:T(8,128)(2,1)S(1)}, bf16[400,384]{1,0:T(8,128)(2,1)S(1)}, u32[]{:S(2)}, u32[]{:S(2)}) collective-permute-start(bf16[400,384]{1,0:T(8,128)(2,1)S(1)} %pad_maximum_fusion.1.rest_0_), channel_id=1, source_target_pairs={{0,8},{8,16},{16,24},{24,28},{28,20},{20,12},{12,4},{4,0},{1,9},{9... | collective-permute-start | bytes 921608 | tf_op jit(solution)/shard_map/ppermute | solution.py:401
  14.7 2.0 collective-permute-start
  16.9 4.3 %collective-permute-done.4.rest_7_ = bf16[400,384]{1,0:T(8,128)(2,1)S(1)} collective-permute-done((bf16[400,384]{1,0:T(8,128)(2,1)S(1)}, bf16[400,384]{1,0:T(8,128)(2,1)S(1)}, u32[]{:S(2)}, u32[]{:S(2)}) %collective-permute-start.4) | collective-permute-done | bytes 307232 | tf_op jit(solution)/shard_map/ppermute | solution.py:401
  23.2 13.2 %collective-permute-done.5.rest_6_ = bf16[400,384]{1,0:T(8,128)(2,1)} collective-permute-done((bf16[400,384]{1,0:T(8,128)(2,1)S(1)}, bf16[400,384]{1,0:T(8,128)(2,1)}, u32[]{:S(2)}, u32[]{:S(2)}) %collective-permute-start.5) | collective-permute-done | bytes 307232 | tf_op jit(solution)/shard_map/ppermute | solution.py:401
  36.4 3.9 %collective-permute-start.6 = (bf16[400,384]{1,0:T(8,128)(2,1)}, bf16[400,384]{1,0:T(8,128)(2,1)S(1)}, u32[]{:S(2)}, u32[]{:S(2)}) collective-permute-start(bf16[400,384]{1,0:T(8,128)(2,1)} %collective-permute-done.5.rest_6_), channel_id=1, source_target_pairs={{0,8},{8,16},{16,24},{24,28},{28,20},{20,12},{12,4},{4,0},{1,9},{9... | collective-permute-start | bytes 921608 | tf_op jit(solution)/shard_map/ppermute | solution.py:401
  49.7 2.4 collective-permute-start.7
  53.3 4.8 %collective-permute-done.7 = bf16[200,384]{1,0:T(8,128)(2,1)S(1)} collective-permute-done((bf16[200,384]{1,0:T(8,128)(2,1)S(1)}, bf16[200,384]{1,0:T(8,128)(2,1)S(1)}, u32[]{:S(2)}, u32[]{:S(2)}) %collective-permute-start.7) | collective-permute-done | bytes 153632 | tf_op jit(solution)/shard_map/ppermute | solution.py:404
  58.1 7.6 %collective-permute-done.8 = bf16[200,384]{1,0:T(8,128)(2,1)S(1)} collective-permute-done((bf16[200,384]{1,0:T(8,128)(2,1)S(1)}, bf16[200,384]{1,0:T(8,128)(2,1)S(1)}, u32[]{:S(2)}, u32[]{:S(2)}) %collective-permute-start.8) | collective-permute-done | bytes 153632 | tf_op jit(solution)/shard_map/ppermute | solution.py:404
  70.6 19.5 %project_and_attend.1 = (bf16[768,1536]{1,0:T(8,128)(2,1)S(1)}, f32[16,768]{1,0:T(8,128)S(1)}, bf16[1152,768]{1,0:T(8,128)(2,1)S(1)}, bf16[1024,384]{1,0:T(8,128...) custom-call(s32[5]{0:T(128)S(1)} %pad_add_fusion.bounds, ...), custom_call_target="tpu_custom_call" | custom-call | flops 3019898880 | bytes 17645568 | tf_op jit(solution)/shard_map/project_and_attend/pallas_call | solution.py:47
  98.8 2.3 collective-permute-done.9.other
  109.1 10.6 %feed_forward_and_back.1 = (f32[1024,768]{1,0:T(8,128)S(1)}, bf16[1024,768]{1,0:T(8,128)(2,1)S(1)}, bf16[1024,576]{1,0:T(8,128)(2,1)S(1)}, bf16[1024,576]{1,0:T(...) custom-call(bf16[1024,768]{1,0:T(8,128)(2,1)S(1)} %copy-done.11, ...), custom_call_target="tpu_custom_call" | custom-call | flops 4529848320 | bytes 18825216 | tf_op jit(solution)/shard_map/feed_forward_and_back/pallas_call | solution.py:47
  119.9 8.2 %feed_weight_grads.1 = (bf16[1024,768]{1,0:T(8,128)(2,1)}, bf16[8,3,96,576]{3,2,1,0:T(8,128)(2,1)}) custom-call(bf16[1024,768]{1,0:T(8,128)(2,1)S(1)} %get-tuple-element.43.second, bf16[1024,576]{1,0:T(8,128)(2,1)S(1)} %get-tuple-element.44.hidden, bf16[1024,576]{1,0:T(8,128)(2,1)S(1)} %get-tuple-element.45.grad_gate, ...), custom_call_target="tpu_custom_call" | custom-call | flops 3623878656 | bytes 13565952 | tf_op jit(solution)/shard_map/feed_weight_grads/pallas_call | solution.py:47
  133.8 27.2 %attention_back.1 = (f32[1024,768]{1,0:T(8,128)}, bf16[1152,1152]{1,0:T(8,128)(2,1)}, bf16[8,4,96,384]{3,2,1,0:T(8,128)(2,1)}) custom-call(s32[8]{0:T(128)S(1)} %compare_select_fusion.2.slots, f32[1024,768]{1,0:T(8,128)} %copy-done, bf16[1024,768]{1,0:T(8,128)(2,1)} %get-tuple-element.33.own, bf16[1024,768]{1,0:T(8,128)(2,1)} %collective-permute-done.10.other, ...), custom_call_target="tpu_custom_call" | custom-call | flops 3623878656 | bytes 27869184 | tf_op jit(solution)/shard_map/attention_back/pallas_call | solution.py:47
  166.1 4.3 %collective-permute-done.14 = bf16[192,384]{1,0:T(8,128)(2,1)S(1)} collective-permute-done((bf16[192,384]{1,0:T(8,128)(2,1)S(1)}, bf16[192,384]{1,0:T(8,128)(2,1)S(1)}, u32[]{:S(2)}, u32[]{:S(2)}) %collective-permute-start.14) | collective-permute-done | bytes 147488 | tf_op jit(solution)/shard_map/ppermute | solution.py:413
  170.6 2.1 collective-permute-start.19
  172.6 10.1 %collective-permute-done.15 = bf16[384,384]{1,0:T(8,128)(2,1)S(1)} collective-permute-done((bf16[384,384]{1,0:T(8,128)(2,1)S(1)}, bf16[384,384]{1,0:T(8,128)(2,1)S(1)}, u32[]{:S(2)}, u32[]{:S(2)}) %collective-permute-start.15) | collective-permute-done | bytes 294944 | tf_op jit(solution)/shard_map/ppermute | solution.py:418
  183.0 2.1 collective-permute-start.20
  185.0 2.9 %first_grad.1.own = bf16[1152,768]{1,0:T(8,128)(2,1)S(1)} custom-call(bf16[1152,1152]{1,0:T(8,128)(2,1)S(1)} %copy-done.8, bf16[768,1536]{1,0:T(8,128)(2,1)S(1)} %copy-done.3), custom_call_target="tpu_custom_call" | custom-call | flops 1811939328 | bytes 6782976 | tf_op jit(solution)/shard_map/first_grad/pallas_call | solution.py:47
  188.1 2.9 %collective-permute-done.16 = bf16[384,384]{1,0:T(8,128)(2,1)S(1)} collective-permute-done((bf16[384,384]{1,0:T(8,128)(2,1)S(1)}, bf16[384,384]{1,0:T(8,128)(2,1)S(1)}, u32[]{:S(2)}, u32[]{:S(2)}) %collective-permute-start.16) | collective-permute-done | bytes 294944 | tf_op jit(solution)/shard_map/ppermute | solution.py:418
  193.4 10.8 %collective-permute-done.17 = bf16[384,384]{1,0:T(8,128)(2,1)S(1)} collective-permute-done((bf16[384,384]{1,0:T(8,128)(2,1)S(1)}, bf16[384,384]{1,0:T(8,128)(2,1)S(1)}, u32[]{:S(2)}, u32[]{:S(2)}) %collective-permute-start.17) | collective-permute-done | bytes 294944 | tf_op jit(solution)/shard_map/ppermute | solution.py:418
  204.2 6.4 %collective-permute-done.21 = bf16[384,384]{1,0:T(8,128)(2,1)S(1)} collective-permute-done((bf16[384,384]{1,0:T(8,128)(2,1)S(1)}, bf16[384,384]{1,0:T(8,128)(2,1)S(1)}, u32[]{:S(2)}, u32[]{:S(2)}) %collective-permute-start.21) | collective-permute-done | bytes 294944 | tf_op jit(solution)/shard_map/ppermute | solution.py:419
  212.0 5.5 %collective-permute-done.22 = bf16[384,384]{1,0:T(8,128)(2,1)S(1)} collective-permute-done((bf16[384,384]{1,0:T(8,128)(2,1)S(1)}, bf16[384,384]{1,0:T(8,128)(2,1)S(1)}, u32[]{:S(2)}, u32[]{:S(2)}) %collective-permute-start.22) | collective-permute-done | bytes 294944 | tf_op jit(solution)/shard_map/ppermute | solution.py:373
  224.2 2.8 %collective-permute-done.12 = bf16[64,768]{1,0:T(8,128)(2,1)S(1)} collective-permute-done((bf16[64,768]{1,0:T(8,128)(2,1)}, bf16[64,768]{1,0:T(8,128)(2,1)S(1)}, u32[]{:S(2)}, u32[]{:S(2)}) %collective-permute-start.12) | collective-permute-done | bytes 98336 | tf_op jit(solution)/shard_map/ppermute | solution.py:365
  233.3 7.8 %token_grad.1 = (bf16[1024,768]{1,0:T(8,128)(2,1)}, f32[1024,768]{1,0:T(8,128)}) custom-call(bf16[1024,768]{1,0:T(8,128)(2,1)S(1)} %copy-done.12, f32[16,768]{1,0:T(8,128)S(1)} %copy-done.28, f32[1024,768]{1,0:T(8,128)S(1)} %copy-done.7, bf16[1152,768]{1,0:T(8,128)(2,1)S(1)} %copy-done.5, bf16[1152,768]{1,0:T(8,128)(2,1)S(1)} %copy-done.10, ...), custom_call_target="tpu_custom_call" | custom-call | flops 15728640 | bytes 19513344 | tf_op jit(solution)/shard_map/token_grad/pallas_call | solution.py:47
  (180 shorter events, 69.6 us)
Async XLA Ops:
  7.2 95.1 %all-gather.3.cloned.1.call-start = ((), (), s32[]{:S(2)}) async-start(), calls=%async_computation.2 | async-start | bytes 3317760 | tf_op jit(solution)/shard_map/all_gather | solution.py:450
  9.2 213.5 %reduce-scatter.2.cloned.1.call-start = ((), (), s32[]{:S(2)}) async-start(), calls=%async_computation.1 | async-start | bytes 3317760 | tf_op jit(solution)/shard_map/reduce_scatter | solution.py:522
  10.9 10.3 %collective-permute-start.4 = (bf16[400,384]{1,0:T(8,128)(2,1)S(1)}, bf16[400,384]{1,0:T(8,128)(2,1)S(1)}, u32[]{:S(2)}, u32[]{:S(2)}) collective-permute-start(bf16[400,384]{1,0:T(8,128)(2,1)S(1)} %pad_maximum_fusion.1.rest_0_), channel_id=1, source_target_pairs={{0,8},{8,16},{16,24},{24,28},{28,20},{20,12},{12,4},{4,0},{1,9},{9... | collective-permute-start | bytes 921608 | tf_op jit(solution)/shard_map/ppermute | solution.py:401
  14.0 9.0 %collective-permute-start.1 = (bf16[400,384]{1,0:T(8,128)(2,1)S(1)}, bf16[400,384]{1,0:T(8,128)(2,1)S(1)}, u32[]{:S(2)}, u32[]{:S(2)}) collective-permute-start(bf16[400,384]{1,0:T(8,128)(2,1)S(1)} %pad_maximum_fusion.1.rest_0_), channel_id=1, source_target_pairs={{8,0},{16,8},{24,16},{28,24},{20,28},{12,20},{4,12},{0,4},{9,1},{1... | collective-permute-start | bytes 921608 | tf_op jit(solution)/shard_map/ppermute | solution.py:401
  14.7 37.7 %collective-permute-start = (bf16[64,768]{1,0:T(8,128)(2,1)}, bf16[64,768]{1,0:T(8,128)(2,1)}, u32[]{:S(2)}, u32[]{:S(2)}) collective-permute-start(bf16[64,768]{1,0:T(8,128)(2,1)} %slice_select_fusion), channel_id=1, source_target_pairs={{0,2},{2,0},{1,3},{3,1},{4,6},{6,4},{5,7},{7,5},{8,10},{10,8},{9,1... | collective-permute-start | bytes 294920 | tf_op jit(solution)/shard_map/ppermute | solution.py:365
  21.2 15.2 %collective-permute-start.5 = (bf16[400,384]{1,0:T(8,128)(2,1)S(1)}, bf16[400,384]{1,0:T(8,128)(2,1)}, u32[]{:S(2)}, u32[]{:S(2)}) collective-permute-start(bf16[400,384]{1,0:T(8,128)(2,1)S(1)} %collective-permute-done.4.rest_7_), channel_id=1, source_target_pairs={{0,8},{8,16},{16,24},{24,28},{28,20},{20,12},{12,4},{4,0},{1,9},{9... | collective-permute-start | bytes 921608 | tf_op jit(solution)/shard_map/ppermute | solution.py:401
  23.0 18.3 %collective-permute-start.2 = (bf16[400,384]{1,0:T(8,128)(2,1)S(1)}, bf16[400,384]{1,0:T(8,128)(2,1)}, u32[]{:S(2)}, u32[]{:S(2)}) collective-permute-start(bf16[400,384]{1,0:T(8,128)(2,1)S(1)} %collective-permute-done.1.rest_1_), channel_id=1, source_target_pairs={{8,0},{16,8},{24,16},{28,24},{20,28},{12,20},{4,12},{0,4},{9,1},{1... | collective-permute-start | bytes 921608 | tf_op jit(solution)/shard_map/ppermute | solution.py:401
  36.4 13.2 %collective-permute-start.6 = (bf16[400,384]{1,0:T(8,128)(2,1)}, bf16[400,384]{1,0:T(8,128)(2,1)S(1)}, u32[]{:S(2)}, u32[]{:S(2)}) collective-permute-start(bf16[400,384]{1,0:T(8,128)(2,1)} %collective-permute-done.5.rest_6_), channel_id=1, source_target_pairs={{0,8},{8,16},{16,24},{24,28},{28,20},{20,12},{12,4},{4,0},{1,9},{9... | collective-permute-start | bytes 921608 | tf_op jit(solution)/shard_map/ppermute | solution.py:401
  41.3 10.7 %collective-permute-start.3 = (bf16[400,384]{1,0:T(8,128)(2,1)}, bf16[400,384]{1,0:T(8,128)(2,1)S(1)}, u32[]{:S(2)}, u32[]{:S(2)}) collective-permute-start(bf16[400,384]{1,0:T(8,128)(2,1)} %collective-permute-done.2.rest_2_), channel_id=1, source_target_pairs={{8,0},{16,8},{24,16},{28,24},{20,28},{12,20},{4,12},{0,4},{9,1},{1... | collective-permute-start | bytes 921608 | tf_op jit(solution)/shard_map/ppermute | solution.py:401
  49.7 8.4 %collective-permute-start.7 = (bf16[200,384]{1,0:T(8,128)(2,1)S(1)}, bf16[200,384]{1,0:T(8,128)(2,1)S(1)}, u32[]{:S(2)}, u32[]{:S(2)}) collective-permute-start(bf16[200,384]{1,0:T(8,128)(2,1)S(1)} %slice.106), channel_id=1, source_target_pairs={{0,8},{8,16},{16,24},{24,28},{28,20},{20,12},{12,4},{4,0},{1,9},{9... | collective-permute-start | bytes 460808 | tf_op jit(solution)/shard_map/ppermute | solution.py:404
  52.1 13.6 %collective-permute-start.8 = (bf16[200,384]{1,0:T(8,128)(2,1)S(1)}, bf16[200,384]{1,0:T(8,128)(2,1)S(1)}, u32[]{:S(2)}, u32[]{:S(2)}) collective-permute-start(bf16[200,384]{1,0:T(8,128)(2,1)S(1)} %slice.107), channel_id=1, source_target_pairs={{8,0},{16,8},{24,16},{28,24},{20,28},{12,20},{4,12},{0,4},{9,1},{1... | collective-permute-start | bytes 460808 | tf_op jit(solution)/shard_map/ppermute | solution.py:404
  119.8 8.4 %collective-permute-start.10 = (bf16[1024,768]{1,0:T(8,128)(2,1)}, bf16[1024,768]{1,0:T(8,128)(2,1)}, u32[]{:S(2)}, u32[]{:S(2)}) collective-permute-start(bf16[1024,768]{1,0:T(8,128)(2,1)} %get-tuple-element.33.own), channel_id=1, source_target_pairs={{0,1},{1,0},{2,3},{3,2},{4,5},{5,4},{6,7},{7,6},{8,9},{9,8},{10,11... | collective-permute-start | bytes 4718600 | tf_op jit(solution)/shard_map/ppermute | solution.py:373
  162.0 8.3 %collective-permute-start.14 = (bf16[192,384]{1,0:T(8,128)(2,1)S(1)}, bf16[192,384]{1,0:T(8,128)(2,1)S(1)}, u32[]{:S(2)}, u32[]{:S(2)}) collective-permute-start(bf16[192,384]{1,0:T(8,128)(2,1)S(1)} %get-tuple-element.61), channel_id=1, source_target_pairs={{0,8},{8,16},{16,24},{24,28},{28,20},{20,12},{12,4},{4,0},{1,9},{9... | collective-permute-start | bytes 442376 | tf_op jit(solution)/shard_map/ppermute | solution.py:413
  163.7 6.8 %collective-permute-start.18 = (bf16[192,384]{1,0:T(8,128)(2,1)S(1)}, bf16[192,384]{1,0:T(8,128)(2,1)S(1)}, u32[]{:S(2)}, u32[]{:S(2)}) collective-permute-start(bf16[192,384]{1,0:T(8,128)(2,1)S(1)} %get-tuple-element.62), channel_id=1, source_target_pairs={{8,0},{16,8},{24,16},{28,24},{20,28},{12,20},{4,12},{0,4},{9,1},{1... | collective-permute-start | bytes 442376 | tf_op jit(solution)/shard_map/ppermute | solution.py:414
  170.4 12.3 %collective-permute-start.15 = (bf16[384,384]{1,0:T(8,128)(2,1)S(1)}, bf16[384,384]{1,0:T(8,128)(2,1)S(1)}, u32[]{:S(2)}, u32[]{:S(2)}) collective-permute-start(bf16[384,384]{1,0:T(8,128)(2,1)S(1)} %bitcast_add_fusion.3), channel_id=1, source_target_pairs={{0,8},{8,16},{16,24},{24,28},{28,20},{20,12},{12,4},{4,0},{1,9},{9... | collective-permute-start | bytes 884744 | tf_op jit(solution)/shard_map/ppermute | solution.py:418
  170.6 12.3 %collective-permute-start.19 = (bf16[384,384]{1,0:T(8,128)(2,1)S(1)}, bf16[384,384]{1,0:T(8,128)(2,1)S(1)}, u32[]{:S(2)}, u32[]{:S(2)}) collective-permute-start(bf16[384,384]{1,0:T(8,128)(2,1)S(1)} %bitcast_add_fusion), channel_id=1, source_target_pairs={{8,0},{16,8},{24,16},{28,24},{20,28},{12,20},{4,12},{0,4},{9,1},{1... | collective-permute-start | bytes 884744 | tf_op jit(solution)/shard_map/ppermute | solution.py:419
  182.8 8.1 %collective-permute-start.16 = (bf16[384,384]{1,0:T(8,128)(2,1)S(1)}, bf16[384,384]{1,0:T(8,128)(2,1)S(1)}, u32[]{:S(2)}, u32[]{:S(2)}) collective-permute-start(bf16[384,384]{1,0:T(8,128)(2,1)S(1)} %bitcast_add_fusion.4), channel_id=1, source_target_pairs={{0,8},{8,16},{16,24},{24,28},{28,20},{20,12},{12,4},{4,0},{1,9},{9... | collective-permute-start | bytes 884744 | tf_op jit(solution)/shard_map/ppermute | solution.py:418
  183.0 8.4 %collective-permute-start.20 = (bf16[384,384]{1,0:T(8,128)(2,1)S(1)}, bf16[384,384]{1,0:T(8,128)(2,1)S(1)}, u32[]{:S(2)}, u32[]{:S(2)}) collective-permute-start(bf16[384,384]{1,0:T(8,128)(2,1)S(1)} %bitcast_add_fusion.1), channel_id=1, source_target_pairs={{8,0},{16,8},{24,16},{28,24},{20,28},{12,20},{4,12},{0,4},{9,1},{1... | collective-permute-start | bytes 884744 | tf_op jit(solution)/shard_map/ppermute | solution.py:419
  188.0 31.1 %collective-permute-start.11 = (bf16[1152,768]{1,0:T(8,128)(2,1)S(1)}, bf16[1152,768]{1,0:T(8,128)(2,1)S(1)}, u32[]{:S(2)}, u32[]{:S(2)}) collective-permute-start(bf16[1152,768]{1,0:T(8,128)(2,1)S(1)} %first_grad.1.own), channel_id=1, source_target_pairs={{0,1},{1,0},{2,3},{3,2},{4,5},{5,4},{6,7},{7,6},{8,9},{9,8},{10,11... | collective-permute-start | bytes 5308424 | tf_op jit(solution)/shard_map/ppermute | solution.py:373
  191.0 13.2 %collective-permute-start.17 = (bf16[384,384]{1,0:T(8,128)(2,1)S(1)}, bf16[384,384]{1,0:T(8,128)(2,1)S(1)}, u32[]{:S(2)}, u32[]{:S(2)}) collective-permute-start(bf16[384,384]{1,0:T(8,128)(2,1)S(1)} %bitcast_add_fusion.5), channel_id=1, source_target_pairs={{0,8},{8,16},{16,24},{24,28},{28,20},{20,12},{12,4},{4,0},{1,9},{9... | collective-permute-start | bytes 884744 | tf_op jit(solution)/shard_map/ppermute | solution.py:418
  191.5 19.1 %collective-permute-start.21 = (bf16[384,384]{1,0:T(8,128)(2,1)S(1)}, bf16[384,384]{1,0:T(8,128)(2,1)S(1)}, u32[]{:S(2)}, u32[]{:S(2)}) collective-permute-start(bf16[384,384]{1,0:T(8,128)(2,1)S(1)} %bitcast_add_fusion.2), channel_id=1, source_target_pairs={{8,0},{16,8},{24,16},{28,24},{20,28},{12,20},{4,12},{0,4},{9,1},{1... | collective-permute-start | bytes 884744 | tf_op jit(solution)/shard_map/ppermute | solution.py:419
  193.4 33.6 %collective-permute-start.13 = (bf16[1024,768]{1,0:T(8,128)(2,1)}, bf16[1024,768]{1,0:T(8,128)(2,1)}, u32[]{:S(2)}, u32[]{:S(2)}) collective-permute-start(bf16[1024,768]{1,0:T(8,128)(2,1)} %get-tuple-element.47.feed_own), channel_id=1, source_target_pairs={{0,1},{1,0},{2,3},{3,2},{4,5},{5,4},{6,7},{7,6},{8,9},{9,8},{10,11... | collective-permute-start | bytes 4718600 | tf_op jit(solution)/shard_map/ppermute | solution.py:373
  210.8 6.8 %collective-permute-start.22 = (bf16[384,384]{1,0:T(8,128)(2,1)S(1)}, bf16[384,384]{1,0:T(8,128)(2,1)S(1)}, u32[]{:S(2)}, u32[]{:S(2)}) collective-permute-start(bf16[384,384]{1,0:T(8,128)(2,1)S(1)} %fusion.1), channel_id=1, source_target_pairs={{0,2},{2,0},{1,3},{3,1},{4,6},{6,4},{5,7},{7,5},{8,10},{10,8},{9,1... | collective-permute-start | bytes 884744 | tf_op jit(solution)/shard_map/ppermute | solution.py:373
  222.6 18.5 %collective-permute-start.23 = (bf16[3,96,576]{2,1,0:T(8,128)(2,1)}, bf16[3,96,576]{2,1,0:T(8,128)(2,1)S(1)}, u32[]{:S(2)}, u32[]{:S(2)}) collective-permute-start(bf16[3,96,576]{2,1,0:T(8,128)(2,1)} %bitcast.64), channel_id=1, source_target_pairs={{0,2},{2,0},{1,3},{3,1},{4,6},{6,4},{5,7},{7,5},{8,10},{10,8},{9,1... | collective-permute-start | bytes 995336 | tf_op jit(solution)/shard_map/ppermute | solution.py:373
  (52 other events, 338.5 us)
Sparse Core Ops, SparseCore 0:
  10.8 70.2 all-gather.2
  128.3 83.2 reduce-scatter.1

commit v3 on v2

--- a/solution.py
+++ b/solution.py
@@ -43,7 +43,7 @@
     smem = pl.BlockSpec(memory_space=pltpu.SMEM)
     moved = sum(x.size * x.dtype.itemsize for x in (*args, *out_shape))
     held = sum(math.prod(x.shape) * jnp.dtype(x.dtype).itemsize for x in kernel[1])
-    limit = min(56 * 2**20, (moved + held) * 9 // 8 + 8 * 2**20)
+    limit = min(56 * 2**20, moved + held + 6 * 2**20)
     return pl.pallas_call(
         kernel[0],
         out_shape=out_shape,
@@ -87,12 +87,6 @@
     return jnp.concatenate([values[:HEAD, :BLOCK], values[HEAD:, BLOCK:]], axis=0).T
 
 
-def stack_weight(src, index, dst):
-    parts, _, depth, _ = src.shape
-    for part in range(parts):
-        dst[part * depth : (part + 1) * depth, :] = src[part, index]
-
-
 def loop(count, body):
     def run(index, carry):
         body(index)
@@ -101,10 +95,8 @@
     lax.fori_loop(0, count, run, 0)
 
 
-def attend_kernel(
-    bounds, slots, tokens, before, after, cosine, sine, *rest
-):
-    pieces, (wide, gain, first, query, key, value, shares, attended, branch) = rest[:-9], rest[-9:]
+def project_kernel(slots, tokens, before, after, cosine, sine, *rest):
+    pieces, (wide, gain, first, query, key, value) = rest[:-6], rest[-6:]
     rows, width = tokens.shape
     extent, local = key.shape
     pairs = local // LANES
@@ -120,7 +112,7 @@
         gain_sum += dot(piece[4 * depth :, :LANES], spread)
     gain[...] = gain_sum
     gains = gain_sum[:1]
-    query_w, key_w, value_w, out_t = (wide.at[:, part * local : (part + 1) * local] for part in range(4))
+    query_w, key_w, value_w = (wide.at[:, part * local : (part + 1) * local] for part in range(3))
 
     def norm_rows(src, dst, size):
         hat, _ = normed(src.astype(f32))
@@ -160,6 +152,13 @@
         rotated(dot(first[pl.ds(start, size), :], query_w[...]), start, size, query, at, HEAD**-0.5)
 
     loop(rows // size, query_step)
+
+
+def attend_kernel(bounds, query, key, value, wide, shares, attended, branch):
+    rows, local = query.shape
+    pairs = local // LANES
+    out_t = wide.at[:, 3 * local :]
+    size = step_of(rows, 256)
     key_at = lax.broadcasted_iota(jnp.int32, (KEYS, KEYS), 0)
     lane_at = lax.broadcasted_iota(jnp.int32, (1, KEYS), 1) % BLOCK
 
@@ -195,15 +194,15 @@
     loop(rows // size, out_step)
 
 
-def feed_kernel(
-    tokens, own, other, gain, weights, cotangent,
-    middle, second, hidden, grad_gate, grad_upper, partial,
-    gate_w, upper_w, down_t,
-):
+def feed_kernel(slots, tokens, own, other, gain, cotangent, *rest):
+    pieces, rest = rest[:-9], rest[-9:]
+    middle, second, hidden, grad_gate, grad_upper, partial, down_t, gate_w, upper_w = rest
     rows, width = tokens.shape
-    stack_weight(weights, 0, gate_w)
-    stack_weight(weights, 1, upper_w)
-    stack_weight(weights, 2, down_t)
+    depth = width // len(pieces)
+    for number, piece in enumerate(pieces):
+        place = pl.ds(pl.multiple_of(slots[number] * depth, depth), depth)
+        for part, whole in enumerate((gate_w, upper_w, down_t)):
+            whole[place, :] = piece[part * depth : (part + 1) * depth, :]
     gains = gain[1:2, :]
     size = step_of(rows, 256)
 
@@ -231,9 +230,8 @@
     loop(rows // size, step)
 
 
-def weight_kernel(second, hidden, grad_gate, grad_upper, cotangent, weights, feed, grads, down_t, total):
+def weight_kernel(slots, second, hidden, grad_gate, grad_upper, cotangent, down_t, feed, grads, total):
     rows, width = second.shape
-    stack_weight(weights, 2, down_t)
     size = step_of(rows, 256)
 
     def step(index):
@@ -241,29 +239,25 @@
         feed[here, :] = dot(hidden[here, :], down_t[...], NT).astype(bf16)
 
     loop(rows // size, step)
-    scatter_grads(second, grad_gate, grads, 0, total)
-    scatter_grads(second, grad_upper, grads, 1, total)
-    scatter_grads(cotangent, hidden, grads, 2, total)
-
-
-def scatter_grads(left, right, grads, number, total, slots=None):
+    scatter_grads(second, grad_gate, grads, 0, total, slots)
+    scatter_grads(second, grad_upper, grads, 1, total, slots)
+    scatter_grads(cotangent, hidden, grads, 2, total, slots)
+
+
+def scatter_grads(left, right, grads, number, total, slots):
     width = left.shape[-1]
-    parts, _, depth, _ = grads.shape
+    parts = grads.shape[0]
+    depth = width // parts
     for start in range(0, width, 2 * LANES):
         total[start : start + 2 * LANES, :] = dot(left[:, start : start + 2 * LANES], right[...], TN).astype(bf16)
     for part in range(parts):
-        place = part * depth if slots is None else pl.multiple_of(slots[part] * depth, depth)
-        grads[part, number] = total[pl.ds(place, depth), :]
-
-
-def back_kernel(
-    slots, middle, own, other, gain, cotangent, wide, first, query, key, value, shares, attended, cosine, sine,
-    grad_middle, grad_proj, grads,
-    low_mid, grad_att, grad_key, grad_value, total,
-):
+        place = pl.ds(pl.multiple_of(slots[part] * depth, depth), depth)
+        grads[part, number * depth : (number + 1) * depth, :] = total[place, :]
+
+
+def middle_kernel(middle, own, other, gain, cotangent, wide, grad_middle, low_mid, grad_att):
     rows, width = middle.shape
-    extent, local = key.shape
-    pairs = local // LANES
+    local = grad_att.shape[1]
     out_t = wide.at[:, 3 * local :]
     gains = gain[1:2, :]
     size = step_of(rows, 256)
@@ -279,6 +273,12 @@
         grad_att[here, :] = dot(mid_low, out_t[...]).astype(bf16)
 
     loop(rows // size, norm_step)
+
+
+def back_kernel(query, key, value, shares, grad_att, cosine, sine, grad_proj, grad_key, grad_value):
+    rows, local = query.shape
+    extent = key.shape[0]
+    pairs = local // LANES
     grad_key[...] = jnp.zeros_like(grad_key)
     grad_value[...] = jnp.zeros_like(grad_value)
     low = lax.broadcasted_iota(jnp.int32, (1, LANES), 1) % HEAD < HEAD // 2
@@ -319,6 +319,10 @@
         grad_proj[here, 2 * local :] = grad_value[here, :].astype(bf16)
 
     loop(extent // BLOCK, turn_step)
+
+
+def grad_kernel(slots, first, grad_proj, low_mid, attended, grads, total):
+    local = attended.shape[1]
     for number in range(3):
         part = grad_proj.at[:, number * local : (number + 1) * local]
         scatter_grads(first, part, grads, number, total, slots)
@@ -391,33 +395,72 @@
     return count, ahead, back, slots.astype(jnp.int32)
 
 
-def ring_gather(mine):
-    count, ahead, back, _ = ring()
-    middle = count // 2
-    half = mine.shape[0] // 2
-    pieces = {0: mine}
-    one = two = mine
-    for hop in range(1, middle):
-        one, two = lax.ppermute(one, "dp", ahead), lax.ppermute(two, "dp", back)
-        pieces[count - hop], pieces[hop] = one, two
-    pieces[middle] = jnp.concatenate(
-        [lax.ppermute(one[:half], "dp", ahead), lax.ppermute(two[half:], "dp", back)]
-    )
-    return [pieces[i] for i in range(count)]
-
-
-def ring_scatter(parts):
-    count, ahead, back, _ = ring()
-    middle = count // 2
-    half = parts.shape[1] // 2
-    one = lax.ppermute(parts[middle, :half], "dp", ahead)
-    two = lax.ppermute(parts[middle, half:], "dp", back)
-    none = jnp.zeros_like(one)
-    one, two = jnp.concatenate([one, none]), jnp.concatenate([none, two])
-    for hop in range(middle - 1, 0, -1):
-        one = lax.ppermute(parts[hop] + one, "dp", ahead)
-        two = lax.ppermute(parts[count - hop] + two, "dp", back)
-    return (parts[0].astype(f32) + one.astype(f32) + two.astype(f32)).astype(bf16)
+def tied(values, others):
+    held = lax.optimization_barrier((tuple(values), tuple(others)))
+    return held[0]
+
+
+def locked(values, chain):
+    held = lax.optimization_barrier((tuple(values), tuple(chain.state)))
+    chain.state = held[1]
+    return held[0]
+
+
+class RingGather:
+    def __init__(self, mine):
+        self.count, self.ahead, self.back, _ = ring()
+        self.pieces = {0: mine}
+        self.state = (mine, mine)
+        self.hops = 0
+
+    def hop(self):
+        self.hops += 1
+        one, two = self.state
+        middle = self.count // 2
+        half = one.shape[0] // 2
+        if self.hops == middle:
+            one, two = one[:half], two[half:]
+        one, two = lax.ppermute(one, "dp", self.ahead), lax.ppermute(two, "dp", self.back)
+        self.state = (one, two)
+        if self.hops == middle:
+            self.pieces[middle] = jnp.concatenate([one, two])
+        else:
+            self.pieces[self.count - self.hops], self.pieces[self.hops] = one, two
+
+    def finish(self):
+        while self.hops < self.count // 2:
+            self.hop()
+        return [self.pieces[i] for i in range(self.count)]
+
+
+class RingScatter:
+    def __init__(self, parts):
+        self.count, self.ahead, self.back, _ = ring()
+        self.parts = parts
+        self.hops = 0
+        self.state = ()
+
+    def hop(self):
+        middle = self.count // 2
+        parts = self.parts
+        half = parts.shape[1] // 2
+        if self.hops == 0:
+            one, two = parts[middle, :half], parts[middle, half:]
+        else:
+            one, two = self.state
+            if self.hops == 1:
+                none = jnp.zeros_like(one)
+                one, two = jnp.concatenate([one, none]), jnp.concatenate([none, two])
+            at = middle - self.hops
+            one, two = parts[at] + one, parts[self.count - at] + two
+        self.state = (lax.ppermute(one, "dp", self.ahead), lax.ppermute(two, "dp", self.back))
+        self.hops += 1
+
+    def finish(self):
+        while self.hops < self.count // 2:
+            self.hop()
+        one, two = self.state
+        return (self.parts[0].astype(f32) + one.astype(f32) + two.astype(f32)).astype(bf16)
 
 
 def tables(lengths, rows):
@@ -444,15 +487,16 @@
     depth = width // groups
     gains = jnp.pad(jnp.stack([gain_one, gain_two]), ((0, PAD - 2), (0, local - depth)))
     mine_one = jnp.concatenate([w_qkv.reshape(3 * depth, local), w_out.T, gains])
-    mine_two = jnp.concatenate([w_in, w_down.T[None]])
-    pieces = ring_gather(mine_one)
+    mine_two = jnp.concatenate([w_in.reshape(2 * depth, units), w_down.T])
+    pieces = RingGather(mine_one).finish()
     slots = ring()[-1]
-    weights_two = lax.all_gather(mine_two, "dp", axis=0, tiled=False)
+    later = RingGather(tied([mine_two], pieces)[0])
+    later.hop()
     before, after = exchange(tokens[:HALF], tokens[rows - HALF :])
     cosine, sine, bounds = tables(lengths, rows)
 
-    wide, gain, first, query, key, value, shares, attended, branch = call(
-        (attend_kernel, []),
+    wide, gain, first, query, key, value = call(
+        (project_kernel, []),
         [
             shape((width, 4 * local), bf16),
             shape((PAD, width), f32),
@@ -460,19 +504,31 @@
             shape((rows, local), bf16),
             shape((extent, local), bf16),
             shape((extent, local), bf16),
+        ],
+        (tokens, before, after, cosine, sine, *pieces),
+        2 * rows * width * local * 5,
+        "project",
+        (slots,),
+    )
+    query, key, value = tied([query, key, value], later.state)
+    later.hop()
+    shares, attended, branch = call(
+        (attend_kernel, []),
+        [
             shape((blocks * pairs, KEYS, KEYS), bf16),
             shape((rows, local), bf16),
             shape((rows, width), bf16),
         ],
-        (tokens, before, after, cosine, sine, *pieces),
-        2 * rows * width * local * 5,
-        "project_and_attend",
-        (bounds, slots),
-    )
+        (query, key, value, wide),
+        2 * rows * width * local * 10,
+        "attend",
+        (bounds,),
+    )
+    branch, = tied([branch], later.state)
     branch_other = swap(branch)
-    plain = [pltpu.VMEM((width, units), bf16)] * 3
-    middle, second, hidden, grad_gate, grad_upper, partial = call(
-        (feed_kernel, plain),
+    pieces_two = later.finish()
+    middle, second, hidden, grad_gate, grad_upper, partial, down_t = call(
+        (feed_kernel, [pltpu.VMEM((width, units), bf16)] * 2),
         [
             shape((rows, width), f32),
             shape((rows, width), bf16),
@@ -480,46 +536,54 @@
             shape((rows, units), bf16),
             shape((rows, units), bf16),
             shape((rows, width), bf16),
+            shape((width, units), bf16),
         ],
-        (tokens, branch, branch_other, gain, weights_two, cotangent),
-        2 * rows * width * units * 5,
+        (tokens, branch, branch_other, gain, cotangent, *pieces_two),
+        2 * rows * width * units * 8,
         "feed_forward_and_back",
+        (slots,),
     )
     partial_other = swap(partial)
     feed, grads_two = call(
-        (weight_kernel, [pltpu.VMEM((width, units), bf16)] * 2),
-        [shape((rows, width), bf16), shape((groups, 3, width // groups, units), bf16)],
-        (second, hidden, grad_gate, grad_upper, cotangent, weights_two),
-        2 * rows * width * units * 4,
+        (weight_kernel, [pltpu.VMEM((width, units), bf16)]),
+        [shape((rows, width), bf16), shape((groups, 3 * depth, units), bf16)],
+        (second, hidden, grad_gate, grad_upper, cotangent, down_t),
+        2 * rows * width * units * 5,
         "feed_weight_grads",
+        (slots,),
     )
     feed_other = swap(feed)
-    grad_middle, grad_proj, grads_one = call(
-        (
-            back_kernel,
-            [
-                pltpu.VMEM((rows, width), bf16),
-                pltpu.VMEM((rows, local), bf16),
-                pltpu.VMEM((extent, local), f32),
-                pltpu.VMEM((extent, local), f32),
-                pltpu.VMEM((width, local), bf16),
-            ],
-        ),
-        [
-            shape((rows, width), f32),
-            shape((extent, 3 * local), bf16),
-            shape((groups, 4, depth, local), bf16),
-        ],
-        (
-            middle, partial, partial_other, gain, cotangent, wide, first, query, key, value, shares, attended,
-            cosine, sine,
-        ),
-        2 * rows * width * local * 6,
+    sums_two = RingScatter(grads_two)
+    sums_two.hop()
+    grad_middle, low_mid, grad_att = call(
+        (middle_kernel, []),
+        [shape((rows, width), f32), shape((rows, width), bf16), shape((rows, local), bf16)],
+        (middle, partial, partial_other, gain, cotangent, wide),
+        2 * rows * width * local * 4,
+        "middle_grad",
+    )
+    grad_att, = locked([grad_att], sums_two)
+    sums_two.hop()
+    grad_proj, = call(
+        (back_kernel, [pltpu.VMEM((extent, local), f32)] * 2),
+        [shape((extent, 3 * local), bf16)],
+        (query, key, value, shares, grad_att, cosine, sine),
+        2 * rows * width * local * 15,
         "attention_back",
+    )
+    grad_proj, = locked([grad_proj], sums_two)
+    sums_two.hop()
+    grads_one, = call(
+        (grad_kernel, [pltpu.VMEM((width, local), bf16)]),
+        [shape((groups, 4 * depth, local), bf16)],
+        (first, grad_proj, low_mid, attended),
+        2 * rows * width * local * 5,
+        "attention_weight_grads",
         (slots,),
     )
-    one = over_ctx(ring_scatter(grads_one.reshape(groups, 4 * depth, local))).reshape(4, depth, local)
-    two = over_ctx(lax.psum_scatter(grads_two, "dp", scatter_dimension=0, tiled=False))
+    sums_two.state = tied(sums_two.state, [grads_one])
+    one = over_ctx(RingScatter(grads_one).finish()).reshape(4, depth, local)
+    two = over_ctx(sums_two.finish()).reshape(3, depth, units)
     first_part, = call(
         (first_kernel, []),
         [shape((extent, width), bf16)],

time: 252 us -> 208 us (0.83)
  local copies, waits for them, and re-layouts: 46.6 us -> 19.2 us
  starting transfers between devices: 25.8 us -> 40.1 us
  between operations: 14.5 us -> 1.07 us
  Pallas kernels: 76.3 us -> 64.7 us
  waiting for transfers between devices: 76.4 us -> 72.5 us
    unnamed x98 -> x45, local copies, waits for them, and re-layouts: 34.8 us -> 10.3 us
    ppermute x16 -> x32, starting transfers between devices: 20.2 us -> 34.2 us  [the longest x16 25.3 us: hop(): lax.ppermute(one, 'dp', self.ahead)]
    pallas_call x6 -> x9, Pallas kernels: 76.3 us -> 64.7 us  [call(): pl.pallas_call(kernel[0], out_shape=out_shape, in_specs=[smem] * len(scal...]
    ppermute x16 -> x32, waiting for transfers between devices: 65.4 us -> 60 us  [the longest x16 42 us: hop(): lax.ppermute(one, 'dp', self.ahead)]
    ppermute x2, waiting for transfers between devices: 2.75 us -> 8.12 us  [exchange(): lax.ppermute(jnp.where(spot == 0, last, initial), 'ctx', [(0, 1), (1, 0)])]
    ppermute x7, waiting for transfers between devices: 8.22 us -> 4.32 us  [swap(): return lax.ppermute(array, axis, [(0, 1), (1, 0)])]
  transfers between devices with their start and end apart: 27 -> 41, of which waited for: 14 -> 20; matrix products, arithmetic and copies ran while one was open for 8% -> 8% of each run, Pallas kernels for 26% -> 24%
where the time goes in v3:
time: 208 us
  waiting for transfers between devices  72.5 us (35%)
  Pallas kernels  64.7 us (31%)
  starting transfers between devices  40.1 us (19%)
  local copies, waits for them, and re-layouts  19.2 us (9%)
  other arithmetic  10.2 us (5%)
    pallas_call x9, Pallas kernels, call(): pl.pallas_call(kernel[0], out_shape=out_shape, in_specs=[smem] * len(scal...  64.7 us
    ppermute x16, waiting for transfers between devices, hop(): lax.ppermute(one, 'dp', self.ahead)  42 us
    ppermute x16, starting transfers between devices, hop(): lax.ppermute(one, 'dp', self.ahead)  25.3 us
    ppermute x16, waiting for transfers between devices, hop(): lax.ppermute(two, 'dp', self.back)  18.1 us
    unnamed x45, local copies, waits for them, and re-layouts  10.3 us
    ppermute x16, starting transfers between devices, hop(): lax.ppermute(two, 'dp', self.back)  8.87 us
    ppermute x2, waiting for transfers between devices, exchange(): lax.ppermute(jnp.where(spot == 0, last, initial), 'ctx', [(0, 1), (1, 0)])  8.12 us
    another operation x4, local copies, waits for them, and re-layouts, tables(): return (jnp.tile(cosine, (1, 2)), jnp.tile(sine, (1, 2)), bounds)  4.46 us
  transfers between devices with their start and end apart: 41, of which 20 were waited for; matrix products, arithmetic and copies ran while one was open for 8% of the time, Pallas kernels for 24%

profile of v3, /device:TPU:0, one launch (start us, length us, event | category | flops | bytes accessed | tf_op | source)
XLA Modules:
  0.0 207.9 jit_solution(11051036541592569919)
XLA Ops:
  2.3 3.1 %collective-permute-start.4 = (bf16[400,384]{1,0:T(8,128)(2,1)S(1)}, bf16[400,384]{1,0:T(8,128)(2,1)S(1)}, u32[]{:S(2)}, u32[]{:S(2)}) collective-permute-start(bf16[400,384]{1,0:T(8,128)(2,1)S(1)} %pad_maximum_fusion.2.rest_0_), channel_id=1, source_target_pairs={{0,8},{8,16},{16,24},{24,28},{28,20},{20,12},{12,4},{4,0},{1,9},{9... | collective-permute-start | bytes 921608 | tf_op jit(solution)/shard_map/ppermute | solution.py:423
  10.6 2.0 collective-permute-done.4.rest_7_
  16.1 5.1 %collective-permute-done.5.rest_6_ = bf16[400,384]{1,0:T(8,128)(2,1)S(1)} collective-permute-done((bf16[400,384]{1,0:T(8,128)(2,1)S(1)}, bf16[400,384]{1,0:T(8,128)(2,1)S(1)}, u32[]{:S(2)}, u32[]{:S(2)}) %collective-permute-start.5) | collective-permute-done | bytes 307232 | tf_op jit(solution)/shard_map/ppermute | solution.py:423
  26.6 2.2 %collective-permute-done.6.rest_5_ = bf16[400,384]{1,0:T(8,128)(2,1)S(1)} collective-permute-done((bf16[400,384]{1,0:T(8,128)(2,1)S(1)}, bf16[400,384]{1,0:T(8,128)(2,1)S(1)}, u32[]{:S(2)}, u32[]{:S(2)}) %collective-permute-start.6) | collective-permute-done | bytes 307232 | tf_op jit(solution)/shard_map/ppermute | solution.py:423
  47.6 7.6 %project.1 = (bf16[768,1536]{1,0:T(8,128)(2,1)S(1)}, f32[16,768]{1,0:T(8,128)S(1)}, bf16[1152,768]{1,0:T(8,128)(2,1)S(1)}, bf16[1024,384]{1,0:T(8,128)(2,1)S(1)}...) custom-call(s32[8]{0:T(128)S(1)} %compare_select_fusion.2.slots, bf16[1024,768]{1,0:T(8,128)(2,1)S(1)} %copy-done, ...), custom_call_target="tpu_custom_call" | custom-call | flops 3019898880 | bytes 12140544 | tf_op jit(solution)/shard_map/project/pallas_call | solution.py:47
  57.3 11.9 %attend.1 = (bf16[24,256,256]{2,1,0:T(8,128)(2,1)S(1)}, bf16[1024,384]{1,0:T(8,128)(2,1)S(1)}, bf16[1024,768]{1,0:T(8,128)(2,1)S(1)}) custom-call(s32[5]{0:T(128)S(1)} %pad_add_fusion.bounds, bf16[1024,384]{1,0:T(8,128)(2,1)S(1)} %get-tuple-element.49.query, bf16[1152,384]{1,0:T(8,128)(2,1)S(1)} %get-tuple-element.50.key, ...), custom_call_target="tpu_custom_call" | custom-call | flops 6039797760 | bytes 10420224 | tf_op jit(solution)/shard_map/attend/pallas_call | solution.py:47
  72.9 8.9 %collective-permute-done.15.rest_5_ = bf16[288,576]{1,0:T(8,128)(2,1)S(1)} collective-permute-done((bf16[288,576]{1,0:T(8,128)(2,1)S(1)}, bf16[288,576]{1,0:T(8,128)(2,1)S(1)}, u32[]{:S(2)}, u32[]{:S(2)}) %collective-permute-start.15) | collective-permute-done | bytes 331808 | tf_op jit(solution)/shard_map/ppermute | solution.py:423
  84.2 3.9 %collective-permute-done.16 = bf16[144,576]{1,0:T(8,128)(2,1)S(1)} collective-permute-done((bf16[144,576]{1,0:T(8,128)(2,1)S(1)}, bf16[144,576]{1,0:T(8,128)(2,1)S(1)}, u32[]{:S(2)}, u32[]{:S(2)}) %collective-permute-start.16) | collective-permute-done | bytes 165920 | tf_op jit(solution)/shard_map/ppermute | solution.py:423
  89.4 10.1 %feed_forward_and_back.1 = (f32[1024,768]{1,0:T(8,128)S(1)}, bf16[1024,768]{1,0:T(8,128)(2,1)S(1)}, bf16[1024,576]{1,0:T(8,128)(2,1)S(1)}, bf16[1024,576]{1,0:T(...) custom-call(s32[8]{0:T(128)S(1)} %compare_select_fusion.2.slots, ...), custom_call_target="tpu_custom_call" | custom-call | flops 7247757312 | bytes 19709952 | tf_op jit(solution)/shard_map/feed_forward_and_back/pallas_call | solution.py:47
  99.5 6.6 %feed_weight_grads.1 = (bf16[1024,768]{1,0:T(8,128)(2,1)S(1)}, bf16[8,288,576]{2,1,0:T(8,128)(2,1)S(1)}) custom-call(s32[8]{0:T(128)S(1)} %compare_select_fusion.2.slots, bf16[1024,768]{1,0:T(8,128)(2,1)S(1)} %get-tuple-element.60.second, bf16[1024,576]{1,0:T(8,128)(2,1)S(1)} %get-tuple-element.61.hidden, bf16[1024,576]{1,0:T(8,128)(2,1)S(1)} %get-tuple-element.62.grad_gate, ...), custom_call_target="tpu_custom_call" | custom-call | flops 4529848320 | bytes 11796480 | tf_op jit(solution)/shard_map/feed_weight_grads/pallas_call | solution.py:47
  108.2 3.4 %middle_grad.1 = (f32[1024,768]{1,0:T(8,128)S(1)}, bf16[1024,768]{1,0:T(8,128)(2,1)S(1)}, bf16[1024,384]{1,0:T(8,128)(2,1)S(1)}) custom-call(f32[1024,768]{1,0:T(8,128)S(1)} %get-tuple-element.55.middle, bf16[1024,768]{1,0:T(8,128)(2,1)S(1)} %get-tuple-element.56.own, bf16[1024,768]{1,0:T(8,128)(2,1)S(1)} %collective-permute-done.18.other, ...), custom_call_target="tpu_custom_call" | custom-call | flops 2415919104 | bytes 15777792 | tf_op jit(solution)/shard_map/middle_grad/pallas_call | solution.py:47
  116.7 11.9 %attention_back.1.grad_proj = bf16[1152,1152]{1,0:T(8,128)(2,1)S(1)} custom-call(bf16[1024,384]{1,0:T(8,128)(2,1)S(1)} %get-tuple-element.49.query, bf16[1152,384]{1,0:T(8,128)(2,1)S(1)} %get-tuple-element.50.key, bf16[1152,384]{1,0:T(8,128)(2,1)S(1)} %get-tuple-element.51.value, bf16[24,256,256]{2,1,0:T(8,128)(2,1)S(1)} %copy-done.15, ...), custom_call_target="tpu_custom_call" | custom-call | flops 9059696640 | bytes 10321920 | tf_op jit(solution)/shard_map/attention_back/pallas_call | solution.py:47
  128.6 4.6 %attention_weight_grads.1 = bf16[8,384,384]{2,1,0:T(8,128)(2,1)S(1)} custom-call(s32[8]{0:T(128)S(1)} %compare_select_fusion.2.slots, bf16[1152,768]{1,0:T(8,128)(2,1)S(1)} %get-tuple-element.73.first, bf16[1152,1152]{1,0:T(8,128)(2,1)S(1)} %attention_back.1.grad_proj, bf16[1024,768]{1,0:T(8,128)(2,1)S(1)} %get-tuple-element.74.low_mid, ...), custom_call_target="tpu_custom_call" | custom-call | flops 3019898880 | bytes 9142272 | tf_op jit(solution)/shard_map/attention_weight_grads/pallas_call | solution.py:47
  134.9 3.6 %collective-permute-done.26 = bf16[192,384]{1,0:T(8,128)(2,1)S(1)} collective-permute-done((bf16[192,384]{1,0:T(8,128)(2,1)S(1)}, bf16[192,384]{1,0:T(8,128)(2,1)S(1)}, u32[]{:S(2)}, u32[]{:S(2)}) %collective-permute-start.26) | collective-permute-done | bytes 147488 | tf_op jit(solution)/shard_map/ppermute | solution.py:456
  142.3 6.2 %collective-permute-done.27 = bf16[384,384]{1,0:T(8,128)(2,1)S(1)} collective-permute-done((bf16[384,384]{1,0:T(8,128)(2,1)S(1)}, bf16[384,384]{1,0:T(8,128)(2,1)S(1)}, u32[]{:S(2)}, u32[]{:S(2)}) %collective-permute-start.27) | collective-permute-done | bytes 294944 | tf_op jit(solution)/shard_map/ppermute | solution.py:456
  150.6 2.9 %first_grad.1.own = bf16[1152,768]{1,0:T(8,128)(2,1)S(1)} custom-call(bf16[1152,1152]{1,0:T(8,128)(2,1)S(1)} %attention_back.1.grad_proj, bf16[768,1536]{1,0:T(8,128)(2,1)S(1)} %get-tuple-element.52.wide), custom_call_target="tpu_custom_call" | custom-call | flops 1811939328 | bytes 6782976 | tf_op jit(solution)/shard_map/first_grad/pallas_call | solution.py:47
  153.6 2.6 %collective-permute-done.35 = bf16[288,576]{1,0:T(8,128)(2,1)S(1)} collective-permute-done((bf16[288,576]{1,0:T(8,128)(2,1)S(1)}, bf16[288,576]{1,0:T(8,128)(2,1)S(1)}, u32[]{:S(2)}, u32[]{:S(2)}) %collective-permute-start.35) | collective-permute-done | bytes 331808 | tf_op jit(solution)/shard_map/ppermute | solution.py:456
  156.2 3.3 %collective-permute-done.28 = bf16[384,384]{1,0:T(8,128)(2,1)S(1)} collective-permute-done((bf16[384,384]{1,0:T(8,128)(2,1)S(1)}, bf16[384,384]{1,0:T(8,128)(2,1)S(1)}, u32[]{:S(2)}, u32[]{:S(2)}) %collective-permute-start.28) | collective-permute-done | bytes 294944 | tf_op jit(solution)/shard_map/ppermute | solution.py:456
  162.2 7.5 %collective-permute-done.31 = bf16[384,384]{1,0:T(8,128)(2,1)S(1)} collective-permute-done((bf16[384,384]{1,0:T(8,128)(2,1)S(1)}, bf16[384,384]{1,0:T(8,128)(2,1)S(1)}, u32[]{:S(2)}, u32[]{:S(2)}) %collective-permute-start.31) | collective-permute-done | bytes 294944 | tf_op jit(solution)/shard_map/ppermute | solution.py:456
  170.0 6.3 %collective-permute-done.38 = bf16[288,576]{1,0:T(8,128)(2,1)S(1)} collective-permute-done((bf16[288,576]{1,0:T(8,128)(2,1)S(1)}, bf16[288,576]{1,0:T(8,128)(2,1)S(1)}, u32[]{:S(2)}, u32[]{:S(2)}) %collective-permute-start.38) | collective-permute-done | bytes 331808 | tf_op jit(solution)/shard_map/ppermute | solution.py:456
  180.2 3.9 %collective-permute-done.39 = bf16[288,576]{1,0:T(8,128)(2,1)S(1)} collective-permute-done((bf16[288,576]{1,0:T(8,128)(2,1)S(1)}, bf16[288,576]{1,0:T(8,128)(2,1)S(1)}, u32[]{:S(2)}, u32[]{:S(2)}) %collective-permute-start.39) | collective-permute-done | bytes 331808 | tf_op jit(solution)/shard_map/ppermute | solution.py:377
  184.9 2.5 %collective-permute-done.29 = bf16[384,384]{1,0:T(8,128)(2,1)S(1)} collective-permute-done((bf16[384,384]{1,0:T(8,128)(2,1)S(1)}, bf16[384,384]{1,0:T(8,128)(2,1)S(1)}, u32[]{:S(2)}, u32[]{:S(2)}) %collective-permute-start.29) | collective-permute-done | bytes 294944 | tf_op jit(solution)/shard_map/ppermute | solution.py:456
  191.4 8.1 %collective-permute-done.24 = bf16[64,768]{1,0:T(8,128)(2,1)S(1)} collective-permute-done((bf16[64,768]{1,0:T(8,128)(2,1)S(1)}, bf16[64,768]{1,0:T(8,128)(2,1)S(1)}, u32[]{:S(2)}, u32[]{:S(2)}) %collective-permute-start.24) | collective-permute-done | bytes 98336 | tf_op jit(solution)/shard_map/ppermute | solution.py:369
  199.5 5.9 %token_grad.1 = (bf16[1024,768]{1,0:T(8,128)(2,1)}, f32[1024,768]{1,0:T(8,128)}) custom-call(bf16[1024,768]{1,0:T(8,128)(2,1)S(1)} %copy-done, f32[16,768]{1,0:T(8,128)S(1)} %get-tuple-element.44.gain, f32[1024,768]{1,0:T(8,128)S(1)} %get-tuple-element.57.grad_middle, bf16[1152,768]{1,0:T(8,128)(2,1)S(1)} %first_grad.1.own, ...), custom_call_target="tpu_custom_call" | custom-call | flops 15728640 | bytes 19513344 | tf_op jit(solution)/shard_map/token_grad/pallas_call | solution.py:47
  (163 shorter events, 73.0 us)
Async XLA Ops:
  2.3 10.3 %collective-permute-start.4 = (bf16[400,384]{1,0:T(8,128)(2,1)S(1)}, bf16[400,384]{1,0:T(8,128)(2,1)S(1)}, u32[]{:S(2)}, u32[]{:S(2)}) collective-permute-start(bf16[400,384]{1,0:T(8,128)(2,1)S(1)} %pad_maximum_fusion.2.rest_0_), channel_id=1, source_target_pairs={{0,8},{8,16},{16,24},{24,28},{28,20},{20,12},{12,4},{4,0},{1,9},{9... | collective-permute-start | bytes 921608 | tf_op jit(solution)/shard_map/ppermute | solution.py:423
  5.4 9.7 %collective-permute-start.1 = (bf16[400,384]{1,0:T(8,128)(2,1)S(1)}, bf16[400,384]{1,0:T(8,128)(2,1)S(1)}, u32[]{:S(2)}, u32[]{:S(2)}) collective-permute-start(bf16[400,384]{1,0:T(8,128)(2,1)S(1)} %pad_maximum_fusion.2.rest_0_), channel_id=1, source_target_pairs={{8,0},{16,8},{24,16},{28,24},{20,28},{12,20},{4,12},{0,4},{9,1},{1... | collective-permute-start | bytes 921608 | tf_op jit(solution)/shard_map/ppermute | solution.py:423
  7.0 33.9 %collective-permute-start = (bf16[64,768]{1,0:T(8,128)(2,1)}, bf16[64,768]{1,0:T(8,128)(2,1)}, u32[]{:S(2)}, u32[]{:S(2)}) collective-permute-start(bf16[64,768]{1,0:T(8,128)(2,1)} %slice_select_fusion), channel_id=1, source_target_pairs={{0,2},{2,0},{1,3},{3,1},{4,6},{6,4},{5,7},{7,5},{8,10},{10,8},{9,1... | collective-permute-start | bytes 294920 | tf_op jit(solution)/shard_map/ppermute | solution.py:369
  38.8 16.4 %collective-permute-start.10 = (bf16[288,576]{1,0:T(8,128)(2,1)S(1)}, bf16[288,576]{1,0:T(8,128)(2,1)S(1)}, u32[]{:S(2)}, u32[]{:S(2)}) collective-permute-start(bf16[288,576]{1,0:T(8,128)(2,1)S(1)} %pad_maximum_fusion.rest_0_), channel_id=1, source_target_pairs={{8,0},{16,8},{24,16},{28,24},{20,28},{12,20},{4,12},{0,4},{9,1},{1... | collective-permute-start | bytes 995336 | tf_op jit(solution)/shard_map/ppermute | solution.py:423
  40.0 15.2 %collective-permute-start.9 = (bf16[288,576]{1,0:T(8,128)(2,1)S(1)}, bf16[288,576]{1,0:T(8,128)(2,1)S(1)}, u32[]{:S(2)}, u32[]{:S(2)}) collective-permute-start(bf16[288,576]{1,0:T(8,128)(2,1)S(1)} %pad_maximum_fusion.rest_0_), channel_id=1, source_target_pairs={{0,8},{8,16},{16,24},{24,28},{28,20},{20,12},{12,4},{4,0},{1,9},{9... | collective-permute-start | bytes 995336 | tf_op jit(solution)/shard_map/ppermute | solution.py:423
  55.2 15.6 %collective-permute-start.11 = (bf16[288,576]{1,0:T(8,128)(2,1)S(1)}, bf16[288,576]{1,0:T(8,128)(2,1)S(1)}, u32[]{:S(2)}, u32[]{:S(2)}) collective-permute-start(bf16[288,576]{1,0:T(8,128)(2,1)S(1)} %collective-permute-done.9.rest_7_), channel_id=1, source_target_pairs={{0,8},{8,16},{16,24},{24,28},{28,20},{20,12},{12,4},{4,0},{1,9},{9... | collective-permute-start | bytes 995336 | tf_op jit(solution)/shard_map/ppermute | solution.py:423
  56.4 14.4 %collective-permute-start.12 = (bf16[288,576]{1,0:T(8,128)(2,1)S(1)}, bf16[288,576]{1,0:T(8,128)(2,1)S(1)}, u32[]{:S(2)}, u32[]{:S(2)}) collective-permute-start(bf16[288,576]{1,0:T(8,128)(2,1)S(1)} %collective-permute-done.10.rest_1_), channel_id=1, source_target_pairs={{8,0},{16,8},{24,16},{28,24},{20,28},{12,20},{4,12},{0,4},{9,1},{1... | collective-permute-start | bytes 995336 | tf_op jit(solution)/shard_map/ppermute | solution.py:423
  70.8 18.5 %collective-permute-start.13 = (bf16[1024,768]{1,0:T(8,128)(2,1)S(1)}, bf16[1024,768]{1,0:T(8,128)(2,1)S(1)}, u32[]{:S(2)}, u32[]{:S(2)}) collective-permute-start(bf16[1024,768]{1,0:T(8,128)(2,1)S(1)} %get-tuple-element.54.own), channel_id=1, source_target_pairs={{0,1},{1,0},{2,3},{3,2},{4,5},{5,4},{6,7},{7,6},{8,9},{9,8},{10,11... | collective-permute-start | bytes 4718600 | tf_op jit(solution)/shard_map/ppermute | solution.py:377
  70.8 11.0 %collective-permute-start.15 = (bf16[288,576]{1,0:T(8,128)(2,1)S(1)}, bf16[288,576]{1,0:T(8,128)(2,1)S(1)}, u32[]{:S(2)}, u32[]{:S(2)}) collective-permute-start(bf16[288,576]{1,0:T(8,128)(2,1)S(1)} %collective-permute-done.11.rest_6_), channel_id=1, source_target_pairs={{0,8},{8,16},{16,24},{24,28},{28,20},{20,12},{12,4},{4,0},{1,9},{9... | collective-permute-start | bytes 995336 | tf_op jit(solution)/shard_map/ppermute | solution.py:423
  72.1 11.0 %collective-permute-start.14 = (bf16[288,576]{1,0:T(8,128)(2,1)S(1)}, bf16[288,576]{1,0:T(8,128)(2,1)S(1)}, u32[]{:S(2)}, u32[]{:S(2)}) collective-permute-start(bf16[288,576]{1,0:T(8,128)(2,1)S(1)} %collective-permute-done.12.rest_2_), channel_id=1, source_target_pairs={{8,0},{16,8},{24,16},{28,24},{20,28},{12,20},{4,12},{0,4},{9,1},{1... | collective-permute-start | bytes 995336 | tf_op jit(solution)/shard_map/ppermute | solution.py:423
  114.6 14.0 %collective-permute-start.21 = (bf16[288,576]{1,0:T(8,128)(2,1)S(1)}, bf16[288,576]{1,0:T(8,128)(2,1)S(1)}, u32[]{:S(2)}, u32[]{:S(2)}) collective-permute-start(bf16[288,576]{1,0:T(8,128)(2,1)S(1)} %get-tuple-element.85), channel_id=1, source_target_pairs={{0,8},{8,16},{16,24},{24,28},{28,20},{20,12},{12,4},{4,0},{1,9},{9... | collective-permute-start | bytes 995336 | tf_op jit(solution)/shard_map/ppermute | solution.py:456
  116.3 12.4 %collective-permute-start.22 = (bf16[288,576]{1,0:T(8,128)(2,1)S(1)}, bf16[288,576]{1,0:T(8,128)(2,1)S(1)}, u32[]{:S(2)}, u32[]{:S(2)}) collective-permute-start(bf16[288,576]{1,0:T(8,128)(2,1)S(1)} %get-tuple-element.84), channel_id=1, source_target_pairs={{8,0},{16,8},{24,16},{28,24},{20,28},{12,20},{4,12},{0,4},{9,1},{1... | collective-permute-start | bytes 995336 | tf_op jit(solution)/shard_map/ppermute | solution.py:456
  138.5 10.0 %collective-permute-start.27 = (bf16[384,384]{1,0:T(8,128)(2,1)S(1)}, bf16[384,384]{1,0:T(8,128)(2,1)S(1)}, u32[]{:S(2)}, u32[]{:S(2)}) collective-permute-start(bf16[384,384]{1,0:T(8,128)(2,1)S(1)} %fusion.7), channel_id=1, source_target_pairs={{0,8},{8,16},{16,24},{24,28},{28,20},{20,12},{12,4},{4,0},{1,9},{9... | collective-permute-start | bytes 884744 | tf_op jit(solution)/shard_map/ppermute | solution.py:456
  140.3 16.0 %collective-permute-start.35 = (bf16[288,576]{1,0:T(8,128)(2,1)S(1)}, bf16[288,576]{1,0:T(8,128)(2,1)S(1)}, u32[]{:S(2)}, u32[]{:S(2)}) collective-permute-start(bf16[288,576]{1,0:T(8,128)(2,1)S(1)} %get-tuple-element.83), channel_id=1, source_target_pairs={{0,8},{8,16},{16,24},{24,28},{28,20},{20,12},{12,4},{4,0},{1,9},{9... | collective-permute-start | bytes 995336 | tf_op jit(solution)/shard_map/ppermute | solution.py:456
  141.8 14.4 %collective-permute-start.36 = (bf16[288,576]{1,0:T(8,128)(2,1)S(1)}, bf16[288,576]{1,0:T(8,128)(2,1)S(1)}, u32[]{:S(2)}, u32[]{:S(2)}) collective-permute-start(bf16[288,576]{1,0:T(8,128)(2,1)S(1)} %get-tuple-element.82), channel_id=1, source_target_pairs={{8,0},{16,8},{24,16},{28,24},{20,28},{12,20},{4,12},{0,4},{9,1},{1... | collective-permute-start | bytes 995336 | tf_op jit(solution)/shard_map/ppermute | solution.py:456
  148.6 10.9 %collective-permute-start.28 = (bf16[384,384]{1,0:T(8,128)(2,1)S(1)}, bf16[384,384]{1,0:T(8,128)(2,1)S(1)}, u32[]{:S(2)}, u32[]{:S(2)}) collective-permute-start(bf16[384,384]{1,0:T(8,128)(2,1)S(1)} %fusion.8), channel_id=1, source_target_pairs={{0,8},{8,16},{16,24},{24,28},{28,20},{20,12},{12,4},{4,0},{1,9},{9... | collective-permute-start | bytes 884744 | tf_op jit(solution)/shard_map/ppermute | solution.py:456
  153.5 36.0 %collective-permute-start.23 = (bf16[1152,768]{1,0:T(8,128)(2,1)S(1)}, bf16[1152,768]{1,0:T(8,128)(2,1)S(1)}, u32[]{:S(2)}, u32[]{:S(2)}) collective-permute-start(bf16[1152,768]{1,0:T(8,128)(2,1)S(1)} %first_grad.1.own), channel_id=1, source_target_pairs={{0,1},{1,0},{2,3},{3,2},{4,5},{5,4},{6,7},{7,6},{8,9},{9,8},{10,11... | collective-permute-start | bytes 5308424 | tf_op jit(solution)/shard_map/ppermute | solution.py:377
  159.6 10.0 %collective-permute-start.31 = (bf16[384,384]{1,0:T(8,128)(2,1)S(1)}, bf16[384,384]{1,0:T(8,128)(2,1)S(1)}, u32[]{:S(2)}, u32[]{:S(2)}) collective-permute-start(bf16[384,384]{1,0:T(8,128)(2,1)S(1)} %get-tuple-element.89), channel_id=1, source_target_pairs={{8,0},{16,8},{24,16},{28,24},{20,28},{12,20},{4,12},{0,4},{9,1},{1... | collective-permute-start | bytes 884744 | tf_op jit(solution)/shard_map/ppermute | solution.py:456
  160.1 10.0 %collective-permute-start.37 = (bf16[288,576]{1,0:T(8,128)(2,1)S(1)}, bf16[288,576]{1,0:T(8,128)(2,1)S(1)}, u32[]{:S(2)}, u32[]{:S(2)}) collective-permute-start(bf16[288,576]{1,0:T(8,128)(2,1)S(1)} %get-tuple-element.80), channel_id=1, source_target_pairs={{0,8},{8,16},{16,24},{24,28},{28,20},{20,12},{12,4},{4,0},{1,9},{9... | collective-permute-start | bytes 995336 | tf_op jit(solution)/shard_map/ppermute | solution.py:456
  161.8 14.5 %collective-permute-start.38 = (bf16[288,576]{1,0:T(8,128)(2,1)S(1)}, bf16[288,576]{1,0:T(8,128)(2,1)S(1)}, u32[]{:S(2)}, u32[]{:S(2)}) collective-permute-start(bf16[288,576]{1,0:T(8,128)(2,1)S(1)} %get-tuple-element.81), channel_id=1, source_target_pairs={{8,0},{16,8},{24,16},{28,24},{20,28},{12,20},{4,12},{0,4},{9,1},{1... | collective-permute-start | bytes 995336 | tf_op jit(solution)/shard_map/ppermute | solution.py:456
  169.7 10.0 %collective-permute-start.32 = (bf16[384,384]{1,0:T(8,128)(2,1)S(1)}, bf16[384,384]{1,0:T(8,128)(2,1)S(1)}, u32[]{:S(2)}, u32[]{:S(2)}) collective-permute-start(bf16[384,384]{1,0:T(8,128)(2,1)S(1)} %fusion.5), channel_id=1, source_target_pairs={{8,0},{16,8},{24,16},{28,24},{20,28},{12,20},{4,12},{0,4},{9,1},{1... | collective-permute-start | bytes 884744 | tf_op jit(solution)/shard_map/ppermute | solution.py:456
  178.0 21.5 %collective-permute-start.25 = (bf16[1024,768]{1,0:T(8,128)(2,1)S(1)}, bf16[1024,768]{1,0:T(8,128)(2,1)S(1)}, u32[]{:S(2)}, u32[]{:S(2)}) collective-permute-start(bf16[1024,768]{1,0:T(8,128)(2,1)S(1)} %get-tuple-element.70.feed_own), channel_id=1, source_target_pairs={{0,1},{1,0},{2,3},{3,2},{4,5},{5,4},{6,7},{7,6},{8,9},{9,8},{10,11... | collective-permute-start | bytes 4718600 | tf_op jit(solution)/shard_map/ppermute | solution.py:377
  189.0 16.4 %collective-permute-start.34 = (bf16[384,384]{1,0:T(8,128)(2,1)S(1)}, bf16[384,384]{1,0:T(8,128)(2,1)S(1)}, u32[]{:S(2)}, u32[]{:S(2)}) collective-permute-start(bf16[384,384]{1,0:T(8,128)(2,1)S(1)} %fusion.3), channel_id=1, source_target_pairs={{0,2},{2,0},{1,3},{3,1},{4,6},{6,4},{5,7},{7,5},{8,10},{10,8},{9,1... | collective-permute-start | bytes 884744 | tf_op jit(solution)/shard_map/ppermute | solution.py:377
  189.6 9.9 %collective-permute-start.24 = (bf16[64,768]{1,0:T(8,128)(2,1)S(1)}, bf16[64,768]{1,0:T(8,128)(2,1)S(1)}, u32[]{:S(2)}, u32[]{:S(2)}) collective-permute-start(bf16[64,768]{1,0:T(8,128)(2,1)S(1)} %fusion.10), channel_id=1, source_target_pairs={{0,2},{2,0},{1,3},{3,1},{4,6},{6,4},{5,7},{7,5},{8,10},{10,8},{9,1... | collective-permute-start | bytes 294920 | tf_op jit(solution)/shard_map/ppermute | solution.py:369
  (39 other events, 246.4 us)

commit v4 on v3

v4 whole, which is shorter than its diff:
```python
import functools
import math

import jax
import jax.numpy as jnp
from jax import lax
from jax.experimental import pallas as pl
from jax.experimental.pallas import tpu as pltpu
from jax.sharding import PartitionSpec as P

HEAD = 64
WINDOW = 128
NSEQ = 4
HALF = WINDOW // 2
PAD = 16
BLOCK = 128
LANES = 128
KEYS = BLOCK + WINDOW

norm_eps = 1e-05
f32 = jnp.float32
bf16 = jnp.bfloat16

NN = (((1,), (0,)), ((), ()))
NT = (((1,), (1,)), ((), ()))
TN = (((0,), (0,)), ((), ()))


def dot(a, b, dims=NN):
    return lax.dot_general(a, b, dims, preferred_element_type=f32)


def step_of(rows, most):
    best = LANES
    for size in range(LANES, most + 1, LANES):
        if rows % size == 0:
            best = size
    return best


def call(kernel, out_shape, args, flops, name, scalars=(), scratch=(), raw=()):
    vmem = pl.BlockSpec(memory_space=pltpu.VMEM)
    smem = pl.BlockSpec(memory_space=pltpu.SMEM)
    anywhere = pl.BlockSpec(memory_space=pl.ANY)
    moved = sum(x.size * x.dtype.itemsize for x in (*args, *out_shape))
    held = sum(math.prod(x.shape) * jnp.dtype(x.dtype).itemsize for x in scratch if x.dtype in (f32, bf16))
    limit = min(56 * 2**20, moved + held + 6 * 2**20)
    return pl.pallas_call(
        kernel,
        out_shape=out_shape,
        in_specs=[smem] * len(scalars) + [vmem] * len(args) + [anywhere] * len(raw),
        out_specs=[vmem] * len(out_shape),
        scratch_shapes=scratch,
        compiler_params=pltpu.CompilerParams(vmem_limit_bytes=limit),
        cost_estimate=pl.CostEstimate(flops=flops, bytes_accessed=moved, transcendentals=0),
        name=name,
    )(*scalars, *args, *raw)


def shape(dims, dtype):
    return jax.ShapeDtypeStruct(dims, dtype)


def normed(values):
    centered = values - jnp.mean(values, axis=-1, keepdims=True)
    spread = jnp.mean(centered * centered, axis=-1, keepdims=True)
    scale = lax.rsqrt(spread + norm_eps)
    return centered * scale, scale


def norm_back(grad, gain, hat, scale):
    inner = grad * gain
    one = jnp.mean(inner, axis=-1, keepdims=True)
    two = jnp.mean(inner * hat, axis=-1, keepdims=True)
    return scale * (inner - one - hat * two)


def turned(values, low):
    return jnp.where(low, pltpu.roll(values, LANES - HEAD // 2, 1), pltpu.roll(values, HEAD // 2, 1))


def halves(values):
    even = (lax.broadcasted_iota(jnp.int32, (1, LANES), 1) < HEAD).astype(f32).astype(bf16)
    return jnp.concatenate([values * even, values * (1 - even)], axis=0)


def joined(values):
    return jnp.concatenate([values[:HEAD, :BLOCK], values[HEAD:, BLOCK:]], axis=0).T


def loop(count, body):
    def run(index, carry):
        body(index)
        return carry

    lax.fori_loop(0, count, run, 0)


def fetch(copies, sems):
    started = []
    for number, (source, target) in enumerate(copies):
        copy = pltpu.make_async_copy(source, target, sems.at[number])
        copy.start()
        started.append(copy)
    for copy in started:
        copy.wait()


def norm_kernel(tokens, before, after, hat):
    rows, width = tokens.shape

    def norm_rows(src, dst, size):
        hat[pl.ds(dst, size), :] = normed(src.astype(f32))[0]

    norm_rows(before[...], 0, HALF)
    norm_rows(after[...], rows + HALF, HALF)

    def norm_step(index):
        at = pl.multiple_of(index * BLOCK, BLOCK)
        norm_rows(tokens[pl.ds(at, BLOCK), :], pl.multiple_of(at + HALF, HALF), BLOCK)

    loop(rows // BLOCK, norm_step)


def project_kernel(plan, slots, thirds, hat, cosine, sine, *rest):
    pieces, (wide, gain, first, query, key, value, gain_held, sems) = rest[:-8], rest[-8:]
    extent, local = key.shape
    rows = query.shape[0]
    width = hat.shape[1]
    pairs = local // LANES
    groups = len(plan)
    depth = width // groups
    part = wide.shape[1] // 3
    copies = []
    for number, sources in enumerate(plan):
        place = pl.ds(pl.multiple_of(slots[number] * depth, depth), depth)
        for third, (piece, row) in enumerate(sources[:3]):
            lanes = pl.ds(pl.multiple_of(thirds[third] * part, LANES), part)
            copies.append((pieces[piece].at[row : row + depth, :], wide.at[place, lanes]))
        piece, row = sources[3]
        copies.append((pieces[piece].at[row : row + PAD, :], gain_held.at[number]))
    fetch(copies, sems)
    lane = lax.broadcasted_iota(jnp.int32, (LANES, width), 1) - lax.broadcasted_iota(jnp.int32, (LANES, width), 0)
    gain_sum = jnp.zeros((PAD, width), f32)
    for number in range(groups):
        spread = jnp.where(lane == slots[number] * depth, 1.0, 0.0).astype(bf16)
        gain_sum += dot(gain_held[number][:, :LANES], spread)
    gain[...] = gain_sum
    gains = gain_sum[:1]
    query_w, key_w, value_w = (wide.at[:, at * local : (at + 1) * local] for at in range(3))
    low = lax.broadcasted_iota(jnp.int32, (1, LANES), 1) % HEAD < HEAD // 2

    def rotated(src, at, size, dst, place, scale):
        co, si = cosine[pl.ds(at, size), :], sine[pl.ds(at, size), :]
        for pair in range(pairs):
            lanes = slice(pair * LANES, (pair + 1) * LANES)
            value = src[:, lanes]
            dst[pl.ds(place, size), lanes] = ((value * co + turned(value, low) * si) * scale).astype(bf16)

    chunk = step_of(extent, 384)

    def key_step(index):
        at = pl.multiple_of(index * chunk, chunk)
        here = pl.ds(at, chunk)
        part = (hat[here, :] * gains).astype(bf16)
        first[here, :] = part
        rotated(dot(part, key_w[...]), at, chunk, key, at, 1.0)
        value[here, :] = dot(part, value_w[...]).astype(bf16)

    loop(extent // chunk, key_step)
    size = step_of(rows, 256)

    def query_step(index):
        at = pl.multiple_of(index * size, size)
        start = pl.multiple_of(at + HALF, HALF)
        rotated(dot(first[pl.ds(start, size), :], query_w[...]), start, size, query, at, HEAD**-0.5)

    loop(rows // size, query_step)


def attend_kernel(pair, bounds, query, key, value, shares, attended):
    rows = query.shape[0]
    lanes = slice(pair * LANES, (pair + 1) * LANES)
    key_at = lax.broadcasted_iota(jnp.int32, (KEYS, KEYS), 0)
    lane_at = lax.broadcasted_iota(jnp.int32, (1, KEYS), 1) % BLOCK

    def attend_step(index):
        at = pl.multiple_of(index * BLOCK, BLOCK)
        origin = bounds[NSEQ] + at - HALF
        own = lane_at + (origin + HALF)
        begin = jnp.zeros_like(own)
        end = jnp.zeros_like(own) + bounds[NSEQ - 1]
        for number in range(NSEQ - 1):
            begin = jnp.where(own >= bounds[number], bounds[number], begin)
        for number in reversed(range(NSEQ - 1)):
            end = jnp.where(own < bounds[number], bounds[number], end)
        least = jnp.maximum(lane_at, begin - origin)
        most = jnp.minimum(lane_at + WINDOW, end - 1 - origin)
        both = halves(query[pl.ds(at, BLOCK), lanes])
        raw = dot(key[pl.ds(at, KEYS), lanes], both, NT)
        scores = jnp.where((key_at >= least) & (key_at <= most), raw, -1e30)
        weight = jnp.exp(scores - jnp.max(scores, axis=0, keepdims=True))
        part = (weight * (1.0 / jnp.sum(weight, axis=0, keepdims=True))).astype(bf16)
        shares[index] = part
        mixed = dot(value[pl.ds(at, KEYS), lanes], part, TN)
        attended[pl.ds(at, BLOCK), :] = joined(mixed).astype(bf16)

    unrolled(rows // BLOCK, attend_step)


def unrolled(count, body, most=4):
    size = max(step for step in range(1, most + 1) if count % step == 0)

    def run(index):
        for step in range(size):
            body(index * size + step)

    loop(count // size, run)


def out_kernel(wide, *rest):
    parts, (attended, branch) = rest[:-2], rest[-2:]
    rows, local = attended.shape
    out_t = wide.at[:, 3 * local :]
    size = step_of(rows, 256)
    for pair, part in enumerate(parts):
        attended[:, pair * LANES : (pair + 1) * LANES] = part[...]

    def out_step(index):
        here = pl.ds(pl.multiple_of(index * size, size), size)
        branch[here, :] = dot(attended[here, :], out_t[...], NT).astype(bf16)

    loop(rows // size, out_step)


def feed_kernel(plan, slots, thirds, tokens, own, other, gain, cotangent, *rest):
    pieces, rest = rest[:-8], rest[-8:]
    middle, second, hidden, grad_gate, grad_upper, partial, whole, sems = rest
    rows, width = tokens.shape
    depth = width // len(plan)
    copies = []
    for number, sources in enumerate(plan):
        place = pl.ds(pl.multiple_of(slots[number] * depth, depth), depth)
        for third, (piece, row) in enumerate(sources):
            copies.append((pieces[piece].at[row : row + depth, :], whole.at[thirds[third], place, :]))
    fetch(copies, sems)
    gate_w, upper_w, down_t = (whole.at[number] for number in range(3))
    gains = gain[1:2, :]
    size = step_of(rows, 256)

    def step(index):
        at = pl.multiple_of(index * size, size)
        here = pl.ds(at, size)
        mid = tokens[here, :].astype(f32) + (own[here, :].astype(f32) + other[here, :].astype(f32))
        middle[here, :] = mid
        hat, _ = normed(mid)
        low = (hat * gains).astype(bf16)
        second[here, :] = low
        gate = dot(low, gate_w[...])
        upper = dot(low, upper_w[...])
        grad = dot(cotangent[here, :], down_t[...])
        share = 0.5 * (1.0 + lax.erf(gate * (0.5**0.5)))
        smooth = gate * share
        slope = share + gate * (jnp.exp(gate * gate * -0.5) * ((2.0 * math.pi) ** -0.5))
        hidden[here, :] = (smooth * upper).astype(bf16)
        gate_low = (grad * upper * slope).astype(bf16)
        upper_low = (grad * smooth).astype(bf16)
        grad_gate[here, :] = gate_low
        grad_upper[here, :] = upper_low
        partial[here, :] = (dot(gate_low, gate_w[...], NT) + dot(upper_low, upper_w[...], NT)).astype(bf16)

    loop(rows // size, step)


def weight_kernel(slots, thirds, second, hidden, grad_gate, grad_upper, cotangent, whole, feed, *rest):
    outs, total = rest[:-1], rest[-1]
    rows, width = second.shape
    size = step_of(rows, 256)
    step_rows = step_of(width, 256)
    for number, (left, right) in enumerate(((second, grad_gate), (second, grad_upper), (cotangent, hidden))):
        for start in range(0, width, step_rows):
            here = slice(start, start + step_rows)
            total[number, here, :] = dot(left[:, here], right[...], TN).astype(bf16)
    spread_out(outs, slots, lambda third, place: total[thirds[third], place, :])

    def step(index):
        here = pl.ds(pl.multiple_of(index * size, size), size)
        feed[here, :] = dot(hidden[here, :], whole[2], NT).astype(bf16)

    loop(rows // size, step)


def hop_order(count):
    middle = count // 2
    order = [middle]
    for hop in range(middle - 1, 0, -1):
        order += [hop, count - hop]
    return order + [0]


def spread_out(outs, slots, block):
    ring_one, ring_two, rest, *others = outs
    ringed = rest.shape[1]
    depth = rest.shape[2]
    order = hop_order(rest.shape[0] + 1)
    spot = 0
    lengths = [other.shape[0] for other in others]
    for number, slot in enumerate(order):
        place = pl.ds(pl.multiple_of(slots[slot] * depth, depth), depth)
        if number == 0:
            for third in range(ringed - 1):
                ring_one[third] = block(third, place)
            ring_two[0] = block(ringed - 1, place)
        else:
            for third in range(ringed):
                rest[number - 1, third] = block(third, place)
        if others:
            where = number - sum(lengths[:spot])
            others[spot][where] = block(2, place)
            if where + 1 == lengths[spot]:
                spot += 1


def spread_shapes(count, ringed, depth, size):
    shapes = [(ringed - 1, depth, size), (1, depth, size), (count - 1, ringed, depth, size)]
    if ringed == 2:
        shapes += [(1, depth, size)] + [(2, depth, size)] * (count // 2 - 1) + [(1, depth, size)]
    return [shape(dims, bf16) for dims in shapes]


def middle_kernel(middle, own, other, gain, cotangent, wide, grad_middle, low_mid, grad_att):
    rows, width = middle.shape
    local = grad_att.shape[1]
    out_t = wide.at[:, 3 * local :]
    gains = gain[1:2, :]
    size = step_of(rows, 256)

    def norm_step(index):
        here = pl.ds(pl.multiple_of(index * size, size), size)
        hat, scale = normed(middle[here, :])
        grad = own[here, :].astype(f32) + other[here, :].astype(f32)
        mid = cotangent[here, :].astype(f32) + norm_back(grad, gains, hat, scale)
        grad_middle[here, :] = mid
        mid_low = mid.astype(bf16)
        low_mid[here, :] = mid_low
        grad_att[here, :] = dot(mid_low, out_t[...]).astype(bf16)

    loop(rows // size, norm_step)


def back_kernel(pair, query, key, value, shares, grad_att, cosine, sine, grad_proj, grad_key, grad_value):
    rows = query.shape[0]
    extent = key.shape[0]
    lanes = slice(pair * LANES, (pair + 1) * LANES)
    grad_key[...] = jnp.zeros_like(grad_key)
    grad_value[...] = jnp.zeros_like(grad_value)
    low = lax.broadcasted_iota(jnp.int32, (1, LANES), 1) % HEAD < HEAD // 2
    zero = jnp.zeros((HALF, LANES), bf16)
    grad_proj[:HALF, :LANES] = zero
    grad_proj[rows + HALF :, :LANES] = zero

    def attend_step(index):
        at = pl.multiple_of(index * BLOCK, BLOCK)
        start = pl.multiple_of(at + HALF, HALF)
        co, si = cosine[pl.ds(start, BLOCK), :], sine[pl.ds(start, BLOCK), :]
        both = halves(query[pl.ds(at, BLOCK), lanes])
        grad = halves(grad_att[pl.ds(at, BLOCK), lanes])
        keys = key[pl.ds(at, KEYS), lanes]
        part = shares[index]
        wide = part.astype(f32)
        grad_shares = dot(value[pl.ds(at, KEYS), lanes], grad, NT)
        delta = jnp.sum(wide * grad_shares, axis=0, keepdims=True)
        raw = (wide * (grad_shares - delta)).astype(bf16)
        grad_query = joined(dot(keys, raw, TN)) * HEAD**-0.5
        grad_proj[pl.ds(start, BLOCK), :LANES] = (grad_query * co - turned(grad_query, low) * si).astype(bf16)
        grad_key[pl.ds(at, KEYS), :] += dot(raw, both)
        grad_value[pl.ds(at, KEYS), :] += dot(part, grad)

    unrolled(rows // BLOCK, attend_step)

    def turn_step(index):
        here = pl.ds(pl.multiple_of(index * BLOCK, BLOCK), BLOCK)
        part = grad_key[here, :]
        turn = part * cosine[here, :] - turned(part, low) * sine[here, :]
        grad_proj[here, LANES : 2 * LANES] = turn.astype(bf16)
        grad_proj[here, 2 * LANES :] = grad_value[here, :].astype(bf16)

    loop(extent // BLOCK, turn_step)


def grad_kernel(pairs, slots, thirds, first, low_mid, attended, *rest):
    parts, grad_proj, outs, total = rest[:pairs], rest[pairs], rest[pairs + 1 : -1], rest[-1]
    local = attended.shape[1]
    width = first.shape[1]
    size = total.shape[1] // 3
    for pair, part in enumerate(parts):
        for number in range(3):
            lanes = slice(number * local + pair * LANES, number * local + (pair + 1) * LANES)
            grad_proj[:, lanes] = part[:, number * LANES : (number + 1) * LANES]
    step_rows = step_of(width, 256)
    for start in range(0, width, step_rows):
        here = slice(start, start + step_rows)
        for number in range(3):
            lanes = slice(number * local, (number + 1) * local)
            total[here, lanes] = dot(first[:, here], grad_proj[:, lanes], TN).astype(bf16)
        total[here, 3 * local :] = dot(low_mid[:, here], attended[...], TN).astype(bf16)

    def block(third, place):
        return total[place, pl.ds(pl.multiple_of(thirds[third] * size, LANES), size)]

    spread_out(outs, slots, block)


def first_kernel(grad_proj, wide, partial):
    extent, inner = grad_proj.shape
    size = step_of(extent, 384)

    def step(index):
        here = pl.ds(pl.multiple_of(index * size, size), size)
        partial[here, :] = dot(grad_proj[here, :], wide[:, :inner], NT).astype(bf16)

    loop(extent // size, step)


def final_kernel(tokens, gain, grad_middle, own, other, before, after, middle, feed_own, feed_other, mixed, token_grad):
    rows, width = tokens.shape
    gains = gain[:1, :]
    size = BLOCK

    def back(here, grad):
        hat, scale = normed(tokens[here, :].astype(f32))
        return norm_back(grad, gains, hat, scale)

    def step(index):
        at = pl.multiple_of(index * size, size)
        here, wider = pl.ds(at, size), pl.ds(pl.multiple_of(at + HALF, HALF), size)
        grad = own[wider, :].astype(f32) + other[wider, :].astype(f32)
        token_grad[here, :] = grad_middle[here, :] + back(here, grad)
        feed = feed_own[here, :].astype(f32) + feed_other[here, :].astype(f32)
        mixed[here, :] = (middle[here, :] + feed).astype(bf16)

    loop(rows // size, step)
    for start, edge in ((0, before), (rows - HALF, after)):
        here = pl.ds(start, HALF)
        token_grad[here, :] += back(here, edge[...].astype(f32))


def exchange(initial, last):
    devices, spot = lax.axis_size("ctx"), lax.axis_index("ctx")
    if devices == 2:
        got = lax.ppermute(jnp.where(spot == 0, last, initial), "ctx", [(0, 1), (1, 0)])
        none = jnp.zeros_like(got)
        return jnp.where(spot == 1, got, none), jnp.where(spot == 0, got, none)
    up = [(i, i + 1) for i in range(devices - 1)]
    return lax.ppermute(last, "ctx", up), lax.ppermute(initial, "ctx", [(j, i) for i, j in up])


def swap(array, axis="tensor"):
    return lax.ppermute(array, axis, [(0, 1), (1, 0)])


def ring():
    count = lax.axis_size("dp")
    order = [2 * i for i in range(count // 2)] + [2 * i + 1 for i in reversed(range(count // 2))]
    ahead = [(order[i], order[(i + 1) % count]) for i in range(count)]
    back = [(j, i) for i, j in ahead]
    index = lax.axis_index("dp")
    spot = jnp.where(index % 2 == 0, index // 2, count - 1 - index // 2)
    place = (spot + jnp.arange(count, dtype=jnp.int32)) % count
    slots = jnp.where(place < count // 2, 2 * place, 2 * (count - 1 - place) + 1)
    return count, ahead, back, slots.astype(jnp.int32)


def tied(values, others):
    held = lax.optimization_barrier((tuple(values), tuple(others)))
    return held[0]


def locked(values, chain):
    held = lax.optimization_barrier((tuple(values), tuple(chain.state)))
    chain.state = held[1]
    return held[0]


def third_places():
    if lax.axis_size("ctx") == 2:
        spot = lax.axis_index("ctx")
        return jnp.stack([2 * spot, jnp.ones_like(spot), 2 - 2 * spot]).astype(jnp.int32)
    return jnp.arange(3, dtype=jnp.int32)


class RingGather:
    def __init__(self, blocks, extra=None):
        self.count, self.ahead, self.back, _ = ring()
        self.depth = blocks[0].shape[0]
        self.split = lax.axis_size("ctx") == 2
        if self.split:
            low = lax.axis_index("ctx") == 0
            mine, other = jnp.where(low, blocks[0], blocks[2]), jnp.where(low, blocks[2], blocks[0])
            ringed = [mine, blocks[1]]
        else:
            ringed = list(blocks)
        self.ringed = len(ringed)
        whole = jnp.concatenate(ringed + ([] if extra is None else [extra]))
        self.pieces = {0: (whole,)}
        self.others = {0: other} if self.split else {}
        self.state = (whole, whole)
        self.hops = 0

    def side(self):
        if not self.split or self.hops == 0:
            return
        one, two = self.state
        depth = self.depth
        if self.hops == self.count // 2:
            self.others[self.hops] = swap(one, "ctx")
        else:
            self.others[self.count - self.hops] = swap(one[:depth], "ctx")
            self.others[self.hops] = swap(two[:depth], "ctx")

    def hop(self):
        one, two = self.state
        middle = self.count // 2
        if self.hops + 1 == middle:
            cut = (self.ringed - 1) * self.depth
            one, two = one[:cut], two[cut:]
        ahead, behind = lax.ppermute(one, "dp", self.ahead), lax.ppermute(two, "dp", self.back)
        self.side()
        self.hops += 1
        one, two = lax.optimization_barrier((ahead, behind))
        self.state = (one, two)
        if self.hops == middle:
            self.pieces[middle] = (one, two)
        else:
            self.pieces[self.count - self.hops], self.pieces[self.hops] = (one,), (two,)

    def finish(self, extra):
        while self.hops < self.count // 2:
            self.hop()
        self.side()
        arrays, plan = [], []
        for slot in range(self.count):
            base, row, sources = len(arrays), 0, []
            held = self.pieces[slot]
            arrays += held
            for third in range(self.ringed):
                if len(held) == 2 and third == self.ringed - 1:
                    base, row = base + 1, 0
                sources.append((base, row))
                row += self.depth
            if self.split:
                sources.append((len(arrays), 0))
                arrays.append(self.others[slot])
            if extra:
                sources.append((base, row))
            plan.append(tuple(sources))
        return tuple(plan), arrays


class RingScatter:
    def __init__(self, outs):
        self.count, self.ahead, self.back, _ = ring()
        self.start = outs[:2]
        self.parts = outs[2]
        self.others = outs[3:]
        self.split = len(self.others) > 0
        self.sides = []
        self.hops = 0
        self.state = ()
        self.side()

    def side(self):
        if self.split and len(self.sides) < len(self.others):
            self.sides.append(swap(self.others[len(self.sides)], "ctx"))

    def summed(self, at, extra):
        part = self.parts[at]
        if extra is not None:
            part = part + jnp.concatenate([extra[None], jnp.zeros_like(part[1:])])
        return part

    def hop(self):
        if self.hops == 0:
            one, two = self.start
            if self.split:
                one = one + self.sides[0]
        else:
            one, two = self.state
            if self.hops == 1:
                one = jnp.concatenate([one, jnp.zeros_like(two)])
                two = jnp.concatenate([jnp.zeros_like(one[:-1]), two])
            at = 2 * self.hops - 2
            first, second = self.sides[self.hops] if self.split else (None, None)
            one, two = self.summed(at, first) + one, self.summed(at + 1, second) + two
        one, two = lax.ppermute(one, "dp", self.ahead), lax.ppermute(two, "dp", self.back)
        self.side()
        self.state = lax.optimization_barrier((one, two))
        self.hops += 1

    def finish(self):
        while self.hops < self.count // 2:
            self.hop()
        one, two = self.state
        last = self.sides[-1][0] if self.split else None
        total = (self.summed(self.count - 2, last).astype(f32) + one.astype(f32) + two.astype(f32)).astype(bf16)
        if not self.split:
            return lax.psum(total, "ctx").astype(f32)
        got = swap(total, "ctx").astype(f32)
        total = total.astype(f32)
        low = lax.axis_index("ctx") == 0
        shared = total[1] + got[1]
        return jnp.stack([jnp.where(low, total[0], got[0]), shared, jnp.where(low, got[0], total[0])])


def tables(lengths, rows):
    place = lax.axis_index("ctx") * rows
    ends = jnp.cumsum(lengths[0])
    starts = ends - lengths[0]
    span = place + jnp.arange(-HALF, rows + HALF, dtype=jnp.int32)
    inside = (span[:, None] >= starts[None, :]) & (span[:, None] < ends[None, :])
    position = span - jnp.sum(jnp.where(inside, starts[None, :], 0), axis=1)
    number = (jnp.arange(HEAD, dtype=jnp.int32) % (HEAD // 2)).astype(f32)
    freq = jnp.exp(number * (-2.0 * math.log(10000.0) / HEAD))
    angle = position.astype(f32)[:, None] * freq[None, :]
    cosine, sine = jnp.cos(angle), jnp.sin(angle)
    sine = jnp.where(jnp.arange(HEAD)[None, :] < HEAD // 2, -sine, sine)
    bounds = jnp.concatenate([ends, place[None]]).astype(jnp.int32)
    return jnp.tile(cosine, (1, 2)), jnp.tile(sine, (1, 2)), bounds


def body(tokens, lengths, gain_one, w_qkv, w_out, gain_two, w_in, w_down, cotangent):
    rows, width = tokens.shape
    local, units = w_out.shape[0], w_down.shape[0]
    pairs, blocks, extent = local // LANES, rows // BLOCK, rows + WINDOW
    groups = lax.axis_size("dp")
    depth = width // groups
    size = 4 * local // 3
    gains = jnp.pad(jnp.stack([gain_one, gain_two]), ((0, PAD - 2), (0, size - depth)))
    joint = jnp.concatenate([w_qkv[0], w_qkv[1], w_qkv[2], w_out.T], axis=1)
    now = RingGather([joint[:, at * size : (at + 1) * size] for at in range(3)], gains)
    now.hop()
    before, after = exchange(tokens[:HALF], tokens[rows - HALF :])
    slots, thirds = ring()[-1], third_places()
    cosine, sine, bounds = tables(lengths, rows)
    hat, = call(
        norm_kernel, [shape((extent, width), f32)], (tokens, before, after), rows * width * 2000, "first_norm"
    )
    while now.hops < groups // 2:
        now.hop()
    blocks_two = tied([w_in[0], w_in[1], w_down.T], now.state)
    later = RingGather(blocks_two)
    later.hop()
    plan, pieces = now.finish(True)
    wide, gain, first, query, key, value = call(
        functools.partial(project_kernel, plan),
        [
            shape((width, 4 * local), bf16),
            shape((PAD, width), f32),
            shape((extent, width), bf16),
            shape((rows, local), bf16),
            shape((extent, local), bf16),
            shape((extent, local), bf16),
        ],
        (hat, cosine, sine),
        2 * rows * width * local * 8,
        "project",
        (slots, thirds),
        [pltpu.VMEM((groups, PAD, size), bf16), pltpu.SemaphoreType.DMA((4 * groups,))],
        pieces,
    )
    shares, attended_parts = [], []
    for pair in range(pairs):
        if pair in (0, pairs - 1):
            query, key, value = locked([query, key, value], later)
            later.hop()
        part, attended = call(
            functools.partial(attend_kernel, pair),
            [shape((blocks, KEYS, KEYS), bf16), shape((rows, LANES), bf16)],
            (query, key, value),
            2 * rows * width * local * 5,
            "attend",
            (bounds,),
        )
        shares.append(part)
        attended_parts.append(attended)
    attended, branch = call(
        out_kernel,
        [shape((rows, local), bf16), shape((rows, width), bf16)],
        (wide, *attended_parts),
        2 * rows * width * local * 2,
        "attention_out",
    )
    branch, = locked([branch], later)
    branch_other = swap(branch)
    plan, pieces = later.finish(False)
    middle, second, hidden, grad_gate, grad_upper, partial, whole = call(
        functools.partial(feed_kernel, plan),
        [
            shape((rows, width), f32),
            shape((rows, width), bf16),
            shape((rows, units), bf16),
            shape((rows, units), bf16),
            shape((rows, units), bf16),
            shape((rows, width), bf16),
            shape((3, width, units), bf16),
        ],
        (tokens, branch, branch_other, gain, cotangent),
        2 * rows * width * units * 8,
        "feed_forward_and_back",
        (slots, thirds),
        [pltpu.SemaphoreType.DMA((3 * groups,))],
        pieces,
    )
    partial_other = swap(partial)
    ringed = now.ringed
    feed, *grads_two = call(
        weight_kernel,
        [shape((rows, width), bf16)] + spread_shapes(groups, ringed, depth, units),
        (second, hidden, grad_gate, grad_upper, cotangent, whole),
        2 * rows * width * units * 5,
        "feed_weight_grads",
        (slots, thirds),
        [pltpu.VMEM((3, width, units), bf16)],
    )
    feed_other = swap(feed)
    sums_two = RingScatter(grads_two)
    grad_middle, low_mid, grad_att = call(
        middle_kernel,
        [shape((rows, width), f32), shape((rows, width), bf16), shape((rows, local), bf16)],
        (middle, partial, partial_other, gain, cotangent, wide),
        2 * rows * width * local * 4,
        "middle_grad",
    )
    sums_two.state = sums_two.sides if sums_two.split else ()
    grad_att, = tied([grad_att], sums_two.state)
    sums_two.hop()
    grad_parts = []
    for pair in range(pairs):
        if pair:
            grad_att, = locked([grad_att, *grad_parts], sums_two)[:1]
            sums_two.hop()
        grad_part, = call(
            functools.partial(back_kernel, pair),
            [shape((extent, 3 * LANES), bf16)],
            (query, key, value, shares[pair], grad_att, cosine, sine),
            2 * rows * width * local * 5,
            "attention_back",
            (),
            [pltpu.VMEM((extent, LANES), f32)] * 2,
        )
        grad_parts.append(grad_part)
    grad_parts = locked(grad_parts, sums_two)
    sums_two.hop()
    grad_proj, *grads_one = call(
        functools.partial(grad_kernel, pairs),
        [shape((extent, 3 * local), bf16)] + spread_shapes(groups, ringed, depth, size),
        (first, low_mid, attended, *grad_parts),
        2 * rows * width * local * 6,
        "attention_weight_grads",
        (slots, thirds),
        [pltpu.VMEM((width, 4 * local), bf16)],
    )
    sums_two.state = tied(sums_two.state, grads_one)
    sums_one = RingScatter(grads_one)
    one = sums_one.finish()
    two = sums_two.finish()
    first_part, = call(
        first_kernel,
        [shape((extent, width), bf16)],
        (grad_proj, wide),
        2 * rows * width * local * 3,
        "first_grad",
    )
    first_other = swap(first_part)

    def edge_sum(at):
        here = slice(at, at + HALF)
        return (first_part[here].astype(f32) + first_other[here].astype(f32)).astype(bf16)

    from_before, from_after = exchange(edge_sum(0), edge_sum(rows + HALF))
    mixed, token_grad = call(
        final_kernel,
        [shape((rows, width), bf16), shape((rows, width), f32)],
        (tokens, gain, grad_middle, first_part, first_other, from_before, from_after, middle, feed, feed_other),
        rows * width * 2000,
        "token_grad",
    )
    joint_grad = jnp.concatenate([one[0], one[1], one[2]], axis=1)
    grad_qkv = [joint_grad[:, at * local : (at + 1) * local] for at in range(4)]
    qkv = jnp.stack(grad_qkv[:3])
    gain_one_grad = jnp.sum(qkv * w_qkv.astype(f32), axis=(0, 2)) / gain_one.astype(f32)
    gain_two_grad = jnp.sum(two[:2] * w_in.astype(f32), axis=(0, 2)) / gain_two.astype(f32)
    both = jnp.stack([gain_one_grad, gain_two_grad])
    both = both + swap(both)
    return (mixed, token_grad, both[0], qkv, grad_qkv[3].T, both[1], two[:2], two[2].T)


def solution(mesh):
    in_specs = (
        P(("dp", "ctx"), None),
        P("dp", None),
        P("dp"),
        P(None, "dp", "tensor"),
        P("tensor", "dp"),
        P("dp"),
        P(None, "dp", "tensor"),
        P("tensor", "dp"),
        P(("dp", "ctx"), None),
    )
    out_specs = (
        P(("dp", "ctx"), None),
        P(("dp", "ctx"), None),
        P("dp"),
        P(None, "dp", "tensor"),
        P("tensor", "dp"),
        P("dp"),
        P(None, "dp", "tensor"),
        P("tensor", "dp"),
    )
    return jax.shard_map(body, mesh=mesh, in_specs=in_specs, out_specs=out_specs, check_vma=False)
```

time: 208 us -> 228 us (1.096)
  starting transfers between devices: 40.1 us -> 60.9 us
  Pallas kernels: 64.7 us -> 73.5 us
  local copies, waits for them, and re-layouts: 19.2 us -> 11.1 us
  waiting for transfers between devices: 72.5 us -> 69.9 us
    ppermute x7 -> x31, waiting for transfers between devices: 4.32 us -> 39.5 us  [swap(): return lax.ppermute(array, axis, [(0, 1), (1, 0)])]
    ppermute x16, waiting for transfers between devices: 42 us -> 14.2 us  [hop(): lax.ppermute(one, 'dp', self.ahead)]
    ppermute x7 -> x31, starting transfers between devices: 2.37 us -> 24.1 us  [swap(): return lax.ppermute(array, axis, [(0, 1), (1, 0)])]
    ppermute x16, starting transfers between devices: 25.3 us -> 10.2 us  [hop(): lax.ppermute(one, 'dp', self.ahead)]
    ppermute x16, starting transfers between devices: 8.87 us -> 23 us  [hop(): lax.ppermute(two, 'dp', self.back)]
    pallas_call x9 -> x15, Pallas kernels: 64.7 us -> 73.5 us  [call(): pl.pallas_call(kernel, out_shape=out_shape, in_specs=[smem] * len(scalars...]
    ppermute x2, waiting for transfers between devices: 8.12 us -> 2.72 us  [exchange(): lax.ppermute(jnp.where(spot == 0, last, initial), 'ctx', [(0, 1), (1, 0)])]
    unnamed x45 -> x34, local copies, waits for them, and re-layouts: 10.3 us -> 4.93 us
  transfers between devices with their start and end apart: 41 -> 65, of which waited for: 20 -> 36; matrix products, arithmetic and copies ran while one was open for 8% -> 6% of each run, Pallas kernels for 24% -> 23%
where the time goes in v4:
time: 228 us
  Pallas kernels  73.5 us (32%)
  waiting for transfers between devices  69.9 us (31%)
  starting transfers between devices  60.9 us (27%)
  local copies, waits for them, and re-layouts  11.1 us (5%)
  other arithmetic  11.1 us (5%)
    pallas_call x15, Pallas kernels, call(): pl.pallas_call(kernel, out_shape=out_shape, in_specs=[smem] * len(scalars...  73.5 us
    ppermute x31, waiting for transfers between devices, swap(): return lax.ppermute(array, axis, [(0, 1), (1, 0)])  39.5 us
    ppermute x31, starting transfers between devices, swap(): return lax.ppermute(array, axis, [(0, 1), (1, 0)])  24.1 us
    ppermute x16, starting transfers between devices, hop(): lax.ppermute(two, 'dp', self.back)  23 us
    ppermute x16, waiting for transfers between devices, hop(): lax.ppermute(one, 'dp', self.ahead)  14.2 us
    ppermute x16, waiting for transfers between devices, hop(): lax.ppermute(two, 'dp', self.back)  13.4 us
    ppermute x16, starting transfers between devices, hop(): lax.ppermute(one, 'dp', self.ahead)  10.2 us
    unnamed x34, local copies, waits for them, and re-layouts  4.93 us
  transfers between devices with their start and end apart: 65, of which 36 were waited for; matrix products, arithmetic and copies ran while one was open for 6% of the time, Pallas kernels for 23%

profile of v4, /device:TPU:0, one launch (start us, length us, event | category | flops | bytes accessed | tf_op | source)
XLA Modules:
  0.0 227.8 jit_solution(2514200497104671308)
XLA Ops:
  3.3 3.0 %collective-permute-start.2 = (bf16[208,512]{1,0:T(8,128)(2,1)S(1)}, bf16[208,512]{1,0:T(8,128)(2,1)S(1)}, u32[]{:S(2)}, u32[]{:S(2)}) collective-permute-start(bf16[208,512]{1,0:T(8,128)(2,1)S(1)} %fusion.7.rest_0_), channel_id=1, source_target_pairs={{8,0},{16,8},{24,16},{28,24},{20,28},{12,20},{4,12},{0,4},{9,1},{1... | collective-permute-start | bytes 638984 | tf_op jit(solution)/shard_map/ppermute | solution.py:527
  18.9 4.0 %collective-permute-done.5.rest_4_ = bf16[208,512]{1,0:T(8,128)(2,1)S(1)} collective-permute-done((bf16[208,512]{1,0:T(8,128)(2,1)S(1)}, bf16[208,512]{1,0:T(8,128)(2,1)S(1)}, u32[]{:S(2)}, u32[]{:S(2)}) %collective-permute-start.5) | collective-permute-done | bytes 213024 | tf_op jit(solution)/shard_map/ppermute | solution.py:527
  27.1 2.9 %collective-permute-done.8.rest_6_ = bf16[208,512]{1,0:T(8,128)(2,1)S(1)} collective-permute-done((bf16[208,512]{1,0:T(8,128)(2,1)S(1)}, bf16[208,512]{1,0:T(8,128)(2,1)S(1)}, u32[]{:S(2)}, u32[]{:S(2)}) %collective-permute-start.8) | collective-permute-done | bytes 213024 | tf_op jit(solution)/shard_map/ppermute | solution.py:527
  49.3 6.4 %project.1 = (bf16[768,1536]{1,0:T(8,128)(2,1)S(1)}, f32[16,768]{1,0:T(8,128)S(1)}, bf16[1152,768]{1,0:T(8,128)(2,1)S(1)}, bf16[1024,384]{1,0:T(8,128)(2,1)S(1)}...) custom-call(s32[8]{0:T(128)S(1)} %compare_select_fusion.2.slots, s32[3]{0:T(128)S(1)} %pad_add_fusion.thirds, ...), custom_call_target="tpu_custom_call" | custom-call | flops 4831838208 | bytes 11452416 | tf_op jit(solution)/shard_map/project/pallas_call | solution.py:48
  57.9 3.7 %attend.4 = (bf16[8,256,256]{2,1,0:T(8,128)(2,1)S(1)}, bf16[1024,128]{1,0:T(8,128)(2,1)S(1)}) custom-call(s32[5]{0:T(128)S(1)} %pad_add_fusion.1.bounds, bf16[1024,384]{1,0:T(8,128)(2,1)S(1)} %get-tuple-element.141.query, bf16[1152,384]{1,0:T(8,128)(2,1)S(1)} %get-tuple-element.142.key, bf16[1152,384]{1,0:T(8,128)(2,1)S(1)} %get-tuple-element.143.value), custom_call_target="tpu_custom_call" | custom-call | flops 3019898880 | bytes 3866624 | tf_op jit(solution)/shard_map/attend/pallas_call | solution.py:48
  61.5 3.7 %attend.3 = (bf16[8,256,256]{2,1,0:T(8,128)(2,1)S(1)}, bf16[1024,128]{1,0:T(8,128)(2,1)S(1)}) custom-call(s32[5]{0:T(128)S(1)} %pad_add_fusion.1.bounds, bf16[1024,384]{1,0:T(8,128)(2,1)S(1)} %get-tuple-element.141.query, bf16[1152,384]{1,0:T(8,128)(2,1)S(1)} %get-tuple-element.142.key, bf16[1152,384]{1,0:T(8,128)(2,1)S(1)} %get-tuple-element.143.value), custom_call_target="tpu_custom_call" | custom-call | flops 3019898880 | bytes 3866624 | tf_op jit(solution)/shard_map/attend/pallas_call | solution.py:48
  67.3 3.7 %attend.5 = (bf16[8,256,256]{2,1,0:T(8,128)(2,1)S(1)}, bf16[1024,128]{1,0:T(8,128)(2,1)S(1)}) custom-call(s32[5]{0:T(128)S(1)} %pad_add_fusion.1.bounds, bf16[1024,384]{1,0:T(8,128)(2,1)S(1)} %get-tuple-element.141.query, bf16[1152,384]{1,0:T(8,128)(2,1)S(1)} %get-tuple-element.142.key, bf16[1152,384]{1,0:T(8,128)(2,1)S(1)} %get-tuple-element.143.value), custom_call_target="tpu_custom_call" | custom-call | flops 3019898880 | bytes 3866624 | tf_op jit(solution)/shard_map/attend/pallas_call | solution.py:48
  92.0 2.6 %collective-permute-done.25.rest_7_ = bf16[96,576]{1,0:T(8,128)(2,1)S(1)} collective-permute-done((bf16[96,576]{1,0:T(8,128)(2,1)S(1)}, bf16[96,576]{1,0:T(8,128)(2,1)S(1)}, u32[]{:S(2)}, u32[]{:S(2)}) %collective-permute-start.25) | collective-permute-done | bytes 110624 | tf_op jit(solution)/shard_map/ppermute | solution.py:459
  96.3 15.0 %feed_forward_and_back.1 = (f32[1024,768]{1,0:T(8,128)S(1)}, bf16[1024,768]{1,0:T(8,128)(2,1)S(1)}, bf16[1024,576]{1,0:T(8,128)(2,1)S(1)}, bf16[1024,576]{1,0:T(...) custom-call(s32[8]{0:T(128)S(1)} %compare_select_fusion.2.slots, ...), custom_call_target="tpu_custom_call" | custom-call | flops 7247757312 | bytes 18825216 | tf_op jit(solution)/shard_map/feed_forward_and_back/pallas_call | solution.py:48
  116.1 6.7 %feed_weight_grads.1 = (bf16[1024,768]{1,0:T(8,128)(2,1)S(1)}, bf16[1,96,576]{2,1,0:T(8,128)(2,1)S(1)}, bf16[1,96,576]{2,1,0:T(8,128)(2,1)S(1)}, bf16[7,2,96,576...) custom-call(s32[8]{0:T(128)S(1)} %compare_select_fusion.2.slots, ...), custom_call_target="tpu_custom_call" | custom-call | flops 4529848320 | bytes 13565952 | tf_op jit(solution)/shard_map/feed_weight_grads/pallas_call | solution.py:48
  127.2 7.1 %collective-permute-done.33 = bf16[1,96,576]{2,1,0:T(8,128)(2,1)S(1)} collective-permute-done((bf16[1,96,576]{2,1,0:T(8,128)(2,1)S(1)}, bf16[1,96,576]{2,1,0:T(8,128)(2,1)S(1)}, u32[]{:S(2)}, u32[]{:S(2)}) %collective-permute-start.33) | collective-permute-done | bytes 110624 | tf_op jit(solution)/shard_map/ppermute | solution.py:459
  135.5 4.0 %collective-permute-done.39 = bf16[2,96,576]{2,1,0:T(8,128)(2,1)S(1)} collective-permute-done((bf16[2,96,576]{2,1,0:T(8,128)(2,1)S(1)}, bf16[2,96,576]{2,1,0:T(8,128)(2,1)S(1)}, u32[]{:S(2)}, u32[]{:S(2)}) %collective-permute-start.39) | collective-permute-done | bytes 221216 | tf_op jit(solution)/shard_map/ppermute | solution.py:459
  139.5 3.6 %middle_grad.1 = (f32[1024,768]{1,0:T(8,128)S(1)}, bf16[1024,768]{1,0:T(8,128)(2,1)S(1)}, bf16[1024,384]{1,0:T(8,128)(2,1)S(1)}) custom-call(f32[1024,768]{1,0:T(8,128)S(1)} %get-tuple-element.155.middle, bf16[1024,768]{1,0:T(8,128)(2,1)S(1)} %get-tuple-element.156.own, bf16[1024,768]{1,0:T(8,128)(2,1)S(1)} %collective-permute-done.32.other, ...), custom_call_target="tpu_custom_call" | custom-call | flops 2415919104 | bytes 15777792 | tf_op jit(solution)/shard_map/middle_grad/pallas_call | solution.py:48
  143.2 4.4 %attention_back.3.rest_0_ = bf16[1152,384]{1,0:T(8,128)(2,1)S(1)} custom-call(bf16[1024,384]{1,0:T(8,128)(2,1)S(1)} %get-tuple-element.141.query, bf16[1152,384]{1,0:T(8,128)(2,1)S(1)} %get-tuple-element.142.key, bf16[1152,384]{1,0:T(8,128)(2,1)S(1)} %get-tuple-element.143.value, bf16[8,256,256]{2,1,0:T(8,128)(2,1)S(1)} %get-tuple-element.161.shares, ...), custom_call_target="tpu_custom_call" | custom-call | flops 3019898880 | bytes 6455296 | tf_op jit(solution)/shard_map/attention_back/pallas_call | solution.py:48
  149.9 4.4 %attention_back.4.rest_1_ = bf16[1152,384]{1,0:T(8,128)(2,1)S(1)} custom-call(bf16[1024,384]{1,0:T(8,128)(2,1)S(1)} %get-tuple-element.141.query, bf16[1152,384]{1,0:T(8,128)(2,1)S(1)} %get-tuple-element.142.key, bf16[1152,384]{1,0:T(8,128)(2,1)S(1)} %get-tuple-element.143.value, bf16[8,256,256]{2,1,0:T(8,128)(2,1)S(1)} %get-tuple-element.170.shares, ...), custom_call_target="tpu_custom_call" | custom-call | flops 3019898880 | bytes 6455296 | tf_op jit(solution)/shard_map/attention_back/pallas_call | solution.py:48
  158.6 4.4 %attention_back.5.rest_2_ = bf16[1152,384]{1,0:T(8,128)(2,1)S(1)} custom-call(bf16[1024,384]{1,0:T(8,128)(2,1)S(1)} %get-tuple-element.141.query, bf16[1152,384]{1,0:T(8,128)(2,1)S(1)} %get-tuple-element.142.key, bf16[1152,384]{1,0:T(8,128)(2,1)S(1)} %get-tuple-element.143.value, bf16[8,256,256]{2,1,0:T(8,128)(2,1)S(1)} %get-tuple-element.176.shares, ...), custom_call_target="tpu_custom_call" | custom-call | flops 3019898880 | bytes 6455296 | tf_op jit(solution)/shard_map/attention_back/pallas_call | solution.py:48
  164.3 4.7 %attention_weight_grads.1 = (bf16[1152,1152]{1,0:T(8,128)(2,1)S(1)}, bf16[1,96,512]{2,1,0:T(8,128)(2,1)S(1)}, bf16[1,96,512]{2,1,0:T(8,128)(2,1)S(1)}, bf16[7,2,...) custom-call(s32[8]{0:T(128)S(1)} %compare_select_fusion.2.slots, ...), custom_call_target="tpu_custom_call" | custom-call | flops 3623878656 | bytes 11796480 | tf_op jit(solution)/shard_map/attention_weight_grads/pallas_call | solution.py:48
  176.5 3.0 %collective-permute-done.50 = bf16[1,96,512]{2,1,0:T(8,128)(2,1)S(1)} collective-permute-done((bf16[1,96,512]{2,1,0:T(8,128)(2,1)S(1)}, bf16[1,96,512]{2,1,0:T(8,128)(2,1)S(1)}, u32[]{:S(2)}, u32[]{:S(2)}) %collective-permute-start.50) | collective-permute-done | bytes 98336 | tf_op jit(solution)/shard_map/ppermute | solution.py:595
  180.2 3.7 %collective-permute-done.48 = bf16[2,96,512]{2,1,0:T(8,128)(2,1)S(1)} collective-permute-done((bf16[2,96,512]{2,1,0:T(8,128)(2,1)S(1)}, bf16[2,96,512]{2,1,0:T(8,128)(2,1)S(1)}, u32[]{:S(2)}, u32[]{:S(2)}) %collective-permute-start.48) | collective-permute-done | bytes 196640 | tf_op jit(solution)/shard_map/ppermute | solution.py:459
  195.9 2.9 %first_grad.1.own = bf16[1152,768]{1,0:T(8,128)(2,1)S(1)} custom-call(bf16[1152,1152]{1,0:T(8,128)(2,1)S(1)} %get-tuple-element.192.grad_proj, bf16[768,1536]{1,0:T(8,128)(2,1)S(1)} %get-tuple-element.123.wide), custom_call_target="tpu_custom_call" | custom-call | flops 1811939328 | bytes 6782976 | tf_op jit(solution)/shard_map/first_grad/pallas_call | solution.py:48
  203.3 3.9 %collective-permute-done.57 = bf16[2,96,512]{2,1,0:T(8,128)(2,1)S(1)} collective-permute-done((bf16[2,96,512]{2,1,0:T(8,128)(2,1)S(1)}, bf16[2,96,512]{2,1,0:T(8,128)(2,1)S(1)}, u32[]{:S(2)}, u32[]{:S(2)}) %collective-permute-start.57) | collective-permute-done | bytes 196640 | tf_op jit(solution)/shard_map/ppermute | solution.py:595
  210.2 3.4 %collective-permute-done.58 = bf16[2,96,512]{2,1,0:T(8,128)(2,1)S(1)} collective-permute-done((bf16[2,96,512]{2,1,0:T(8,128)(2,1)S(1)}, bf16[2,96,512]{2,1,0:T(8,128)(2,1)S(1)}, u32[]{:S(2)}, u32[]{:S(2)}) %collective-permute-start.58) | collective-permute-done | bytes 196640 | tf_op jit(solution)/shard_map/ppermute | solution.py:459
  219.0 2.7 %collective-permute-done.43 = bf16[64,768]{1,0:T(8,128)(2,1)S(1)} collective-permute-done((bf16[64,768]{1,0:T(8,128)(2,1)S(1)}, bf16[64,768]{1,0:T(8,128)(2,1)S(1)}, u32[]{:S(2)}, u32[]{:S(2)}) %collective-permute-start.43) | collective-permute-done | bytes 98336 | tf_op jit(solution)/shard_map/ppermute | solution.py:451
  221.7 6.0 %token_grad.1 = (bf16[1024,768]{1,0:T(8,128)(2,1)}, f32[1024,768]{1,0:T(8,128)}) custom-call(bf16[1024,768]{1,0:T(8,128)(2,1)S(1)} %copy-done, f32[16,768]{1,0:T(8,128)S(1)} %get-tuple-element.122.gain, f32[1024,768]{1,0:T(8,128)S(1)} %get-tuple-element.157.grad_middle, bf16[1152,768]{1,0:T(8,128)(2,1)S(1)} %first_grad.1.own, ...), custom_call_target="tpu_custom_call" | custom-call | flops 1572864000 | bytes 19513344 | tf_op jit(solution)/shard_map/token_grad/pallas_call | solution.py:48
  (223 shorter events, 116.3 us)
Async XLA Ops:
  3.3 13.4 %collective-permute-start.2 = (bf16[208,512]{1,0:T(8,128)(2,1)S(1)}, bf16[208,512]{1,0:T(8,128)(2,1)S(1)}, u32[]{:S(2)}, u32[]{:S(2)}) collective-permute-start(bf16[208,512]{1,0:T(8,128)(2,1)S(1)} %fusion.7.rest_0_), channel_id=1, source_target_pairs={{8,0},{16,8},{24,16},{28,24},{20,28},{12,20},{4,12},{0,4},{9,1},{1... | collective-permute-start | bytes 638984 | tf_op jit(solution)/shard_map/ppermute | solution.py:527
  6.3 10.4 %collective-permute-start.1 = (bf16[208,512]{1,0:T(8,128)(2,1)S(1)}, bf16[208,512]{1,0:T(8,128)(2,1)S(1)}, u32[]{:S(2)}, u32[]{:S(2)}) collective-permute-start(bf16[208,512]{1,0:T(8,128)(2,1)S(1)} %fusion.7.rest_0_), channel_id=1, source_target_pairs={{0,8},{8,16},{16,24},{24,28},{28,20},{20,12},{12,4},{4,0},{1,9},{9... | collective-permute-start | bytes 638984 | tf_op jit(solution)/shard_map/ppermute | solution.py:527
  8.0 18.2 %collective-permute-start = (bf16[64,768]{1,0:T(8,128)(2,1)}, bf16[64,768]{1,0:T(8,128)(2,1)}, u32[]{:S(2)}, u32[]{:S(2)}) collective-permute-start(bf16[64,768]{1,0:T(8,128)(2,1)} %slice_select_fusion.1), channel_id=1, source_target_pairs={{0,2},{2,0},{1,3},{3,1},{4,6},{6,4},{5,7},{7,5},{8,10},{10,8},{9,1... | collective-permute-start | bytes 294920 | tf_op jit(solution)/shard_map/ppermute | solution.py:451
  45.1 10.6 %collective-permute-start.17 = (bf16[192,576]{1,0:T(8,128)(2,1)S(1)}, bf16[192,576]{1,0:T(8,128)(2,1)S(1)}, u32[]{:S(2)}, u32[]{:S(2)}) collective-permute-start(bf16[192,576]{1,0:T(8,128)(2,1)S(1)} %pad_maximum_fusion.2.rest_0_), channel_id=1, source_target_pairs={{8,0},{16,8},{24,16},{28,24},{20,28},{12,20},{4,12},{0,4},{9,1},{1... | collective-permute-start | bytes 663560 | tf_op jit(solution)/shard_map/ppermute | solution.py:527
  46.7 9.1 %collective-permute-start.16 = (bf16[192,576]{1,0:T(8,128)(2,1)S(1)}, bf16[192,576]{1,0:T(8,128)(2,1)S(1)}, u32[]{:S(2)}, u32[]{:S(2)}) collective-permute-start(bf16[192,576]{1,0:T(8,128)(2,1)S(1)} %pad_maximum_fusion.2.rest_0_), channel_id=1, source_target_pairs={{0,8},{8,16},{16,24},{24,28},{28,20},{20,12},{12,4},{4,0},{1,9},{9... | collective-permute-start | bytes 663560 | tf_op jit(solution)/shard_map/ppermute | solution.py:527
  55.8 9.5 %collective-permute-start.18 = (bf16[192,576]{1,0:T(8,128)(2,1)S(1)}, bf16[192,576]{1,0:T(8,128)(2,1)S(1)}, u32[]{:S(2)}, u32[]{:S(2)}) collective-permute-start(bf16[192,576]{1,0:T(8,128)(2,1)S(1)} %collective-permute-done.16.rest_15_), channel_id=1, source_target_pairs={{0,8},{8,16},{16,24},{24,28},{28,20},{20,12},{12,4},{4,0},{1,9},{9... | collective-permute-start | bytes 663560 | tf_op jit(solution)/shard_map/ppermute | solution.py:527
  72.8 23.5 %collective-permute-start.22 = (bf16[1024,768]{1,0:T(8,128)(2,1)S(1)}, bf16[1024,768]{1,0:T(8,128)(2,1)S(1)}, u32[]{:S(2)}, u32[]{:S(2)}) collective-permute-start(bf16[1024,768]{1,0:T(8,128)(2,1)S(1)} %get-tuple-element.150.own), channel_id=1, source_target_pairs={{0,1},{1,0},{2,3},{3,2},{4,5},{5,4},{6,7},{7,6},{8,9},{9,8},{10,11... | collective-permute-start | bytes 4718600 | tf_op jit(solution)/shard_map/ppermute | solution.py:459
  79.4 10.0 %collective-permute-start.30 = (bf16[96,576]{1,0:T(8,128)(2,1)S(1)}, bf16[96,576]{1,0:T(8,128)(2,1)S(1)}, u32[]{:S(2)}, u32[]{:S(2)}) collective-permute-start(bf16[96,576]{1,0:T(8,128)(2,1)S(1)} %slice.210), channel_id=1, source_target_pairs={{0,2},{2,0},{1,3},{3,1},{4,6},{6,4},{5,7},{7,5},{8,10},{10,8},{9,1... | collective-permute-start | bytes 331784 | tf_op jit(solution)/shard_map/ppermute | solution.py:459
  81.5 10.5 %collective-permute-start.29 = (bf16[96,576]{1,0:T(8,128)(2,1)S(1)}, bf16[96,576]{1,0:T(8,128)(2,1)S(1)}, u32[]{:S(2)}, u32[]{:S(2)}) collective-permute-start(bf16[96,576]{1,0:T(8,128)(2,1)S(1)} %slice.208), channel_id=1, source_target_pairs={{0,2},{2,0},{1,3},{3,1},{4,6},{6,4},{5,7},{7,5},{8,10},{10,8},{9,1... | collective-permute-start | bytes 331784 | tf_op jit(solution)/shard_map/ppermute | solution.py:459
  84.1 10.5 %collective-permute-start.25 = (bf16[96,576]{1,0:T(8,128)(2,1)S(1)}, bf16[96,576]{1,0:T(8,128)(2,1)S(1)}, u32[]{:S(2)}, u32[]{:S(2)}) collective-permute-start(bf16[96,576]{1,0:T(8,128)(2,1)S(1)} %get-tuple-element.249), channel_id=1, source_target_pairs={{0,2},{2,0},{1,3},{3,1},{4,6},{6,4},{5,7},{7,5},{8,10},{10,8},{9,1... | collective-permute-start | bytes 331784 | tf_op jit(solution)/shard_map/ppermute | solution.py:459
  86.8 9.5 %collective-permute-start.28 = (bf16[96,576]{1,0:T(8,128)(2,1)S(1)}, bf16[96,576]{1,0:T(8,128)(2,1)S(1)}, u32[]{:S(2)}, u32[]{:S(2)}) collective-permute-start(bf16[96,576]{1,0:T(8,128)(2,1)S(1)} %collective-permute-done.26.rest_8_), channel_id=1, source_target_pairs={{0,2},{2,0},{1,3},{3,1},{4,6},{6,4},{5,7},{7,5},{8,10},{10,8},{9,1... | collective-permute-start | bytes 331784 | tf_op jit(solution)/shard_map/ppermute | solution.py:459
  113.4 26.1 %collective-permute-start.32 = (bf16[1024,768]{1,0:T(8,128)(2,1)S(1)}, bf16[1024,768]{1,0:T(8,128)(2,1)S(1)}, u32[]{:S(2)}, u32[]{:S(2)}) collective-permute-start(bf16[1024,768]{1,0:T(8,128)(2,1)S(1)} %get-tuple-element.156.own), channel_id=1, source_target_pairs={{0,1},{1,0},{2,3},{3,2},{4,5},{5,4},{6,7},{7,6},{8,9},{9,8},{10,11... | collective-permute-start | bytes 4718600 | tf_op jit(solution)/shard_map/ppermute | solution.py:459
  122.8 12.0 %collective-permute-start.36 = (bf16[2,96,576]{2,1,0:T(8,128)(2,1)S(1)}, bf16[2,96,576]{2,1,0:T(8,128)(2,1)S(1)}, u32[]{:S(2)}, u32[]{:S(2)}) collective-permute-start(bf16[2,96,576]{2,1,0:T(8,128)(2,1)S(1)} %get-tuple-element.178), channel_id=1, source_target_pairs={{0,2},{2,0},{1,3},{3,1},{4,6},{6,4},{5,7},{7,5},{8,10},{10,8},{9,1... | collective-permute-start | bytes 663560 | tf_op jit(solution)/shard_map/ppermute | solution.py:459
  123.6 10.7 %collective-permute-start.33 = (bf16[1,96,576]{2,1,0:T(8,128)(2,1)S(1)}, bf16[1,96,576]{2,1,0:T(8,128)(2,1)S(1)}, u32[]{:S(2)}, u32[]{:S(2)}) collective-permute-start(bf16[1,96,576]{2,1,0:T(8,128)(2,1)S(1)} %get-tuple-element.168), channel_id=1, source_target_pairs={{0,2},{2,0},{1,3},{3,1},{4,6},{6,4},{5,7},{7,5},{8,10},{10,8},{9,1... | collective-permute-start | bytes 331784 | tf_op jit(solution)/shard_map/ppermute | solution.py:459
  124.9 14.6 %collective-permute-start.39 = (bf16[2,96,576]{2,1,0:T(8,128)(2,1)S(1)}, bf16[2,96,576]{2,1,0:T(8,128)(2,1)S(1)}, u32[]{:S(2)}, u32[]{:S(2)}) collective-permute-start(bf16[2,96,576]{2,1,0:T(8,128)(2,1)S(1)} %get-tuple-element.184), channel_id=1, source_target_pairs={{0,2},{2,0},{1,3},{3,1},{4,6},{6,4},{5,7},{7,5},{8,10},{10,8},{9,1... | collective-permute-start | bytes 663560 | tf_op jit(solution)/shard_map/ppermute | solution.py:459
  125.6 13.9 %collective-permute-start.35 = (bf16[1,96,576]{2,1,0:T(8,128)(2,1)S(1)}, bf16[1,96,576]{2,1,0:T(8,128)(2,1)S(1)}, u32[]{:S(2)}, u32[]{:S(2)}) collective-permute-start(bf16[1,96,576]{2,1,0:T(8,128)(2,1)S(1)} %get-tuple-element.172), channel_id=1, source_target_pairs={{8,0},{16,8},{24,16},{28,24},{20,28},{12,20},{4,12},{0,4},{9,1},{1... | collective-permute-start | bytes 331784 | tf_op jit(solution)/shard_map/ppermute | solution.py:595
  134.8 36.3 %collective-permute-start.60 = (bf16[2,96,576]{2,1,0:T(8,128)(2,1)S(1)}, bf16[2,96,576]{2,1,0:T(8,128)(2,1)S(1)}, u32[]{:S(2)}, u32[]{:S(2)}) collective-permute-start(bf16[2,96,576]{2,1,0:T(8,128)(2,1)S(1)} %get-tuple-element.213), channel_id=1, source_target_pairs={{0,2},{2,0},{1,3},{3,1},{4,6},{6,4},{5,7},{7,5},{8,10},{10,8},{9,1... | collective-permute-start | bytes 663560 | tf_op jit(solution)/shard_map/ppermute | solution.py:459
  169.8 20.5 %collective-permute-start.59 = (bf16[1,96,576]{2,1,0:T(8,128)(2,1)S(1)}, bf16[1,96,576]{2,1,0:T(8,128)(2,1)S(1)}, u32[]{:S(2)}, u32[]{:S(2)}) collective-permute-start(bf16[1,96,576]{2,1,0:T(8,128)(2,1)S(1)} %get-tuple-element.212), channel_id=1, source_target_pairs={{0,2},{2,0},{1,3},{3,1},{4,6},{6,4},{5,7},{7,5},{8,10},{10,8},{9,1... | collective-permute-start | bytes 331784 | tf_op jit(solution)/shard_map/ppermute | solution.py:459
  171.9 26.9 %collective-permute-start.46 = (bf16[2,96,512]{2,1,0:T(8,128)(2,1)S(1)}, bf16[2,96,512]{2,1,0:T(8,128)(2,1)S(1)}, u32[]{:S(2)}, u32[]{:S(2)}) collective-permute-start(bf16[2,96,512]{2,1,0:T(8,128)(2,1)S(1)} %get-tuple-element.198), channel_id=1, source_target_pairs={{0,2},{2,0},{1,3},{3,1},{4,6},{6,4},{5,7},{7,5},{8,10},{10,8},{9,1... | collective-permute-start | bytes 589832 | tf_op jit(solution)/shard_map/ppermute | solution.py:459
  172.6 11.4 %collective-permute-start.48 = (bf16[2,96,512]{2,1,0:T(8,128)(2,1)S(1)}, bf16[2,96,512]{2,1,0:T(8,128)(2,1)S(1)}, u32[]{:S(2)}, u32[]{:S(2)}) collective-permute-start(bf16[2,96,512]{2,1,0:T(8,128)(2,1)S(1)} %get-tuple-element.200), channel_id=1, source_target_pairs={{0,2},{2,0},{1,3},{3,1},{4,6},{6,4},{5,7},{7,5},{8,10},{10,8},{9,1... | collective-permute-start | bytes 589832 | tf_op jit(solution)/shard_map/ppermute | solution.py:459
  175.8 10.3 %collective-permute-start.47 = (bf16[2,96,512]{2,1,0:T(8,128)(2,1)S(1)}, bf16[2,96,512]{2,1,0:T(8,128)(2,1)S(1)}, u32[]{:S(2)}, u32[]{:S(2)}) collective-permute-start(bf16[2,96,512]{2,1,0:T(8,128)(2,1)S(1)} %get-tuple-element.199), channel_id=1, source_target_pairs={{0,2},{2,0},{1,3},{3,1},{4,6},{6,4},{5,7},{7,5},{8,10},{10,8},{9,1... | collective-permute-start | bytes 589832 | tf_op jit(solution)/shard_map/ppermute | solution.py:459
  190.4 9.2 %collective-permute-start.63 = (bf16[2,96,576]{2,1,0:T(8,128)(2,1)S(1)}, bf16[2,96,576]{2,1,0:T(8,128)(2,1)S(1)}, u32[]{:S(2)}, u32[]{:S(2)}) collective-permute-start(bf16[2,96,576]{2,1,0:T(8,128)(2,1)S(1)} %get-tuple-element.227), channel_id=1, source_target_pairs={{0,2},{2,0},{1,3},{3,1},{4,6},{6,4},{5,7},{7,5},{8,10},{10,8},{9,1... | collective-permute-start | bytes 663560 | tf_op jit(solution)/shard_map/ppermute | solution.py:459
  195.9 25.8 %collective-permute-start.44 = (bf16[1024,768]{1,0:T(8,128)(2,1)S(1)}, bf16[1024,768]{1,0:T(8,128)(2,1)S(1)}, u32[]{:S(2)}, u32[]{:S(2)}) collective-permute-start(bf16[1024,768]{1,0:T(8,128)(2,1)S(1)} %get-tuple-element.193.feed_own), channel_id=1, source_target_pairs={{0,1},{1,0},{2,3},{3,2},{4,5},{5,4},{6,7},{7,6},{8,9},{9,8},{10,11... | collective-permute-start | bytes 4718600 | tf_op jit(solution)/shard_map/ppermute | solution.py:459
  199.6 17.1 %collective-permute-start.42 = (bf16[1152,768]{1,0:T(8,128)(2,1)S(1)}, bf16[1152,768]{1,0:T(8,128)(2,1)S(1)}, u32[]{:S(2)}, u32[]{:S(2)}) collective-permute-start(bf16[1152,768]{1,0:T(8,128)(2,1)S(1)} %first_grad.1.own), channel_id=1, source_target_pairs={{0,1},{1,0},{2,3},{3,2},{4,5},{5,4},{6,7},{7,6},{8,9},{9,8},{10,11... | collective-permute-start | bytes 5308424 | tf_op jit(solution)/shard_map/ppermute | solution.py:459
  (60 other events, 381.4 us)

commit v5 on v3

v5 whole, which is shorter than its diff:
```python
import functools
import math

import jax
import jax.numpy as jnp
from jax import lax
from jax.experimental import pallas as pl
from jax.experimental.pallas import tpu as pltpu
from jax.sharding import PartitionSpec as P

HEAD = 64
WINDOW = 128
NSEQ = 4
HALF = WINDOW // 2
PAD = 16
BLOCK = 128
LANES = 128
KEYS = BLOCK + WINDOW

norm_eps = 1e-05
f32 = jnp.float32
bf16 = jnp.bfloat16

NN = (((1,), (0,)), ((), ()))
NT = (((1,), (1,)), ((), ()))
TN = (((0,), (0,)), ((), ()))


def dot(a, b, dims=NN):
    return lax.dot_general(a, b, dims, preferred_element_type=f32)


def step_of(rows, most):
    best = LANES
    for size in range(LANES, most + 1, LANES):
        if rows % size == 0:
            best = size
    return best


def call(kernel, out_shape, args, flops, name, scalars=(), scratch=(), raw=()):
    vmem = pl.BlockSpec(memory_space=pltpu.VMEM)
    smem = pl.BlockSpec(memory_space=pltpu.SMEM)
    anywhere = pl.BlockSpec(memory_space=pl.ANY)
    moved = sum(x.size * x.dtype.itemsize for x in (*args, *out_shape))
    held = sum(math.prod(x.shape) * jnp.dtype(x.dtype).itemsize for x in scratch if x.dtype in (f32, bf16))
    limit = min(56 * 2**20, moved // 3 + held + 4 * 2**20)
    return pl.pallas_call(
        kernel,
        out_shape=out_shape,
        in_specs=[smem] * len(scalars) + [vmem] * len(args) + [anywhere] * len(raw),
        out_specs=[vmem] * len(out_shape),
        scratch_shapes=scratch,
        compiler_params=pltpu.CompilerParams(vmem_limit_bytes=limit),
        cost_estimate=pl.CostEstimate(flops=flops, bytes_accessed=moved, transcendentals=0),
        name=name,
    )(*scalars, *args, *raw)


def shape(dims, dtype):
    return jax.ShapeDtypeStruct(dims, dtype)


def normed(values):
    centered = values - jnp.mean(values, axis=-1, keepdims=True)
    spread = jnp.mean(centered * centered, axis=-1, keepdims=True)
    scale = lax.rsqrt(spread + norm_eps)
    return centered * scale, scale


def norm_back(grad, gain, hat, scale):
    inner = grad * gain
    one = jnp.mean(inner, axis=-1, keepdims=True)
    two = jnp.mean(inner * hat, axis=-1, keepdims=True)
    return scale * (inner - one - hat * two)


def turned(values, low):
    return jnp.where(low, pltpu.roll(values, LANES - HEAD // 2, 1), pltpu.roll(values, HEAD // 2, 1))


def halves(values):
    even = (lax.broadcasted_iota(jnp.int32, (1, LANES), 1) < HEAD).astype(f32).astype(bf16)
    return jnp.concatenate([values * even, values * (1 - even)], axis=0)


def joined(values):
    return jnp.concatenate([values[:HEAD, :BLOCK], values[HEAD:, BLOCK:]], axis=0).T


def loop(count, body):
    def run(index, carry):
        body(index)
        return carry

    lax.fori_loop(0, count, run, 0)


def fetch(copies, sems):
    started = []
    for number, (source, target) in enumerate(copies):
        copy = pltpu.make_async_copy(source, target, sems.at[number])
        copy.start()
        started.append(copy)
    for copy in started:
        copy.wait()


def norm_kernel(tokens, before, after, hat):
    rows, width = tokens.shape

    def norm_rows(src, dst, size):
        hat[pl.ds(dst, size), :] = normed(src.astype(f32))[0]

    norm_rows(before[...], 0, HALF)
    norm_rows(after[...], rows + HALF, HALF)

    def norm_step(index):
        at = pl.multiple_of(index * BLOCK, BLOCK)
        norm_rows(tokens[pl.ds(at, BLOCK), :], pl.multiple_of(at + HALF, HALF), BLOCK)

    loop(rows // BLOCK, norm_step)


def piece_plan(count, sizes, break_at):
    plan, used = [], 0
    for slot in range(count):
        row, sources = 0, []
        for number, size in enumerate(sizes):
            if slot == count // 2 and number == break_at:
                used, row = used + 1, 0
            sources.append((used, row))
            row += size
        plan.append(tuple(sources))
        used += 1
    return plan


def project_kernel(slots, hat, cosine, sine, *rest):
    pieces, (wide, gain, first, query, key, value, gain_held, sems) = rest[:-8], rest[-8:]
    extent, local = key.shape
    rows = query.shape[0]
    width = hat.shape[1]
    pairs = local // LANES
    groups = gain_held.shape[0]
    depth = width // groups
    plan = piece_plan(groups, [depth] * 4 + [PAD], 2)
    copies = []
    for number, sources in enumerate(plan):
        place = pl.ds(pl.multiple_of(slots[number] * depth, depth), depth)
        for part, (piece, row) in enumerate(sources[:4]):
            lanes = slice(part * local, (part + 1) * local)
            copies.append((pieces[piece].at[row : row + depth, :], wide.at[place, lanes]))
        piece, row = sources[4]
        copies.append((pieces[piece].at[row : row + PAD, :], gain_held.at[number]))
    fetch(copies, sems)
    lane = lax.broadcasted_iota(jnp.int32, (LANES, width), 1) - lax.broadcasted_iota(jnp.int32, (LANES, width), 0)
    gain_sum = jnp.zeros((PAD, width), f32)
    for number in range(groups):
        spread = jnp.where(lane == slots[number] * depth, 1.0, 0.0).astype(bf16)
        gain_sum += dot(gain_held[number][:, :LANES], spread)
    gain[...] = gain_sum
    gains = gain_sum[:1]
    query_w, key_w, value_w = (wide.at[:, at * local : (at + 1) * local] for at in range(3))
    low = lax.broadcasted_iota(jnp.int32, (1, LANES), 1) % HEAD < HEAD // 2

    def rotated(src, at, size, dst, place, scale):
        co, si = cosine[pl.ds(at, size), :], sine[pl.ds(at, size), :]
        for pair in range(pairs):
            lanes = slice(pair * LANES, (pair + 1) * LANES)
            value = src[:, lanes]
            dst[pl.ds(place, size), lanes] = ((value * co + turned(value, low) * si) * scale).astype(bf16)

    chunk = step_of(extent, 384)

    def key_step(index):
        at = pl.multiple_of(index * chunk, chunk)
        here = pl.ds(at, chunk)
        part = (hat[here, :] * gains).astype(bf16)
        first[here, :] = part
        rotated(dot(part, key_w[...]), at, chunk, key, at, 1.0)
        value[here, :] = dot(part, value_w[...]).astype(bf16)

    loop(extent // chunk, key_step)
    size = step_of(rows, 256)

    def query_step(index):
        at = pl.multiple_of(index * size, size)
        start = pl.multiple_of(at + HALF, HALF)
        rotated(dot(first[pl.ds(start, size), :], query_w[...]), start, size, query, at, HEAD**-0.5)

    loop(rows // size, query_step)


def attend_kernel(bounds, query, key, value, wide, shares, attended, branch):
    rows, local = query.shape
    pairs = local // LANES
    key_at = lax.broadcasted_iota(jnp.int32, (KEYS, KEYS), 0)
    lane_at = lax.broadcasted_iota(jnp.int32, (1, KEYS), 1) % BLOCK

    def attend_step(index):
        at = pl.multiple_of(index * BLOCK, BLOCK)
        origin = bounds[NSEQ] + at - HALF
        own = lane_at + (origin + HALF)
        begin = jnp.zeros_like(own)
        end = jnp.zeros_like(own) + bounds[NSEQ - 1]
        for number in range(NSEQ - 1):
            begin = jnp.where(own >= bounds[number], bounds[number], begin)
        for number in reversed(range(NSEQ - 1)):
            end = jnp.where(own < bounds[number], bounds[number], end)
        least = jnp.maximum(lane_at, begin - origin)
        most = jnp.minimum(lane_at + WINDOW, end - 1 - origin)
        allowed = (key_at >= least) & (key_at <= most)
        for pair in range(pairs):
            lanes = slice(pair * LANES, (pair + 1) * LANES)
            both = halves(query[pl.ds(at, BLOCK), lanes])
            scores = jnp.where(allowed, dot(key[pl.ds(at, KEYS), lanes], both, NT), -1e30)
            weight = jnp.exp(scores - jnp.max(scores, axis=0, keepdims=True))
            part = (weight * (1.0 / jnp.sum(weight, axis=0, keepdims=True))).astype(bf16)
            shares[index * pairs + pair] = part
            mixed = dot(value[pl.ds(at, KEYS), lanes], part, TN)
            attended[pl.ds(at, BLOCK), lanes] = joined(mixed).astype(bf16)

    loop(rows // BLOCK, attend_step)
    out_t = wide.at[:, 3 * local :]
    size = step_of(rows, 256)

    def out_step(index):
        here = pl.ds(pl.multiple_of(index * size, size), size)
        branch[here, :] = dot(attended[here, :], out_t[...], NT).astype(bf16)

    loop(rows // size, out_step)


def feed_kernel(slots, parts_at, tokens, own, other, gain, cotangent, *rest):
    pieces, rest = rest[:-8], rest[-8:]
    middle, second, hidden, grad_gate, grad_upper, partial, whole, sems = rest
    rows, width = tokens.shape
    groups = slots.shape[0]
    depth = width // groups
    sides = len(pieces) // groups
    size = depth // sides
    copies = []
    for number in range(groups):
        for side in range(sides):
            start = slots[number] * depth + parts_at[side] * size
            place = pl.ds(pl.multiple_of(start, size), size)
            copies.append((pieces[number * sides + side], whole.at[:, place, :]))
    fetch(copies, sems)
    gate_w, upper_w, down_t = (whole.at[number] for number in range(3))
    gains = gain[1:2, :]
    size = step_of(rows, 256)

    def step(index):
        at = pl.multiple_of(index * size, size)
        here = pl.ds(at, size)
        mid = tokens[here, :].astype(f32) + (own[here, :].astype(f32) + other[here, :].astype(f32))
        middle[here, :] = mid
        hat, _ = normed(mid)
        low = (hat * gains).astype(bf16)
        second[here, :] = low
        gate = dot(low, gate_w[...])
        upper = dot(low, upper_w[...])
        grad = dot(cotangent[here, :], down_t[...])
        share = 0.5 * (1.0 + lax.erf(gate * (0.5**0.5)))
        smooth = gate * share
        slope = share + gate * (jnp.exp(gate * gate * -0.5) * ((2.0 * math.pi) ** -0.5))
        hidden[here, :] = (smooth * upper).astype(bf16)
        gate_low = (grad * upper * slope).astype(bf16)
        upper_low = (grad * smooth).astype(bf16)
        grad_gate[here, :] = gate_low
        grad_upper[here, :] = upper_low
        partial[here, :] = (dot(gate_low, gate_w[...], NT) + dot(upper_low, upper_w[...], NT)).astype(bf16)

    loop(rows // size, step)


def feed_out_kernel(hidden, whole, feed):
    rows = hidden.shape[0]
    size = step_of(rows, 256)

    def step(index):
        here = pl.ds(pl.multiple_of(index * size, size), size)
        feed[here, :] = dot(hidden[here, :], whole[2], NT).astype(bf16)

    loop(rows // size, step)


def weight_kernel(slots, parts_at, second, hidden, grad_gate, grad_upper, cotangent, *rest):
    outs, total = rest[:-1], rest[-1]
    rows, width = second.shape
    step_rows = step_of(width, 256)
    for number, (left, right) in enumerate(((second, grad_gate), (second, grad_upper), (cotangent, hidden))):
        for start in range(0, width, step_rows):
            here = slice(start, start + step_rows)
            total[number, here, :] = dot(left[:, here], right[...], TN).astype(bf16)
    size = outs[0].shape[2]
    for number, slot in enumerate(hop_order(outs[0].shape[0])):
        for side, out in enumerate(outs):
            start = slots[slot] * (size * len(outs)) + parts_at[side] * size
            out[number] = total[:, pl.ds(pl.multiple_of(start, size), size), :]


def hop_order(count):
    middle = count // 2
    order = [middle]
    for hop in range(middle - 1, 0, -1):
        order += [hop, count - hop]
    return order + [0]


def middle_kernel(middle, own, other, gain, cotangent, wide, grad_middle, low_mid, grad_att):
    rows, width = middle.shape
    local = grad_att.shape[1]
    out_t = wide.at[:, 3 * local :]
    gains = gain[1:2, :]
    size = step_of(rows, 256)

    def norm_step(index):
        here = pl.ds(pl.multiple_of(index * size, size), size)
        hat, scale = normed(middle[here, :])
        grad = own[here, :].astype(f32) + other[here, :].astype(f32)
        mid = cotangent[here, :].astype(f32) + norm_back(grad, gains, hat, scale)
        grad_middle[here, :] = mid
        mid_low = mid.astype(bf16)
        low_mid[here, :] = mid_low
        grad_att[here, :] = dot(mid_low, out_t[...]).astype(bf16)

    loop(rows // size, norm_step)


def back_kernel(query, key, value, shares, grad_att, cosine, sine, grad_proj, grad_key, grad_value):
    rows, local = query.shape
    extent = key.shape[0]
    pairs = local // LANES
    grad_key[...] = jnp.zeros_like(grad_key)
    grad_value[...] = jnp.zeros_like(grad_value)
    low = lax.broadcasted_iota(jnp.int32, (1, LANES), 1) % HEAD < HEAD // 2
    zero = jnp.zeros((HALF, local), bf16)
    grad_proj[:HALF, :local] = zero
    grad_proj[rows + HALF :, :local] = zero

    def attend_step(index):
        at = pl.multiple_of(index * BLOCK, BLOCK)
        start = pl.multiple_of(at + HALF, HALF)
        co, si = cosine[pl.ds(start, BLOCK), :], sine[pl.ds(start, BLOCK), :]
        found = []
        for pair in range(pairs):
            lanes = slice(pair * LANES, (pair + 1) * LANES)
            both = halves(query[pl.ds(at, BLOCK), lanes])
            grad = halves(grad_att[pl.ds(at, BLOCK), lanes])
            keys = key[pl.ds(at, KEYS), lanes]
            part = shares[index * pairs + pair]
            wide = part.astype(f32)
            grad_shares = dot(value[pl.ds(at, KEYS), lanes], grad, NT)
            delta = jnp.sum(wide * grad_shares, axis=0, keepdims=True)
            raw = (wide * (grad_shares - delta)).astype(bf16)
            grad_query = joined(dot(keys, raw, TN)) * HEAD**-0.5
            turn = (grad_query * co - turned(grad_query, low) * si).astype(bf16)
            found.append((lanes, turn, dot(raw, both), dot(part, grad)))
        for lanes, turn, key_part, value_part in found:
            grad_proj[pl.ds(start, BLOCK), lanes] = turn
            grad_key[pl.ds(at, KEYS), lanes] += key_part
            grad_value[pl.ds(at, KEYS), lanes] += value_part

    loop(rows // BLOCK, attend_step)

    def turn_step(index):
        here = pl.ds(pl.multiple_of(index * BLOCK, BLOCK), BLOCK)
        co, si = cosine[here, :], sine[here, :]
        for pair in range(pairs):
            lanes = slice(pair * LANES, (pair + 1) * LANES)
            part = grad_key[here, lanes]
            turn = slice(local + pair * LANES, local + (pair + 1) * LANES)
            grad_proj[here, turn] = (part * co - turned(part, low) * si).astype(bf16)
        grad_proj[here, 2 * local :] = grad_value[here, :].astype(bf16)

    loop(extent // BLOCK, turn_step)


def grad_kernel(slots, first, grad_proj, low_mid, attended, grads, total):
    local = attended.shape[1]
    width = first.shape[1]
    depth = grads.shape[2]
    step_rows = step_of(width, 256)
    for start in range(0, width, step_rows):
        here = slice(start, start + step_rows)
        for number in range(3):
            lanes = slice(number * local, (number + 1) * local)
            total[number, here, :] = dot(first[:, here], grad_proj[:, lanes], TN).astype(bf16)
        total[3, here, :] = dot(low_mid[:, here], attended[...], TN).astype(bf16)
    for number, slot in enumerate(hop_order(grads.shape[0])):
        grads[number] = total[:, pl.ds(pl.multiple_of(slots[slot] * depth, depth), depth), :]


def first_kernel(grad_proj, wide, partial):
    extent, inner = grad_proj.shape
    size = step_of(extent, 384)

    def step(index):
        here = pl.ds(pl.multiple_of(index * size, size), size)
        partial[here, :] = dot(grad_proj[here, :], wide[:, :inner], NT).astype(bf16)

    loop(extent // size, step)


def final_kernel(tokens, gain, grad_middle, own, other, before, after, middle, feed_own, feed_other, mixed, token_grad):
    rows, width = tokens.shape
    gains = gain[:1, :]
    size = BLOCK

    def back(here, grad):
        hat, scale = normed(tokens[here, :].astype(f32))
        return norm_back(grad, gains, hat, scale)

    def step(index):
        at = pl.multiple_of(index * size, size)
        here, wider = pl.ds(at, size), pl.ds(pl.multiple_of(at + HALF, HALF), size)
        grad = own[wider, :].astype(f32) + other[wider, :].astype(f32)
        token_grad[here, :] = grad_middle[here, :] + back(here, grad)
        feed = feed_own[here, :].astype(f32) + feed_other[here, :].astype(f32)
        mixed[here, :] = (middle[here, :] + feed).astype(bf16)

    loop(rows // size, step)
    for start, edge in ((0, before), (rows - HALF, after)):
        here = pl.ds(start, HALF)
        token_grad[here, :] += back(here, edge[...].astype(f32))


def exchange(initial, last):
    devices, spot = lax.axis_size("ctx"), lax.axis_index("ctx")
    if devices == 2:
        got = lax.ppermute(jnp.where(spot == 0, last, initial), "ctx", [(0, 1), (1, 0)])
        none = jnp.zeros_like(got)
        return jnp.where(spot == 1, got, none), jnp.where(spot == 0, got, none)
    up = [(i, i + 1) for i in range(devices - 1)]
    return lax.ppermute(last, "ctx", up), lax.ppermute(initial, "ctx", [(j, i) for i, j in up])


def swap(array, axis="tensor"):
    return lax.ppermute(array, axis, [(0, 1), (1, 0)])


def ring():
    count = lax.axis_size("dp")
    order = [2 * i for i in range(count // 2)] + [2 * i + 1 for i in reversed(range(count // 2))]
    ahead = [(order[i], order[(i + 1) % count]) for i in range(count)]
    back = [(j, i) for i, j in ahead]
    index = lax.axis_index("dp")
    spot = jnp.where(index % 2 == 0, index // 2, count - 1 - index // 2)
    place = (spot + jnp.arange(count, dtype=jnp.int32)) % count
    slots = jnp.where(place < count // 2, 2 * place, 2 * (count - 1 - place) + 1)
    return count, ahead, back, slots.astype(jnp.int32)


def tied(values, others):
    held = lax.optimization_barrier((tuple(values), tuple(others)))
    return held[0]


class RingGather:
    def __init__(self, block, cut):
        self.count, self.ahead, self.back, _ = ring()
        self.cut = cut
        self.pieces = {0: (block,)}
        self.state = (block, block)
        self.hops = 0

    def hop(self):
        one, two = self.state
        middle = self.count // 2
        if self.hops + 1 == middle:
            one, two = one[: self.cut], two[self.cut :]
        one, two = lax.ppermute(one, "dp", self.ahead), lax.ppermute(two, "dp", self.back)
        self.hops += 1
        one, two = lax.optimization_barrier((one, two))
        self.state = (one, two)
        if self.hops == middle:
            self.pieces[middle] = (one, two)
        else:
            self.pieces[self.count - self.hops], self.pieces[self.hops] = (one,), (two,)

    def after(self, others):
        self.state = tied(self.state, others)


class RingScatter:
    def __init__(self, parts, axis):
        self.count, self.ahead, self.back, _ = ring()
        self.parts = parts
        self.axis = axis
        self.hops = 0
        self.state = ()

    def part(self, at):
        total = self.parts[0][at]
        for part in self.parts[1:]:
            total = total + part[at]
        return total

    def hop(self):
        if self.hops == 0:
            one, two = jnp.split(self.part(0), 2, axis=self.axis)
        else:
            one, two = self.state
            if self.hops == 1:
                none = jnp.zeros_like(one)
                one = jnp.concatenate([one, none], axis=self.axis)
                two = jnp.concatenate([none, two], axis=self.axis)
            at = 2 * self.hops - 1
            one, two = self.part(at) + one, self.part(at + 1) + two
        one, two = lax.ppermute(one, "dp", self.ahead), lax.ppermute(two, "dp", self.back)
        self.state = lax.optimization_barrier((one, two))
        self.hops += 1

    def after(self, others):
        self.state = tied(self.state, others)

    def total(self):
        one, two = self.state
        return (self.part(self.count - 1).astype(f32) + one.astype(f32) + two.astype(f32)).astype(bf16)


def tables(lengths, rows):
    place = lax.axis_index("ctx") * rows
    ends = jnp.cumsum(lengths[0])
    starts = ends - lengths[0]
    span = place + jnp.arange(-HALF, rows + HALF, dtype=jnp.int32)
    inside = (span[:, None] >= starts[None, :]) & (span[:, None] < ends[None, :])
    position = span - jnp.sum(jnp.where(inside, starts[None, :], 0), axis=1)
    lane = jnp.arange(LANES, dtype=jnp.int32)
    number = (lane % (HEAD // 2)).astype(f32)
    freq = jnp.exp(number * (-2.0 * math.log(10000.0) / HEAD))
    angle = position.astype(f32)[:, None] * freq[None, :]
    sine = jnp.sin(angle)
    sine = jnp.where((lane % HEAD < HEAD // 2)[None, :], -sine, sine)
    bounds = jnp.concatenate([ends, place[None]]).astype(jnp.int32)
    return jnp.cos(angle), sine, bounds


def body(tokens, lengths, gain_one, w_qkv, w_out, gain_two, w_in, w_down, cotangent):
    rows, width = tokens.shape
    local, units = w_out.shape[0], w_down.shape[0]
    pairs, blocks, extent = local // LANES, rows // BLOCK, rows + WINDOW
    groups = lax.axis_size("dp")
    depth = width // groups
    middle_hop = groups // 2
    split = lax.axis_size("ctx") == 2
    spot = lax.axis_index("ctx")
    low = spot == 0
    gains = jnp.pad(jnp.stack([gain_one, gain_two]), ((0, PAD - 2), (0, local - depth)))
    mine_one = jnp.concatenate([w_qkv.reshape(3 * depth, local), w_out.T, gains])
    now = RingGather(mine_one, 2 * depth)
    now.hop()
    before, after = exchange(tokens[:HALF], tokens[rows - HALF :])
    slots = ring()[-1]
    mine_two = jnp.concatenate([w_in, w_down.T[None]])
    if split:
        sides = [mine_two[:, : depth // 2], mine_two[:, depth // 2 :]]
        mine_two, other_two = jnp.where(low, sides[0], sides[1]), jnp.where(low, sides[1], sides[0])
        parts_at = jnp.stack([spot, 1 - spot]).astype(jnp.int32)
    else:
        parts_at = jnp.zeros((1,), jnp.int32)
    later = RingGather(tied([mine_two], now.state)[0], 1)
    now.hop()
    later.hop()
    cosine, sine, bounds = tables(lengths, rows)
    later.after(now.state)
    while now.hops < middle_hop:
        now.hop()
        later.hop()
        later.after(now.state)
    while later.hops < middle_hop:
        later.hop()
    hat, = call(
        norm_kernel, [shape((extent, width), f32)], (tokens, before, after), rows * width * 2000, "first_norm"
    )
    pieces = [piece for slot in range(groups) for piece in now.pieces[slot]]
    wide, gain, first, query, key, value = call(
        project_kernel,
        [
            shape((width, 4 * local), bf16),
            shape((PAD, width), f32),
            shape((extent, width), bf16),
            shape((rows, local), bf16),
            shape((extent, local), bf16),
            shape((extent, local), bf16),
        ],
        (hat, cosine, sine),
        2 * rows * width * local * 8,
        "project",
        (slots,),
        [pltpu.VMEM((groups, PAD, local), bf16), pltpu.SemaphoreType.DMA((5 * groups,))],
        pieces,
    )
    held = {slot: later.pieces[slot][0] for slot in range(groups) if slot != middle_hop}
    held[middle_hop] = jnp.concatenate(later.pieces[middle_hop])
    if split:
        early = [slot for hop in range(1, middle_hop // 2 + 1) for slot in (hop, groups - hop)]
        late = [slot for slot in range(1, groups) if slot not in early]
        others = {0: other_two}
        for batch in (early, late):
            got = swap(jnp.stack([held[slot] for slot in batch]), "ctx")
            if batch is early:
                query, key, value = tied([query, key, value], [got])
            for number, slot in enumerate(batch):
                others[slot] = got[number]
        query, key, value = tied([query, key, value], later.state)
        pieces = [piece for slot in range(groups) for piece in (held[slot], others[slot])]
    else:
        got = held[middle_hop]
        pieces = [held[slot] for slot in range(groups)]
    shares, attended, branch = call(
        attend_kernel,
        [
            shape((blocks * pairs, KEYS, KEYS), bf16),
            shape((rows, local), bf16),
            shape((rows, width), bf16),
        ],
        (query, key, value, wide),
        2 * rows * width * local * 16,
        "attend",
        (bounds,),
    )
    branch, = tied([branch], [got])
    branch_other = swap(branch)
    middle, second, hidden, grad_gate, grad_upper, partial, whole = call(
        feed_kernel,
        [
            shape((rows, width), f32),
            shape((rows, width), bf16),
            shape((rows, units), bf16),
            shape((rows, units), bf16),
            shape((rows, units), bf16),
            shape((rows, width), bf16),
            shape((3, width, units), bf16),
        ],
        (tokens, branch, branch_other, gain, cotangent),
        2 * rows * width * units * 8,
        "feed_forward_and_back",
        (slots, parts_at),
        [pltpu.SemaphoreType.DMA((len(pieces),))],
        pieces,
    )
    partial_other = swap(partial)
    ways = 2 if split else 1
    grads_two = call(
        weight_kernel,
        [shape((groups, 3, depth // ways, units), bf16)] * ways,
        (second, hidden, grad_gate, grad_upper, cotangent),
        2 * rows * width * units * 5,
        "feed_weight_grads",
        (slots, parts_at),
        [pltpu.VMEM((3, width, units), bf16)],
    )
    if split:
        grads_two = [grads_two[0], swap(grads_two[1], "ctx")]
    feed, = call(
        feed_out_kernel,
        [shape((rows, width), bf16)],
        (hidden, whole),
        2 * rows * width * units,
        "feed_out",
    )
    feed_other = swap(feed)
    grad_middle, low_mid, grad_att = call(
        middle_kernel,
        [shape((rows, width), f32), shape((rows, width), bf16), shape((rows, local), bf16)],
        (middle, partial, partial_other, gain, cotangent, wide),
        2 * rows * width * local * 4,
        "middle_grad",
    )
    grad_proj, = call(
        back_kernel,
        [shape((extent, 3 * local), bf16)],
        (query, key, value, shares, grad_att, cosine, sine),
        2 * rows * width * local * 16,
        "attention_back",
        (),
        [pltpu.VMEM((extent, local), f32)] * 2,
    )
    grads_one, = call(
        grad_kernel,
        [shape((groups, 4, depth, local), bf16)],
        (first, grad_proj, low_mid, attended),
        2 * rows * width * local * 6,
        "attention_weight_grads",
        (slots,),
        [pltpu.VMEM((4, width, local), bf16)],
    )
    sums_one = RingScatter([grads_one], 0)
    sums_one.hop()
    sums_two = RingScatter(tied(grads_two, sums_one.state), 1)
    sums_two.hop()
    first_part, = call(
        first_kernel,
        [shape((extent, width), bf16)],
        (tied([grad_proj], [grads_one])[0], wide),
        2 * rows * width * local * 3,
        "first_grad",
    )
    first_other = swap(first_part)

    def edge_sum(at):
        here = slice(at, at + HALF)
        return (first_part[here].astype(f32) + first_other[here].astype(f32)).astype(bf16)

    sums_one.after([first_part, feed])
    while sums_one.hops < middle_hop - 1:
        sums_one.hop()
        sums_two.after(sums_one.state)
        sums_two.hop()
    from_before, from_after = exchange(edge_sum(0), edge_sum(rows + HALF))
    sums_one.after([from_before, from_after])
    sums_one.hop()
    sums_two.after(sums_one.state)
    sums_two.hop()
    mixed, token_grad = call(
        final_kernel,
        [shape((rows, width), bf16), shape((rows, width), f32)],
        (tokens, gain, grad_middle, first_part, first_other, from_before, from_after, middle, feed, feed_other),
        rows * width * 2000,
        "token_grad",
    )
    one, two = tied([sums_one.total()], [mixed, token_grad])[0], sums_two.total()
    if split:
        one = one.astype(f32) + swap(one, "ctx").astype(f32)
        got = swap(two, "ctx")
        two = jnp.concatenate([jnp.where(low, two, got), jnp.where(low, got, two)], axis=1).astype(f32)
    else:
        one, two = lax.psum(one, "ctx").astype(f32), lax.psum(two, "ctx").astype(f32)
    gain_one_grad = jnp.sum(one[:3] * w_qkv.astype(f32), axis=(0, 2)) / gain_one.astype(f32)
    gain_two_grad = jnp.sum(two[:2] * w_in.astype(f32), axis=(0, 2)) / gain_two.astype(f32)
    both = jnp.stack([gain_one_grad, gain_two_grad])
    both = both + swap(both)
    return (mixed, token_grad, both[0], one[:3], one[3].T, both[1], two[:2], two[2].T)


def solution(mesh):
    in_specs = (
        P(("dp", "ctx"), None),
        P("dp", None),
        P("dp"),
        P(None, "dp", "tensor"),
        P("tensor", "dp"),
        P("dp"),
        P(None, "dp", "tensor"),
        P("tensor", "dp"),
        P(("dp", "ctx"), None),
    )
    out_specs = (
        P(("dp", "ctx"), None),
        P(("dp", "ctx"), None),
        P("dp"),
        P(None, "dp", "tensor"),
        P("tensor", "dp"),
        P("dp"),
        P(None, "dp", "tensor"),
        P("tensor", "dp"),
    )
    return jax.shard_map(body, mesh=mesh, in_specs=in_specs, out_specs=out_specs, check_vma=False)
```

time: 208 us -> 201 us (0.966)
  waiting for transfers between devices: 72.5 us -> 53.7 us
  Pallas kernels: 64.7 us -> 72.4 us
  other arithmetic: 10.2 us -> 14.6 us
  local copies, waits for them, and re-layouts: 19.2 us -> 15.7 us
  starting transfers between devices: 40.1 us -> 42.7 us
    ppermute x16, waiting for transfers between devices: 42 us -> 20.9 us  [hop(): lax.ppermute(one, 'dp', self.ahead)]
    ppermute x16, starting transfers between devices: 25.3 us -> 11.3 us  [hop(): lax.ppermute(one, 'dp', self.ahead)]
    ppermute x16, starting transfers between devices: 8.87 us -> 22.8 us  [hop(): lax.ppermute(two, 'dp', self.back)]
    pallas_call x9 -> x11, Pallas kernels: 64.7 us -> 72.4 us  [call(): pl.pallas_call(kernel, out_shape=out_shape, in_specs=[smem] * len(scalars...]
    ppermute x2, waiting for transfers between devices: 8.12 us -> 0.97 us  [exchange(): lax.ppermute(jnp.where(spot == 0, last, initial), 'ctx', [(0, 1), (1, 0)])]
    ppermute x7 -> x10, waiting for transfers between devices: 4.32 us -> 9.58 us  [swap(): return lax.ppermute(array, axis, [(0, 1), (1, 0)])]
    another operation x4 -> x0, local copies, waits for them, and re-layouts: 4.46 us -> none  [tables(): return (jnp.tile(cosine, (1, 2)), jnp.tile(sine, (1, 2)), bounds)]
    ppermute x16, waiting for transfers between devices: 18.1 us -> 22.2 us  [hop(): lax.ppermute(two, 'dp', self.back)]
  transfers between devices with their start and end apart: 41 -> 44, of which waited for: 20 -> 24; matrix products, arithmetic and copies ran while one was open for 8% -> 8% of each run, Pallas kernels for 24% -> 29%
where the time goes in v5:
time: 201 us; the launch traced here: 200 us
  Pallas kernels  72.4 us (36%)
  waiting for transfers between devices  53.7 us (27%)
  starting transfers between devices  42.7 us (21%)
  local copies, waits for them, and re-layouts  15.7 us (8%)
  other arithmetic  14.6 us (7%)
    pallas_call x11, Pallas kernels, call(): pl.pallas_call(kernel, out_shape=out_shape, in_specs=[smem] * len(scalars...  72.4 us
    ppermute x16, starting transfers between devices, hop(): lax.ppermute(two, 'dp', self.back)  22.8 us
    ppermute x16, waiting for transfers between devices, hop(): lax.ppermute(two, 'dp', self.back)  22.2 us
    ppermute x16, waiting for transfers between devices, hop(): lax.ppermute(one, 'dp', self.ahead)  20.9 us
    unnamed x85, local copies, waits for them, and re-layouts  11.8 us
    ppermute x16, starting transfers between devices, hop(): lax.ppermute(one, 'dp', self.ahead)  11.3 us
    ppermute x10, waiting for transfers between devices, swap(): return lax.ppermute(array, axis, [(0, 1), (1, 0)])  9.58 us
    ppermute x10, starting transfers between devices, swap(): return lax.ppermute(array, axis, [(0, 1), (1, 0)])  5.2 us
  transfers between devices with their start and end apart: 44, of which 24 were waited for; matrix products, arithmetic and copies ran while one was open for 8% of the time, Pallas kernels for 29%

profile of v5, /device:TPU:0, one launch (start us, length us, event | category | flops | bytes accessed | tf_op | source)
XLA Modules:
  0.0 200.5 jit_solution(5092533149612753141)
XLA Ops:
  2.4 3.0 %collective-permute-start.2 = (bf16[400,384]{1,0:T(8,128)(2,1)S(1)}, bf16[400,384]{1,0:T(8,128)(2,1)}, u32[]{:S(2)}, u32[]{:S(2)}) collective-permute-start(bf16[400,384]{1,0:T(8,128)(2,1)S(1)} %pad_maximum_fusion.2.rest_0_), channel_id=1, source_target_pairs={{8,0},{16,8},{24,16},{28,24},{20,28},{12,20},{4,12},{0,4},{9,1},{1... | collective-permute-start | bytes 921608 | tf_op jit(solution)/shard_map/ppermute | solution.py:474
  10.8 2.1 %collective-permute-done.2.rest_1_ = bf16[400,384]{1,0:T(8,128)(2,1)} collective-permute-done((bf16[400,384]{1,0:T(8,128)(2,1)S(1)}, bf16[400,384]{1,0:T(8,128)(2,1)}, u32[]{:S(2)}, u32[]{:S(2)}) %collective-permute-start.2) | collective-permute-done | bytes 307232 | tf_op jit(solution)/shard_map/ppermute | solution.py:474
  16.2 2.1 %negate_select_fusion = (f32[1152,128]{1,0:T(8,128)S(1)}, f32[1152,128]{1,0:T(8,128)S(1)}) fusion(f32[128]{0:T(128)S(1)} %fusion.20, f32[1152]{0:T(1024)S(1)} %subtract_convert_fusion, pred[128]{0:T(512)(128)(4,1)S(1)} %fusion.21), kind=kLoop, calls=%fused_computation | loop fusion | flops 442368 | bytes 1184896 | tf_op jit(solution)/shard_map/jit(_where)/select_n | solution.py:536
  32.3 5.8 %collective-permute-done.11.rest_12_ = bf16[3,48,576]{2,1,0:T(8,128)(2,1)S(1)} collective-permute-done((bf16[3,48,576]{2,1,0:T(8,128)(2,1)}, bf16[3,48,576]{2,1,0:T(8,128)(2,1)S(1)}, u32[]{:S(2)}, u32[]{:S(2)}) %collective-permute-start.11) | collective-permute-done | bytes 165920 | tf_op jit(solution)/shard_map/ppermute | solution.py:474
  42.4 2.0 %first_norm.1.hat = f32[1152,768]{1,0:T(8,128)S(1)} custom-call(bf16[1024,768]{1,0:T(8,128)(2,1)S(1)} %copy-done, bf16[64,768]{1,0:T(8,128)(2,1)S(1)} %get-tuple-element.208.before, bf16[64,768]{1,0:T(8,128)(2,1)S(1)} %get-tuple-element.207.after), custom_call_target="tpu_custom_call" | custom-call | flops 1572864000 | bytes 5308416 | tf_op jit(solution)/shard_map/first_norm/pallas_call | solution.py:48
  49.6 7.4 %project.1 = (bf16[768,1536]{1,0:T(8,128)(2,1)S(1)}, f32[16,768]{1,0:T(8,128)S(1)}, bf16[1152,768]{1,0:T(8,128)(2,1)S(1)}, bf16[1024,384]{1,0:T(8,128)(2,1)S(1)}...) custom-call(s32[8]{0:T(128)S(1)} %compare_select_fusion.2.slots, f32[1152,768]{1,0:T(8,128)S(1)} %first_norm.1.hat, ...), custom_call_target="tpu_custom_call" | custom-call | flops 4831838208 | bytes 11452416 | tf_op jit(solution)/shard_map/project/pallas_call | solution.py:48
  60.2 3.2 %collective-permute-done.13 = bf16[4,3,48,576]{3,2,1,0:T(8,128)(2,1)S(1)} collective-permute-done((bf16[4,3,48,576]{3,2,1,0:T(8,128)(2,1)S(1)}, bf16[4,3,48,576]{3,2,1,0:T(8,128)(2,1)S(1)}, u32[]{:S(2)}, u32[]{:S(2)}) %collective-permute-start.13) | collective-permute-done | bytes 663584 | tf_op jit(solution)/shard_map/ppermute | solution.py:441
  63.4 13.1 %attend.1 = (bf16[24,256,256]{2,1,0:T(8,128)(2,1)S(1)}, bf16[1024,384]{1,0:T(8,128)(2,1)S(1)}, bf16[1024,768]{1,0:T(8,128)(2,1)}) custom-call(s32[5]{0:T(128)S(1)} %pad_add_fusion.1.bounds, bf16[1024,384]{1,0:T(8,128)(2,1)S(1)} %get-tuple-element.121.query, bf16[1152,384]{1,0:T(8,128)(2,1)S(1)} %get-tuple-element.122.key, ...), custom_call_target="tpu_custom_call" | custom-call | flops 9663676416 | bytes 10420224 | tf_op jit(solution)/shard_map/attend/pallas_call | solution.py:48
  89.7 13.7 %feed_forward_and_back.1 = (f32[1024,768]{1,0:T(8,128)S(1)}, bf16[1024,768]{1,0:T(8,128)(2,1)S(1)}, bf16[1024,576]{1,0:T(8,128)(2,1)S(1)}, bf16[1024,576]{1,0:T(...) custom-call(s32[8]{0:T(128)S(1)} %compare_select_fusion.2.slots, ...), custom_call_target="tpu_custom_call" | custom-call | flops 7247757312 | bytes 18825216 | tf_op jit(solution)/shard_map/feed_forward_and_back/pallas_call | solution.py:48
  103.6 4.6 %feed_weight_grads.1 = (bf16[8,3,48,576]{3,2,1,0:T(8,128)(2,1)S(1)}, bf16[8,3,48,576]{3,2,1,0:T(8,128)(2,1)S(1)}) custom-call(s32[8]{0:T(128)S(1)} %compare_select_fusion.2.slots, s32[2]{0:T(128)S(1)} %pad_add_fusion.parts_at, bf16[1024,768]{1,0:T(8,128)(2,1)S(1)} %get-tuple-element.153.second, bf16[1024,576]{1,0:T(8,128)(2,1)S(1)} %get-tuple-element.136.hidden, ...), custom_call_target="tpu_custom_call" | custom-call | flops 4529848320 | bytes 9338880 | tf_op jit(solution)/shard_map/feed_weight_grads/pallas_call | solution.py:48
  108.2 2.3 %collective-permute-start.33 = (bf16[8,3,48,576]{3,2,1,0:T(8,128)(2,1)S(1)}, bf16[8,3,48,576]{3,2,1,0:T(8,128)(2,1)S(1)}, u32[]{:S(2)}, u32[]{:S(2)}) collective-permute-start(bf16[8,3,48,576]{3,2,1,0:T(8,128)(2,1)S(1)} %get-tuple-element.157), channel_id=1, source_target_pairs={{0,2},{2,0},{1,3},{3,1},{4,6},{6,4},{5,7},{7,5},{8,10},{10,8},{9,1... | collective-permute-start | bytes 3981320 | tf_op jit(solution)/shard_map/ppermute | solution.py:441
  110.5 3.5 %middle_grad.1 = (f32[1024,768]{1,0:T(8,128)S(1)}, bf16[1024,768]{1,0:T(8,128)(2,1)S(1)}, bf16[1024,384]{1,0:T(8,128)(2,1)S(1)}) custom-call(f32[1024,768]{1,0:T(8,128)S(1)} %get-tuple-element.127.middle, bf16[1024,768]{1,0:T(8,128)(2,1)S(1)} %get-tuple-element.128.own, bf16[1024,768]{1,0:T(8,128)(2,1)S(1)} %collective-permute-done.20.other, ...), custom_call_target="tpu_custom_call" | custom-call | flops 2415919104 | bytes 15777792 | tf_op jit(solution)/shard_map/middle_grad/pallas_call | solution.py:48
  114.1 12.6 %attention_back.1.grad_proj = bf16[1152,1152]{1,0:T(8,128)(2,1)S(1)} custom-call(bf16[1024,384]{1,0:T(8,128)(2,1)S(1)} %copy-done.32, bf16[1152,384]{1,0:T(8,128)(2,1)S(1)} %copy-done.28, bf16[1152,384]{1,0:T(8,128)(2,1)S(1)} %copy-done.30, bf16[24,256,256]{2,1,0:T(8,128)(2,1)S(1)} %copy-done.34, bf16[1024,384]{1,0:T(8,128)(2,1)S(1)} %get-tuple-element.131.grad_att, ...), custom_call_target="tpu_custom_call" | custom-call | flops 9663676416 | bytes 10321920 | tf_op jit(solution)/shard_map/attention_back/pallas_call | solution.py:48
  126.7 4.7 %attention_weight_grads.1 = bf16[8,4,96,384]{3,2,1,0:T(8,128)(2,1)S(1)} custom-call(s32[8]{0:T(128)S(1)} %compare_select_fusion.2.slots, bf16[1152,768]{1,0:T(8,128)(2,1)S(1)} %copy-done.24, bf16[1152,1152]{1,0:T(8,128)(2,1)S(1)} %attention_back.1.grad_proj, bf16[1024,768]{1,0:T(8,128)(2,1)S(1)} %get-tuple-element.133.low_mid, bf16[1024,384]{1,0:T(8,128)(2,1)S(1)} %copy-done.26), custom_call_target="tpu_custom_call" | custom-call | flops 3623878656 | bytes 9142272 | tf_op jit(solution)/shard_map/attention_weight_grads/pallas_call | solution.py:48
  131.4 2.9 %first_grad.1.own = bf16[1152,768]{1,0:T(8,128)(2,1)S(1)} custom-call(bf16[1152,1152]{1,0:T(8,128)(2,1)S(1)} %attention_back.1.grad_proj, bf16[768,1536]{1,0:T(8,128)(2,1)S(1)} %get-tuple-element.124.wide), custom_call_target="tpu_custom_call" | custom-call | flops 1811939328 | bytes 6782976 | tf_op jit(solution)/shard_map/first_grad/pallas_call | solution.py:48
  136.6 2.0 %feed_out.1.feed_own = bf16[1024,768]{1,0:T(8,128)(2,1)S(1)} custom-call(bf16[1024,576]{1,0:T(8,128)(2,1)S(1)} %get-tuple-element.136.hidden, bf16[3,768,576]{2,1,0:T(8,128)(2,1)S(1)} %get-tuple-element.137.whole), custom_call_target="tpu_custom_call" | custom-call | flops 905969664 | bytes 5406720 | tf_op jit(solution)/shard_map/feed_out/pallas_call | solution.py:48
  138.6 2.1 %collective-permute-done.25 = bf16[2,96,384]{2,1,0:T(8,128)(2,1)S(1)} collective-permute-done((bf16[2,96,384]{2,1,0:T(8,128)(2,1)S(1)}, bf16[2,96,384]{2,1,0:T(8,128)(2,1)S(1)}, u32[]{:S(2)}, u32[]{:S(2)}) %collective-permute-start.25) | collective-permute-done | bytes 147488 | tf_op jit(solution)/shard_map/ppermute | solution.py:512
  147.6 6.5 %collective-permute-done.35 = bf16[3,24,576]{2,1,0:T(8,128)(2,1)S(1)} collective-permute-done((bf16[3,24,576]{2,1,0:T(8,128)(2,1)S(1)}, bf16[3,24,576]{2,1,0:T(8,128)(2,1)S(1)}, u32[]{:S(2)}, u32[]{:S(2)}) %collective-permute-start.35) | collective-permute-done | bytes 82976 | tf_op jit(solution)/shard_map/ppermute | solution.py:512
  159.6 3.8 %collective-permute-done.37 = bf16[3,48,576]{2,1,0:T(8,128)(2,1)S(1)} collective-permute-done((bf16[3,48,576]{2,1,0:T(8,128)(2,1)S(1)}, bf16[3,48,576]{2,1,0:T(8,128)(2,1)S(1)}, u32[]{:S(2)}, u32[]{:S(2)}) %collective-permute-start.37) | collective-permute-done | bytes 165920 | tf_op jit(solution)/shard_map/ppermute | solution.py:512
  163.5 7.2 %collective-permute-done.36 = bf16[3,48,576]{2,1,0:T(8,128)(2,1)S(1)} collective-permute-done((bf16[3,48,576]{2,1,0:T(8,128)(2,1)S(1)}, bf16[3,48,576]{2,1,0:T(8,128)(2,1)S(1)}, u32[]{:S(2)}, u32[]{:S(2)}) %collective-permute-start.36) | collective-permute-done | bytes 165920 | tf_op jit(solution)/shard_map/ppermute | solution.py:512
  177.6 2.3 %collective-permute-done.39 = bf16[3,48,576]{2,1,0:T(8,128)(2,1)S(1)} collective-permute-done((bf16[3,48,576]{2,1,0:T(8,128)(2,1)S(1)}, bf16[3,48,576]{2,1,0:T(8,128)(2,1)S(1)}, u32[]{:S(2)}, u32[]{:S(2)}) %collective-permute-start.39) | collective-permute-done | bytes 165920 | tf_op jit(solution)/shard_map/ppermute | solution.py:512
  180.3 5.9 %token_grad.1 = (bf16[1024,768]{1,0:T(8,128)(2,1)}, f32[1024,768]{1,0:T(8,128)}) custom-call(bf16[1024,768]{1,0:T(8,128)(2,1)S(1)} %copy-done.1, f32[16,768]{1,0:T(8,128)S(1)} %copy-done.13, f32[1024,768]{1,0:T(8,128)S(1)} %get-tuple-element.129.grad_middle, bf16[1152,768]{1,0:T(8,128)(2,1)S(1)} %first_grad.1.own, ...), custom_call_target="tpu_custom_call" | custom-call | flops 1572864000 | bytes 19513344 | tf_op jit(solution)/shard_map/token_grad/pallas_call | solution.py:48
  188.5 3.3 %collective-permute-done.41 = bf16[3,48,576]{2,1,0:T(8,128)(2,1)S(1)} collective-permute-done((bf16[3,48,576]{2,1,0:T(8,128)(2,1)S(1)}, bf16[3,48,576]{2,1,0:T(8,128)(2,1)S(1)}, u32[]{:S(2)}, u32[]{:S(2)}) %collective-permute-start.41) | collective-permute-done | bytes 165920 | tf_op jit(solution)/shard_map/ppermute | solution.py:512
  192.1 3.3 %collective-permute-done.32 = bf16[4,96,384]{2,1,0:T(8,128)(2,1)S(1)} collective-permute-done((bf16[4,96,384]{2,1,0:T(8,128)(2,1)S(1)}, bf16[4,96,384]{2,1,0:T(8,128)(2,1)S(1)}, u32[]{:S(2)}, u32[]{:S(2)}) %collective-permute-start.32) | collective-permute-done | bytes 294944 | tf_op jit(solution)/shard_map/ppermute | solution.py:441
  (209 shorter events, 79.7 us)
Async XLA Ops:
  2.4 10.5 %collective-permute-start.2 = (bf16[400,384]{1,0:T(8,128)(2,1)S(1)}, bf16[400,384]{1,0:T(8,128)(2,1)}, u32[]{:S(2)}, u32[]{:S(2)}) collective-permute-start(bf16[400,384]{1,0:T(8,128)(2,1)S(1)} %pad_maximum_fusion.2.rest_0_), channel_id=1, source_target_pairs={{8,0},{16,8},{24,16},{28,24},{20,28},{12,20},{4,12},{0,4},{9,1},{1... | collective-permute-start | bytes 921608 | tf_op jit(solution)/shard_map/ppermute | solution.py:474
  5.4 8.8 %collective-permute-start.1 = (bf16[400,384]{1,0:T(8,128)(2,1)S(1)}, bf16[400,384]{1,0:T(8,128)(2,1)}, u32[]{:S(2)}, u32[]{:S(2)}) collective-permute-start(bf16[400,384]{1,0:T(8,128)(2,1)S(1)} %pad_maximum_fusion.2.rest_0_), channel_id=1, source_target_pairs={{0,8},{8,16},{16,24},{24,28},{28,20},{20,12},{12,4},{4,0},{1,9},{9... | collective-permute-start | bytes 921608 | tf_op jit(solution)/shard_map/ppermute | solution.py:474
  7.2 24.1 %collective-permute-start = (bf16[64,768]{1,0:T(8,128)(2,1)}, bf16[64,768]{1,0:T(8,128)(2,1)}, u32[]{:S(2)}, u32[]{:S(2)}) collective-permute-start(bf16[64,768]{1,0:T(8,128)(2,1)} %slice_select_fusion), channel_id=1, source_target_pairs={{0,2},{2,0},{1,3},{3,1},{4,6},{6,4},{5,7},{7,5},{8,10},{10,8},{9,1... | collective-permute-start | bytes 294920 | tf_op jit(solution)/shard_map/ppermute | solution.py:433
  14.2 9.6 %collective-permute-start.4 = (bf16[400,384]{1,0:T(8,128)(2,1)}, bf16[400,384]{1,0:T(8,128)(2,1)}, u32[]{:S(2)}, u32[]{:S(2)}) collective-permute-start(bf16[400,384]{1,0:T(8,128)(2,1)} %collective-permute-done.2.rest_1_), channel_id=1, source_target_pairs={{8,0},{16,8},{24,16},{28,24},{20,28},{12,20},{4,12},{0,4},{9,1},{1... | collective-permute-start | bytes 921608 | tf_op jit(solution)/shard_map/ppermute | solution.py:474
  15.8 9.3 %collective-permute-start.3 = (bf16[400,384]{1,0:T(8,128)(2,1)}, bf16[400,384]{1,0:T(8,128)(2,1)}, u32[]{:S(2)}, u32[]{:S(2)}) collective-permute-start(bf16[400,384]{1,0:T(8,128)(2,1)} %collective-permute-done.1.rest_8_), channel_id=1, source_target_pairs={{0,8},{8,16},{16,24},{24,28},{28,20},{20,12},{12,4},{4,0},{1,9},{9... | collective-permute-start | bytes 921608 | tf_op jit(solution)/shard_map/ppermute | solution.py:474
  25.1 13.1 %collective-permute-start.6 = (bf16[400,384]{1,0:T(8,128)(2,1)}, bf16[400,384]{1,0:T(8,128)(2,1)S(1)}, u32[]{:S(2)}, u32[]{:S(2)}) collective-permute-start(bf16[400,384]{1,0:T(8,128)(2,1)} %collective-permute-done.4.rest_2_), channel_id=1, source_target_pairs={{8,0},{16,8},{24,16},{28,24},{20,28},{12,20},{4,12},{0,4},{9,1},{1... | collective-permute-start | bytes 921608 | tf_op jit(solution)/shard_map/ppermute | solution.py:474
  26.6 11.5 %collective-permute-start.5 = (bf16[400,384]{1,0:T(8,128)(2,1)}, bf16[400,384]{1,0:T(8,128)(2,1)S(1)}, u32[]{:S(2)}, u32[]{:S(2)}) collective-permute-start(bf16[400,384]{1,0:T(8,128)(2,1)} %collective-permute-done.3.rest_7_), channel_id=1, source_target_pairs={{0,8},{8,16},{16,24},{24,28},{28,20},{20,12},{12,4},{4,0},{1,9},{9... | collective-permute-start | bytes 921608 | tf_op jit(solution)/shard_map/ppermute | solution.py:474
  29.4 8.8 %collective-permute-start.11 = (bf16[3,48,576]{2,1,0:T(8,128)(2,1)}, bf16[3,48,576]{2,1,0:T(8,128)(2,1)S(1)}, u32[]{:S(2)}, u32[]{:S(2)}) collective-permute-start(bf16[3,48,576]{2,1,0:T(8,128)(2,1)} %collective-permute-done.9.rest_14_), channel_id=1, source_target_pairs={{0,8},{8,16},{16,24},{24,28},{28,20},{20,12},{12,4},{4,0},{1,9},{9... | collective-permute-start | bytes 497672 | tf_op jit(solution)/shard_map/ppermute | solution.py:474
  38.2 9.0 %collective-permute-start.7 = (bf16[192,384]{1,0:T(8,128)(2,1)S(1)}, bf16[192,384]{1,0:T(8,128)(2,1)S(1)}, u32[]{:S(2)}, u32[]{:S(2)}) collective-permute-start(bf16[192,384]{1,0:T(8,128)(2,1)S(1)} %slice.153), channel_id=1, source_target_pairs={{0,8},{8,16},{16,24},{24,28},{28,20},{20,12},{12,4},{4,0},{1,9},{9... | collective-permute-start | bytes 442376 | tf_op jit(solution)/shard_map/ppermute | solution.py:474
  38.7 8.5 %collective-permute-start.8 = (bf16[208,384]{1,0:T(8,128)(2,1)S(1)}, bf16[208,384]{1,0:T(8,128)(2,1)S(1)}, u32[]{:S(2)}, u32[]{:S(2)}) collective-permute-start(bf16[208,384]{1,0:T(8,128)(2,1)S(1)} %slice.154), channel_id=1, source_target_pairs={{8,0},{16,8},{24,16},{28,24},{20,28},{12,20},{4,12},{0,4},{9,1},{1... | collective-permute-start | bytes 479240 | tf_op jit(solution)/shard_map/ppermute | solution.py:474
  45.6 17.8 %collective-permute-start.13 = (bf16[4,3,48,576]{3,2,1,0:T(8,128)(2,1)S(1)}, bf16[4,3,48,576]{3,2,1,0:T(8,128)(2,1)S(1)}, u32[]{:S(2)}, u32[]{:S(2)}) collective-permute-start(bf16[4,3,48,576]{3,2,1,0:T(8,128)(2,1)S(1)} %pad_maximum_fusion), channel_id=1, source_target_pairs={{0,2},{2,0},{1,3},{3,1},{4,6},{6,4},{5,7},{7,5},{8,10},{10,8},{9,1... | collective-permute-start | bytes 1990664 | tf_op jit(solution)/shard_map/ppermute | solution.py:441
  47.2 10.9 %collective-permute-start.16 = (bf16[1,48,576]{2,1,0:T(8,128)(2,1)S(1)}, bf16[1,48,576]{2,1,0:T(8,128)(2,1)S(1)}, u32[]{:S(2)}, u32[]{:S(2)}) collective-permute-start(bf16[1,48,576]{2,1,0:T(8,128)(2,1)S(1)} %slice.157), channel_id=1, source_target_pairs={{0,8},{8,16},{16,24},{24,28},{28,20},{20,12},{12,4},{4,0},{1,9},{9... | collective-permute-start | bytes 165896 | tf_op jit(solution)/shard_map/ppermute | solution.py:474
  47.8 10.4 %collective-permute-start.17 = (bf16[2,48,576]{2,1,0:T(8,128)(2,1)S(1)}, bf16[2,48,576]{2,1,0:T(8,128)(2,1)S(1)}, u32[]{:S(2)}, u32[]{:S(2)}) collective-permute-start(bf16[2,48,576]{2,1,0:T(8,128)(2,1)S(1)} %slice.158), channel_id=1, source_target_pairs={{8,0},{16,8},{24,16},{28,24},{20,28},{12,20},{4,12},{0,4},{9,1},{1... | collective-permute-start | bytes 331784 | tf_op jit(solution)/shard_map/ppermute | solution.py:474
  59.4 21.4 %collective-permute-start.18 = (bf16[3,3,48,576]{3,2,1,0:T(8,128)(2,1)S(1)}, bf16[3,3,48,576]{3,2,1,0:T(8,128)(2,1)S(1)}, u32[]{:S(2)}, u32[]{:S(2)}) collective-permute-start(bf16[3,3,48,576]{3,2,1,0:T(8,128)(2,1)S(1)} %pad_maximum_fusion.1), channel_id=1, source_target_pairs={{0,2},{2,0},{1,3},{3,1},{4,6},{6,4},{5,7},{7,5},{8,10},{10,8},{9,1... | collective-permute-start | bytes 1493000 | tf_op jit(solution)/shard_map/ppermute | solution.py:441
  108.2 35.1 %collective-permute-start.33 = (bf16[8,3,48,576]{3,2,1,0:T(8,128)(2,1)S(1)}, bf16[8,3,48,576]{3,2,1,0:T(8,128)(2,1)S(1)}, u32[]{:S(2)}, u32[]{:S(2)}) collective-permute-start(bf16[8,3,48,576]{3,2,1,0:T(8,128)(2,1)S(1)} %get-tuple-element.157), channel_id=1, source_target_pairs={{0,2},{2,0},{1,3},{3,1},{4,6},{6,4},{5,7},{7,5},{8,10},{10,8},{9,1... | collective-permute-start | bytes 3981320 | tf_op jit(solution)/shard_map/ppermute | solution.py:441
  134.3 36.3 %collective-permute-start.21 = (bf16[1152,768]{1,0:T(8,128)(2,1)S(1)}, bf16[1152,768]{1,0:T(8,128)(2,1)S(1)}, u32[]{:S(2)}, u32[]{:S(2)}) collective-permute-start(bf16[1152,768]{1,0:T(8,128)(2,1)S(1)} %first_grad.1.own), channel_id=1, source_target_pairs={{0,1},{1,0},{2,3},{3,2},{4,5},{5,4},{6,7},{7,6},{8,9},{9,8},{10,11... | collective-permute-start | bytes 5308424 | tf_op jit(solution)/shard_map/ppermute | solution.py:441
  143.4 12.2 %collective-permute-start.27 = (bf16[4,96,384]{2,1,0:T(8,128)(2,1)S(1)}, bf16[4,96,384]{2,1,0:T(8,128)(2,1)S(1)}, u32[]{:S(2)}, u32[]{:S(2)}) collective-permute-start(bf16[4,96,384]{2,1,0:T(8,128)(2,1)S(1)} %get-tuple-element.188), channel_id=1, source_target_pairs={{8,0},{16,8},{24,16},{28,24},{20,28},{12,20},{4,12},{0,4},{9,1},{1... | collective-permute-start | bytes 884744 | tf_op jit(solution)/shard_map/ppermute | solution.py:512
  145.2 10.4 %collective-permute-start.26 = (bf16[4,96,384]{2,1,0:T(8,128)(2,1)S(1)}, bf16[4,96,384]{2,1,0:T(8,128)(2,1)S(1)}, u32[]{:S(2)}, u32[]{:S(2)}) collective-permute-start(bf16[4,96,384]{2,1,0:T(8,128)(2,1)S(1)} %get-tuple-element.189), channel_id=1, source_target_pairs={{0,8},{8,16},{16,24},{24,28},{28,20},{20,12},{12,4},{4,0},{1,9},{9... | collective-permute-start | bytes 884744 | tf_op jit(solution)/shard_map/ppermute | solution.py:512
  145.5 8.6 %collective-permute-start.35 = (bf16[3,24,576]{2,1,0:T(8,128)(2,1)S(1)}, bf16[3,24,576]{2,1,0:T(8,128)(2,1)S(1)}, u32[]{:S(2)}, u32[]{:S(2)}) collective-permute-start(bf16[3,24,576]{2,1,0:T(8,128)(2,1)S(1)} %get-tuple-element.203), channel_id=1, source_target_pairs={{8,0},{16,8},{24,16},{28,24},{20,28},{12,20},{4,12},{0,4},{9,1},{1... | collective-permute-start | bytes 248840 | tf_op jit(solution)/shard_map/ppermute | solution.py:512
  154.1 26.2 %collective-permute-start.23 = (bf16[1024,768]{1,0:T(8,128)(2,1)S(1)}, bf16[1024,768]{1,0:T(8,128)(2,1)S(1)}, u32[]{:S(2)}, u32[]{:S(2)}) collective-permute-start(bf16[1024,768]{1,0:T(8,128)(2,1)S(1)} %feed_out.1.feed_own), channel_id=1, source_target_pairs={{0,1},{1,0},{2,3},{3,2},{4,5},{5,4},{6,7},{7,6},{8,9},{9,8},{10,11... | collective-permute-start | bytes 4718600 | tf_op jit(solution)/shard_map/ppermute | solution.py:441
  157.5 13.2 %collective-permute-start.29 = (bf16[4,96,384]{2,1,0:T(8,128)(2,1)S(1)}, bf16[4,96,384]{2,1,0:T(8,128)(2,1)S(1)}, u32[]{:S(2)}, u32[]{:S(2)}) collective-permute-start(bf16[4,96,384]{2,1,0:T(8,128)(2,1)S(1)} %get-tuple-element.186), channel_id=1, source_target_pairs={{8,0},{16,8},{24,16},{28,24},{20,28},{12,20},{4,12},{0,4},{9,1},{1... | collective-permute-start | bytes 884744 | tf_op jit(solution)/shard_map/ppermute | solution.py:512
  157.9 12.8 %collective-permute-start.28 = (bf16[4,96,384]{2,1,0:T(8,128)(2,1)S(1)}, bf16[4,96,384]{2,1,0:T(8,128)(2,1)S(1)}, u32[]{:S(2)}, u32[]{:S(2)}) collective-permute-start(bf16[4,96,384]{2,1,0:T(8,128)(2,1)S(1)} %get-tuple-element.187), channel_id=1, source_target_pairs={{0,8},{8,16},{16,24},{24,28},{28,20},{20,12},{12,4},{4,0},{1,9},{9... | collective-permute-start | bytes 884744 | tf_op jit(solution)/shard_map/ppermute | solution.py:512
  175.5 10.7 %collective-permute-start.31 = (bf16[4,96,384]{2,1,0:T(8,128)(2,1)S(1)}, bf16[4,96,384]{2,1,0:T(8,128)(2,1)S(1)}, u32[]{:S(2)}, u32[]{:S(2)}) collective-permute-start(bf16[4,96,384]{2,1,0:T(8,128)(2,1)S(1)} %get-tuple-element.184), channel_id=1, source_target_pairs={{8,0},{16,8},{24,16},{28,24},{20,28},{12,20},{4,12},{0,4},{9,1},{1... | collective-permute-start | bytes 884744 | tf_op jit(solution)/shard_map/ppermute | solution.py:512
  175.9 10.3 %collective-permute-start.30 = (bf16[4,96,384]{2,1,0:T(8,128)(2,1)S(1)}, bf16[4,96,384]{2,1,0:T(8,128)(2,1)S(1)}, u32[]{:S(2)}, u32[]{:S(2)}) collective-permute-start(bf16[4,96,384]{2,1,0:T(8,128)(2,1)S(1)} %get-tuple-element.185), channel_id=1, source_target_pairs={{0,8},{8,16},{16,24},{24,28},{28,20},{20,12},{12,4},{4,0},{1,9},{9... | collective-permute-start | bytes 884744 | tf_op jit(solution)/shard_map/ppermute | solution.py:512
  (62 other events, 438.2 us)

commit v6 on v5

--- a/solution.py
+++ b/solution.py
@@ -38,18 +38,18 @@
     return best
 
 
-def call(kernel, out_shape, args, flops, name, scalars=(), scratch=(), raw=()):
+def call(kernel, out_shape, args, flops, name, scalars=(), scratch=(), raw=(), raw_out=()):
     vmem = pl.BlockSpec(memory_space=pltpu.VMEM)
     smem = pl.BlockSpec(memory_space=pltpu.SMEM)
     anywhere = pl.BlockSpec(memory_space=pl.ANY)
     moved = sum(x.size * x.dtype.itemsize for x in (*args, *out_shape))
     held = sum(math.prod(x.shape) * jnp.dtype(x.dtype).itemsize for x in scratch if x.dtype in (f32, bf16))
-    limit = min(56 * 2**20, moved // 3 + held + 4 * 2**20)
+    limit = min(56 * 2**20, moved // 2 + held + 4 * 2**20)
     return pl.pallas_call(
         kernel,
-        out_shape=out_shape,
+        out_shape=[*out_shape, *raw_out],
         in_specs=[smem] * len(scalars) + [vmem] * len(args) + [anywhere] * len(raw),
-        out_specs=[vmem] * len(out_shape),
+        out_specs=[vmem] * len(out_shape) + [pl.BlockSpec(memory_space=pltpu.HBM)] * len(raw_out),
         scratch_shapes=scratch,
         compiler_params=pltpu.CompilerParams(vmem_limit_bytes=limit),
         cost_estimate=pl.CostEstimate(flops=flops, bytes_accessed=moved, transcendentals=0),
@@ -96,12 +96,16 @@
     lax.fori_loop(0, count, run, 0)
 
 
-def fetch(copies, sems):
+def begin(copies, sems):
     started = []
     for number, (source, target) in enumerate(copies):
         copy = pltpu.make_async_copy(source, target, sems.at[number])
         copy.start()
         started.append(copy)
+    return started
+
+
+def end(started):
     for copy in started:
         copy.wait()
 
@@ -153,7 +157,7 @@
             copies.append((pieces[piece].at[row : row + depth, :], wide.at[place, lanes]))
         piece, row = sources[4]
         copies.append((pieces[piece].at[row : row + PAD, :], gain_held.at[number]))
-    fetch(copies, sems)
+    end(begin(copies, sems))
     lane = lax.broadcasted_iota(jnp.int32, (LANES, width), 1) - lax.broadcasted_iota(jnp.int32, (LANES, width), 0)
     gain_sum = jnp.zeros((PAD, width), f32)
     for number in range(groups):
@@ -192,36 +196,67 @@
     loop(rows // size, query_step)
 
 
-def attend_kernel(bounds, query, key, value, wide, shares, attended, branch):
+def attend_kernel(chosen, last, bounds, query, key, value, *rest):
+    if last:
+        wide, first, done, attended, branch, *kept, held, sems = rest
+        shares, kept = kept[0], kept[1:]
+    else:
+        attended, shares, held, sems = rest
     rows, local = query.shape
-    pairs = local // LANES
+    count = len(chosen)
+    started = []
+    if last:
+        started = begin(list(zip((first, query, key, value), kept)), sems.at[2 * count :])
+        attended[...] = done[...]
     key_at = lax.broadcasted_iota(jnp.int32, (KEYS, KEYS), 0)
     lane_at = lax.broadcasted_iota(jnp.int32, (1, KEYS), 1) % BLOCK
 
-    def attend_step(index):
+    def out_copy(index, number, side):
+        return pltpu.make_async_copy(
+            held.at[side, number], shares.at[index * count + number], sems.at[side * count + number]
+        )
+
+    def attend_step(index, side, old):
         at = pl.multiple_of(index * BLOCK, BLOCK)
         origin = bounds[NSEQ] + at - HALF
         own = lane_at + (origin + HALF)
-        begin = jnp.zeros_like(own)
-        end = jnp.zeros_like(own) + bounds[NSEQ - 1]
+        begin_at = jnp.zeros_like(own)
+        end_at = jnp.zeros_like(own) + bounds[NSEQ - 1]
         for number in range(NSEQ - 1):
-            begin = jnp.where(own >= bounds[number], bounds[number], begin)
+            begin_at = jnp.where(own >= bounds[number], bounds[number], begin_at)
         for number in reversed(range(NSEQ - 1)):
-            end = jnp.where(own < bounds[number], bounds[number], end)
-        least = jnp.maximum(lane_at, begin - origin)
-        most = jnp.minimum(lane_at + WINDOW, end - 1 - origin)
+            end_at = jnp.where(own < bounds[number], bounds[number], end_at)
+        least = jnp.maximum(lane_at, begin_at - origin)
+        most = jnp.minimum(lane_at + WINDOW, end_at - 1 - origin)
         allowed = (key_at >= least) & (key_at <= most)
-        for pair in range(pairs):
+        for number, pair in enumerate(chosen):
             lanes = slice(pair * LANES, (pair + 1) * LANES)
             both = halves(query[pl.ds(at, BLOCK), lanes])
             scores = jnp.where(allowed, dot(key[pl.ds(at, KEYS), lanes], both, NT), -1e30)
             weight = jnp.exp(scores - jnp.max(scores, axis=0, keepdims=True))
             part = (weight * (1.0 / jnp.sum(weight, axis=0, keepdims=True))).astype(bf16)
-            shares[index * pairs + pair] = part
+            if old is not None:
+                out_copy(old, number, side).wait()
+            held[side, number] = part
+            out_copy(index, number, side).start()
             mixed = dot(value[pl.ds(at, KEYS), lanes], part, TN)
             attended[pl.ds(at, BLOCK), lanes] = joined(mixed).astype(bf16)
 
-    loop(rows // BLOCK, attend_step)
+    steps = rows // BLOCK
+    attend_step(0, 0, None)
+    attend_step(1, 1, None)
+
+    def two_steps(index):
+        for side in range(2):
+            attend_step(2 * index + 2 + side, side, 2 * index + side)
+
+    loop(steps // 2 - 1, two_steps)
+    for side in range(2):
+        for number in range(count):
+            out_copy(steps - 2 + side, number, side).wait()
+    end(started)
+    if not last:
+        return
     out_t = wide.at[:, 3 * local :]
     size = step_of(rows, 256)
 
@@ -232,33 +267,34 @@
     loop(rows // size, out_step)
 
 
-def feed_kernel(slots, parts_at, tokens, own, other, gain, cotangent, *rest):
+def feed_kernel(slots, tokens, own, other, gain, cotangent, *rest):
     pieces, rest = rest[:-8], rest[-8:]
     middle, second, hidden, grad_gate, grad_upper, partial, whole, sems = rest
     rows, width = tokens.shape
     groups = slots.shape[0]
     depth = width // groups
-    sides = len(pieces) // groups
-    size = depth // sides
     copies = []
-    for number in range(groups):
-        for side in range(sides):
-            start = slots[number] * depth + parts_at[side] * size
-            place = pl.ds(pl.multiple_of(start, size), size)
-            copies.append((pieces[number * sides + side], whole.at[:, place, :]))
-    fetch(copies, sems)
+    for number, sources in enumerate(piece_plan(groups, [depth] * 3, 1)):
+        place = pl.ds(pl.multiple_of(slots[number] * depth, depth), depth)
+        for part, (piece, row) in enumerate(sources):
+            copies.append((pieces[piece].at[row : row + depth, :], whole.at[part, place, :]))
+    started = begin(copies, sems)
     gate_w, upper_w, down_t = (whole.at[number] for number in range(3))
     gains = gain[1:2, :]
     size = step_of(rows, 256)
 
-    def step(index):
-        at = pl.multiple_of(index * size, size)
-        here = pl.ds(at, size)
+    def norm_step(index):
+        here = pl.ds(pl.multiple_of(index * size, size), size)
         mid = tokens[here, :].astype(f32) + (own[here, :].astype(f32) + other[here, :].astype(f32))
         middle[here, :] = mid
-        hat, _ = normed(mid)
-        low = (hat * gains).astype(bf16)
-        second[here, :] = low
+        second[here, :] = (normed(mid)[0] * gains).astype(bf16)
+
+    loop(rows // size, norm_step)
+    end(started)
+
+    def step(index):
+        here = pl.ds(pl.multiple_of(index * size, size), size)
+        low = second[here, :]
         gate = dot(low, gate_w[...])
         upper = dot(low, upper_w[...])
         grad = dot(cotangent[here, :], down_t[...])
@@ -286,19 +322,16 @@
     loop(rows // size, step)
 
 
-def weight_kernel(slots, parts_at, second, hidden, grad_gate, grad_upper, cotangent, *rest):
-    outs, total = rest[:-1], rest[-1]
+def weight_kernel(slots, second, hidden, grad_gate, grad_upper, cotangent, grads, total):
     rows, width = second.shape
     step_rows = step_of(width, 256)
     for number, (left, right) in enumerate(((second, grad_gate), (second, grad_upper), (cotangent, hidden))):
         for start in range(0, width, step_rows):
             here = slice(start, start + step_rows)
             total[number, here, :] = dot(left[:, here], right[...], TN).astype(bf16)
-    size = outs[0].shape[2]
-    for number, slot in enumerate(hop_order(outs[0].shape[0])):
-        for side, out in enumerate(outs):
-            start = slots[slot] * (size * len(outs)) + parts_at[side] * size
-            out[number] = total[:, pl.ds(pl.multiple_of(start, size), size), :]
+    depth = grads.shape[2]
+    for number, slot in enumerate(hop_order(grads.shape[0])):
+        grads[number] = total[:, pl.ds(pl.multiple_of(slots[slot] * depth, depth), depth), :]
 
 
 def hop_order(count):
@@ -329,59 +362,63 @@
     loop(rows // size, norm_step)
 
 
-def back_kernel(query, key, value, shares, grad_att, cosine, sine, grad_proj, grad_key, grad_value):
-    rows, local = query.shape
+def back_kernel(chosen, query, key, value, shares, grad_att, cosine, sine, *rest):
+    parts, (grad_key, grad_value) = rest[:-2], rest[-2:]
+    rows = query.shape[0]
     extent = key.shape[0]
-    pairs = local // LANES
+    count = len(chosen)
     grad_key[...] = jnp.zeros_like(grad_key)
     grad_value[...] = jnp.zeros_like(grad_value)
     low = lax.broadcasted_iota(jnp.int32, (1, LANES), 1) % HEAD < HEAD // 2
-    zero = jnp.zeros((HALF, local), bf16)
-    grad_proj[:HALF, :local] = zero
-    grad_proj[rows + HALF :, :local] = zero
+    zero = jnp.zeros((HALF, LANES), bf16)
+    for part in parts:
+        part[:HALF, :LANES] = zero
+        part[rows + HALF :, :LANES] = zero
 
     def attend_step(index):
         at = pl.multiple_of(index * BLOCK, BLOCK)
         start = pl.multiple_of(at + HALF, HALF)
         co, si = cosine[pl.ds(start, BLOCK), :], sine[pl.ds(start, BLOCK), :]
-        found = []
-        for pair in range(pairs):
+        for number, pair in enumerate(chosen):
             lanes = slice(pair * LANES, (pair + 1) * LANES)
+            here = slice(number * LANES, (number + 1) * LANES)
             both = halves(query[pl.ds(at, BLOCK), lanes])
             grad = halves(grad_att[pl.ds(at, BLOCK), lanes])
             keys = key[pl.ds(at, KEYS), lanes]
-            part = shares[index * pairs + pair]
+            part = shares[index * count + number]
             wide = part.astype(f32)
             grad_shares = dot(value[pl.ds(at, KEYS), lanes], grad, NT)
             delta = jnp.sum(wide * grad_shares, axis=0, keepdims=True)
             raw = (wide * (grad_shares - delta)).astype(bf16)
             grad_query = joined(dot(keys, raw, TN)) * HEAD**-0.5
             turn = (grad_query * co - turned(grad_query, low) * si).astype(bf16)
-            found.append((lanes, turn, dot(raw, both), dot(part, grad)))
-        for lanes, turn, key_part, value_part in found:
-            grad_proj[pl.ds(start, BLOCK), lanes] = turn
-            grad_key[pl.ds(at, KEYS), lanes] += key_part
-            grad_value[pl.ds(at, KEYS), lanes] += value_part
+            parts[number][pl.ds(start, BLOCK), :LANES] = turn
+            grad_key[pl.ds(at, KEYS), here] += dot(raw, both)
+            grad_value[pl.ds(at, KEYS), here] += dot(part, grad)
 
     loop(rows // BLOCK, attend_step)
 
     def turn_step(index):
         here = pl.ds(pl.multiple_of(index * BLOCK, BLOCK), BLOCK)
         co, si = cosine[here, :], sine[here, :]
-        for pair in range(pairs):
-            lanes = slice(pair * LANES, (pair + 1) * LANES)
+        for number, out in enumerate(parts):
+            lanes = slice(number * LANES, (number + 1) * LANES)
             part = grad_key[here, lanes]
-            turn = slice(local + pair * LANES, local + (pair + 1) * LANES)
-            grad_proj[here, turn] = (part * co - turned(part, low) * si).astype(bf16)
-        grad_proj[here, 2 * local :] = grad_value[here, :].astype(bf16)
+            out[here, LANES : 2 * LANES] = (part * co - turned(part, low) * si).astype(bf16)
+            out[here, 2 * LANES :] = grad_value[here, lanes].astype(bf16)
 
     loop(extent // BLOCK, turn_step)
 
 
-def grad_kernel(slots, first, grad_proj, low_mid, attended, grads, total):
+def grad_kernel(slots, first, low_mid, attended, *rest):
+    parts, (grad_proj, grads_a, grads_b, total) = rest[:-4], rest[-4:]
     local = attended.shape[1]
     width = first.shape[1]
-    depth = grads.shape[2]
+    depth = grads_a.shape[2]
+    for pair, part in enumerate(parts):
+        for number in range(3):
+            lanes = slice(number * local + pair * LANES, number * local + (pair + 1) * LANES)
+            grad_proj[:, lanes] = part[:, number * LANES : (number + 1) * LANES]
     step_rows = step_of(width, 256)
     for start in range(0, width, step_rows):
         here = slice(start, start + step_rows)
@@ -389,8 +426,10 @@
             lanes = slice(number * local, (number + 1) * local)
             total[number, here, :] = dot(first[:, here], grad_proj[:, lanes], TN).astype(bf16)
         total[3, here, :] = dot(low_mid[:, here], attended[...], TN).astype(bf16)
-    for number, slot in enumerate(hop_order(grads.shape[0])):
-        grads[number] = total[:, pl.ds(pl.multiple_of(slots[slot] * depth, depth), depth), :]
+    for number, slot in enumerate(hop_order(grads_a.shape[0])):
+        place = pl.ds(pl.multiple_of(slots[slot] * depth, depth), depth)
+        grads_a[number] = total[:2, place, :]
+        grads_b[number] = total[2:, place, :]
 
 
 def first_kernel(grad_proj, wide, partial):
@@ -435,6 +474,12 @@
         return jnp.where(spot == 1, got, none), jnp.where(spot == 0, got, none)
     up = [(i, i + 1) for i in range(devices - 1)]
     return lax.ppermute(last, "ctx", up), lax.ppermute(initial, "ctx", [(j, i) for i, j in up])
+
+
+def over_ctx(array):
+    if lax.axis_size("ctx") == 2:
+        return array.astype(f32) + swap(array, "ctx").astype(f32)
+    return lax.psum(array, "ctx").astype(f32)
 
 
 def swap(array, axis="tensor"):
@@ -455,6 +500,12 @@
 
 def tied(values, others):
     held = lax.optimization_barrier((tuple(values), tuple(others)))
+    return held[0]
+
+
+def locked(values, chain):
+    held = lax.optimization_barrier((tuple(values), tuple(chain.state)))
+    chain.state = held[1]
     return held[0]
 
 
@@ -545,33 +596,18 @@
     groups = lax.axis_size("dp")
     depth = width // groups
     middle_hop = groups // 2
-    split = lax.axis_size("ctx") == 2
-    spot = lax.axis_index("ctx")
-    low = spot == 0
     gains = jnp.pad(jnp.stack([gain_one, gain_two]), ((0, PAD - 2), (0, local - depth)))
     mine_one = jnp.concatenate([w_qkv.reshape(3 * depth, local), w_out.T, gains])
     now = RingGather(mine_one, 2 * depth)
     now.hop()
     before, after = exchange(tokens[:HALF], tokens[rows - HALF :])
     slots = ring()[-1]
-    mine_two = jnp.concatenate([w_in, w_down.T[None]])
-    if split:
-        sides = [mine_two[:, : depth // 2], mine_two[:, depth // 2 :]]
-        mine_two, other_two = jnp.where(low, sides[0], sides[1]), jnp.where(low, sides[1], sides[0])
-        parts_at = jnp.stack([spot, 1 - spot]).astype(jnp.int32)
-    else:
-        parts_at = jnp.zeros((1,), jnp.int32)
-    later = RingGather(tied([mine_two], now.state)[0], 1)
-    now.hop()
-    later.hop()
     cosine, sine, bounds = tables(lengths, rows)
-    later.after(now.state)
     while now.hops < middle_hop:
         now.hop()
-        later.hop()
-        later.after(now.state)
-    while later.hops < middle_hop:
-        later.hop()
+    mine_two = jnp.concatenate([w_in.reshape(2 * depth, units), w_down.T])
+    later = RingGather(tied([mine_two], now.state)[0], depth)
+    later.hop()
     hat, = call(
         norm_kernel, [shape((extent, width), f32)], (tokens, before, after), rows * width * 2000, "first_norm"
     )
@@ -593,37 +629,47 @@
         [pltpu.VMEM((groups, PAD, local), bf16), pltpu.SemaphoreType.DMA((5 * groups,))],
         pieces,
     )
-    held = {slot: later.pieces[slot][0] for slot in range(groups) if slot != middle_hop}
-    held[middle_hop] = jnp.concatenate(later.pieces[middle_hop])
-    if split:
-        early = [slot for hop in range(1, middle_hop // 2 + 1) for slot in (hop, groups - hop)]
-        late = [slot for slot in range(1, groups) if slot not in early]
-        others = {0: other_two}
-        for batch in (early, late):
-            got = swap(jnp.stack([held[slot] for slot in batch]), "ctx")
-            if batch is early:
-                query, key, value = tied([query, key, value], [got])
-            for number, slot in enumerate(batch):
-                others[slot] = got[number]
-        query, key, value = tied([query, key, value], later.state)
-        pieces = [piece for slot in range(groups) for piece in (held[slot], others[slot])]
-    else:
-        got = held[middle_hop]
-        pieces = [held[slot] for slot in range(groups)]
-    shares, attended, branch = call(
-        attend_kernel,
-        [
-            shape((blocks * pairs, KEYS, KEYS), bf16),
-            shape((rows, local), bf16),
-            shape((rows, width), bf16),
-        ],
-        (query, key, value, wide),
-        2 * rows * width * local * 16,
+    early, late = tuple(range(pairs - 1)), (pairs - 1,)
+
+    def share_shapes(chosen):
+        return (
+            shape((blocks * len(chosen), KEYS, KEYS), bf16),
+            [pltpu.VMEM((2, len(chosen), KEYS, KEYS), bf16), pltpu.SemaphoreType.DMA((2 * len(chosen) + 4,))],
+        )
+
+    query, key, value = tied([query, key, value], later.state)
+    later.hop()
+    out, scratch = share_shapes(early)
+    attended, shares_early = call(
+        functools.partial(attend_kernel, early, False),
+        [shape((rows, local), bf16)],
+        (query, key, value),
+        2 * rows * width * local * 10,
         "attend",
         (bounds,),
-    )
-    branch, = tied([branch], [got])
+        scratch,
+        (),
+        [out],
+    )
+    attended, = locked([attended], later)
+    later.hop()
+    out, scratch = share_shapes(late)
+    attended, branch, shares_late, first, query, key, value = call(
+        functools.partial(attend_kernel, late, True),
+        [shape((rows, local), bf16), shape((rows, width), bf16)],
+        (query, key, value, wide, first, attended),
+        2 * rows * width * local * 7,
+        "attend",
+        (bounds,),
+        scratch,
+        (),
+        [out] + [shape(x.shape, bf16) for x in (first, query, key, value)],
+    )
     branch_other = swap(branch)
+    later.after([branch])
+    while later.hops < middle_hop:
+        later.hop()
+    pieces = [piece for slot in range(groups) for piece in later.pieces[slot]]
     middle, second, hidden, grad_gate, grad_upper, partial, whole = call(
         feed_kernel,
         [
@@ -638,31 +684,22 @@
         (tokens, branch, branch_other, gain, cotangent),
         2 * rows * width * units * 8,
         "feed_forward_and_back",
-        (slots, parts_at),
-        [pltpu.SemaphoreType.DMA((len(pieces),))],
+        (slots,),
+        [pltpu.SemaphoreType.DMA((3 * groups,))],
         pieces,
     )
     partial_other = swap(partial)
-    ways = 2 if split else 1
-    grads_two = call(
+    grads_two, = call(
         weight_kernel,
-        [shape((groups, 3, depth // ways, units), bf16)] * ways,
+        [shape((groups, 3, depth, units), bf16)],
         (second, hidden, grad_gate, grad_upper, cotangent),
         2 * rows * width * units * 5,
         "feed_weight_grads",
-        (slots, parts_at),
+        (slots,),
         [pltpu.VMEM((3, width, units), bf16)],
     )
-    if split:
-        grads_two = [grads_two[0], swap(grads_two[1], "ctx")]
-    feed, = call(
-        feed_out_kernel,
-        [shape((rows, width), bf16)],
-        (hidden, whole),
-        2 * rows * width * units,
-        "feed_out",
-    )
-    feed_other = swap(feed)
+    sums_two = RingScatter([grads_two], 1)
+    sums_two.hop()
     grad_middle, low_mid, grad_att = call(
         middle_kernel,
         [shape((rows, width), f32), shape((rows, width), bf16), shape((rows, local), bf16)],
@@ -670,32 +707,50 @@
         2 * rows * width * local * 4,
         "middle_grad",
     )
-    grad_proj, = call(
-        back_kernel,
-        [shape((extent, 3 * local), bf16)],
-        (query, key, value, shares, grad_att, cosine, sine),
-        2 * rows * width * local * 16,
-        "attention_back",
-        (),
-        [pltpu.VMEM((extent, local), f32)] * 2,
-    )
-    grads_one, = call(
+    grad_att, = locked([grad_att], sums_two)
+    sums_two.hop()
+    grad_parts = []
+    for chosen, shares in ((early, shares_early), (late, shares_late)):
+        if grad_parts:
+            grad_att, *grad_parts = locked([grad_att, *grad_parts], sums_two)
+            sums_two.hop()
+        grad_parts += call(
+            functools.partial(back_kernel, chosen),
+            [shape((extent, 3 * LANES), bf16)] * len(chosen),
+            (query, key, value, shares, grad_att, cosine, sine),
+            2 * rows * width * local * 5 * len(chosen),
+            "attention_back",
+            (),
+            [pltpu.VMEM((extent, len(chosen) * LANES), f32)] * 2,
+        )
+    feed, = call(
+        feed_out_kernel,
+        [shape((rows, width), bf16)],
+        (tied([hidden], grad_parts[: len(early)])[0], whole),
+        2 * rows * width * units,
+        "feed_out",
+    )
+    feed_other = swap(feed)
+    grad_parts = tied(grad_parts, [feed, *sums_two.state])
+    grad_proj, *grads_one = call(
         grad_kernel,
-        [shape((groups, 4, depth, local), bf16)],
-        (first, grad_proj, low_mid, attended),
+        [shape((extent, 3 * local), bf16)] + [shape((groups, 2, depth, local), bf16)] * 2,
+        (first, low_mid, attended, *grad_parts),
         2 * rows * width * local * 6,
         "attention_weight_grads",
         (slots,),
         [pltpu.VMEM((4, width, local), bf16)],
     )
-    sums_one = RingScatter([grads_one], 0)
-    sums_one.hop()
-    sums_two = RingScatter(tied(grads_two, sums_one.state), 1)
-    sums_two.hop()
+    sums_one = [RingScatter([part], 0) for part in grads_one]
+    sums_one[0].hop()
+    sums_one[1].hop()
+    sums_two.after(sums_one[0].state)
+    while sums_two.hops < middle_hop:
+        sums_two.hop()
     first_part, = call(
         first_kernel,
         [shape((extent, width), bf16)],
-        (tied([grad_proj], [grads_one])[0], wide),
+        (tied([grad_proj], grads_one)[0], wide),
         2 * rows * width * local * 3,
         "first_grad",
     )
@@ -705,16 +760,15 @@
         here = slice(at, at + HALF)
         return (first_part[here].astype(f32) + first_other[here].astype(f32)).astype(bf16)
 
-    sums_one.after([first_part, feed])
-    while sums_one.hops < middle_hop - 1:
-        sums_one.hop()
-        sums_two.after(sums_one.state)
-        sums_two.hop()
+    for chain in sums_one:
+        chain.after([first_part, feed])
+    while sums_one[0].hops < middle_hop - 1:
+        for chain in sums_one:
+            chain.hop()
     from_before, from_after = exchange(edge_sum(0), edge_sum(rows + HALF))
-    sums_one.after([from_before, from_after])
-    sums_one.hop()
-    sums_two.after(sums_one.state)
-    sums_two.hop()
+    for chain in sums_one:
+        chain.after([from_before, from_after])
+        chain.hop()
     mixed, token_grad = call(
         final_kernel,
         [shape((rows, width), bf16), shape((rows, width), f32)],
@@ -722,13 +776,9 @@
         rows * width * 2000,
         "token_grad",
     )
-    one, two = tied([sums_one.total()], [mixed, token_grad])[0], sums_two.total()
-    if split:
-        one = one.astype(f32) + swap(one, "ctx").astype(f32)
-        got = swap(two, "ctx")
-        two = jnp.concatenate([jnp.where(low, two, got), jnp.where(low, got, two)], axis=1).astype(f32)
-    else:
-        one, two = lax.psum(one, "ctx").astype(f32), lax.psum(two, "ctx").astype(f32)
+    two = over_ctx(sums_two.total())
+    one = [over_ctx(sums_one[0].total()), over_ctx(sums_one[1].total())]
+    one = jnp.concatenate(one)
     gain_one_grad = jnp.sum(one[:3] * w_qkv.astype(f32), axis=(0, 2)) / gain_one.astype(f32)
     gain_two_grad = jnp.sum(two[:2] * w_in.astype(f32), axis=(0, 2)) / gain_two.astype(f32)
     both = jnp.stack([gain_one_grad, gain_two_grad])

time: 201 us -> 212 us (1.055)
  waiting for transfers between devices: 53.7 us -> 68.6 us
  local copies, waits for them, and re-layouts: 15.7 us -> 2.1 us
  Pallas kernels: 72.4 us -> 81.3 us
  starting transfers between devices: 42.7 us -> 49.3 us
  other arithmetic: 14.6 us -> 9.67 us
    ppermute x16 -> x20, starting transfers between devices: 11.3 us -> 23.8 us  [hop(): lax.ppermute(one, 'dp', self.ahead)]
    ppermute x16 -> x20, waiting for transfers between devices: 22.2 us -> 34.3 us  [hop(): lax.ppermute(two, 'dp', self.back)]
    unnamed x85 -> x14, local copies, waits for them, and re-layouts: 11.8 us -> 0.03 us
    pallas_call x11 -> x13, Pallas kernels: 72.4 us -> 81.3 us  [call(): pl.pallas_call(kernel, out_shape=[*out_shape, *raw_out], in_specs=[smem]...]
    ppermute x16 -> x20, starting transfers between devices: 22.8 us -> 17.9 us  [hop(): lax.ppermute(two, 'dp', self.back)]
    ppermute x16 -> x20, waiting for transfers between devices: 20.9 us -> 25.6 us  [hop(): lax.ppermute(one, 'dp', self.ahead)]
    ppermute x10 -> x8, waiting for transfers between devices: 9.58 us -> 6.27 us  [swap(): return lax.ppermute(array, axis, [(0, 1), (1, 0)])]
    squeeze x2 -> x1, local copies, waits for them, and re-layouts: 2.55 us -> 0.03 us  [part(): total = self.parts[0][at]]
  transfers between devices with their start and end apart: 44 -> 50, of which waited for: 24 -> 25; matrix products, arithmetic and copies ran while one was open for 8% -> 4% of each run, Pallas kernels for 29% -> 23%
where the time goes in v6:
time: 212 us
  Pallas kernels  81.3 us (38%)
  waiting for transfers between devices  68.6 us (32%)
  starting transfers between devices  49.3 us (23%)
  other arithmetic  9.67 us (5%)
    pallas_call x13, Pallas kernels, call(): pl.pallas_call(kernel, out_shape=[*out_shape, *raw_out], in_specs=[smem]...  81.3 us
    ppermute x20, waiting for transfers between devices, hop(): lax.ppermute(two, 'dp', self.back)  34.3 us
    ppermute x20, waiting for transfers between devices, hop(): lax.ppermute(one, 'dp', self.ahead)  25.6 us
    ppermute x20, starting transfers between devices, hop(): lax.ppermute(one, 'dp', self.ahead)  23.8 us
    ppermute x20, starting transfers between devices, hop(): lax.ppermute(two, 'dp', self.back)  17.9 us
    ppermute x8, waiting for transfers between devices, swap(): return lax.ppermute(array, axis, [(0, 1), (1, 0)])  6.27 us
  transfers between devices with their start and end apart: 50, of which 25 were waited for; matrix products, arithmetic and copies ran while one was open for 4% of the time, Pallas kernels for 23%

profile of v6, /device:TPU:0, one launch (start us, length us, event | category | flops | bytes accessed | tf_op | source)
XLA Modules:
  0.0 212.1 jit_solution(4642773078873496462)
XLA Ops:
  2.4 3.0 %collective-permute-start.2 = (bf16[400,384]{1,0:T(8,128)(2,1)S(1)}, bf16[400,384]{1,0:T(8,128)(2,1)S(1)}, u32[]{:S(2)}, u32[]{:S(2)}) collective-permute-start(bf16[400,384]{1,0:T(8,128)(2,1)S(1)} %pad_maximum_fusion.2.rest_0_), channel_id=1, source_target_pairs={{8,0},{16,8},{24,16},{28,24},{20,28},{12,20},{4,12},{0,4},{9,1},{1... | collective-permute-start | bytes 921608 | tf_op jit(solution)/shard_map/ppermute | solution.py:525
  10.2 2.5 %collective-permute-done.2.rest_1_ = bf16[400,384]{1,0:T(8,128)(2,1)S(1)} collective-permute-done((bf16[400,384]{1,0:T(8,128)(2,1)S(1)}, bf16[400,384]{1,0:T(8,128)(2,1)S(1)}, u32[]{:S(2)}, u32[]{:S(2)}) %collective-permute-start.2) | collective-permute-done | bytes 307232 | tf_op jit(solution)/shard_map/ppermute | solution.py:525
  18.3 3.6 %collective-permute-done.4.rest_2_ = bf16[400,384]{1,0:T(8,128)(2,1)S(1)} collective-permute-done((bf16[400,384]{1,0:T(8,128)(2,1)S(1)}, bf16[400,384]{1,0:T(8,128)(2,1)S(1)}, u32[]{:S(2)}, u32[]{:S(2)}) %collective-permute-start.4) | collective-permute-done | bytes 307232 | tf_op jit(solution)/shard_map/ppermute | solution.py:525
  25.4 4.7 %collective-permute-done.6.rest_3_ = bf16[400,384]{1,0:T(8,128)(2,1)S(1)} collective-permute-done((bf16[400,384]{1,0:T(8,128)(2,1)S(1)}, bf16[400,384]{1,0:T(8,128)(2,1)S(1)}, u32[]{:S(2)}, u32[]{:S(2)}) %collective-permute-start.6) | collective-permute-done | bytes 307232 | tf_op jit(solution)/shard_map/ppermute | solution.py:525
  36.0 4.6 %collective-permute-done.7.rest_4_ = bf16[192,384]{1,0:T(8,128)(2,1)S(1)} collective-permute-done((bf16[192,384]{1,0:T(8,128)(2,1)S(1)}, bf16[192,384]{1,0:T(8,128)(2,1)S(1)}, u32[]{:S(2)}, u32[]{:S(2)}) %collective-permute-start.7) | collective-permute-done | bytes 147488 | tf_op jit(solution)/shard_map/ppermute | solution.py:525
  42.6 6.5 %project.1 = (bf16[768,1536]{1,0:T(8,128)(2,1)S(1)}, f32[16,768]{1,0:T(8,128)S(1)}, bf16[1152,768]{1,0:T(8,128)(2,1)S(1)}, bf16[1024,384]{1,0:T(8,128)(2,1)S(1)}...) custom-call(s32[8]{0:T(128)S(1)} %compare_select_fusion.2.slots, f32[1152,768]{1,0:T(8,128)S(1)} %first_norm.1.hat, ...), custom_call_target="tpu_custom_call" | custom-call | flops 4831838208 | bytes 11452416 | tf_op jit(solution)/shard_map/project/pallas_call | solution.py:48
  54.4 10.2 %attend.2 = (bf16[1024,384]{1,0:T(8,128)(2,1)S(1)}, bf16[16,256,256]{2,1,0:T(8,128)(2,1)S(1)}) custom-call(s32[5]{0:T(128)S(1)} %pad_add_fusion.bounds, bf16[1024,384]{1,0:T(8,128)(2,1)S(1)} %get-tuple-element.127.query, bf16[1152,384]{1,0:T(8,128)(2,1)S(1)} %get-tuple-element.128.key, bf16[1152,384]{1,0:T(8,128)(2,1)S(1)} %get-tuple-element.129.value), custom_call_target="tpu_custom_call" | custom-call | flops 6039797760 | bytes 3342336 | tf_op jit(solution)/shard_map/attend/pallas_call | solution.py:48
  64.6 8.3 %attend.3 = (bf16[1024,384]{1,0:T(8,128)(2,1)S(1)}, bf16[1024,768]{1,0:T(8,128)(2,1)S(1)}, bf16[8,256,256]{2,1,0:T(8,128)(2,1)S(1)}, bf16[1152,768]{1,0:T(8,128)...) custom-call(s32[5]{0:T(128)S(1)} %pad_add_fusion.bounds, ...), custom_call_target="tpu_custom_call" | custom-call | flops 4227858432 | bytes 9830400 | tf_op jit(solution)/shard_map/attend/pallas_call | solution.py:48
  75.0 8.9 %collective-permute-done.14.rest_6_ = bf16[288,576]{1,0:T(8,128)(2,1)S(1)} collective-permute-done((bf16[288,576]{1,0:T(8,128)(2,1)S(1)}, bf16[288,576]{1,0:T(8,128)(2,1)S(1)}, u32[]{:S(2)}, u32[]{:S(2)}) %collective-permute-start.14) | collective-permute-done | bytes 331808 | tf_op jit(solution)/shard_map/ppermute | solution.py:525
  87.0 4.0 %collective-permute-done.16.rest_4_ = bf16[96,576]{1,0:T(8,128)(2,1)S(1)} collective-permute-done((bf16[96,576]{1,0:T(8,128)(2,1)S(1)}, bf16[96,576]{1,0:T(8,128)(2,1)S(1)}, u32[]{:S(2)}, u32[]{:S(2)}) %collective-permute-start.16) | collective-permute-done | bytes 110624 | tf_op jit(solution)/shard_map/ppermute | solution.py:525
  91.9 15.1 %feed_forward_and_back.1 = (f32[1024,768]{1,0:T(8,128)S(1)}, bf16[1024,768]{1,0:T(8,128)(2,1)S(1)}, bf16[1024,576]{1,0:T(8,128)(2,1)S(1)}, bf16[1024,576]{1,0:T(...) custom-call(s32[8]{0:T(128)S(1)} %compare_select_fusion.2.slots, ...), custom_call_target="tpu_custom_call" | custom-call | flops 7247757312 | bytes 18825216 | tf_op jit(solution)/shard_map/feed_forward_and_back/pallas_call | solution.py:48
  107.1 4.7 %feed_weight_grads.1 = bf16[8,3,96,576]{3,2,1,0:T(8,128)(2,1)S(1)} custom-call(s32[8]{0:T(128)S(1)} %compare_select_fusion.2.slots, bf16[1024,768]{1,0:T(8,128)(2,1)S(1)} %get-tuple-element.152.second, bf16[1024,576]{1,0:T(8,128)(2,1)S(1)} %get-tuple-element.173.hidden, bf16[1024,576]{1,0:T(8,128)(2,1)S(1)} %get-tuple-element.154.grad_gate, ...), custom_call_target="tpu_custom_call" | custom-call | flops 4529848320 | bytes 9338880 | tf_op jit(solution)/shard_map/feed_weight_grads/pallas_call | solution.py:48
  114.0 5.0 %collective-permute-done.20 = bf16[3,48,576]{2,1,0:T(8,128)(2,1)S(1)} collective-permute-done((bf16[3,48,576]{2,1,0:T(8,128)(2,1)S(1)}, bf16[3,48,576]{2,1,0:T(8,128)(2,1)S(1)}, u32[]{:S(2)}, u32[]{:S(2)}) %collective-permute-start.20) | collective-permute-done | bytes 165920 | tf_op jit(solution)/shard_map/ppermute | solution.py:563
  119.8 3.6 %middle_grad.1 = (f32[1024,768]{1,0:T(8,128)S(1)}, bf16[1024,768]{1,0:T(8,128)(2,1)S(1)}, bf16[1024,384]{1,0:T(8,128)(2,1)S(1)}) custom-call(f32[1024,768]{1,0:T(8,128)S(1)} %get-tuple-element.145.middle, bf16[1024,768]{1,0:T(8,128)(2,1)S(1)} %get-tuple-element.146.own, bf16[1024,768]{1,0:T(8,128)(2,1)S(1)} %collective-permute-done.18.other, ...), custom_call_target="tpu_custom_call" | custom-call | flops 2415919104 | bytes 15777792 | tf_op jit(solution)/shard_map/middle_grad/pallas_call | solution.py:48
  125.5 9.2 %attention_back.2 = (bf16[1152,384]{1,0:T(8,128)(2,1)S(1)}, bf16[1152,384]{1,0:T(8,128)(2,1)S(1)}) custom-call(bf16[1024,384]{1,0:T(8,128)(2,1)S(1)} %get-tuple-element.159.query, bf16[1152,384]{1,0:T(8,128)(2,1)S(1)} %get-tuple-element.160.key, bf16[1152,384]{1,0:T(8,128)(2,1)S(1)} %get-tuple-element.161.value, ...), custom_call_target="tpu_custom_call" | custom-call | flops 6039797760 | bytes 8388608 | tf_op jit(solution)/shard_map/attention_back/pallas_call | solution.py:48
  139.0 5.9 %attention_back.3.rest_2_ = bf16[1152,384]{1,0:T(8,128)(2,1)S(1)} custom-call(bf16[1024,384]{1,0:T(8,128)(2,1)S(1)} %get-tuple-element.159.query, bf16[1152,384]{1,0:T(8,128)(2,1)S(1)} %get-tuple-element.160.key, bf16[1152,384]{1,0:T(8,128)(2,1)S(1)} %get-tuple-element.161.value, bf16[8,256,256]{2,1,0:T(8,128)(2,1)S(1)} %get-tuple-element.171.shares, ...), custom_call_target="tpu_custom_call" | custom-call | flops 3019898880 | bytes 6455296 | tf_op jit(solution)/shard_map/attention_back/pallas_call | solution.py:48
  145.0 4.8 %attention_weight_grads.1 = (bf16[1152,1152]{1,0:T(8,128)(2,1)S(1)}, bf16[8,2,96,384]{3,2,1,0:T(8,128)(2,1)S(1)}, bf16[8,2,96,384]{3,2,1,0:T(8,128)(2,1)S(1)}) custom-call(s32[8]{0:T(128)S(1)} %compare_select_fusion.2.slots, bf16[1152,768]{1,0:T(8,128)(2,1)S(1)} %get-tuple-element.148.first, bf16[1024,768]{1,0:T(8,128)(2,1)S(1)} %get-tuple-element.149.low_mid, ...), custom_call_target="tpu_custom_call" | custom-call | flops 3623878656 | bytes 11796480 | tf_op jit(solution)/shard_map/attention_weight_grads/pallas_call | solution.py:48
  154.0 2.9 %first_grad.1.own = bf16[1152,768]{1,0:T(8,128)(2,1)S(1)} custom-call(bf16[1152,1152]{1,0:T(8,128)(2,1)S(1)} %get-tuple-element.182.grad_proj, bf16[768,1536]{1,0:T(8,128)(2,1)S(1)} %get-tuple-element.130.rest_0_.wide), custom_call_target="tpu_custom_call" | custom-call | flops 1811939328 | bytes 6782976 | tf_op jit(solution)/shard_map/first_grad/pallas_call | solution.py:48
  161.4 2.4 %collective-permute-done.40 = bf16[2,96,384]{2,1,0:T(8,128)(2,1)S(1)} collective-permute-done((bf16[2,96,384]{2,1,0:T(8,128)(2,1)S(1)}, bf16[2,96,384]{2,1,0:T(8,128)(2,1)S(1)}, u32[]{:S(2)}, u32[]{:S(2)}) %collective-permute-start.40) | collective-permute-done | bytes 147488 | tf_op jit(solution)/shard_map/ppermute | solution.py:563
  165.9 8.5 %collective-permute-done.31 = bf16[2,96,384]{2,1,0:T(8,128)(2,1)S(1)} collective-permute-done((bf16[2,96,384]{2,1,0:T(8,128)(2,1)S(1)}, bf16[2,96,384]{2,1,0:T(8,128)(2,1)S(1)}, u32[]{:S(2)}, u32[]{:S(2)}) %collective-permute-start.31) | collective-permute-done | bytes 147488 | tf_op jit(solution)/shard_map/ppermute | solution.py:563
  180.7 2.7 %collective-permute-done.33 = bf16[2,96,384]{2,1,0:T(8,128)(2,1)S(1)} collective-permute-done((bf16[2,96,384]{2,1,0:T(8,128)(2,1)S(1)}, bf16[2,96,384]{2,1,0:T(8,128)(2,1)S(1)}, u32[]{:S(2)}, u32[]{:S(2)}) %collective-permute-start.33) | collective-permute-done | bytes 147488 | tf_op jit(solution)/shard_map/ppermute | solution.py:563
  189.7 2.4 %collective-permute-done.26 = bf16[64,768]{1,0:T(8,128)(2,1)S(1)} collective-permute-done((bf16[64,768]{1,0:T(8,128)(2,1)S(1)}, bf16[64,768]{1,0:T(8,128)(2,1)S(1)}, u32[]{:S(2)}, u32[]{:S(2)}) %collective-permute-start.26) | collective-permute-done | bytes 98336 | tf_op jit(solution)/shard_map/ppermute | solution.py:472
  196.4 6.1 %token_grad.1 = (bf16[1024,768]{1,0:T(8,128)(2,1)}, f32[1024,768]{1,0:T(8,128)}) custom-call(bf16[1024,768]{1,0:T(8,128)(2,1)S(1)} %copy-done, f32[16,768]{1,0:T(8,128)S(1)} %get-tuple-element.120.gain, f32[1024,768]{1,0:T(8,128)S(1)} %get-tuple-element.147.grad_middle, bf16[1152,768]{1,0:T(8,128)(2,1)S(1)} %first_grad.1.own, ...), custom_call_target="tpu_custom_call" | custom-call | flops 1572864000 | bytes 19513344 | tf_op jit(solution)/shard_map/token_grad/pallas_call | solution.py:48
  204.7 3.0 %collective-permute-done.36 = bf16[2,96,384]{2,1,0:T(8,128)(2,1)S(1)} collective-permute-done((bf16[2,96,384]{2,1,0:T(8,128)(2,1)S(1)}, bf16[2,96,384]{2,1,0:T(8,128)(2,1)S(1)}, u32[]{:S(2)}, u32[]{:S(2)}) %collective-permute-start.36) | collective-permute-done | bytes 147488 | tf_op jit(solution)/shard_map/ppermute | solution.py:486
  (151 shorter events, 78.5 us)
Async XLA Ops:
  2.4 10.3 %collective-permute-start.2 = (bf16[400,384]{1,0:T(8,128)(2,1)S(1)}, bf16[400,384]{1,0:T(8,128)(2,1)S(1)}, u32[]{:S(2)}, u32[]{:S(2)}) collective-permute-start(bf16[400,384]{1,0:T(8,128)(2,1)S(1)} %pad_maximum_fusion.2.rest_0_), channel_id=1, source_target_pairs={{8,0},{16,8},{24,16},{28,24},{20,28},{12,20},{4,12},{0,4},{9,1},{1... | collective-permute-start | bytes 921608 | tf_op jit(solution)/shard_map/ppermute | solution.py:525
  6.6 27.2 %collective-permute-start = (bf16[64,768]{1,0:T(8,128)(2,1)S(1)}, bf16[64,768]{1,0:T(8,128)(2,1)S(1)}, u32[]{:S(2)}, u32[]{:S(2)}) collective-permute-start(bf16[64,768]{1,0:T(8,128)(2,1)S(1)} %slice_select_fusion), channel_id=1, source_target_pairs={{0,2},{2,0},{1,3},{3,1},{4,6},{6,4},{5,7},{7,5},{8,10},{10,8},{9,1... | collective-permute-start | bytes 294920 | tf_op jit(solution)/shard_map/ppermute | solution.py:472
  40.5 10.4 %collective-permute-start.10 = (bf16[288,576]{1,0:T(8,128)(2,1)S(1)}, bf16[288,576]{1,0:T(8,128)(2,1)S(1)}, u32[]{:S(2)}, u32[]{:S(2)}) collective-permute-start(bf16[288,576]{1,0:T(8,128)(2,1)S(1)} %pad_maximum_fusion.1.rest_0_), channel_id=1, source_target_pairs={{8,0},{16,8},{24,16},{28,24},{20,28},{12,20},{4,12},{0,4},{9,1},{1... | collective-permute-start | bytes 995336 | tf_op jit(solution)/shard_map/ppermute | solution.py:525
  41.1 11.2 %collective-permute-start.9 = (bf16[288,576]{1,0:T(8,128)(2,1)S(1)}, bf16[288,576]{1,0:T(8,128)(2,1)S(1)}, u32[]{:S(2)}, u32[]{:S(2)}) collective-permute-start(bf16[288,576]{1,0:T(8,128)(2,1)S(1)} %pad_maximum_fusion.1.rest_0_), channel_id=1, source_target_pairs={{0,8},{8,16},{16,24},{24,28},{28,20},{20,12},{12,4},{4,0},{1,9},{9... | collective-permute-start | bytes 995336 | tf_op jit(solution)/shard_map/ppermute | solution.py:525
  52.4 12.2 %collective-permute-start.11 = (bf16[288,576]{1,0:T(8,128)(2,1)S(1)}, bf16[288,576]{1,0:T(8,128)(2,1)S(1)}, u32[]{:S(2)}, u32[]{:S(2)}) collective-permute-start(bf16[288,576]{1,0:T(8,128)(2,1)S(1)} %collective-permute-done.9.rest_8_), channel_id=1, source_target_pairs={{0,8},{8,16},{16,24},{24,28},{28,20},{20,12},{12,4},{4,0},{1,9},{9... | collective-permute-start | bytes 995336 | tf_op jit(solution)/shard_map/ppermute | solution.py:525
  53.3 11.3 %collective-permute-start.12 = (bf16[288,576]{1,0:T(8,128)(2,1)S(1)}, bf16[288,576]{1,0:T(8,128)(2,1)S(1)}, u32[]{:S(2)}, u32[]{:S(2)}) collective-permute-start(bf16[288,576]{1,0:T(8,128)(2,1)S(1)} %collective-permute-done.10.rest_1_), channel_id=1, source_target_pairs={{8,0},{16,8},{24,16},{28,24},{20,28},{12,20},{4,12},{0,4},{9,1},{1... | collective-permute-start | bytes 995336 | tf_op jit(solution)/shard_map/ppermute | solution.py:525
  72.9 19.0 %collective-permute-start.13 = (bf16[1024,768]{1,0:T(8,128)(2,1)S(1)}, bf16[1024,768]{1,0:T(8,128)(2,1)S(1)}, u32[]{:S(2)}, u32[]{:S(2)}) collective-permute-start(bf16[1024,768]{1,0:T(8,128)(2,1)S(1)} %get-tuple-element.136.own), channel_id=1, source_target_pairs={{0,1},{1,0},{2,3},{3,2},{4,5},{5,4},{6,7},{7,6},{8,9},{9,8},{10,11... | collective-permute-start | bytes 4718600 | tf_op jit(solution)/shard_map/ppermute | solution.py:486
  73.0 11.0 %collective-permute-start.14 = (bf16[288,576]{1,0:T(8,128)(2,1)S(1)}, bf16[288,576]{1,0:T(8,128)(2,1)S(1)}, u32[]{:S(2)}, u32[]{:S(2)}) collective-permute-start(bf16[288,576]{1,0:T(8,128)(2,1)S(1)} %collective-permute-done.11.rest_7_), channel_id=1, source_target_pairs={{0,8},{8,16},{16,24},{24,28},{28,20},{20,12},{12,4},{4,0},{1,9},{9... | collective-permute-start | bytes 995336 | tf_op jit(solution)/shard_map/ppermute | solution.py:525
  73.9 10.7 %collective-permute-start.15 = (bf16[288,576]{1,0:T(8,128)(2,1)S(1)}, bf16[288,576]{1,0:T(8,128)(2,1)S(1)}, u32[]{:S(2)}, u32[]{:S(2)}) collective-permute-start(bf16[288,576]{1,0:T(8,128)(2,1)S(1)} %collective-permute-done.12.rest_2_), channel_id=1, source_target_pairs={{8,0},{16,8},{24,16},{28,24},{20,28},{12,20},{4,12},{0,4},{9,1},{1... | collective-permute-start | bytes 995336 | tf_op jit(solution)/shard_map/ppermute | solution.py:525
  107.0 12.8 %collective-permute-start.18 = (bf16[1024,768]{1,0:T(8,128)(2,1)S(1)}, bf16[1024,768]{1,0:T(8,128)(2,1)S(1)}, u32[]{:S(2)}, u32[]{:S(2)}) collective-permute-start(bf16[1024,768]{1,0:T(8,128)(2,1)S(1)} %get-tuple-element.146.own), channel_id=1, source_target_pairs={{0,1},{1,0},{2,3},{3,2},{4,5},{5,4},{6,7},{7,6},{8,9},{9,8},{10,11... | collective-permute-start | bytes 4718600 | tf_op jit(solution)/shard_map/ppermute | solution.py:486
  123.5 11.3 %collective-permute-start.22 = (bf16[3,96,576]{2,1,0:T(8,128)(2,1)S(1)}, bf16[3,96,576]{2,1,0:T(8,128)(2,1)S(1)}, u32[]{:S(2)}, u32[]{:S(2)}) collective-permute-start(bf16[3,96,576]{2,1,0:T(8,128)(2,1)S(1)} %get-tuple-element.223), channel_id=1, source_target_pairs={{8,0},{16,8},{24,16},{28,24},{20,28},{12,20},{4,12},{0,4},{9,1},{1... | collective-permute-start | bytes 995336 | tf_op jit(solution)/shard_map/ppermute | solution.py:563
  123.9 10.9 %collective-permute-start.21 = (bf16[3,96,576]{2,1,0:T(8,128)(2,1)S(1)}, bf16[3,96,576]{2,1,0:T(8,128)(2,1)S(1)}, u32[]{:S(2)}, u32[]{:S(2)}) collective-permute-start(bf16[3,96,576]{2,1,0:T(8,128)(2,1)S(1)} %get-tuple-element.224), channel_id=1, source_target_pairs={{0,8},{8,16},{16,24},{24,28},{28,20},{20,12},{12,4},{4,0},{1,9},{9... | collective-permute-start | bytes 995336 | tf_op jit(solution)/shard_map/ppermute | solution.py:563
  134.9 10.1 %collective-permute-start.24 = (bf16[3,96,576]{2,1,0:T(8,128)(2,1)S(1)}, bf16[3,96,576]{2,1,0:T(8,128)(2,1)S(1)}, u32[]{:S(2)}, u32[]{:S(2)}) collective-permute-start(bf16[3,96,576]{2,1,0:T(8,128)(2,1)S(1)} %get-tuple-element.221), channel_id=1, source_target_pairs={{8,0},{16,8},{24,16},{28,24},{20,28},{12,20},{4,12},{0,4},{9,1},{1... | collective-permute-start | bytes 995336 | tf_op jit(solution)/shard_map/ppermute | solution.py:563
  135.3 9.6 %collective-permute-start.23 = (bf16[3,96,576]{2,1,0:T(8,128)(2,1)S(1)}, bf16[3,96,576]{2,1,0:T(8,128)(2,1)S(1)}, u32[]{:S(2)}, u32[]{:S(2)}) collective-permute-start(bf16[3,96,576]{2,1,0:T(8,128)(2,1)S(1)} %get-tuple-element.222), channel_id=1, source_target_pairs={{0,8},{8,16},{16,24},{24,28},{28,20},{20,12},{12,4},{4,0},{1,9},{9... | collective-permute-start | bytes 995336 | tf_op jit(solution)/shard_map/ppermute | solution.py:563
  156.9 30.4 %collective-permute-start.25 = (bf16[1152,768]{1,0:T(8,128)(2,1)S(1)}, bf16[1152,768]{1,0:T(8,128)(2,1)S(1)}, u32[]{:S(2)}, u32[]{:S(2)}) collective-permute-start(bf16[1152,768]{1,0:T(8,128)(2,1)S(1)} %first_grad.1.own), channel_id=1, source_target_pairs={{0,1},{1,0},{2,3},{3,2},{4,5},{5,4},{6,7},{7,6},{8,9},{9,8},{10,11... | collective-permute-start | bytes 5308424 | tf_op jit(solution)/shard_map/ppermute | solution.py:486
  159.3 17.2 %collective-permute-start.47 = (bf16[3,96,576]{2,1,0:T(8,128)(2,1)S(1)}, bf16[3,96,576]{2,1,0:T(8,128)(2,1)S(1)}, u32[]{:S(2)}, u32[]{:S(2)}) collective-permute-start(bf16[3,96,576]{2,1,0:T(8,128)(2,1)S(1)} %get-tuple-element.219), channel_id=1, source_target_pairs={{8,0},{16,8},{24,16},{28,24},{20,28},{12,20},{4,12},{0,4},{9,1},{1... | collective-permute-start | bytes 995336 | tf_op jit(solution)/shard_map/ppermute | solution.py:563
  159.7 16.7 %collective-permute-start.46 = (bf16[3,96,576]{2,1,0:T(8,128)(2,1)S(1)}, bf16[3,96,576]{2,1,0:T(8,128)(2,1)S(1)}, u32[]{:S(2)}, u32[]{:S(2)}) collective-permute-start(bf16[3,96,576]{2,1,0:T(8,128)(2,1)S(1)} %get-tuple-element.220), channel_id=1, source_target_pairs={{0,8},{8,16},{16,24},{24,28},{28,20},{20,12},{12,4},{4,0},{1,9},{9... | collective-permute-start | bytes 995336 | tf_op jit(solution)/shard_map/ppermute | solution.py:563
  163.8 10.6 %collective-permute-start.31 = (bf16[2,96,384]{2,1,0:T(8,128)(2,1)S(1)}, bf16[2,96,384]{2,1,0:T(8,128)(2,1)S(1)}, u32[]{:S(2)}, u32[]{:S(2)}) collective-permute-start(bf16[2,96,384]{2,1,0:T(8,128)(2,1)S(1)} %get-tuple-element.229), channel_id=1, source_target_pairs={{8,0},{16,8},{24,16},{28,24},{20,28},{12,20},{4,12},{0,4},{9,1},{1... | collective-permute-start | bytes 442376 | tf_op jit(solution)/shard_map/ppermute | solution.py:563
  164.2 10.6 %collective-permute-start.30 = (bf16[2,96,384]{2,1,0:T(8,128)(2,1)S(1)}, bf16[2,96,384]{2,1,0:T(8,128)(2,1)S(1)}, u32[]{:S(2)}, u32[]{:S(2)}) collective-permute-start(bf16[2,96,384]{2,1,0:T(8,128)(2,1)S(1)} %get-tuple-element.230), channel_id=1, source_target_pairs={{0,8},{8,16},{16,24},{24,28},{28,20},{20,12},{12,4},{4,0},{1,9},{9... | collective-permute-start | bytes 442376 | tf_op jit(solution)/shard_map/ppermute | solution.py:563
  176.6 9.7 %collective-permute-start.48 = (bf16[3,96,576]{2,1,0:T(8,128)(2,1)S(1)}, bf16[3,96,576]{2,1,0:T(8,128)(2,1)S(1)}, u32[]{:S(2)}, u32[]{:S(2)}) collective-permute-start(bf16[3,96,576]{2,1,0:T(8,128)(2,1)S(1)} %fusion.1), channel_id=1, source_target_pairs={{0,2},{2,0},{1,3},{3,1},{4,6},{6,4},{5,7},{7,5},{8,10},{10,8},{9,1... | collective-permute-start | bytes 995336 | tf_op jit(solution)/shard_map/ppermute | solution.py:486
  180.7 15.6 %collective-permute-start.27 = (bf16[1024,768]{1,0:T(8,128)(2,1)S(1)}, bf16[1024,768]{1,0:T(8,128)(2,1)S(1)}, u32[]{:S(2)}, u32[]{:S(2)}) collective-permute-start(bf16[1024,768]{1,0:T(8,128)(2,1)S(1)} %feed_out.1.feed_own), channel_id=1, source_target_pairs={{0,1},{1,0},{2,3},{3,2},{4,5},{5,4},{6,7},{7,6},{8,9},{9,8},{10,11... | collective-permute-start | bytes 4718600 | tf_op jit(solution)/shard_map/ppermute | solution.py:486
  192.2 10.3 %collective-permute-start.35 = (bf16[2,96,384]{2,1,0:T(8,128)(2,1)S(1)}, bf16[2,96,384]{2,1,0:T(8,128)(2,1)S(1)}, u32[]{:S(2)}, u32[]{:S(2)}) collective-permute-start(bf16[2,96,384]{2,1,0:T(8,128)(2,1)S(1)} %get-tuple-element.225), channel_id=1, source_target_pairs={{8,0},{16,8},{24,16},{28,24},{20,28},{12,20},{4,12},{0,4},{9,1},{1... | collective-permute-start | bytes 442376 | tf_op jit(solution)/shard_map/ppermute | solution.py:563
  192.6 9.8 %collective-permute-start.34 = (bf16[2,96,384]{2,1,0:T(8,128)(2,1)S(1)}, bf16[2,96,384]{2,1,0:T(8,128)(2,1)S(1)}, u32[]{:S(2)}, u32[]{:S(2)}) collective-permute-start(bf16[2,96,384]{2,1,0:T(8,128)(2,1)S(1)} %get-tuple-element.226), channel_id=1, source_target_pairs={{0,8},{8,16},{16,24},{24,28},{28,20},{20,12},{12,4},{4,0},{1,9},{9... | collective-permute-start | bytes 442376 | tf_op jit(solution)/shard_map/ppermute | solution.py:563
  194.3 9.8 %collective-permute-start.44 = (bf16[2,96,384]{2,1,0:T(8,128)(2,1)S(1)}, bf16[2,96,384]{2,1,0:T(8,128)(2,1)S(1)}, u32[]{:S(2)}, u32[]{:S(2)}) collective-permute-start(bf16[2,96,384]{2,1,0:T(8,128)(2,1)S(1)} %get-tuple-element.231), channel_id=1, source_target_pairs={{8,0},{16,8},{24,16},{28,24},{20,28},{12,20},{4,12},{0,4},{9,1},{1... | collective-permute-start | bytes 442376 | tf_op jit(solution)/shard_map/ppermute | solution.py:563
  (33 other events, 291.7 us)

commit v7 on v5

--- a/solution.py
+++ b/solution.py
@@ -38,23 +38,22 @@
     return best
 
 
-def call(kernel, out_shape, args, flops, name, scalars=(), scratch=(), raw=()):
+def call(kernel, out_shape, args, flops, name, scalars=(), scratch=()):
     vmem = pl.BlockSpec(memory_space=pltpu.VMEM)
     smem = pl.BlockSpec(memory_space=pltpu.SMEM)
-    anywhere = pl.BlockSpec(memory_space=pl.ANY)
     moved = sum(x.size * x.dtype.itemsize for x in (*args, *out_shape))
     held = sum(math.prod(x.shape) * jnp.dtype(x.dtype).itemsize for x in scratch if x.dtype in (f32, bf16))
-    limit = min(56 * 2**20, moved // 3 + held + 4 * 2**20)
+    limit = min(56 * 2**20, moved // 2 + held + 4 * 2**20)
     return pl.pallas_call(
         kernel,
         out_shape=out_shape,
-        in_specs=[smem] * len(scalars) + [vmem] * len(args) + [anywhere] * len(raw),
+        in_specs=[smem] * len(scalars) + [vmem] * len(args),
         out_specs=[vmem] * len(out_shape),
         scratch_shapes=scratch,
         compiler_params=pltpu.CompilerParams(vmem_limit_bytes=limit),
         cost_estimate=pl.CostEstimate(flops=flops, bytes_accessed=moved, transcendentals=0),
         name=name,
-    )(*scalars, *args, *raw)
+    )(*scalars, *args)
 
 
 def shape(dims, dtype):
@@ -94,16 +93,6 @@
         return carry
 
     lax.fori_loop(0, count, run, 0)
-
-
-def fetch(copies, sems):
-    started = []
-    for number, (source, target) in enumerate(copies):
-        copy = pltpu.make_async_copy(source, target, sems.at[number])
-        copy.start()
-        started.append(copy)
-    for copy in started:
-        copy.wait()
 
 
 def norm_kernel(tokens, before, after, hat):
@@ -137,28 +126,24 @@
 
 
 def project_kernel(slots, hat, cosine, sine, *rest):
-    pieces, (wide, gain, first, query, key, value, gain_held, sems) = rest[:-8], rest[-8:]
+    pieces, (wide, gain, first, query, key, value) = rest[:-6], rest[-6:]
     extent, local = key.shape
     rows = query.shape[0]
     width = hat.shape[1]
     pairs = local // LANES
-    groups = gain_held.shape[0]
+    groups = slots.shape[0]
     depth = width // groups
     plan = piece_plan(groups, [depth] * 4 + [PAD], 2)
-    copies = []
+    lane = lax.broadcasted_iota(jnp.int32, (LANES, width), 1) - lax.broadcasted_iota(jnp.int32, (LANES, width), 0)
+    gain_sum = jnp.zeros((PAD, width), f32)
     for number, sources in enumerate(plan):
-        place = pl.ds(pl.multiple_of(slots[number] * depth, depth), depth)
+        start = pl.multiple_of(slots[number] * depth, depth)
         for part, (piece, row) in enumerate(sources[:4]):
             lanes = slice(part * local, (part + 1) * local)
-            copies.append((pieces[piece].at[row : row + depth, :], wide.at[place, lanes]))
+            wide[pl.ds(start, depth), lanes] = pieces[piece][row : row + depth, :]
         piece, row = sources[4]
-        copies.append((pieces[piece].at[row : row + PAD, :], gain_held.at[number]))
-    fetch(copies, sems)
-    lane = lax.broadcasted_iota(jnp.int32, (LANES, width), 1) - lax.broadcasted_iota(jnp.int32, (LANES, width), 0)
-    gain_sum = jnp.zeros((PAD, width), f32)
-    for number in range(groups):
-        spread = jnp.where(lane == slots[number] * depth, 1.0, 0.0).astype(bf16)
-        gain_sum += dot(gain_held[number][:, :LANES], spread)
+        spread = jnp.where(lane == start, 1.0, 0.0).astype(bf16)
+        gain_sum += dot(pieces[piece][row : row + PAD, :LANES], spread)
     gain[...] = gain_sum
     gains = gain_sum[:1]
     query_w, key_w, value_w = (wide.at[:, at * local : (at + 1) * local] for at in range(3))
@@ -232,21 +217,15 @@
     loop(rows // size, out_step)
 
 
-def feed_kernel(slots, parts_at, tokens, own, other, gain, cotangent, *rest):
-    pieces, rest = rest[:-8], rest[-8:]
-    middle, second, hidden, grad_gate, grad_upper, partial, whole, sems = rest
+def feed_kernel(plan, slots, parts_at, tokens, own, other, gain, cotangent, *rest):
+    pieces, rest = rest[:-7], rest[-7:]
+    middle, second, hidden, grad_gate, grad_upper, partial, whole = rest
     rows, width = tokens.shape
-    groups = slots.shape[0]
-    depth = width // groups
-    sides = len(pieces) // groups
-    size = depth // sides
-    copies = []
-    for number in range(groups):
-        for side in range(sides):
-            start = slots[number] * depth + parts_at[side] * size
-            place = pl.ds(pl.multiple_of(start, size), size)
-            copies.append((pieces[number * sides + side], whole.at[:, place, :]))
-    fetch(copies, sems)
+    depth = width // slots.shape[0]
+    size = depth // (1 + max(side for _, side, _, _, _ in plan))
+    for slot, side, part, piece, at in plan:
+        start = slots[slot] * depth + parts_at[side] * size
+        whole[part, pl.ds(pl.multiple_of(start, size), size), :] = pieces[piece][at]
     gate_w, upper_w, down_t = (whole.at[number] for number in range(3))
     gains = gain[1:2, :]
     size = step_of(rows, 256)
@@ -561,17 +540,14 @@
         parts_at = jnp.stack([spot, 1 - spot]).astype(jnp.int32)
     else:
         parts_at = jnp.zeros((1,), jnp.int32)
+    now.hop()
+    cosine, sine, bounds = tables(lengths, rows)
     later = RingGather(tied([mine_two], now.state)[0], 1)
-    now.hop()
-    later.hop()
-    cosine, sine, bounds = tables(lengths, rows)
-    later.after(now.state)
     while now.hops < middle_hop:
+        if now.hops > 2:
+            later.after(now.state)
+        later.hop()
         now.hop()
-        later.hop()
-        later.after(now.state)
-    while later.hops < middle_hop:
-        later.hop()
     hat, = call(
         norm_kernel, [shape((extent, width), f32)], (tokens, before, after), rows * width * 2000, "first_norm"
     )
@@ -586,30 +562,26 @@
             shape((extent, local), bf16),
             shape((extent, local), bf16),
         ],
-        (hat, cosine, sine),
+        (hat, cosine, sine, *pieces),
         2 * rows * width * local * 8,
         "project",
         (slots,),
-        [pltpu.VMEM((groups, PAD, local), bf16), pltpu.SemaphoreType.DMA((5 * groups,))],
-        pieces,
-    )
-    held = {slot: later.pieces[slot][0] for slot in range(groups) if slot != middle_hop}
-    held[middle_hop] = jnp.concatenate(later.pieces[middle_hop])
+    )
+    later.after(now.state)
+    batches, others = [], []
+
+    def trade(slots_now):
+        batches.append(slots_now)
+        others.append(swap(jnp.stack([later.pieces[slot][0] for slot in slots_now]), "ctx"))
+
     if split:
-        early = [slot for hop in range(1, middle_hop // 2 + 1) for slot in (hop, groups - hop)]
-        late = [slot for slot in range(1, groups) if slot not in early]
-        others = {0: other_two}
-        for batch in (early, late):
-            got = swap(jnp.stack([held[slot] for slot in batch]), "ctx")
-            if batch is early:
-                query, key, value = tied([query, key, value], [got])
-            for number, slot in enumerate(batch):
-                others[slot] = got[number]
-        query, key, value = tied([query, key, value], later.state)
-        pieces = [piece for slot in range(groups) for piece in (held[slot], others[slot])]
-    else:
-        got = held[middle_hop]
-        pieces = [held[slot] for slot in range(groups)]
+        trade([groups - 1, 1])
+    later.hop()
+    query, key, value = tied([query, key, value], [*later.state, *others])
+    if split:
+        trade([slot for slot in later.pieces if slot not in (0, 1, groups - 1)])
+    while later.hops < middle_hop:
+        later.hop()
     shares, attended, branch = call(
         attend_kernel,
         [
@@ -622,10 +594,27 @@
         "attend",
         (bounds,),
     )
-    branch, = tied([branch], [got])
+    branch, *later.state = tied([branch, *later.state], others)
     branch_other = swap(branch)
+    plan, pieces = [], []
+    for slot in range(groups):
+        part = 0
+        for piece in later.pieces[slot]:
+            for at in range(piece.shape[0]):
+                plan.append((slot, 0, part, len(pieces), at))
+                part += 1
+            pieces.append(piece)
+    if split:
+        batches.append([middle_hop])
+        others.append(swap(jnp.concatenate(later.state), "ctx")[None])
+        batches.append([0])
+        others.append(other_two[None])
+        for batch, other in zip(batches, others):
+            for number, slot in enumerate(batch):
+                plan += [(slot, 1, part, len(pieces), (number, part)) for part in range(3)]
+            pieces.append(other)
     middle, second, hidden, grad_gate, grad_upper, partial, whole = call(
-        feed_kernel,
+        functools.partial(feed_kernel, tuple(plan)),
         [
             shape((rows, width), f32),
             shape((rows, width), bf16),
@@ -635,12 +624,10 @@
             shape((rows, width), bf16),
             shape((3, width, units), bf16),
         ],
-        (tokens, branch, branch_other, gain, cotangent),
+        (tokens, branch, branch_other, gain, cotangent, *pieces),
         2 * rows * width * units * 8,
         "feed_forward_and_back",
         (slots, parts_at),
-        [pltpu.SemaphoreType.DMA((len(pieces),))],
-        pieces,
     )
     partial_other = swap(partial)
     ways = 2 if split else 1
@@ -655,14 +642,7 @@
     )
     if split:
         grads_two = [grads_two[0], swap(grads_two[1], "ctx")]
-    feed, = call(
-        feed_out_kernel,
-        [shape((rows, width), bf16)],
-        (hidden, whole),
-        2 * rows * width * units,
-        "feed_out",
-    )
-    feed_other = swap(feed)
+    middle, = tied([middle], grads_two[:1])
     grad_middle, low_mid, grad_att = call(
         middle_kernel,
         [shape((rows, width), f32), shape((rows, width), bf16), shape((rows, local), bf16)],
@@ -692,10 +672,18 @@
     sums_one.hop()
     sums_two = RingScatter(tied(grads_two, sums_one.state), 1)
     sums_two.hop()
+    feed, = call(
+        feed_out_kernel,
+        [shape((rows, width), bf16)],
+        (tied([hidden], [grads_one])[0], whole),
+        2 * rows * width * units,
+        "feed_out",
+    )
+    feed_other = swap(feed)
     first_part, = call(
         first_kernel,
         [shape((extent, width), bf16)],
-        (tied([grad_proj], [grads_one])[0], wide),
+        (tied([grad_proj], sums_one.state)[0], wide),
         2 * rows * width * local * 3,
         "first_grad",
     )
@@ -705,8 +693,7 @@
         here = slice(at, at + HALF)
         return (first_part[here].astype(f32) + first_other[here].astype(f32)).astype(bf16)
 
-    sums_one.after([first_part, feed])
-    while sums_one.hops < middle_hop - 1:
+    while sums_one.hops < middle_hop - 2:
         sums_one.hop()
         sums_two.after(sums_one.state)
         sums_two.hop()
@@ -714,6 +701,9 @@
     sums_one.after([from_before, from_after])
     sums_one.hop()
     sums_two.after(sums_one.state)
+    sums_two.hop()
+    tokens, = tied([tokens], sums_one.state)
+    sums_one.hop()
     sums_two.hop()
     mixed, token_grad = call(
         final_kernel,

time: 201 us -> 234 us (1.16)
  waiting for transfers between devices: 53.7 us -> 81.6 us
  local copies, waits for them, and re-layouts: 15.7 us -> 24.8 us
    ppermute x10 -> x11, waiting for transfers between devices: 9.58 us -> 39.3 us  [swap(): return lax.ppermute(array, axis, [(0, 1), (1, 0)])]
    unnamed x85 -> x102, local copies, waits for them, and re-layouts: 11.8 us -> 23.5 us
    ppermute x16, waiting for transfers between devices: 20.9 us -> 11.8 us  [hop(): lax.ppermute(one, 'dp', self.ahead)]
    ppermute x16, waiting for transfers between devices: 22.2 us -> 30.5 us  [hop(): lax.ppermute(two, 'dp', self.back)]
    ppermute x16, starting transfers between devices: 22.8 us -> 26.3 us  [hop(): lax.ppermute(two, 'dp', self.back)]
    ppermute x16, starting transfers between devices: 11.3 us -> 7.99 us  [hop(): lax.ppermute(one, 'dp', self.ahead)]
    squeeze x2 -> x0, local copies, waits for them, and re-layouts: 2.55 us -> none  [body(): others[slot] = got[number]]
    ppermute x10 -> x11, starting transfers between devices: 5.2 us -> 6.56 us  [swap(): return lax.ppermute(array, axis, [(0, 1), (1, 0)])]
  transfers between devices with their start and end apart: 44 -> 45, of which waited for: 24 -> 21; matrix products, arithmetic and copies ran while one was open for 8% -> 4% of each run, Pallas kernels for 29% -> 16%
where the time goes in v7:
time: 234 us
  waiting for transfers between devices  81.6 us (35%)
  Pallas kernels  70.1 us (30%)
  starting transfers between devices  43.4 us (19%)
  local copies, waits for them, and re-layouts  24.8 us (11%)
  other arithmetic  12.5 us (5%)
    pallas_call x11, Pallas kernels, call(): pl.pallas_call(kernel, out_shape=out_shape, in_specs=[smem] * len(scalars...  70.1 us
    ppermute x11, waiting for transfers between devices, swap(): return lax.ppermute(array, axis, [(0, 1), (1, 0)])  39.3 us
    ppermute x16, waiting for transfers between devices, hop(): lax.ppermute(two, 'dp', self.back)  30.5 us
    ppermute x16, starting transfers between devices, hop(): lax.ppermute(two, 'dp', self.back)  26.3 us
    unnamed x102, local copies, waits for them, and re-layouts  23.5 us
    ppermute x16, waiting for transfers between devices, hop(): lax.ppermute(one, 'dp', self.ahead)  11.8 us
    ppermute x16, starting transfers between devices, hop(): lax.ppermute(one, 'dp', self.ahead)  7.99 us
    ppermute x11, starting transfers between devices, swap(): return lax.ppermute(array, axis, [(0, 1), (1, 0)])  6.56 us
  transfers between devices with their start and end apart: 45, of which 21 were waited for; matrix products, arithmetic and copies ran while one was open for 4% of the time, Pallas kernels for 16%

profile of v7, /device:TPU:0, one launch (start us, length us, event | category | flops | bytes accessed | tf_op | source)
XLA Modules:
  0.0 233.8 jit_solution(15194456874233046723)
XLA Ops:
  2.4 3.0 %collective-permute-start.2 = (bf16[400,384]{1,0:T(8,128)(2,1)S(1)}, bf16[400,384]{1,0:T(8,128)(2,1)}, u32[]{:S(2)}, u32[]{:S(2)}) collective-permute-start(bf16[400,384]{1,0:T(8,128)(2,1)S(1)} %pad_maximum_fusion.2.rest_0_), channel_id=1, source_target_pairs={{8,0},{16,8},{24,16},{28,24},{20,28},{12,20},{4,12},{0,4},{9,1},{1... | collective-permute-start | bytes 921608 | tf_op jit(solution)/shard_map/ppermute | solution.py:453
  10.8 2.1 collective-permute-done.2.rest_1_
  16.3 2.1 negate_select_fusion
  19.2 3.2 %collective-permute-done.4.rest_2_ = bf16[400,384]{1,0:T(8,128)(2,1)} collective-permute-done((bf16[400,384]{1,0:T(8,128)(2,1)}, bf16[400,384]{1,0:T(8,128)(2,1)}, u32[]{:S(2)}, u32[]{:S(2)}) %collective-permute-start.4) | collective-permute-done | bytes 307232 | tf_op jit(solution)/shard_map/ppermute | solution.py:453
  27.8 6.6 %collective-permute-done.10.rest_1_ = bf16[3,48,576]{2,1,0:T(8,128)(2,1)S(1)} collective-permute-done((bf16[3,48,576]{2,1,0:T(8,128)(2,1)S(1)}, bf16[3,48,576]{2,1,0:T(8,128)(2,1)S(1)}, u32[]{:S(2)}, u32[]{:S(2)}) %collective-permute-start.10) | collective-permute-done | bytes 165920 | tf_op jit(solution)/shard_map/ppermute | solution.py:453
  34.5 2.3 collective-permute-done.9.rest_8_
  41.0 2.0 first_norm.1.hat
  48.6 6.5 %project.1 = (bf16[768,1536]{1,0:T(8,128)(2,1)S(1)}, f32[16,768]{1,0:T(8,128)S(1)}, bf16[1152,768]{1,0:T(8,128)(2,1)S(1)}, bf16[1024,384]{1,0:T(8,128)(2,1)S(1)}...) custom-call(s32[8]{0:T(128)S(1)} %compare_select_fusion.2.slots, f32[1152,768]{1,0:T(8,128)S(1)} %first_norm.1.hat, ...), custom_call_target="tpu_custom_call" | custom-call | flops 4831838208 | bytes 13910016 | tf_op jit(solution)/shard_map/project/pallas_call | solution.py:47
  61.1 13.1 %attend.1 = (bf16[24,256,256]{2,1,0:T(8,128)(2,1)S(1)}, bf16[1024,384]{1,0:T(8,128)(2,1)S(1)}, bf16[1024,768]{1,0:T(8,128)(2,1)}) custom-call(s32[5]{0:T(128)S(1)} %pad_add_fusion.bounds, bf16[1024,384]{1,0:T(8,128)(2,1)S(1)} %get-tuple-element.110.query, bf16[1152,384]{1,0:T(8,128)(2,1)S(1)} %get-tuple-element.111.key, ...), custom_call_target="tpu_custom_call" | custom-call | flops 9663676416 | bytes 10420224 | tf_op jit(solution)/shard_map/attend/pallas_call | solution.py:47
  82.3 6.8 %collective-permute-done.20 = bf16[3,48,576]{2,1,0:T(8,128)(2,1)} collective-permute-done((bf16[3,48,576]{2,1,0:T(8,128)(2,1)}, bf16[3,48,576]{2,1,0:T(8,128)(2,1)}, u32[]{:S(2)}, u32[]{:S(2)}) %collective-permute-start.20) | collective-permute-done | bytes 165920 | tf_op jit(solution)/shard_map/ppermute | solution.py:420
  103.9 11.9 %feed_forward_and_back.1 = (f32[1024,768]{1,0:T(8,128)S(1)}, bf16[1024,768]{1,0:T(8,128)(2,1)S(1)}, bf16[1024,576]{1,0:T(8,128)(2,1)S(1)}, bf16[1024,576]{1,0:T(...) custom-call(s32[8]{0:T(128)S(1)} %compare_select_fusion.2.slots, ...), custom_call_target="tpu_custom_call" | custom-call | flops 7247757312 | bytes 21479424 | tf_op jit(solution)/shard_map/feed_forward_and_back/pallas_call | solution.py:47
  115.9 4.7 %feed_weight_grads.1 = (bf16[8,3,48,576]{3,2,1,0:T(8,128)(2,1)S(1)}, bf16[8,3,48,576]{3,2,1,0:T(8,128)(2,1)S(1)}) custom-call(s32[8]{0:T(128)S(1)} %compare_select_fusion.2.slots, s32[2]{0:T(128)S(1)} %pad_add_fusion.1.parts_at, bf16[1024,768]{1,0:T(8,128)(2,1)S(1)} %get-tuple-element.123.second, bf16[1024,576]{1,0:T(8,128)(2,1)S(1)} %get-tuple-element.144.hidden, ...), custom_call_target="tpu_custom_call" | custom-call | flops 4529848320 | bytes 9338880 | tf_op jit(solution)/shard_map/feed_weight_grads/pallas_call | solution.py:47
  120.7 3.5 %middle_grad.1 = (f32[1024,768]{1,0:T(8,128)S(1)}, bf16[1024,768]{1,0:T(8,128)(2,1)S(1)}, bf16[1024,384]{1,0:T(8,128)(2,1)S(1)}) custom-call(f32[1024,768]{1,0:T(8,128)S(1)} %get-tuple-element.128.middle, bf16[1024,768]{1,0:T(8,128)(2,1)S(1)} %get-tuple-element.129.own, bf16[1024,768]{1,0:T(8,128)(2,1)S(1)} %collective-permute-done.21.other, ...), custom_call_target="tpu_custom_call" | custom-call | flops 2415919104 | bytes 15777792 | tf_op jit(solution)/shard_map/middle_grad/pallas_call | solution.py:47
  124.3 12.6 %attention_back.1.grad_proj = bf16[1152,1152]{1,0:T(8,128)(2,1)S(1)} custom-call(bf16[1024,384]{1,0:T(8,128)(2,1)S(1)} %copy-done.42, bf16[1152,384]{1,0:T(8,128)(2,1)S(1)} %copy-done.38, bf16[1152,384]{1,0:T(8,128)(2,1)S(1)} %copy-done.40, bf16[24,256,256]{2,1,0:T(8,128)(2,1)S(1)} %copy-done.44, bf16[1024,384]{1,0:T(8,128)(2,1)S(1)} %get-tuple-element.130.grad_att, ...), custom_call_target="tpu_custom_call" | custom-call | flops 9663676416 | bytes 10321920 | tf_op jit(solution)/shard_map/attention_back/pallas_call | solution.py:47
  137.0 4.7 %attention_weight_grads.1 = bf16[8,4,96,384]{3,2,1,0:T(8,128)(2,1)S(1)} custom-call(s32[8]{0:T(128)S(1)} %compare_select_fusion.2.slots, bf16[1152,768]{1,0:T(8,128)(2,1)S(1)} %copy-done.34, bf16[1152,1152]{1,0:T(8,128)(2,1)S(1)} %attention_back.1.grad_proj, bf16[1024,768]{1,0:T(8,128)(2,1)S(1)} %get-tuple-element.131.low_mid, bf16[1024,384]{1,0:T(8,128)(2,1)S(1)} %copy-done.36), custom_call_target="tpu_custom_call" | custom-call | flops 3623878656 | bytes 9142272 | tf_op jit(solution)/shard_map/attention_weight_grads/pallas_call | solution.py:47
  144.3 3.7 %collective-permute-done.23 = bf16[2,96,384]{2,1,0:T(8,128)(2,1)S(1)} collective-permute-done((bf16[2,96,384]{2,1,0:T(8,128)(2,1)S(1)}, bf16[2,96,384]{2,1,0:T(8,128)(2,1)S(1)}, u32[]{:S(2)}, u32[]{:S(2)}) %collective-permute-start.23) | collective-permute-done | bytes 147488 | tf_op jit(solution)/shard_map/ppermute | solution.py:491
  149.3 3.0 %first_grad.1.own = bf16[1152,768]{1,0:T(8,128)(2,1)S(1)} custom-call(bf16[1152,1152]{1,0:T(8,128)(2,1)S(1)} %attention_back.1.grad_proj, bf16[768,1536]{1,0:T(8,128)(2,1)S(1)} %get-tuple-element.113.wide), custom_call_target="tpu_custom_call" | custom-call | flops 1811939328 | bytes 6782976 | tf_op jit(solution)/shard_map/first_grad/pallas_call | solution.py:47
  152.4 25.6 %collective-permute-done.34 = bf16[8,3,48,576]{3,2,1,0:T(8,128)(2,1)S(1)} collective-permute-done((bf16[8,3,48,576]{3,2,1,0:T(8,128)(2,1)S(1)}, bf16[8,3,48,576]{3,2,1,0:T(8,128)(2,1)S(1)}, u32[]{:S(2)}, u32[]{:S(2)}) %collective-permute-start.34) | collective-permute-done | bytes 1327136 | tf_op jit(solution)/shard_map/ppermute | solution.py:420
  182.8 2.0 feed_out.1.feed_own
  184.9 3.1 %collective-permute-done.36 = bf16[3,24,576]{2,1,0:T(8,128)(2,1)S(1)} collective-permute-done((bf16[3,24,576]{2,1,0:T(8,128)(2,1)S(1)}, bf16[3,24,576]{2,1,0:T(8,128)(2,1)S(1)}, u32[]{:S(2)}, u32[]{:S(2)}) %collective-permute-start.36) | collective-permute-done | bytes 82976 | tf_op jit(solution)/shard_map/ppermute | solution.py:491
  193.7 7.8 %collective-permute-done.38 = bf16[3,48,576]{2,1,0:T(8,128)(2,1)S(1)} collective-permute-done((bf16[3,48,576]{2,1,0:T(8,128)(2,1)S(1)}, bf16[3,48,576]{2,1,0:T(8,128)(2,1)S(1)}, u32[]{:S(2)}, u32[]{:S(2)}) %collective-permute-start.38) | collective-permute-done | bytes 165920 | tf_op jit(solution)/shard_map/ppermute | solution.py:491
  207.2 3.3 %collective-permute-done.40 = bf16[3,48,576]{2,1,0:T(8,128)(2,1)S(1)} collective-permute-done((bf16[3,48,576]{2,1,0:T(8,128)(2,1)S(1)}, bf16[3,48,576]{2,1,0:T(8,128)(2,1)S(1)}, u32[]{:S(2)}, u32[]{:S(2)}) %collective-permute-start.40) | collective-permute-done | bytes 165920 | tf_op jit(solution)/shard_map/ppermute | solution.py:491
  214.3 6.1 %token_grad.1 = (bf16[1024,768]{1,0:T(8,128)(2,1)}, f32[1024,768]{1,0:T(8,128)}) custom-call(bf16[1024,768]{1,0:T(8,128)(2,1)S(1)} %copy-done.2, f32[16,768]{1,0:T(8,128)S(1)} %copy-done.13, f32[1024,768]{1,0:T(8,128)S(1)} %get-tuple-element.143.grad_middle, bf16[1152,768]{1,0:T(8,128)(2,1)S(1)} %first_grad.1.own, ...), custom_call_target="tpu_custom_call" | custom-call | flops 1572864000 | bytes 19513344 | tf_op jit(solution)/shard_map/token_grad/pallas_call | solution.py:47
  222.8 5.1 %collective-permute-done.43 = bf16[3,48,576]{2,1,0:T(8,128)(2,1)S(1)} collective-permute-done((bf16[3,48,576]{2,1,0:T(8,128)(2,1)S(1)}, bf16[3,48,576]{2,1,0:T(8,128)(2,1)S(1)}, u32[]{:S(2)}, u32[]{:S(2)}) %collective-permute-start.43) | collective-permute-done | bytes 165920 | tf_op jit(solution)/shard_map/ppermute | solution.py:420
  (226 shorter events, 87.7 us)
Async XLA Ops:
  2.4 10.5 %collective-permute-start.2 = (bf16[400,384]{1,0:T(8,128)(2,1)S(1)}, bf16[400,384]{1,0:T(8,128)(2,1)}, u32[]{:S(2)}, u32[]{:S(2)}) collective-permute-start(bf16[400,384]{1,0:T(8,128)(2,1)S(1)} %pad_maximum_fusion.2.rest_0_), channel_id=1, source_target_pairs={{8,0},{16,8},{24,16},{28,24},{20,28},{12,20},{4,12},{0,4},{9,1},{1... | collective-permute-start | bytes 921608 | tf_op jit(solution)/shard_map/ppermute | solution.py:453
  7.3 20.5 %collective-permute-start = (bf16[64,768]{1,0:T(8,128)(2,1)}, bf16[64,768]{1,0:T(8,128)(2,1)S(1)}, u32[]{:S(2)}, u32[]{:S(2)}) collective-permute-start(bf16[64,768]{1,0:T(8,128)(2,1)} %slice_select_fusion), channel_id=1, source_target_pairs={{0,2},{2,0},{1,3},{3,1},{4,6},{6,4},{5,7},{7,5},{8,10},{10,8},{9,1... | collective-permute-start | bytes 294920 | tf_op jit(solution)/shard_map/ppermute | solution.py:412
  23.7 13.1 %collective-permute-start.6 = (bf16[400,384]{1,0:T(8,128)(2,1)}, bf16[400,384]{1,0:T(8,128)(2,1)S(1)}, u32[]{:S(2)}, u32[]{:S(2)}) collective-permute-start(bf16[400,384]{1,0:T(8,128)(2,1)} %collective-permute-done.4.rest_2_), channel_id=1, source_target_pairs={{8,0},{16,8},{24,16},{28,24},{20,28},{12,20},{4,12},{0,4},{9,1},{1... | collective-permute-start | bytes 921608 | tf_op jit(solution)/shard_map/ppermute | solution.py:453
  25.2 11.5 %collective-permute-start.5 = (bf16[400,384]{1,0:T(8,128)(2,1)}, bf16[400,384]{1,0:T(8,128)(2,1)S(1)}, u32[]{:S(2)}, u32[]{:S(2)}) collective-permute-start(bf16[400,384]{1,0:T(8,128)(2,1)} %collective-permute-done.3.rest_7_), channel_id=1, source_target_pairs={{0,8},{8,16},{16,24},{24,28},{28,20},{20,12},{12,4},{4,0},{1,9},{9... | collective-permute-start | bytes 921608 | tf_op jit(solution)/shard_map/ppermute | solution.py:453
  27.4 9.4 %collective-permute-start.9 = (bf16[3,48,576]{2,1,0:T(8,128)(2,1)S(1)}, bf16[3,48,576]{2,1,0:T(8,128)(2,1)S(1)}, u32[]{:S(2)}, u32[]{:S(2)}) collective-permute-start(bf16[3,48,576]{2,1,0:T(8,128)(2,1)S(1)} %get-tuple-element.99.rest_0_), channel_id=1, source_target_pairs={{0,8},{8,16},{16,24},{24,28},{28,20},{20,12},{12,4},{4,0},{1,9},{9... | collective-permute-start | bytes 497672 | tf_op jit(solution)/shard_map/ppermute | solution.py:453
  43.1 18.0 %collective-permute-start.15 = (bf16[2,3,48,576]{3,2,1,0:T(8,128)(2,1)S(1)}, bf16[2,3,48,576]{3,2,1,0:T(8,128)(2,1)S(1)}, u32[]{:S(2)}, u32[]{:S(2)}) collective-permute-start(bf16[2,3,48,576]{3,2,1,0:T(8,128)(2,1)S(1)} %pad_maximum_fusion.1), channel_id=1, source_target_pairs={{0,2},{2,0},{1,3},{3,1},{4,6},{6,4},{5,7},{7,5},{8,10},{10,8},{9,1... | collective-permute-start | bytes 995336 | tf_op jit(solution)/shard_map/ppermute | solution.py:420
  46.6 10.4 %collective-permute-start.13 = (bf16[3,48,576]{2,1,0:T(8,128)(2,1)S(1)}, bf16[3,48,576]{2,1,0:T(8,128)(2,1)S(1)}, u32[]{:S(2)}, u32[]{:S(2)}) collective-permute-start(bf16[3,48,576]{2,1,0:T(8,128)(2,1)S(1)} %collective-permute-done.11.rest_7_), channel_id=1, source_target_pairs={{0,8},{8,16},{16,24},{24,28},{28,20},{20,12},{12,4},{4,0},{1,9},{9... | collective-permute-start | bytes 497672 | tf_op jit(solution)/shard_map/ppermute | solution.py:453
  47.1 9.9 %collective-permute-start.14 = (bf16[3,48,576]{2,1,0:T(8,128)(2,1)S(1)}, bf16[3,48,576]{2,1,0:T(8,128)(2,1)S(1)}, u32[]{:S(2)}, u32[]{:S(2)}) collective-permute-start(bf16[3,48,576]{2,1,0:T(8,128)(2,1)S(1)} %collective-permute-done.12.rest_2_), channel_id=1, source_target_pairs={{8,0},{16,8},{24,16},{28,24},{20,28},{12,20},{4,12},{0,4},{9,1},{1... | collective-permute-start | bytes 497672 | tf_op jit(solution)/shard_map/ppermute | solution.py:453
  57.0 22.5 %collective-permute-start.16 = (bf16[1,48,576]{2,1,0:T(8,128)(2,1)S(1)}, bf16[1,48,576]{2,1,0:T(8,128)(2,1)S(1)}, u32[]{:S(2)}, u32[]{:S(2)}) collective-permute-start(bf16[1,48,576]{2,1,0:T(8,128)(2,1)S(1)} %slice.136), channel_id=1, source_target_pairs={{0,8},{8,16},{16,24},{24,28},{28,20},{20,12},{12,4},{4,0},{1,9},{9... | collective-permute-start | bytes 165896 | tf_op jit(solution)/shard_map/ppermute | solution.py:453
  57.5 22.0 %collective-permute-start.17 = (bf16[2,48,576]{2,1,0:T(8,128)(2,1)S(1)}, bf16[2,48,576]{2,1,0:T(8,128)(2,1)S(1)}, u32[]{:S(2)}, u32[]{:S(2)}) collective-permute-start(bf16[2,48,576]{2,1,0:T(8,128)(2,1)S(1)} %slice.137), channel_id=1, source_target_pairs={{8,0},{16,8},{24,16},{28,24},{20,28},{12,20},{4,12},{0,4},{9,1},{1... | collective-permute-start | bytes 331784 | tf_op jit(solution)/shard_map/ppermute | solution.py:453
  59.5 20.0 %collective-permute-start.18 = (bf16[4,3,48,576]{3,2,1,0:T(8,128)(2,1)S(1)}, bf16[4,3,48,576]{3,2,1,0:T(8,128)(2,1)S(1)}, u32[]{:S(2)}, u32[]{:S(2)}) collective-permute-start(bf16[4,3,48,576]{3,2,1,0:T(8,128)(2,1)S(1)} %pad_maximum_fusion), channel_id=1, source_target_pairs={{0,2},{2,0},{1,3},{3,1},{4,6},{6,4},{5,7},{7,5},{8,10},{10,8},{9,1... | collective-permute-start | bytes 1990664 | tf_op jit(solution)/shard_map/ppermute | solution.py:420
  143.8 34.1 %collective-permute-start.34 = (bf16[8,3,48,576]{3,2,1,0:T(8,128)(2,1)S(1)}, bf16[8,3,48,576]{3,2,1,0:T(8,128)(2,1)S(1)}, u32[]{:S(2)}, u32[]{:S(2)}) collective-permute-start(bf16[8,3,48,576]{3,2,1,0:T(8,128)(2,1)S(1)} %get-tuple-element.151), channel_id=1, source_target_pairs={{0,2},{2,0},{1,3},{3,1},{4,6},{6,4},{5,7},{7,5},{8,10},{10,8},{9,1... | collective-permute-start | bytes 3981320 | tf_op jit(solution)/shard_map/ppermute | solution.py:420
  152.3 27.8 %collective-permute-start.26 = (bf16[1152,768]{1,0:T(8,128)(2,1)S(1)}, bf16[1152,768]{1,0:T(8,128)(2,1)S(1)}, u32[]{:S(2)}, u32[]{:S(2)}) collective-permute-start(bf16[1152,768]{1,0:T(8,128)(2,1)S(1)} %first_grad.1.own), channel_id=1, source_target_pairs={{0,1},{1,0},{2,3},{3,2},{4,5},{5,4},{6,7},{7,6},{8,9},{9,8},{10,11... | collective-permute-start | bytes 5308424 | tf_op jit(solution)/shard_map/ppermute | solution.py:420
  178.0 11.3 %collective-permute-start.25 = (bf16[4,96,384]{2,1,0:T(8,128)(2,1)S(1)}, bf16[4,96,384]{2,1,0:T(8,128)(2,1)S(1)}, u32[]{:S(2)}, u32[]{:S(2)}) collective-permute-start(bf16[4,96,384]{2,1,0:T(8,128)(2,1)S(1)} %get-tuple-element.180), channel_id=1, source_target_pairs={{8,0},{16,8},{24,16},{28,24},{20,28},{12,20},{4,12},{0,4},{9,1},{1... | collective-permute-start | bytes 884744 | tf_op jit(solution)/shard_map/ppermute | solution.py:491
  179.6 9.7 %collective-permute-start.24 = (bf16[4,96,384]{2,1,0:T(8,128)(2,1)S(1)}, bf16[4,96,384]{2,1,0:T(8,128)(2,1)S(1)}, u32[]{:S(2)}, u32[]{:S(2)}) collective-permute-start(bf16[4,96,384]{2,1,0:T(8,128)(2,1)S(1)} %get-tuple-element.181), channel_id=1, source_target_pairs={{0,8},{8,16},{16,24},{24,28},{28,20},{20,12},{12,4},{4,0},{1,9},{9... | collective-permute-start | bytes 884744 | tf_op jit(solution)/shard_map/ppermute | solution.py:491
  180.2 9.1 %collective-permute-start.27 = (bf16[64,768]{1,0:T(8,128)(2,1)S(1)}, bf16[64,768]{1,0:T(8,128)(2,1)S(1)}, u32[]{:S(2)}, u32[]{:S(2)}) collective-permute-start(bf16[64,768]{1,0:T(8,128)(2,1)S(1)} %fusion.11), channel_id=1, source_target_pairs={{0,2},{2,0},{1,3},{3,1},{4,6},{6,4},{5,7},{7,5},{8,10},{10,8},{9,1... | collective-permute-start | bytes 294920 | tf_op jit(solution)/shard_map/ppermute | solution.py:412
  188.0 26.3 %collective-permute-start.30 = (bf16[1024,768]{1,0:T(8,128)(2,1)S(1)}, bf16[1024,768]{1,0:T(8,128)(2,1)S(1)}, u32[]{:S(2)}, u32[]{:S(2)}) collective-permute-start(bf16[1024,768]{1,0:T(8,128)(2,1)S(1)} %feed_out.1.feed_own), channel_id=1, source_target_pairs={{0,1},{1,0},{2,3},{3,2},{4,5},{5,4},{6,7},{7,6},{8,9},{9,8},{10,11... | collective-permute-start | bytes 4718600 | tf_op jit(solution)/shard_map/ppermute | solution.py:420
  189.4 13.4 %collective-permute-start.29 = (bf16[4,96,384]{2,1,0:T(8,128)(2,1)S(1)}, bf16[4,96,384]{2,1,0:T(8,128)(2,1)S(1)}, u32[]{:S(2)}, u32[]{:S(2)}) collective-permute-start(bf16[4,96,384]{2,1,0:T(8,128)(2,1)S(1)} %get-tuple-element.178), channel_id=1, source_target_pairs={{8,0},{16,8},{24,16},{28,24},{20,28},{12,20},{4,12},{0,4},{9,1},{1... | collective-permute-start | bytes 884744 | tf_op jit(solution)/shard_map/ppermute | solution.py:491
  191.0 11.8 %collective-permute-start.28 = (bf16[4,96,384]{2,1,0:T(8,128)(2,1)S(1)}, bf16[4,96,384]{2,1,0:T(8,128)(2,1)S(1)}, u32[]{:S(2)}, u32[]{:S(2)}) collective-permute-start(bf16[4,96,384]{2,1,0:T(8,128)(2,1)S(1)} %get-tuple-element.179), channel_id=1, source_target_pairs={{0,8},{8,16},{16,24},{24,28},{28,20},{20,12},{12,4},{4,0},{1,9},{9... | collective-permute-start | bytes 884744 | tf_op jit(solution)/shard_map/ppermute | solution.py:491
  191.6 9.9 %collective-permute-start.38 = (bf16[3,48,576]{2,1,0:T(8,128)(2,1)S(1)}, bf16[3,48,576]{2,1,0:T(8,128)(2,1)S(1)}, u32[]{:S(2)}, u32[]{:S(2)}) collective-permute-start(bf16[3,48,576]{2,1,0:T(8,128)(2,1)S(1)} %get-tuple-element.174), channel_id=1, source_target_pairs={{8,0},{16,8},{24,16},{28,24},{20,28},{12,20},{4,12},{0,4},{9,1},{1... | collective-permute-start | bytes 497672 | tf_op jit(solution)/shard_map/ppermute | solution.py:491
  193.2 9.6 %collective-permute-start.37 = (bf16[3,48,576]{2,1,0:T(8,128)(2,1)S(1)}, bf16[3,48,576]{2,1,0:T(8,128)(2,1)S(1)}, u32[]{:S(2)}, u32[]{:S(2)}) collective-permute-start(bf16[3,48,576]{2,1,0:T(8,128)(2,1)S(1)} %get-tuple-element.175), channel_id=1, source_target_pairs={{0,8},{8,16},{16,24},{24,28},{28,20},{20,12},{12,4},{4,0},{1,9},{9... | collective-permute-start | bytes 497672 | tf_op jit(solution)/shard_map/ppermute | solution.py:491
  205.1 15.3 %collective-permute-start.32 = (bf16[4,96,384]{2,1,0:T(8,128)(2,1)S(1)}, bf16[4,96,384]{2,1,0:T(8,128)(2,1)S(1)}, u32[]{:S(2)}, u32[]{:S(2)}) collective-permute-start(bf16[4,96,384]{2,1,0:T(8,128)(2,1)S(1)} %get-tuple-element.176), channel_id=1, source_target_pairs={{8,0},{16,8},{24,16},{28,24},{20,28},{12,20},{4,12},{0,4},{9,1},{1... | collective-permute-start | bytes 884744 | tf_op jit(solution)/shard_map/ppermute | solution.py:491
  206.7 13.7 %collective-permute-start.31 = (bf16[4,96,384]{2,1,0:T(8,128)(2,1)S(1)}, bf16[4,96,384]{2,1,0:T(8,128)(2,1)S(1)}, u32[]{:S(2)}, u32[]{:S(2)}) collective-permute-start(bf16[4,96,384]{2,1,0:T(8,128)(2,1)S(1)} %get-tuple-element.177), channel_id=1, source_target_pairs={{0,8},{8,16},{16,24},{24,28},{28,20},{20,12},{12,4},{4,0},{1,9},{9... | collective-permute-start | bytes 884744 | tf_op jit(solution)/shard_map/ppermute | solution.py:491
  221.2 9.8 %collective-permute-start.33 = (bf16[4,96,384]{2,1,0:T(8,128)(2,1)S(1)}, bf16[4,96,384]{2,1,0:T(8,128)(2,1)S(1)}, u32[]{:S(2)}, u32[]{:S(2)}) collective-permute-start(bf16[4,96,384]{2,1,0:T(8,128)(2,1)S(1)} %fusion.1), channel_id=1, source_target_pairs={{0,2},{2,0},{1,3},{3,1},{4,6},{6,4},{5,7},{7,5},{8,10},{10,8},{9,1... | collective-permute-start | bytes 884744 | tf_op jit(solution)/shard_map/ppermute | solution.py:420
  (72 other events, 455.4 us)

commit v8 on v6

--- a/solution.py
+++ b/solution.py
@@ -13,6 +13,7 @@
 NSEQ = 4
 HALF = WINDOW // 2
 PAD = 16
+SPARE = 6
 BLOCK = 128
 LANES = 128
 KEYS = BLOCK + WINDOW
@@ -38,23 +39,22 @@
     return best
 
 
-def call(kernel, out_shape, args, flops, name, scalars=(), scratch=(), raw=(), raw_out=()):
+def call(kernel, out_shape, args, flops, name, scalars=(), scratch=()):
     vmem = pl.BlockSpec(memory_space=pltpu.VMEM)
     smem = pl.BlockSpec(memory_space=pltpu.SMEM)
-    anywhere = pl.BlockSpec(memory_space=pl.ANY)
     moved = sum(x.size * x.dtype.itemsize for x in (*args, *out_shape))
     held = sum(math.prod(x.shape) * jnp.dtype(x.dtype).itemsize for x in scratch if x.dtype in (f32, bf16))
-    limit = min(56 * 2**20, moved // 2 + held + 4 * 2**20)
+    limit = held + SPARE * 2**20
     return pl.pallas_call(
         kernel,
-        out_shape=[*out_shape, *raw_out],
-        in_specs=[smem] * len(scalars) + [vmem] * len(args) + [anywhere] * len(raw),
-        out_specs=[vmem] * len(out_shape) + [pl.BlockSpec(memory_space=pltpu.HBM)] * len(raw_out),
+        out_shape=out_shape,
+        in_specs=[smem] * len(scalars) + [vmem] * len(args),
+        out_specs=[vmem] * len(out_shape),
         scratch_shapes=scratch,
         compiler_params=pltpu.CompilerParams(vmem_limit_bytes=limit),
         cost_estimate=pl.CostEstimate(flops=flops, bytes_accessed=moved, transcendentals=0),
         name=name,
-    )(*scalars, *args, *raw)
+    )(*scalars, *args)
 
 
 def shape(dims, dtype):
@@ -94,20 +94,6 @@
         return carry
 
     lax.fori_loop(0, count, run, 0)
-
-
-def begin(copies, sems):
-    started = []
-    for number, (source, target) in enumerate(copies):
-        copy = pltpu.make_async_copy(source, target, sems.at[number])
-        copy.start()
-        started.append(copy)
-    return started
-
-
-def end(started):
-    for copy in started:
-        copy.wait()
 
 
 def norm_kernel(tokens, before, after, hat):
@@ -141,28 +127,24 @@
 
 
 def project_kernel(slots, hat, cosine, sine, *rest):
-    pieces, (wide, gain, first, query, key, value, gain_held, sems) = rest[:-8], rest[-8:]
+    pieces, (wide, gain, first, query, key, value) = rest[:-6], rest[-6:]
     extent, local = key.shape
     rows = query.shape[0]
     width = hat.shape[1]
     pairs = local // LANES
-    groups = gain_held.shape[0]
+    groups = slots.shape[0]
     depth = width // groups
     plan = piece_plan(groups, [depth] * 4 + [PAD], 2)
-    copies = []
+    lane = lax.broadcasted_iota(jnp.int32, (LANES, width), 1) - lax.broadcasted_iota(jnp.int32, (LANES, width), 0)
+    gain_sum = jnp.zeros((PAD, width), f32)
     for number, sources in enumerate(plan):
-        place = pl.ds(pl.multiple_of(slots[number] * depth, depth), depth)
+        start = pl.multiple_of(slots[number] * depth, depth)
         for part, (piece, row) in enumerate(sources[:4]):
             lanes = slice(part * local, (part + 1) * local)
-            copies.append((pieces[piece].at[row : row + depth, :], wide.at[place, lanes]))
+            wide[pl.ds(start, depth), lanes] = pieces[piece][row : row + depth, :]
         piece, row = sources[4]
-        copies.append((pieces[piece].at[row : row + PAD, :], gain_held.at[number]))
-    end(begin(copies, sems))
-    lane = lax.broadcasted_iota(jnp.int32, (LANES, width), 1) - lax.broadcasted_iota(jnp.int32, (LANES, width), 0)
-    gain_sum = jnp.zeros((PAD, width), f32)
-    for number in range(groups):
-        spread = jnp.where(lane == slots[number] * depth, 1.0, 0.0).astype(bf16)
-        gain_sum += dot(gain_held[number][:, :LANES], spread)
+        spread = jnp.where(lane == start, 1.0, 0.0).astype(bf16)
+        gain_sum += dot(pieces[piece][row : row + PAD, :LANES], spread)
     gain[...] = gain_sum
     gains = gain_sum[:1]
     query_w, key_w, value_w = (wide.at[:, at * local : (at + 1) * local] for at in range(3))
@@ -198,36 +180,27 @@
 
 def attend_kernel(chosen, last, bounds, query, key, value, *rest):
     if last:
-        wide, first, done, attended, branch, *kept, held, sems = rest
-        shares, kept = kept[0], kept[1:]
+        wide, done, shares, attended, branch = rest
+        attended[...] = done[...]
     else:
-        attended, shares, held, sems = rest
+        shares, attended = rest
     rows, local = query.shape
     count = len(chosen)
-    started = []
-    if last:
-        started = begin(list(zip((first, query, key, value), kept)), sems.at[2 * count :])
-        attended[...] = done[...]
     key_at = lax.broadcasted_iota(jnp.int32, (KEYS, KEYS), 0)
     lane_at = lax.broadcasted_iota(jnp.int32, (1, KEYS), 1) % BLOCK
 
-    def out_copy(index, number, side):
-        return pltpu.make_async_copy(
-            held.at[side, number], shares.at[index * count + number], sems.at[side * count + number]
-        )
-
-    def attend_step(index, side, old):
+    def attend_step(index):
         at = pl.multiple_of(index * BLOCK, BLOCK)
         origin = bounds[NSEQ] + at - HALF
         own = lane_at + (origin + HALF)
-        begin_at = jnp.zeros_like(own)
-        end_at = jnp.zeros_like(own) + bounds[NSEQ - 1]
+        begin = jnp.zeros_like(own)
+        end = jnp.zeros_like(own) + bounds[NSEQ - 1]
         for number in range(NSEQ - 1):
-            begin_at = jnp.where(own >= bounds[number], bounds[number], begin_at)
+            begin = jnp.where(own >= bounds[number], bounds[number], begin)
         for number in reversed(range(NSEQ - 1)):
-            end_at = jnp.where(own < bounds[number], bounds[number], end_at)
-        least = jnp.maximum(lane_at, begin_at - origin)
-        most = jnp.minimum(lane_at + WINDOW, end_at - 1 - origin)
+            end = jnp.where(own < bounds[number], bounds[number], end)
+        least = jnp.maximum(lane_at, begin - origin)
+        most = jnp.minimum(lane_at + WINDOW, end - 1 - origin)
         allowed = (key_at >= least) & (key_at <= most)
         for number, pair in enumerate(chosen):
             lanes = slice(pair * LANES, (pair + 1) * LANES)
@@ -235,26 +208,11 @@
             scores = jnp.where(allowed, dot(key[pl.ds(at, KEYS), lanes], both, NT), -1e30)
             weight = jnp.exp(scores - jnp.max(scores, axis=0, keepdims=True))
             part = (weight * (1.0 / jnp.sum(weight, axis=0, keepdims=True))).astype(bf16)
-            if old is not None:
-                out_copy(old, number, side).wait()
-            held[side, number] = part
-            out_copy(index, number, side).start()
+            shares[index * count + number] = part
             mixed = dot(value[pl.ds(at, KEYS), lanes], part, TN)
             attended[pl.ds(at, BLOCK), lanes] = joined(mixed).astype(bf16)
 
-    steps = rows // BLOCK
-    attend_step(0, 0, None)
-    attend_step(1, 1, None)
-
-    def two_steps(index):
-        for side in range(2):
-            attend_step(2 * index + 2 + side, side, 2 * index + side)
-
-    loop(steps // 2 - 1, two_steps)
-    for side in range(2):
-        for number in range(count):
-            out_copy(steps - 2 + side, number, side).wait()
-    end(started)
+    loop(rows // BLOCK, attend_step)
     if not last:
         return
     out_t = wide.at[:, 3 * local :]
@@ -268,33 +226,25 @@
 
 
 def feed_kernel(slots, tokens, own, other, gain, cotangent, *rest):
-    pieces, rest = rest[:-8], rest[-8:]
-    middle, second, hidden, grad_gate, grad_upper, partial, whole, sems = rest
+    pieces, rest = rest[:-7], rest[-7:]
+    middle, second, hidden, grad_gate, grad_upper, partial, whole = rest
     rows, width = tokens.shape
     groups = slots.shape[0]
     depth = width // groups
-    copies = []
     for number, sources in enumerate(piece_plan(groups, [depth] * 3, 1)):
         place = pl.ds(pl.multiple_of(slots[number] * depth, depth), depth)
         for part, (piece, row) in enumerate(sources):
-            copies.append((pieces[piece].at[row : row + depth, :], whole.at[part, place, :]))
-    started = begin(copies, sems)
+            whole[part, place, :] = pieces[piece][row : row + depth, :]
     gate_w, upper_w, down_t = (whole.at[number] for number in range(3))
     gains = gain[1:2, :]
     size = step_of(rows, 256)
 
-    def norm_step(index):
+    def step(index):
         here = pl.ds(pl.multiple_of(index * size, size), size)
         mid = tokens[here, :].astype(f32) + (own[here, :].astype(f32) + other[here, :].astype(f32))
         middle[here, :] = mid
-        second[here, :] = (normed(mid)[0] * gains).astype(bf16)
-
-    loop(rows // size, norm_step)
-    end(started)
-
-    def step(index):
-        here = pl.ds(pl.multiple_of(index * size, size), size)
-        low = second[here, :]
+        low = (normed(mid)[0] * gains).astype(bf16)
+        second[here, :] = low
         gate = dot(low, gate_w[...])
         upper = dot(low, upper_w[...])
         grad = dot(cotangent[here, :], down_t[...])
@@ -362,11 +312,11 @@
     loop(rows // size, norm_step)
 
 
-def back_kernel(chosen, query, key, value, shares, grad_att, cosine, sine, *rest):
-    parts, (grad_key, grad_value) = rest[:-2], rest[-2:]
+def back_kernel(chosen, query, key, value, grad_att, cosine, sine, *rest):
+    held, parts, (grad_key, grad_value) = rest[: len(chosen)], rest[len(chosen) : -2], rest[-2:]
     rows = query.shape[0]
     extent = key.shape[0]
-    count = len(chosen)
+    flat = [(part, number, len(group)) for part, group in zip(held, chosen) for number in range(len(group))]
     grad_key[...] = jnp.zeros_like(grad_key)
     grad_value[...] = jnp.zeros_like(grad_value)
     low = lax.broadcasted_iota(jnp.int32, (1, LANES), 1) % HEAD < HEAD // 2
@@ -379,13 +329,12 @@
         at = pl.multiple_of(index * BLOCK, BLOCK)
         start = pl.multiple_of(at + HALF, HALF)
         co, si = cosine[pl.ds(start, BLOCK), :], sine[pl.ds(start, BLOCK), :]
-        for number, pair in enumerate(chosen):
-            lanes = slice(pair * LANES, (pair + 1) * LANES)
-            here = slice(number * LANES, (number + 1) * LANES)
+        for number, (shares, spot, count) in enumerate(flat):
+            lanes = slice(number * LANES, (number + 1) * LANES)
             both = halves(query[pl.ds(at, BLOCK), lanes])
             grad = halves(grad_att[pl.ds(at, BLOCK), lanes])
             keys = key[pl.ds(at, KEYS), lanes]
-            part = shares[index * count + number]
+            part = shares[index * count + spot]
             wide = part.astype(f32)
             grad_shares = dot(value[pl.ds(at, KEYS), lanes], grad, NT)
             delta = jnp.sum(wide * grad_shares, axis=0, keepdims=True)
@@ -393,8 +342,8 @@
             grad_query = joined(dot(keys, raw, TN)) * HEAD**-0.5
             turn = (grad_query * co - turned(grad_query, low) * si).astype(bf16)
             parts[number][pl.ds(start, BLOCK), :LANES] = turn
-            grad_key[pl.ds(at, KEYS), here] += dot(raw, both)
-            grad_value[pl.ds(at, KEYS), here] += dot(part, grad)
+            grad_key[pl.ds(at, KEYS), lanes] += dot(raw, both)
+            grad_value[pl.ds(at, KEYS), lanes] += dot(part, grad)
 
     loop(rows // BLOCK, attend_step)
 
@@ -622,48 +571,36 @@
             shape((extent, local), bf16),
             shape((extent, local), bf16),
         ],
-        (hat, cosine, sine),
+        (hat, cosine, sine, *pieces),
         2 * rows * width * local * 8,
         "project",
         (slots,),
-        [pltpu.VMEM((groups, PAD, local), bf16), pltpu.SemaphoreType.DMA((5 * groups,))],
-        pieces,
     )
     early, late = tuple(range(pairs - 1)), (pairs - 1,)
-
-    def share_shapes(chosen):
-        return (
-            shape((blocks * len(chosen), KEYS, KEYS), bf16),
-            [pltpu.VMEM((2, len(chosen), KEYS, KEYS), bf16), pltpu.SemaphoreType.DMA((2 * len(chosen) + 4,))],
-        )
 
     query, key, value = tied([query, key, value], later.state)
     later.hop()
-    out, scratch = share_shapes(early)
-    attended, shares_early = call(
+    shares_early, attended = call(
         functools.partial(attend_kernel, early, False),
-        [shape((rows, local), bf16)],
+        [shape((blocks * len(early), KEYS, KEYS), bf16), shape((rows, local), bf16)],
         (query, key, value),
         2 * rows * width * local * 10,
         "attend",
         (bounds,),
-        scratch,
-        (),
-        [out],
     )
     attended, = locked([attended], later)
     later.hop()
-    out, scratch = share_shapes(late)
-    attended, branch, shares_late, first, query, key, value = call(
+    shares_late, attended, branch = call(
         functools.partial(attend_kernel, late, True),
-        [shape((rows, local), bf16), shape((rows, width), bf16)],
-        (query, key, value, wide, first, attended),
+        [
+            shape((blocks * len(late), KEYS, KEYS), bf16),
+            shape((rows, local), bf16),
+            shape((rows, width), bf16),
+        ],
+        (query, key, value, wide, attended),
         2 * rows * width * local * 7,
         "attend",
         (bounds,),
-        scratch,
-        (),
-        [out] + [shape(x.shape, bf16) for x in (first, query, key, value)],
     )
     branch_other = swap(branch)
     later.after([branch])
@@ -681,12 +618,10 @@
             shape((rows, width), bf16),
             shape((3, width, units), bf16),
         ],
-        (tokens, branch, branch_other, gain, cotangent),
+        (tokens, branch, branch_other, gain, cotangent, *pieces),
         2 * rows * width * units * 8,
         "feed_forward_and_back",
         (slots,),
-        [pltpu.SemaphoreType.DMA((3 * groups,))],
-        pieces,
     )
     partial_other = swap(partial)
     grads_two, = call(
@@ -698,6 +633,7 @@
         (slots,),
         [pltpu.VMEM((3, width, units), bf16)],
     )
+    grads_two, = tied([grads_two], [partial_other])
     sums_two = RingScatter([grads_two], 1)
     sums_two.hop()
     grad_middle, low_mid, grad_att = call(
@@ -709,29 +645,17 @@
     )
     grad_att, = locked([grad_att], sums_two)
     sums_two.hop()
-    grad_parts = []
-    for chosen, shares in ((early, shares_early), (late, shares_late)):
-        if grad_parts:
-            grad_att, *grad_parts = locked([grad_att, *grad_parts], sums_two)
-            sums_two.hop()
-        grad_parts += call(
-            functools.partial(back_kernel, chosen),
-            [shape((extent, 3 * LANES), bf16)] * len(chosen),
-            (query, key, value, shares, grad_att, cosine, sine),
-            2 * rows * width * local * 5 * len(chosen),
-            "attention_back",
-            (),
-            [pltpu.VMEM((extent, len(chosen) * LANES), f32)] * 2,
-        )
-    feed, = call(
-        feed_out_kernel,
-        [shape((rows, width), bf16)],
-        (tied([hidden], grad_parts[: len(early)])[0], whole),
-        2 * rows * width * units,
-        "feed_out",
-    )
-    feed_other = swap(feed)
-    grad_parts = tied(grad_parts, [feed, *sums_two.state])
+    grad_parts = call(
+        functools.partial(back_kernel, (early, late)),
+        [shape((extent, 3 * LANES), bf16)] * pairs,
+        (query, key, value, grad_att, cosine, sine, shares_early, shares_late),
+        2 * rows * width * local * 15,
+        "attention_back",
+        (),
+        [pltpu.VMEM((extent, local), f32)] * 2,
+    )
+    grad_parts = locked(grad_parts, sums_two)
+    sums_two.hop()
     grad_proj, *grads_one = call(
         grad_kernel,
         [shape((extent, 3 * local), bf16)] + [shape((groups, 2, depth, local), bf16)] * 2,
@@ -741,33 +665,41 @@
         (slots,),
         [pltpu.VMEM((4, width, local), bf16)],
     )
+    feed, = call(
+        feed_out_kernel,
+        [shape((rows, width), bf16)],
+        (tied([hidden], grads_one)[0], whole),
+        2 * rows * width * units,
+        "feed_out",
+    )
+    feed_other = swap(feed)
+    first_part, = call(
+        first_kernel,
+        [shape((extent, width), bf16)],
+        (grad_proj, wide),
+        2 * rows * width * local * 3,
+        "first_grad",
+    )
+    first_other = swap(first_part)
+    grads_one = tied(grads_one, [*sums_two.state, feed, first_part])
     sums_one = [RingScatter([part], 0) for part in grads_one]
     sums_one[0].hop()
     sums_one[1].hop()
-    sums_two.after(sums_one[0].state)
     while sums_two.hops < middle_hop:
         sums_two.hop()
-    first_part, = call(
-        first_kernel,
-        [shape((extent, width), bf16)],
-        (tied([grad_proj], grads_one)[0], wide),
-        2 * rows * width * local * 3,
-        "first_grad",
-    )
-    first_other = swap(first_part)
 
     def edge_sum(at):
         here = slice(at, at + HALF)
         return (first_part[here].astype(f32) + first_other[here].astype(f32)).astype(bf16)
 
+    from_before, from_after = exchange(edge_sum(0), edge_sum(rows + HALF))
     for chain in sums_one:
-        chain.after([first_part, feed])
+        chain.after([from_before, from_after])
     while sums_one[0].hops < middle_hop - 1:
         for chain in sums_one:
             chain.hop()
-    from_before, from_after = exchange(edge_sum(0), edge_sum(rows + HALF))
+    tokens, = tied([tokens], sums_one[0].state)
     for chain in sums_one:
-        chain.after([from_before, from_after])
         chain.hop()
     mixed, token_grad = call(
         final_kernel,
@@ -777,8 +709,8 @@
         "token_grad",
     )
     two = over_ctx(sums_two.total())
-    one = [over_ctx(sums_one[0].total()), over_ctx(sums_one[1].total())]
-    one = jnp.concatenate(one)
+    one = tied([chain.total() for chain in sums_one], [mixed, token_grad])
+    one = jnp.concatenate([over_ctx(part) for part in one])
     gain_one_grad = jnp.sum(one[:3] * w_qkv.astype(f32), axis=(0, 2)) / gain_one.astype(f32)
     gain_two_grad = jnp.sum(two[:2] * w_in.astype(f32), axis=(0, 2)) / gain_two.astype(f32)
     both = jnp.stack([gain_one_grad, gain_two_grad])

time: 212 us -> 197 us (0.929)
  Pallas kernels: 81.3 us -> 69 us
  waiting for transfers between devices: 68.6 us -> 66.3 us
    pallas_call x13 -> x12, Pallas kernels: 81.3 us -> 69 us  [call(): pl.pallas_call(kernel, out_shape=out_shape, in_specs=[smem] * len(scalars...]
    ppermute x20, waiting for transfers between devices: 34.3 us -> 30.9 us  [hop(): lax.ppermute(two, 'dp', self.back)]
  transfers between devices with their start and end apart: 50 -> 50, of which waited for: 25 -> 31; matrix products, arithmetic and copies ran while one was open for 4% -> 4% of each run, Pallas kernels for 23% -> 26%
where the time goes in v8:
time: 197 us
  Pallas kernels  69 us (35%)
  waiting for transfers between devices  66.3 us (34%)
  starting transfers between devices  49.2 us (25%)
  other arithmetic  9.61 us (5%)
  local copies, waits for them, and re-layouts  2.1 us (1%)
    pallas_call x12, Pallas kernels, call(): pl.pallas_call(kernel, out_shape=out_shape, in_specs=[smem] * len(scalars...  69 us
    ppermute x20, waiting for transfers between devices, hop(): lax.ppermute(two, 'dp', self.back)  30.9 us
    ppermute x20, waiting for transfers between devices, hop(): lax.ppermute(one, 'dp', self.ahead)  27.7 us
    ppermute x20, starting transfers between devices, hop(): lax.ppermute(one, 'dp', self.ahead)  22.7 us
    ppermute x20, starting transfers between devices, hop(): lax.ppermute(two, 'dp', self.back)  19.8 us
    ppermute x8, waiting for transfers between devices, swap(): return lax.ppermute(array, axis, [(0, 1), (1, 0)])  4.65 us
    ppermute x8, starting transfers between devices, swap(): return lax.ppermute(array, axis, [(0, 1), (1, 0)])  3.96 us
  transfers between devices with their start and end apart: 50, of which 31 were waited for; matrix products, arithmetic and copies ran while one was open for 4% of the time, Pallas kernels for 26%

profile of v8, /device:TPU:0, one launch (start us, length us, event | category | flops | bytes accessed | tf_op | source)
XLA Modules:
  0.0 197.3 jit_solution(9530696832843319170)
XLA Ops:
  2.4 3.0 %collective-permute-start.2 = (bf16[400,384]{1,0:T(8,128)(2,1)S(1)}, bf16[400,384]{1,0:T(8,128)(2,1)S(1)}, u32[]{:S(2)}, u32[]{:S(2)}) collective-permute-start(bf16[400,384]{1,0:T(8,128)(2,1)S(1)} %pad_maximum_fusion.2.rest_0_), channel_id=1, source_target_pairs={{8,0},{16,8},{24,16},{28,24},{20,28},{12,20},{4,12},{0,4},{9,1},{1... | collective-permute-start | bytes 921608 | tf_op jit(solution)/shard_map/ppermute | solution.py:474
  10.2 2.5 %collective-permute-done.2.rest_1_ = bf16[400,384]{1,0:T(8,128)(2,1)S(1)} collective-permute-done((bf16[400,384]{1,0:T(8,128)(2,1)S(1)}, bf16[400,384]{1,0:T(8,128)(2,1)S(1)}, u32[]{:S(2)}, u32[]{:S(2)}) %collective-permute-start.2) | collective-permute-done | bytes 307232 | tf_op jit(solution)/shard_map/ppermute | solution.py:474
  18.3 3.6 %collective-permute-done.4.rest_2_ = bf16[400,384]{1,0:T(8,128)(2,1)S(1)} collective-permute-done((bf16[400,384]{1,0:T(8,128)(2,1)S(1)}, bf16[400,384]{1,0:T(8,128)(2,1)S(1)}, u32[]{:S(2)}, u32[]{:S(2)}) %collective-permute-start.4) | collective-permute-done | bytes 307232 | tf_op jit(solution)/shard_map/ppermute | solution.py:474
  25.4 4.7 %collective-permute-done.6.rest_3_ = bf16[400,384]{1,0:T(8,128)(2,1)S(1)} collective-permute-done((bf16[400,384]{1,0:T(8,128)(2,1)S(1)}, bf16[400,384]{1,0:T(8,128)(2,1)S(1)}, u32[]{:S(2)}, u32[]{:S(2)}) %collective-permute-start.6) | collective-permute-done | bytes 307232 | tf_op jit(solution)/shard_map/ppermute | solution.py:474
  36.0 4.6 %collective-permute-done.7.rest_4_ = bf16[192,384]{1,0:T(8,128)(2,1)S(1)} collective-permute-done((bf16[192,384]{1,0:T(8,128)(2,1)S(1)}, bf16[192,384]{1,0:T(8,128)(2,1)S(1)}, u32[]{:S(2)}, u32[]{:S(2)}) %collective-permute-start.7) | collective-permute-done | bytes 147488 | tf_op jit(solution)/shard_map/ppermute | solution.py:474
  42.6 5.8 %project.1 = (bf16[768,1536]{1,0:T(8,128)(2,1)S(1)}, f32[16,768]{1,0:T(8,128)S(1)}, bf16[1152,768]{1,0:T(8,128)(2,1)S(1)}, bf16[1024,384]{1,0:T(8,128)(2,1)S(1)}...) custom-call(s32[8]{0:T(128)S(1)} %compare_select_fusion.2.slots, f32[1152,768]{1,0:T(8,128)S(1)} %first_norm.1.hat, ...), custom_call_target="tpu_custom_call" | custom-call | flops 4831838208 | bytes 13910016 | tf_op jit(solution)/shard_map/project/pallas_call | solution.py:48
  48.4 2.6 %collective-permute-done.10.rest_1_ = bf16[288,576]{1,0:T(8,128)(2,1)S(1)} collective-permute-done((bf16[288,576]{1,0:T(8,128)(2,1)S(1)}, bf16[288,576]{1,0:T(8,128)(2,1)S(1)}, u32[]{:S(2)}, u32[]{:S(2)}) %collective-permute-start.10) | collective-permute-done | bytes 331808 | tf_op jit(solution)/shard_map/ppermute | solution.py:474
  54.4 7.8 %attend.2 = (bf16[16,256,256]{2,1,0:T(8,128)(2,1)S(1)}, bf16[1024,384]{1,0:T(8,128)(2,1)S(1)}) custom-call(s32[5]{0:T(128)S(1)} %pad_add_fusion.bounds, bf16[1024,384]{1,0:T(8,128)(2,1)S(1)} %get-tuple-element.120.query, bf16[1152,384]{1,0:T(8,128)(2,1)S(1)} %get-tuple-element.121.key, bf16[1152,384]{1,0:T(8,128)(2,1)S(1)} %get-tuple-element.122.value), custom_call_target="tpu_custom_call" | custom-call | flops 6039797760 | bytes 5439488 | tf_op jit(solution)/shard_map/attend/pallas_call | solution.py:48
  62.2 6.6 %attend.3 = (bf16[8,256,256]{2,1,0:T(8,128)(2,1)S(1)}, bf16[1024,384]{1,0:T(8,128)(2,1)S(1)}, bf16[1024,768]{1,0:T(8,128)(2,1)S(1)}) custom-call(s32[5]{0:T(128)S(1)} %pad_add_fusion.bounds, bf16[1024,384]{1,0:T(8,128)(2,1)S(1)} %get-tuple-element.120.query, bf16[1152,384]{1,0:T(8,128)(2,1)S(1)} %get-tuple-element.121.key, ...), custom_call_target="tpu_custom_call" | custom-call | flops 4227858432 | bytes 9109504 | tf_op jit(solution)/shard_map/attend/pallas_call | solution.py:48
  71.0 8.9 %collective-permute-done.14.rest_6_ = bf16[288,576]{1,0:T(8,128)(2,1)S(1)} collective-permute-done((bf16[288,576]{1,0:T(8,128)(2,1)S(1)}, bf16[288,576]{1,0:T(8,128)(2,1)S(1)}, u32[]{:S(2)}, u32[]{:S(2)}) %collective-permute-start.14) | collective-permute-done | bytes 331808 | tf_op jit(solution)/shard_map/ppermute | solution.py:474
  82.9 3.9 %collective-permute-done.16.rest_4_ = bf16[96,576]{1,0:T(8,128)(2,1)S(1)} collective-permute-done((bf16[96,576]{1,0:T(8,128)(2,1)S(1)}, bf16[96,576]{1,0:T(8,128)(2,1)S(1)}, u32[]{:S(2)}, u32[]{:S(2)}) %collective-permute-start.16) | collective-permute-done | bytes 110624 | tf_op jit(solution)/shard_map/ppermute | solution.py:474
  87.8 10.5 %feed_forward_and_back.1 = (f32[1024,768]{1,0:T(8,128)S(1)}, bf16[1024,768]{1,0:T(8,128)(2,1)S(1)}, bf16[1024,576]{1,0:T(8,128)(2,1)S(1)}, bf16[1024,576]{1,0:T(...) custom-call(s32[8]{0:T(128)S(1)} %compare_select_fusion.2.slots, ...), custom_call_target="tpu_custom_call" | custom-call | flops 7247757312 | bytes 21479424 | tf_op jit(solution)/shard_map/feed_forward_and_back/pallas_call | solution.py:48
  98.5 4.8 %feed_weight_grads.1 = bf16[8,3,96,576]{3,2,1,0:T(8,128)(2,1)S(1)} custom-call(s32[8]{0:T(128)S(1)} %compare_select_fusion.2.slots, bf16[1024,768]{1,0:T(8,128)(2,1)S(1)} %get-tuple-element.143.second, bf16[1024,576]{1,0:T(8,128)(2,1)S(1)} %get-tuple-element.169.hidden, bf16[1024,576]{1,0:T(8,128)(2,1)S(1)} %get-tuple-element.145.grad_gate, ...), custom_call_target="tpu_custom_call" | custom-call | flops 4529848320 | bytes 9338880 | tf_op jit(solution)/shard_map/feed_weight_grads/pallas_call | solution.py:48
  105.4 3.5 %middle_grad.1 = (f32[1024,768]{1,0:T(8,128)S(1)}, bf16[1024,768]{1,0:T(8,128)(2,1)S(1)}, bf16[1024,384]{1,0:T(8,128)(2,1)S(1)}) custom-call(f32[1024,768]{1,0:T(8,128)S(1)} %get-tuple-element.138.middle, bf16[1024,768]{1,0:T(8,128)(2,1)S(1)} %get-tuple-element.139.own, bf16[1024,768]{1,0:T(8,128)(2,1)S(1)} %collective-permute-done.18.other, ...), custom_call_target="tpu_custom_call" | custom-call | flops 2415919104 | bytes 15777792 | tf_op jit(solution)/shard_map/middle_grad/pallas_call | solution.py:48
  113.4 12.3 %attention_back.1 = (bf16[1152,384]{1,0:T(8,128)(2,1)S(1)}, bf16[1152,384]{1,0:T(8,128)(2,1)S(1)}, bf16[1152,384]{1,0:T(8,128)(2,1)S(1)}) custom-call(bf16[1024,384]{1,0:T(8,128)(2,1)S(1)} %get-tuple-element.120.query, bf16[1152,384]{1,0:T(8,128)(2,1)S(1)} %get-tuple-element.121.key, bf16[1152,384]{1,0:T(8,128)(2,1)S(1)} %get-tuple-element.122.value, ...), custom_call_target="tpu_custom_call" | custom-call | flops 9059696640 | bytes 10321920 | tf_op jit(solution)/shard_map/attention_back/pallas_call | solution.py:48
  127.9 4.8 %attention_weight_grads.1 = (bf16[1152,1152]{1,0:T(8,128)(2,1)S(1)}, bf16[8,2,96,384]{3,2,1,0:T(8,128)(2,1)S(1)}, bf16[8,2,96,384]{3,2,1,0:T(8,128)(2,1)S(1)}) custom-call(s32[8]{0:T(128)S(1)} %compare_select_fusion.2.slots, bf16[1152,768]{1,0:T(8,128)(2,1)S(1)} %get-tuple-element.113.first, bf16[1024,768]{1,0:T(8,128)(2,1)S(1)} %get-tuple-element.140.low_mid, ...), custom_call_target="tpu_custom_call" | custom-call | flops 3623878656 | bytes 11796480 | tf_op jit(solution)/shard_map/attention_weight_grads/pallas_call | solution.py:48
  132.7 2.9 %first_grad.1.own = bf16[1152,768]{1,0:T(8,128)(2,1)S(1)} custom-call(bf16[1152,1152]{1,0:T(8,128)(2,1)S(1)} %get-tuple-element.171.grad_proj, bf16[768,1536]{1,0:T(8,128)(2,1)S(1)} %get-tuple-element.123.rest_0_.wide), custom_call_target="tpu_custom_call" | custom-call | flops 1811939328 | bytes 6782976 | tf_op jit(solution)/shard_map/first_grad/pallas_call | solution.py:48
  139.9 6.9 %collective-permute-done.47 = bf16[3,96,576]{2,1,0:T(8,128)(2,1)S(1)} collective-permute-done((bf16[3,96,576]{2,1,0:T(8,128)(2,1)S(1)}, bf16[3,96,576]{2,1,0:T(8,128)(2,1)S(1)}, u32[]{:S(2)}, u32[]{:S(2)}) %collective-permute-start.47) | collective-permute-done | bytes 331808 | tf_op jit(solution)/shard_map/ppermute | solution.py:512
  151.3 2.5 %collective-permute-done.26 = bf16[1,96,384]{2,1,0:T(8,128)(2,1)S(1)} collective-permute-done((bf16[1,96,384]{2,1,0:T(8,128)(2,1)S(1)}, bf16[1,96,384]{2,1,0:T(8,128)(2,1)S(1)}, u32[]{:S(2)}, u32[]{:S(2)}) %collective-permute-start.26) | collective-permute-done | bytes 73760 | tf_op jit(solution)/shard_map/ppermute | solution.py:512
  155.2 2.9 %collective-permute-done.36 = bf16[1,96,384]{2,1,0:T(8,128)(2,1)S(1)} collective-permute-done((bf16[1,96,384]{2,1,0:T(8,128)(2,1)S(1)}, bf16[1,96,384]{2,1,0:T(8,128)(2,1)S(1)}, u32[]{:S(2)}, u32[]{:S(2)}) %collective-permute-start.36) | collective-permute-done | bytes 73760 | tf_op jit(solution)/shard_map/ppermute | solution.py:512
  159.9 3.0 %collective-permute-done.28 = bf16[64,768]{1,0:T(8,128)(2,1)S(1)} collective-permute-done((bf16[64,768]{1,0:T(8,128)(2,1)S(1)}, bf16[64,768]{1,0:T(8,128)(2,1)S(1)}, u32[]{:S(2)}, u32[]{:S(2)}) %collective-permute-start.28) | collective-permute-done | bytes 98336 | tf_op jit(solution)/shard_map/ppermute | solution.py:421
  167.2 2.6 %collective-permute-done.39 = bf16[2,96,384]{2,1,0:T(8,128)(2,1)S(1)} collective-permute-done((bf16[2,96,384]{2,1,0:T(8,128)(2,1)S(1)}, bf16[2,96,384]{2,1,0:T(8,128)(2,1)S(1)}, u32[]{:S(2)}, u32[]{:S(2)}) %collective-permute-start.39) | collective-permute-done | bytes 147488 | tf_op jit(solution)/shard_map/ppermute | solution.py:512
  181.4 5.9 %token_grad.1 = (bf16[1024,768]{1,0:T(8,128)(2,1)}, f32[1024,768]{1,0:T(8,128)}) custom-call(bf16[1024,768]{1,0:T(8,128)(2,1)S(1)} %copy-done, f32[16,768]{1,0:T(8,128)S(1)} %get-tuple-element.129.gain, f32[1024,768]{1,0:T(8,128)S(1)} %get-tuple-element.182.grad_middle, bf16[1152,768]{1,0:T(8,128)(2,1)S(1)} %first_grad.1.own, ...), custom_call_target="tpu_custom_call" | custom-call | flops 1572864000 | bytes 19513344 | tf_op jit(solution)/shard_map/token_grad/pallas_call | solution.py:48
  190.3 2.4 %collective-permute-done.44 = bf16[2,96,384]{2,1,0:T(8,128)(2,1)S(1)} collective-permute-done((bf16[2,96,384]{2,1,0:T(8,128)(2,1)S(1)}, bf16[2,96,384]{2,1,0:T(8,128)(2,1)S(1)}, u32[]{:S(2)}, u32[]{:S(2)}) %collective-permute-start.44) | collective-permute-done | bytes 147488 | tf_op jit(solution)/shard_map/ppermute | solution.py:435
  (150 shorter events, 77.1 us)
Async XLA Ops:
  2.4 10.3 %collective-permute-start.2 = (bf16[400,384]{1,0:T(8,128)(2,1)S(1)}, bf16[400,384]{1,0:T(8,128)(2,1)S(1)}, u32[]{:S(2)}, u32[]{:S(2)}) collective-permute-start(bf16[400,384]{1,0:T(8,128)(2,1)S(1)} %pad_maximum_fusion.2.rest_0_), channel_id=1, source_target_pairs={{8,0},{16,8},{24,16},{28,24},{20,28},{12,20},{4,12},{0,4},{9,1},{1... | collective-permute-start | bytes 921608 | tf_op jit(solution)/shard_map/ppermute | solution.py:474
  5.4 8.7 %collective-permute-start.1 = (bf16[400,384]{1,0:T(8,128)(2,1)S(1)}, bf16[400,384]{1,0:T(8,128)(2,1)S(1)}, u32[]{:S(2)}, u32[]{:S(2)}) collective-permute-start(bf16[400,384]{1,0:T(8,128)(2,1)S(1)} %pad_maximum_fusion.2.rest_0_), channel_id=1, source_target_pairs={{0,8},{8,16},{16,24},{24,28},{28,20},{20,12},{12,4},{4,0},{1,9},{9... | collective-permute-start | bytes 921608 | tf_op jit(solution)/shard_map/ppermute | solution.py:474
  6.6 27.2 %collective-permute-start = (bf16[64,768]{1,0:T(8,128)(2,1)S(1)}, bf16[64,768]{1,0:T(8,128)(2,1)S(1)}, u32[]{:S(2)}, u32[]{:S(2)}) collective-permute-start(bf16[64,768]{1,0:T(8,128)(2,1)S(1)} %slice_select_fusion), channel_id=1, source_target_pairs={{0,2},{2,0},{1,3},{3,1},{4,6},{6,4},{5,7},{7,5},{8,10},{10,8},{9,1... | collective-permute-start | bytes 294920 | tf_op jit(solution)/shard_map/ppermute | solution.py:421
  14.1 7.8 %collective-permute-start.4 = (bf16[400,384]{1,0:T(8,128)(2,1)S(1)}, bf16[400,384]{1,0:T(8,128)(2,1)S(1)}, u32[]{:S(2)}, u32[]{:S(2)}) collective-permute-start(bf16[400,384]{1,0:T(8,128)(2,1)S(1)} %collective-permute-done.2.rest_1_), channel_id=1, source_target_pairs={{8,0},{16,8},{24,16},{28,24},{20,28},{12,20},{4,12},{0,4},{9,1},{1... | collective-permute-start | bytes 921608 | tf_op jit(solution)/shard_map/ppermute | solution.py:474
  31.7 8.8 %collective-permute-start.8 = (bf16[208,384]{1,0:T(8,128)(2,1)S(1)}, bf16[208,384]{1,0:T(8,128)(2,1)S(1)}, u32[]{:S(2)}, u32[]{:S(2)}) collective-permute-start(bf16[208,384]{1,0:T(8,128)(2,1)S(1)} %slice.129), channel_id=1, source_target_pairs={{8,0},{16,8},{24,16},{28,24},{20,28},{12,20},{4,12},{0,4},{9,1},{1... | collective-permute-start | bytes 479240 | tf_op jit(solution)/shard_map/ppermute | solution.py:474
  40.5 10.4 %collective-permute-start.10 = (bf16[288,576]{1,0:T(8,128)(2,1)S(1)}, bf16[288,576]{1,0:T(8,128)(2,1)S(1)}, u32[]{:S(2)}, u32[]{:S(2)}) collective-permute-start(bf16[288,576]{1,0:T(8,128)(2,1)S(1)} %pad_maximum_fusion.1.rest_0_), channel_id=1, source_target_pairs={{8,0},{16,8},{24,16},{28,24},{20,28},{12,20},{4,12},{0,4},{9,1},{1... | collective-permute-start | bytes 995336 | tf_op jit(solution)/shard_map/ppermute | solution.py:474
  41.1 11.2 %collective-permute-start.9 = (bf16[288,576]{1,0:T(8,128)(2,1)S(1)}, bf16[288,576]{1,0:T(8,128)(2,1)S(1)}, u32[]{:S(2)}, u32[]{:S(2)}) collective-permute-start(bf16[288,576]{1,0:T(8,128)(2,1)S(1)} %pad_maximum_fusion.1.rest_0_), channel_id=1, source_target_pairs={{0,8},{8,16},{16,24},{24,28},{28,20},{20,12},{12,4},{4,0},{1,9},{9... | collective-permute-start | bytes 995336 | tf_op jit(solution)/shard_map/ppermute | solution.py:474
  52.4 9.8 %collective-permute-start.11 = (bf16[288,576]{1,0:T(8,128)(2,1)S(1)}, bf16[288,576]{1,0:T(8,128)(2,1)S(1)}, u32[]{:S(2)}, u32[]{:S(2)}) collective-permute-start(bf16[288,576]{1,0:T(8,128)(2,1)S(1)} %collective-permute-done.9.rest_8_), channel_id=1, source_target_pairs={{0,8},{8,16},{16,24},{24,28},{28,20},{20,12},{12,4},{4,0},{1,9},{9... | collective-permute-start | bytes 995336 | tf_op jit(solution)/shard_map/ppermute | solution.py:474
  53.3 8.9 %collective-permute-start.12 = (bf16[288,576]{1,0:T(8,128)(2,1)S(1)}, bf16[288,576]{1,0:T(8,128)(2,1)S(1)}, u32[]{:S(2)}, u32[]{:S(2)}) collective-permute-start(bf16[288,576]{1,0:T(8,128)(2,1)S(1)} %collective-permute-done.10.rest_1_), channel_id=1, source_target_pairs={{8,0},{16,8},{24,16},{28,24},{20,28},{12,20},{4,12},{0,4},{9,1},{1... | collective-permute-start | bytes 995336 | tf_op jit(solution)/shard_map/ppermute | solution.py:474
  68.8 19.0 %collective-permute-start.13 = (bf16[1024,768]{1,0:T(8,128)(2,1)S(1)}, bf16[1024,768]{1,0:T(8,128)(2,1)S(1)}, u32[]{:S(2)}, u32[]{:S(2)}) collective-permute-start(bf16[1024,768]{1,0:T(8,128)(2,1)S(1)} %get-tuple-element.128.own), channel_id=1, source_target_pairs={{0,1},{1,0},{2,3},{3,2},{4,5},{5,4},{6,7},{7,6},{8,9},{9,8},{10,11... | collective-permute-start | bytes 4718600 | tf_op jit(solution)/shard_map/ppermute | solution.py:435
  68.9 11.0 %collective-permute-start.14 = (bf16[288,576]{1,0:T(8,128)(2,1)S(1)}, bf16[288,576]{1,0:T(8,128)(2,1)S(1)}, u32[]{:S(2)}, u32[]{:S(2)}) collective-permute-start(bf16[288,576]{1,0:T(8,128)(2,1)S(1)} %collective-permute-done.11.rest_7_), channel_id=1, source_target_pairs={{0,8},{8,16},{16,24},{24,28},{28,20},{20,12},{12,4},{4,0},{1,9},{9... | collective-permute-start | bytes 995336 | tf_op jit(solution)/shard_map/ppermute | solution.py:474
  69.9 10.7 %collective-permute-start.15 = (bf16[288,576]{1,0:T(8,128)(2,1)S(1)}, bf16[288,576]{1,0:T(8,128)(2,1)S(1)}, u32[]{:S(2)}, u32[]{:S(2)}) collective-permute-start(bf16[288,576]{1,0:T(8,128)(2,1)S(1)} %collective-permute-done.12.rest_2_), channel_id=1, source_target_pairs={{8,0},{16,8},{24,16},{28,24},{20,28},{12,20},{4,12},{0,4},{9,1},{1... | collective-permute-start | bytes 995336 | tf_op jit(solution)/shard_map/ppermute | solution.py:474
  111.3 14.4 %collective-permute-start.22 = (bf16[3,96,576]{2,1,0:T(8,128)(2,1)S(1)}, bf16[3,96,576]{2,1,0:T(8,128)(2,1)S(1)}, u32[]{:S(2)}, u32[]{:S(2)}) collective-permute-start(bf16[3,96,576]{2,1,0:T(8,128)(2,1)S(1)} %get-tuple-element.210), channel_id=1, source_target_pairs={{8,0},{16,8},{24,16},{28,24},{20,28},{12,20},{4,12},{0,4},{9,1},{1... | collective-permute-start | bytes 995336 | tf_op jit(solution)/shard_map/ppermute | solution.py:512
  111.8 13.9 %collective-permute-start.21 = (bf16[3,96,576]{2,1,0:T(8,128)(2,1)S(1)}, bf16[3,96,576]{2,1,0:T(8,128)(2,1)S(1)}, u32[]{:S(2)}, u32[]{:S(2)}) collective-permute-start(bf16[3,96,576]{2,1,0:T(8,128)(2,1)S(1)} %get-tuple-element.211), channel_id=1, source_target_pairs={{0,8},{8,16},{16,24},{24,28},{28,20},{20,12},{12,4},{4,0},{1,9},{9... | collective-permute-start | bytes 995336 | tf_op jit(solution)/shard_map/ppermute | solution.py:512
  125.8 9.8 %collective-permute-start.24 = (bf16[3,96,576]{2,1,0:T(8,128)(2,1)S(1)}, bf16[3,96,576]{2,1,0:T(8,128)(2,1)S(1)}, u32[]{:S(2)}, u32[]{:S(2)}) collective-permute-start(bf16[3,96,576]{2,1,0:T(8,128)(2,1)S(1)} %get-tuple-element.208), channel_id=1, source_target_pairs={{8,0},{16,8},{24,16},{28,24},{20,28},{12,20},{4,12},{0,4},{9,1},{1... | collective-permute-start | bytes 995336 | tf_op jit(solution)/shard_map/ppermute | solution.py:512
  126.3 9.4 %collective-permute-start.23 = (bf16[3,96,576]{2,1,0:T(8,128)(2,1)S(1)}, bf16[3,96,576]{2,1,0:T(8,128)(2,1)S(1)}, u32[]{:S(2)}, u32[]{:S(2)}) collective-permute-start(bf16[3,96,576]{2,1,0:T(8,128)(2,1)S(1)} %get-tuple-element.209), channel_id=1, source_target_pairs={{0,8},{8,16},{16,24},{24,28},{28,20},{20,12},{12,4},{4,0},{1,9},{9... | collective-permute-start | bytes 995336 | tf_op jit(solution)/shard_map/ppermute | solution.py:512
  135.6 22.6 %collective-permute-start.27 = (bf16[1152,768]{1,0:T(8,128)(2,1)S(1)}, bf16[1152,768]{1,0:T(8,128)(2,1)S(1)}, u32[]{:S(2)}, u32[]{:S(2)}) collective-permute-start(bf16[1152,768]{1,0:T(8,128)(2,1)S(1)} %first_grad.1.own), channel_id=1, source_target_pairs={{0,1},{1,0},{2,3},{3,2},{4,5},{5,4},{6,7},{7,6},{8,9},{9,8},{10,11... | collective-permute-start | bytes 5308424 | tf_op jit(solution)/shard_map/ppermute | solution.py:435
  135.8 11.0 %collective-permute-start.47 = (bf16[3,96,576]{2,1,0:T(8,128)(2,1)S(1)}, bf16[3,96,576]{2,1,0:T(8,128)(2,1)S(1)}, u32[]{:S(2)}, u32[]{:S(2)}) collective-permute-start(bf16[3,96,576]{2,1,0:T(8,128)(2,1)S(1)} %get-tuple-element.206), channel_id=1, source_target_pairs={{8,0},{16,8},{24,16},{28,24},{20,28},{12,20},{4,12},{0,4},{9,1},{1... | collective-permute-start | bytes 995336 | tf_op jit(solution)/shard_map/ppermute | solution.py:512
  136.2 10.7 %collective-permute-start.46 = (bf16[3,96,576]{2,1,0:T(8,128)(2,1)S(1)}, bf16[3,96,576]{2,1,0:T(8,128)(2,1)S(1)}, u32[]{:S(2)}, u32[]{:S(2)}) collective-permute-start(bf16[3,96,576]{2,1,0:T(8,128)(2,1)S(1)} %get-tuple-element.207), channel_id=1, source_target_pairs={{0,8},{8,16},{16,24},{24,28},{28,20},{20,12},{12,4},{4,0},{1,9},{9... | collective-permute-start | bytes 995336 | tf_op jit(solution)/shard_map/ppermute | solution.py:512
  147.1 11.0 %collective-permute-start.48 = (bf16[3,96,576]{2,1,0:T(8,128)(2,1)S(1)}, bf16[3,96,576]{2,1,0:T(8,128)(2,1)S(1)}, u32[]{:S(2)}, u32[]{:S(2)}) collective-permute-start(bf16[3,96,576]{2,1,0:T(8,128)(2,1)S(1)} %fusion.1), channel_id=1, source_target_pairs={{0,2},{2,0},{1,3},{3,1},{4,6},{6,4},{5,7},{7,5},{8,10},{10,8},{9,1... | collective-permute-start | bytes 995336 | tf_op jit(solution)/shard_map/ppermute | solution.py:435
  155.2 26.2 %collective-permute-start.33 = (bf16[1024,768]{1,0:T(8,128)(2,1)S(1)}, bf16[1024,768]{1,0:T(8,128)(2,1)S(1)}, u32[]{:S(2)}, u32[]{:S(2)}) collective-permute-start(bf16[1024,768]{1,0:T(8,128)(2,1)S(1)} %feed_out.1.feed_own), channel_id=1, source_target_pairs={{0,1},{1,0},{2,3},{3,2},{4,5},{5,4},{6,7},{7,6},{8,9},{9,8},{10,11... | collective-permute-start | bytes 4718600 | tf_op jit(solution)/shard_map/ppermute | solution.py:435
  176.5 10.8 %collective-permute-start.43 = (bf16[2,96,384]{2,1,0:T(8,128)(2,1)S(1)}, bf16[2,96,384]{2,1,0:T(8,128)(2,1)S(1)}, u32[]{:S(2)}, u32[]{:S(2)}) collective-permute-start(bf16[2,96,384]{2,1,0:T(8,128)(2,1)S(1)} %get-tuple-element.212), channel_id=1, source_target_pairs={{8,0},{16,8},{24,16},{28,24},{20,28},{12,20},{4,12},{0,4},{9,1},{1... | collective-permute-start | bytes 442376 | tf_op jit(solution)/shard_map/ppermute | solution.py:512
  177.5 9.8 %collective-permute-start.42 = (bf16[2,96,384]{2,1,0:T(8,128)(2,1)S(1)}, bf16[2,96,384]{2,1,0:T(8,128)(2,1)S(1)}, u32[]{:S(2)}, u32[]{:S(2)}) collective-permute-start(bf16[2,96,384]{2,1,0:T(8,128)(2,1)S(1)} %get-tuple-element.213), channel_id=1, source_target_pairs={{0,8},{8,16},{16,24},{24,28},{28,20},{20,12},{12,4},{4,0},{1,9},{9... | collective-permute-start | bytes 442376 | tf_op jit(solution)/shard_map/ppermute | solution.py:512
  179.3 8.0 %collective-permute-start.35 = (bf16[2,96,384]{2,1,0:T(8,128)(2,1)S(1)}, bf16[2,96,384]{2,1,0:T(8,128)(2,1)S(1)}, u32[]{:S(2)}, u32[]{:S(2)}) collective-permute-start(bf16[2,96,384]{2,1,0:T(8,128)(2,1)S(1)} %get-tuple-element.220), channel_id=1, source_target_pairs={{8,0},{16,8},{24,16},{28,24},{20,28},{12,20},{4,12},{0,4},{9,1},{1... | collective-permute-start | bytes 442376 | tf_op jit(solution)/shard_map/ppermute | solution.py:512
  (33 other events, 280.8 us)

commit v9 on v8

--- a/solution.py
+++ b/solution.py
@@ -14,6 +14,7 @@
 HALF = WINDOW // 2
 PAD = 16
 SPARE = 6
+SHARE = 8
 BLOCK = 128
 LANES = 128
 KEYS = BLOCK + WINDOW
@@ -52,7 +53,7 @@
         out_specs=[vmem] * len(out_shape),
         scratch_shapes=scratch,
         compiler_params=pltpu.CompilerParams(vmem_limit_bytes=limit),
-        cost_estimate=pl.CostEstimate(flops=flops, bytes_accessed=moved, transcendentals=0),
+        cost_estimate=pl.CostEstimate(flops=flops // SHARE, bytes_accessed=moved // SHARE, transcendentals=0),
         name=name,
     )(*scalars, *args)
 
@@ -134,7 +135,10 @@
     pairs = local // LANES
     groups = slots.shape[0]
     depth = width // groups
-    plan = piece_plan(groups, [depth] * 4 + [PAD], 2)
+    half = piece_plan(groups, [depth] * 2, 1)
+    later = piece_plan(groups, [depth] * 2 + [PAD], 1)
+    shift = groups + 1
+    plan = [one + tuple((piece + shift, row) for piece, row in two) for one, two in zip(half, later)]
     lane = lax.broadcasted_iota(jnp.int32, (LANES, width), 1) - lax.broadcasted_iota(jnp.int32, (LANES, width), 0)
     gain_sum = jnp.zeros((PAD, width), f32)
     for number, sources in enumerate(plan):
@@ -359,26 +363,31 @@
     loop(extent // BLOCK, turn_step)
 
 
-def grad_kernel(slots, first, low_mid, attended, *rest):
-    parts, (grad_proj, grads_a, grads_b, total) = rest[:-4], rest[-4:]
-    local = attended.shape[1]
-    width = first.shape[1]
-    depth = grads_a.shape[2]
+def grad_kernel_one(slots, first, *rest):
+    parts, (grad_proj, grads, total) = rest[:-3], rest[-3:]
+    local = len(parts) * LANES
     for pair, part in enumerate(parts):
         for number in range(3):
             lanes = slice(number * local + pair * LANES, number * local + (pair + 1) * LANES)
             grad_proj[:, lanes] = part[:, number * LANES : (number + 1) * LANES]
+    weight_grads([(first, grad_proj.at[:, at * local : (at + 1) * local]) for at in range(2)], slots, grads, total)
+
+
+def grad_kernel_two(slots, first, grad_proj, low_mid, attended, grads, total):
+    local = attended.shape[1]
+    weight_grads([(first, grad_proj.at[:, 2 * local :]), (low_mid, attended)], slots, grads, total)
+
+
+def weight_grads(sides, slots, grads, total):
+    width = total.shape[1]
+    depth = grads.shape[2]
     step_rows = step_of(width, 256)
-    for start in range(0, width, step_rows):
-        here = slice(start, start + step_rows)
-        for number in range(3):
-            lanes = slice(number * local, (number + 1) * local)
-            total[number, here, :] = dot(first[:, here], grad_proj[:, lanes], TN).astype(bf16)
-        total[3, here, :] = dot(low_mid[:, here], attended[...], TN).astype(bf16)
-    for number, slot in enumerate(hop_order(grads_a.shape[0])):
-        place = pl.ds(pl.multiple_of(slots[slot] * depth, depth), depth)
-        grads_a[number] = total[:2, place, :]
-        grads_b[number] = total[2:, place, :]
+    for number, (left, right) in enumerate(sides):
+        for start in range(0, width, step_rows):
+            here = slice(start, start + step_rows)
+            total[number, here, :] = dot(left[:, here], right[...], TN).astype(bf16)
+    for number, slot in enumerate(hop_order(grads.shape[0])):
+        grads[number] = total[:, pl.ds(pl.multiple_of(slots[slot] * depth, depth), depth), :]
 
 
 def first_kernel(grad_proj, wide, partial):
@@ -458,6 +467,15 @@
     return held[0]
 
 
+def alternate(first, second):
+    if len(second.past) > 1:
+        first.after(second.past[-2])
+    first.hop()
+    if len(first.past) > 1:
+        second.after(first.past[-2])
+    second.hop()
+
+
 class RingGather:
     def __init__(self, block, cut):
         self.count, self.ahead, self.back, _ = ring()
@@ -465,6 +483,7 @@
         self.pieces = {0: (block,)}
         self.state = (block, block)
         self.hops = 0
+        self.past = []
 
     def hop(self):
         one, two = self.state
@@ -475,6 +494,7 @@
         self.hops += 1
         one, two = lax.optimization_barrier((one, two))
         self.state = (one, two)
+        self.past.append(self.state)
         if self.hops == middle:
             self.pieces[middle] = (one, two)
         else:
@@ -491,6 +511,7 @@
         self.axis = axis
         self.hops = 0
         self.state = ()
+        self.past = []
 
     def part(self, at):
         total = self.parts[0][at]
@@ -511,6 +532,7 @@
             one, two = self.part(at) + one, self.part(at + 1) + two
         one, two = lax.ppermute(one, "dp", self.ahead), lax.ppermute(two, "dp", self.back)
         self.state = lax.optimization_barrier((one, two))
+        self.past.append(self.state)
         self.hops += 1
 
     def after(self, others):
@@ -546,21 +568,24 @@
     depth = width // groups
     middle_hop = groups // 2
     gains = jnp.pad(jnp.stack([gain_one, gain_two]), ((0, PAD - 2), (0, local - depth)))
-    mine_one = jnp.concatenate([w_qkv.reshape(3 * depth, local), w_out.T, gains])
-    now = RingGather(mine_one, 2 * depth)
-    now.hop()
+    middle_hop = groups // 2
+    now = [
+        RingGather(w_qkv[:2].reshape(2 * depth, local), depth),
+        RingGather(jnp.concatenate([w_qkv[2], w_out.T, gains]), depth),
+    ]
+    alternate(*now)
     before, after = exchange(tokens[:HALF], tokens[rows - HALF :])
     slots = ring()[-1]
     cosine, sine, bounds = tables(lengths, rows)
-    while now.hops < middle_hop:
-        now.hop()
+    while now[0].hops < middle_hop:
+        alternate(*now)
     mine_two = jnp.concatenate([w_in.reshape(2 * depth, units), w_down.T])
-    later = RingGather(tied([mine_two], now.state)[0], depth)
+    later = RingGather(tied([mine_two], [*now[0].state, *now[1].past[-2]])[0], depth)
     later.hop()
     hat, = call(
         norm_kernel, [shape((extent, width), f32)], (tokens, before, after), rows * width * 2000, "first_norm"
     )
-    pieces = [piece for slot in range(groups) for piece in now.pieces[slot]]
+    pieces = [piece for chain in now for slot in range(groups) for piece in chain.pieces[slot]]
     wide, gain, first, query, key, value = call(
         project_kernel,
         [
@@ -578,7 +603,7 @@
     )
     early, late = tuple(range(pairs - 1)), (pairs - 1,)
 
-    query, key, value = tied([query, key, value], later.state)
+    query, key, value = locked([query, key, value], later)
     later.hop()
     shares_early, attended = call(
         functools.partial(attend_kernel, early, False),
@@ -602,8 +627,8 @@
         "attend",
         (bounds,),
     )
+    branch, = locked([branch], later)
     branch_other = swap(branch)
-    later.after([branch])
     while later.hops < middle_hop:
         later.hop()
     pieces = [piece for slot in range(groups) for piece in later.pieces[slot]]
@@ -656,15 +681,34 @@
     )
     grad_parts = locked(grad_parts, sums_two)
     sums_two.hop()
-    grad_proj, *grads_one = call(
-        grad_kernel,
-        [shape((extent, 3 * local), bf16)] + [shape((groups, 2, depth, local), bf16)] * 2,
-        (first, low_mid, attended, *grad_parts),
-        2 * rows * width * local * 6,
-        "attention_weight_grads",
+    grad_proj, grads_a = call(
+        grad_kernel_one,
+        [shape((extent, 3 * local), bf16), shape((groups, 2, depth, local), bf16)],
+        (first, *grad_parts),
+        2 * rows * width * local * 3,
+        "query_key_grads",
         (slots,),
-        [pltpu.VMEM((4, width, local), bf16)],
-    )
+        [pltpu.VMEM((2, width, local), bf16)],
+    )
+    first_part, = call(
+        first_kernel,
+        [shape((extent, width), bf16)],
+        (grad_proj, wide),
+        2 * rows * width * local * 3,
+        "first_grad",
+    )
+    first_other = swap(first_part)
+    low_mid, grad_value_proj = tied([low_mid, grad_proj], [first_part, *sums_two.state])
+    grads_b, = call(
+        grad_kernel_two,
+        [shape((groups, 2, depth, local), bf16)],
+        (first, grad_value_proj, low_mid, attended),
+        2 * rows * width * local * 3,
+        "value_out_grads",
+        (slots,),
+        [pltpu.VMEM((2, width, local), bf16)],
+    )
+    grads_one = [grads_a, grads_b]
     feed, = call(
         feed_out_kernel,
         [shape((rows, width), bf16)],
@@ -673,18 +717,9 @@
         "feed_out",
     )
     feed_other = swap(feed)
-    first_part, = call(
-        first_kernel,
-        [shape((extent, width), bf16)],
-        (grad_proj, wide),
-        2 * rows * width * local * 3,
-        "first_grad",
-    )
-    first_other = swap(first_part)
-    grads_one = tied(grads_one, [*sums_two.state, feed, first_part])
     sums_one = [RingScatter([part], 0) for part in grads_one]
-    sums_one[0].hop()
-    sums_one[1].hop()
+    alternate(*sums_one)
+    sums_two.after(sums_one[0].state)
     while sums_two.hops < middle_hop:
         sums_two.hop()
 
@@ -693,14 +728,11 @@
         return (first_part[here].astype(f32) + first_other[here].astype(f32)).astype(bf16)
 
     from_before, from_after = exchange(edge_sum(0), edge_sum(rows + HALF))
-    for chain in sums_one:
-        chain.after([from_before, from_after])
     while sums_one[0].hops < middle_hop - 1:
-        for chain in sums_one:
-            chain.hop()
+        alternate(*sums_one)
+    sums_one[1].after([from_before, from_after])
     tokens, = tied([tokens], sums_one[0].state)
-    for chain in sums_one:
-        chain.hop()
+    alternate(*sums_one)
     mixed, token_grad = call(
         final_kernel,
         [shape((rows, width), bf16), shape((rows, width), f32)],

time: 197 us -> 195 us (0.990)
  waiting for transfers between devices: 66.3 us -> 46.5 us
  local copies, waits for them, and re-layouts: 2.1 us -> 9.02 us
  starting transfers between devices: 49.2 us -> 55 us
  other arithmetic: 9.61 us -> 11.9 us
    ppermute x20 -> x24, waiting for transfers between devices: 30.9 us -> 19.2 us  [hop(): lax.ppermute(two, 'dp', self.back)]
    ppermute x20 -> x24, starting transfers between devices: 19.8 us -> 31.2 us  [hop(): lax.ppermute(two, 'dp', self.back)]
    ppermute x20 -> x24, waiting for transfers between devices: 27.7 us -> 18 us  [hop(): lax.ppermute(one, 'dp', self.ahead)]
    ppermute x20 -> x24, starting transfers between devices: 22.7 us -> 18.5 us  [hop(): lax.ppermute(one, 'dp', self.ahead)]
    ppermute x8, waiting for transfers between devices: 4.65 us -> 8.33 us  [swap(): return lax.ppermute(array, axis, [(0, 1), (1, 0)])]
    unnamed x14 -> x40, local copies, waits for them, and re-layouts: 0.03 us -> 3.36 us
    ppermute x2, waiting for transfers between devices: 3.05 us -> 0.98 us  [exchange(): lax.ppermute(jnp.where(spot == 0, last, initial), 'ctx', [(0, 1), (1, 0)])]
    pallas_call x12 -> x13, Pallas kernels: 69 us -> 70.5 us  [call(): pl.pallas_call(kernel, out_shape=out_shape, in_specs=[smem] * len(scalars...]
  transfers between devices with their start and end apart: 50 -> 58, of which waited for: 31 -> 30; matrix products, arithmetic and copies ran while one was open for 4% -> 8% of each run, Pallas kernels for 26% -> 31%
where the time goes in v9:
time: 195 us; the launch traced here: 194 us
  Pallas kernels  70.5 us (36%)
  starting transfers between devices  55 us (28%)
  waiting for transfers between devices  46.5 us (24%)
  other arithmetic  11.9 us (6%)
  local copies, waits for them, and re-layouts  9.02 us (5%)
    pallas_call x13, Pallas kernels, call(): pl.pallas_call(kernel, out_shape=out_shape, in_specs=[smem] * len(scalars...  70.5 us
    ppermute x24, starting transfers between devices, hop(): lax.ppermute(two, 'dp', self.back)  31.2 us
    ppermute x24, waiting for transfers between devices, hop(): lax.ppermute(two, 'dp', self.back)  19.2 us
    ppermute x24, starting transfers between devices, hop(): lax.ppermute(one, 'dp', self.ahead)  18.5 us
    ppermute x24, waiting for transfers between devices, hop(): lax.ppermute(one, 'dp', self.ahead)  18 us
    ppermute x8, waiting for transfers between devices, swap(): return lax.ppermute(array, axis, [(0, 1), (1, 0)])  8.33 us
  transfers between devices with their start and end apart: 58, of which 30 were waited for; matrix products, arithmetic and copies ran while one was open for 8% of the time, Pallas kernels for 31%

profile of v9, /device:TPU:0, one launch (start us, length us, event | category | flops | bytes accessed | tf_op | source)
XLA Modules:
  0.0 194.2 jit_solution(9930496134069843989)
XLA Ops:
  1.6 3.0 %collective-permute-start.2 = (bf16[192,384]{1,0:T(8,128)(2,1)S(1)}, bf16[192,384]{1,0:T(8,128)(2,1)S(1)}, u32[]{:S(2)}, u32[]{:S(2)}) collective-permute-start(bf16[192,384]{1,0:T(8,128)(2,1)S(1)} %bitcast.102), channel_id=1, source_target_pairs={{8,0},{16,8},{24,16},{28,24},{20,28},{12,20},{4,12},{0,4},{9,1},{1... | collective-permute-start | bytes 442376 | tf_op jit(solution)/shard_map/ppermute | solution.py:493
  28.2 2.1 %negate_select_fusion = (f32[1152,128]{1,0:T(8,128)S(1)}, f32[1152,128]{1,0:T(8,128)S(1)}) fusion(f32[128]{0:T(128)S(1)} %fusion.21, f32[1152]{0:T(1024)S(1)} %subtract_convert_fusion, pred[128]{0:T(512)(128)(4,1)S(1)} %fusion.22), kind=kLoop, calls=%fused_computation | loop fusion | flops 442368 | bytes 1184896 | tf_op jit(solution)/shard_map/jit(_where)/select_n | solution.py:558
  33.6 2.0 %collective-permute-done.12.rest_5_ = bf16[96,384]{1,0:T(8,128)(2,1)S(1)} collective-permute-done((bf16[96,384]{1,0:T(8,128)(2,1)S(1)}, bf16[96,384]{1,0:T(8,128)(2,1)S(1)}, u32[]{:S(2)}, u32[]{:S(2)}) %collective-permute-start.12) | collective-permute-done | bytes 73760 | tf_op jit(solution)/shard_map/ppermute | solution.py:493
  44.7 2.0 %first_norm.1.hat = f32[1152,768]{1,0:T(8,128)S(1)} custom-call(bf16[1024,768]{1,0:T(8,128)(2,1)S(1)} %copy-done, bf16[64,768]{1,0:T(8,128)(2,1)S(1)} %get-tuple-element.293.before, bf16[64,768]{1,0:T(8,128)(2,1)S(1)} %get-tuple-element.292.after), custom_call_target="tpu_custom_call" | custom-call | flops 196608000 | bytes 663552 | tf_op jit(solution)/shard_map/first_norm/pallas_call | solution.py:49
  47.7 6.5 %project.1 = (bf16[768,1536]{1,0:T(8,128)(2,1)S(1)}, f32[16,768]{1,0:T(8,128)S(1)}, bf16[1152,768]{1,0:T(8,128)(2,1)S(1)}, bf16[1024,384]{1,0:T(8,128)(2,1)S(1)}...) custom-call(s32[8]{0:T(128)S(1)} %compare_select_fusion.2.slots, f32[1152,768]{1,0:T(8,128)S(1)} %first_norm.1.hat, ...), custom_call_target="tpu_custom_call" | custom-call | flops 603979776 | bytes 1738752 | tf_op jit(solution)/shard_map/project/pallas_call | solution.py:49
  56.3 7.7 %attend.2 = (bf16[16,256,256]{2,1,0:T(8,128)(2,1)S(1)}, bf16[1024,384]{1,0:T(8,128)(2,1)S(1)}) custom-call(s32[5]{0:T(128)S(1)} %pad_add_fusion.bounds, bf16[1024,384]{1,0:T(8,128)(2,1)S(1)} %get-tuple-element.168.query, bf16[1152,384]{1,0:T(8,128)(2,1)S(1)} %get-tuple-element.169.key, bf16[1152,384]{1,0:T(8,128)(2,1)S(1)} %get-tuple-element.170.value), custom_call_target="tpu_custom_call" | custom-call | flops 754974720 | bytes 679936 | tf_op jit(solution)/shard_map/attend/pallas_call | solution.py:49
  67.5 6.6 %attend.3 = (bf16[8,256,256]{2,1,0:T(8,128)(2,1)S(1)}, bf16[1024,384]{1,0:T(8,128)(2,1)S(1)}, bf16[1024,768]{1,0:T(8,128)(2,1)S(1)}) custom-call(s32[5]{0:T(128)S(1)} %pad_add_fusion.bounds, bf16[1024,384]{1,0:T(8,128)(2,1)S(1)} %get-tuple-element.168.query, bf16[1152,384]{1,0:T(8,128)(2,1)S(1)} %get-tuple-element.169.key, ...), custom_call_target="tpu_custom_call" | custom-call | flops 528482304 | bytes 1138688 | tf_op jit(solution)/shard_map/attend/pallas_call | solution.py:49
  77.4 3.8 %collective-permute-done.24.rest_4_ = bf16[96,576]{1,0:T(8,128)(2,1)S(1)} collective-permute-done((bf16[96,576]{1,0:T(8,128)(2,1)S(1)}, bf16[96,576]{1,0:T(8,128)(2,1)S(1)}, u32[]{:S(2)}, u32[]{:S(2)}) %collective-permute-start.24) | collective-permute-done | bytes 110624 | tf_op jit(solution)/shard_map/ppermute | solution.py:493
  81.3 2.5 %collective-permute-done.25.rest_5_ = bf16[192,576]{1,0:T(8,128)(2,1)S(1)} collective-permute-done((bf16[192,576]{1,0:T(8,128)(2,1)S(1)}, bf16[192,576]{1,0:T(8,128)(2,1)S(1)}, u32[]{:S(2)}, u32[]{:S(2)}) %collective-permute-start.25) | collective-permute-done | bytes 221216 | tf_op jit(solution)/shard_map/ppermute | solution.py:493
  83.8 10.8 %feed_forward_and_back.1 = (f32[1024,768]{1,0:T(8,128)S(1)}, bf16[1024,768]{1,0:T(8,128)(2,1)S(1)}, bf16[1024,576]{1,0:T(8,128)(2,1)S(1)}, bf16[1024,576]{1,0:T(...) custom-call(s32[8]{0:T(128)S(1)} %compare_select_fusion.2.slots, ...), custom_call_target="tpu_custom_call" | custom-call | flops 905969664 | bytes 2684928 | tf_op jit(solution)/shard_map/feed_forward_and_back/pallas_call | solution.py:49
  94.6 4.7 %feed_weight_grads.1 = bf16[8,3,96,576]{3,2,1,0:T(8,128)(2,1)S(1)} custom-call(s32[8]{0:T(128)S(1)} %compare_select_fusion.2.slots, bf16[1024,768]{1,0:T(8,128)(2,1)S(1)} %get-tuple-element.192.second, bf16[1024,576]{1,0:T(8,128)(2,1)S(1)} %get-tuple-element.234.hidden, bf16[1024,576]{1,0:T(8,128)(2,1)S(1)} %get-tuple-element.194.grad_gate, ...), custom_call_target="tpu_custom_call" | custom-call | flops 566231040 | bytes 1167360 | tf_op jit(solution)/shard_map/feed_weight_grads/pallas_call | solution.py:49
  101.5 3.5 %middle_grad.1 = (f32[1024,768]{1,0:T(8,128)S(1)}, bf16[1024,768]{1,0:T(8,128)(2,1)S(1)}, bf16[1024,384]{1,0:T(8,128)(2,1)S(1)}) custom-call(f32[1024,768]{1,0:T(8,128)S(1)} %get-tuple-element.189.middle, bf16[1024,768]{1,0:T(8,128)(2,1)S(1)} %get-tuple-element.190.own, bf16[1024,768]{1,0:T(8,128)(2,1)S(1)} %collective-permute-done.26.other, ...), custom_call_target="tpu_custom_call" | custom-call | flops 301989888 | bytes 1972224 | tf_op jit(solution)/shard_map/middle_grad/pallas_call | solution.py:49
  108.7 12.2 %attention_back.1 = (bf16[1152,384]{1,0:T(8,128)(2,1)S(1)}, bf16[1152,384]{1,0:T(8,128)(2,1)S(1)}, bf16[1152,384]{1,0:T(8,128)(2,1)S(1)}) custom-call(bf16[1024,384]{1,0:T(8,128)(2,1)S(1)} %get-tuple-element.168.query, bf16[1152,384]{1,0:T(8,128)(2,1)S(1)} %get-tuple-element.169.key, bf16[1152,384]{1,0:T(8,128)(2,1)S(1)} %get-tuple-element.170.value, ...), custom_call_target="tpu_custom_call" | custom-call | flops 1132462080 | bytes 1290240 | tf_op jit(solution)/shard_map/attention_back/pallas_call | solution.py:49
  123.2 3.0 %query_key_grads.1 = (bf16[1152,1152]{1,0:T(8,128)(2,1)S(1)}, bf16[8,2,96,384]{3,2,1,0:T(8,128)(2,1)S(1)}) custom-call(s32[8]{0:T(128)S(1)} %compare_select_fusion.2.slots, bf16[1152,768]{1,0:T(8,128)(2,1)S(1)} %get-tuple-element.161.first, bf16[1152,384]{1,0:T(8,128)(2,1)S(1)} %get-tuple-element.209.rest_0_, ...), custom_call_target="tpu_custom_call" | custom-call | flops 226492416 | bytes 1032192 | tf_op jit(solution)/shard_map/query_key_grads/pallas_call | solution.py:49
  128.3 2.9 %first_grad.1.own = bf16[1152,768]{1,0:T(8,128)(2,1)S(1)} custom-call(bf16[1152,1152]{1,0:T(8,128)(2,1)S(1)} %get-tuple-element.223.grad_proj, bf16[768,1536]{1,0:T(8,128)(2,1)S(1)} %get-tuple-element.171.rest_0_.wide), custom_call_target="tpu_custom_call" | custom-call | flops 226492416 | bytes 847872 | tf_op jit(solution)/shard_map/first_grad/pallas_call | solution.py:49
  135.8 2.7 %value_out_grads.1 = bf16[8,2,96,384]{3,2,1,0:T(8,128)(2,1)S(1)} custom-call(s32[8]{0:T(128)S(1)} %compare_select_fusion.2.slots, bf16[1152,768]{1,0:T(8,128)(2,1)S(1)} %get-tuple-element.161.first, bf16[1152,1152]{1,0:T(8,128)(2,1)S(1)} %get-tuple-element.223.grad_proj, bf16[1024,768]{1,0:T(8,128)(2,1)S(1)} %get-tuple-element.224.low_mid, ...), custom_call_target="tpu_custom_call" | custom-call | flops 226492416 | bytes 995328 | tf_op jit(solution)/shard_map/value_out_grads/pallas_call | solution.py:49
  141.2 2.0 %feed_out.1.feed_own = bf16[1024,768]{1,0:T(8,128)(2,1)S(1)} custom-call(bf16[1024,576]{1,0:T(8,128)(2,1)S(1)} %get-tuple-element.234.hidden, bf16[3,768,576]{2,1,0:T(8,128)(2,1)S(1)} %get-tuple-element.235.whole), custom_call_target="tpu_custom_call" | custom-call | flops 113246208 | bytes 675840 | tf_op jit(solution)/shard_map/feed_out/pallas_call | solution.py:49
  148.7 2.5 %collective-permute-done.45 = bf16[2,96,384]{2,1,0:T(8,128)(2,1)S(1)} collective-permute-done((bf16[2,96,384]{2,1,0:T(8,128)(2,1)S(1)}, bf16[2,96,384]{2,1,0:T(8,128)(2,1)S(1)}, u32[]{:S(2)}, u32[]{:S(2)}) %collective-permute-start.45) | collective-permute-done | bytes 147488 | tf_op jit(solution)/shard_map/ppermute | solution.py:533
  156.5 5.4 %collective-permute-done.55 = bf16[3,96,576]{2,1,0:T(8,128)(2,1)S(1)} collective-permute-done((bf16[3,96,576]{2,1,0:T(8,128)(2,1)S(1)}, bf16[3,96,576]{2,1,0:T(8,128)(2,1)S(1)}, u32[]{:S(2)}, u32[]{:S(2)}) %collective-permute-start.55) | collective-permute-done | bytes 331808 | tf_op jit(solution)/shard_map/ppermute | solution.py:533
  164.8 2.2 %collective-permute-done.46 = bf16[2,96,384]{2,1,0:T(8,128)(2,1)S(1)} collective-permute-done((bf16[2,96,384]{2,1,0:T(8,128)(2,1)S(1)}, bf16[2,96,384]{2,1,0:T(8,128)(2,1)S(1)}, u32[]{:S(2)}, u32[]{:S(2)}) %collective-permute-start.46) | collective-permute-done | bytes 147488 | tf_op jit(solution)/shard_map/ppermute | solution.py:533
  167.7 2.3 %collective-permute-done.48 = bf16[2,96,384]{2,1,0:T(8,128)(2,1)S(1)} collective-permute-done((bf16[2,96,384]{2,1,0:T(8,128)(2,1)S(1)}, bf16[2,96,384]{2,1,0:T(8,128)(2,1)S(1)}, u32[]{:S(2)}, u32[]{:S(2)}) %collective-permute-start.48) | collective-permute-done | bytes 147488 | tf_op jit(solution)/shard_map/ppermute | solution.py:533
  170.6 3.9 %collective-permute-done.56 = bf16[3,96,576]{2,1,0:T(8,128)(2,1)S(1)} collective-permute-done((bf16[3,96,576]{2,1,0:T(8,128)(2,1)S(1)}, bf16[3,96,576]{2,1,0:T(8,128)(2,1)S(1)}, u32[]{:S(2)}, u32[]{:S(2)}) %collective-permute-start.56) | collective-permute-done | bytes 331808 | tf_op jit(solution)/shard_map/ppermute | solution.py:444
  178.7 5.9 %token_grad.1 = (bf16[1024,768]{1,0:T(8,128)(2,1)}, f32[1024,768]{1,0:T(8,128)}) custom-call(bf16[1024,768]{1,0:T(8,128)(2,1)S(1)} %copy-done, f32[16,768]{1,0:T(8,128)S(1)} %get-tuple-element.184.gain, f32[1024,768]{1,0:T(8,128)S(1)} %get-tuple-element.233.grad_middle, bf16[1152,768]{1,0:T(8,128)(2,1)S(1)} %first_grad.1.own, ...), custom_call_target="tpu_custom_call" | custom-call | flops 196608000 | bytes 2439168 | tf_op jit(solution)/shard_map/token_grad/pallas_call | solution.py:49
  187.5 2.4 %collective-permute-done.52 = bf16[2,96,384]{2,1,0:T(8,128)(2,1)S(1)} collective-permute-done((bf16[2,96,384]{2,1,0:T(8,128)(2,1)S(1)}, bf16[2,96,384]{2,1,0:T(8,128)(2,1)S(1)}, u32[]{:S(2)}, u32[]{:S(2)}) %collective-permute-start.52) | collective-permute-done | bytes 147488 | tf_op jit(solution)/shard_map/ppermute | solution.py:444
  (197 shorter events, 90.2 us)
Async XLA Ops:
  1.6 12.9 %collective-permute-start.2 = (bf16[192,384]{1,0:T(8,128)(2,1)S(1)}, bf16[192,384]{1,0:T(8,128)(2,1)S(1)}, u32[]{:S(2)}, u32[]{:S(2)}) collective-permute-start(bf16[192,384]{1,0:T(8,128)(2,1)S(1)} %bitcast.102), channel_id=1, source_target_pairs={{8,0},{16,8},{24,16},{28,24},{20,28},{12,20},{4,12},{0,4},{9,1},{1... | collective-permute-start | bytes 442376 | tf_op jit(solution)/shard_map/ppermute | solution.py:493
  4.6 9.9 %collective-permute-start.1 = (bf16[192,384]{1,0:T(8,128)(2,1)S(1)}, bf16[192,384]{1,0:T(8,128)(2,1)S(1)}, u32[]{:S(2)}, u32[]{:S(2)}) collective-permute-start(bf16[192,384]{1,0:T(8,128)(2,1)S(1)} %bitcast.103), channel_id=1, source_target_pairs={{0,8},{8,16},{16,24},{24,28},{28,20},{20,12},{12,4},{4,0},{1,9},{9... | collective-permute-start | bytes 442376 | tf_op jit(solution)/shard_map/ppermute | solution.py:493
  7.2 10.7 %collective-permute-start.6 = (bf16[208,384]{1,0:T(8,128)(2,1)S(1)}, bf16[208,384]{1,0:T(8,128)(2,1)S(1)}, u32[]{:S(2)}, u32[]{:S(2)}) collective-permute-start(bf16[208,384]{1,0:T(8,128)(2,1)S(1)} %pad_maximum_fusion.2.rest_9_), channel_id=1, source_target_pairs={{8,0},{16,8},{24,16},{28,24},{20,28},{12,20},{4,12},{0,4},{9,1},{1... | collective-permute-start | bytes 479240 | tf_op jit(solution)/shard_map/ppermute | solution.py:493
  9.1 8.8 %collective-permute-start.5 = (bf16[208,384]{1,0:T(8,128)(2,1)S(1)}, bf16[208,384]{1,0:T(8,128)(2,1)S(1)}, u32[]{:S(2)}, u32[]{:S(2)}) collective-permute-start(bf16[208,384]{1,0:T(8,128)(2,1)S(1)} %pad_maximum_fusion.2.rest_9_), channel_id=1, source_target_pairs={{0,8},{8,16},{16,24},{24,28},{28,20},{20,12},{12,4},{4,0},{1,9},{9... | collective-permute-start | bytes 479240 | tf_op jit(solution)/shard_map/ppermute | solution.py:493
  11.0 32.7 %collective-permute-start = (bf16[64,768]{1,0:T(8,128)(2,1)}, bf16[64,768]{1,0:T(8,128)(2,1)}, u32[]{:S(2)}, u32[]{:S(2)}) collective-permute-start(bf16[64,768]{1,0:T(8,128)(2,1)} %slice_select_fusion), channel_id=1, source_target_pairs={{0,2},{2,0},{1,3},{3,1},{4,6},{6,4},{5,7},{7,5},{8,10},{10,8},{9,1... | collective-permute-start | bytes 294920 | tf_op jit(solution)/shard_map/ppermute | solution.py:430
  17.9 8.1 %collective-permute-start.9 = (bf16[208,384]{1,0:T(8,128)(2,1)S(1)}, bf16[208,384]{1,0:T(8,128)(2,1)}, u32[]{:S(2)}, u32[]{:S(2)}) collective-permute-start(bf16[208,384]{1,0:T(8,128)(2,1)S(1)} %collective-permute-done.5.rest_17_), channel_id=1, source_target_pairs={{0,8},{8,16},{16,24},{24,28},{28,20},{20,12},{12,4},{4,0},{1,9},{9... | collective-permute-start | bytes 479240 | tf_op jit(solution)/shard_map/ppermute | solution.py:493
  37.7 16.4 %collective-permute-start.18 = (bf16[288,576]{1,0:T(8,128)(2,1)S(1)}, bf16[288,576]{1,0:T(8,128)(2,1)}, u32[]{:S(2)}, u32[]{:S(2)}) collective-permute-start(bf16[288,576]{1,0:T(8,128)(2,1)S(1)} %pad_maximum_fusion.1.rest_0_), channel_id=1, source_target_pairs={{8,0},{16,8},{24,16},{28,24},{20,28},{12,20},{4,12},{0,4},{9,1},{1... | collective-permute-start | bytes 995336 | tf_op jit(solution)/shard_map/ppermute | solution.py:493
  39.3 14.8 %collective-permute-start.17 = (bf16[288,576]{1,0:T(8,128)(2,1)S(1)}, bf16[288,576]{1,0:T(8,128)(2,1)}, u32[]{:S(2)}, u32[]{:S(2)}) collective-permute-start(bf16[288,576]{1,0:T(8,128)(2,1)S(1)} %pad_maximum_fusion.1.rest_0_), channel_id=1, source_target_pairs={{0,8},{8,16},{16,24},{24,28},{28,20},{20,12},{12,4},{4,0},{1,9},{9... | collective-permute-start | bytes 995336 | tf_op jit(solution)/shard_map/ppermute | solution.py:493
  54.1 10.3 %collective-permute-start.19 = (bf16[288,576]{1,0:T(8,128)(2,1)}, bf16[288,576]{1,0:T(8,128)(2,1)S(1)}, u32[]{:S(2)}, u32[]{:S(2)}) collective-permute-start(bf16[288,576]{1,0:T(8,128)(2,1)} %collective-permute-done.17.rest_8_), channel_id=1, source_target_pairs={{0,8},{8,16},{16,24},{24,28},{28,20},{20,12},{12,4},{4,0},{1,9},{9... | collective-permute-start | bytes 995336 | tf_op jit(solution)/shard_map/ppermute | solution.py:493
  54.8 10.7 %collective-permute-start.20 = (bf16[288,576]{1,0:T(8,128)(2,1)}, bf16[288,576]{1,0:T(8,128)(2,1)S(1)}, u32[]{:S(2)}, u32[]{:S(2)}) collective-permute-start(bf16[288,576]{1,0:T(8,128)(2,1)} %collective-permute-done.18.rest_1_), channel_id=1, source_target_pairs={{8,0},{16,8},{24,16},{28,24},{20,28},{12,20},{4,12},{0,4},{9,1},{1... | collective-permute-start | bytes 995336 | tf_op jit(solution)/shard_map/ppermute | solution.py:493
  65.5 8.6 %collective-permute-start.21 = (bf16[288,576]{1,0:T(8,128)(2,1)S(1)}, bf16[288,576]{1,0:T(8,128)(2,1)S(1)}, u32[]{:S(2)}, u32[]{:S(2)}) collective-permute-start(bf16[288,576]{1,0:T(8,128)(2,1)S(1)} %collective-permute-done.19.rest_7_), channel_id=1, source_target_pairs={{0,8},{8,16},{16,24},{24,28},{28,20},{20,12},{12,4},{4,0},{1,9},{9... | collective-permute-start | bytes 995336 | tf_op jit(solution)/shard_map/ppermute | solution.py:493
  75.1 8.7 %collective-permute-start.23 = (bf16[1024,768]{1,0:T(8,128)(2,1)S(1)}, bf16[1024,768]{1,0:T(8,128)(2,1)S(1)}, u32[]{:S(2)}, u32[]{:S(2)}) collective-permute-start(bf16[1024,768]{1,0:T(8,128)(2,1)S(1)} %get-tuple-element.183.own), channel_id=1, source_target_pairs={{0,1},{1,0},{2,3},{3,2},{4,5},{5,4},{6,7},{7,6},{8,9},{9,8},{10,11... | collective-permute-start | bytes 4718600 | tf_op jit(solution)/shard_map/ppermute | solution.py:444
  75.1 8.7 %collective-permute-start.25 = (bf16[192,576]{1,0:T(8,128)(2,1)S(1)}, bf16[192,576]{1,0:T(8,128)(2,1)S(1)}, u32[]{:S(2)}, u32[]{:S(2)}) collective-permute-start(bf16[192,576]{1,0:T(8,128)(2,1)S(1)} %slice.147), channel_id=1, source_target_pairs={{8,0},{16,8},{24,16},{28,24},{20,28},{12,20},{4,12},{0,4},{9,1},{1... | collective-permute-start | bytes 663560 | tf_op jit(solution)/shard_map/ppermute | solution.py:493
  106.7 14.3 %collective-permute-start.30 = (bf16[3,96,576]{2,1,0:T(8,128)(2,1)S(1)}, bf16[3,96,576]{2,1,0:T(8,128)(2,1)S(1)}, u32[]{:S(2)}, u32[]{:S(2)}) collective-permute-start(bf16[3,96,576]{2,1,0:T(8,128)(2,1)S(1)} %get-tuple-element.270), channel_id=1, source_target_pairs={{8,0},{16,8},{24,16},{28,24},{20,28},{12,20},{4,12},{0,4},{9,1},{1... | collective-permute-start | bytes 995336 | tf_op jit(solution)/shard_map/ppermute | solution.py:533
  108.3 12.7 %collective-permute-start.29 = (bf16[3,96,576]{2,1,0:T(8,128)(2,1)S(1)}, bf16[3,96,576]{2,1,0:T(8,128)(2,1)S(1)}, u32[]{:S(2)}, u32[]{:S(2)}) collective-permute-start(bf16[3,96,576]{2,1,0:T(8,128)(2,1)S(1)} %get-tuple-element.271), channel_id=1, source_target_pairs={{0,8},{8,16},{16,24},{24,28},{28,20},{20,12},{12,4},{4,0},{1,9},{9... | collective-permute-start | bytes 995336 | tf_op jit(solution)/shard_map/ppermute | solution.py:533
  121.1 14.7 %collective-permute-start.36 = (bf16[3,96,576]{2,1,0:T(8,128)(2,1)S(1)}, bf16[3,96,576]{2,1,0:T(8,128)(2,1)S(1)}, u32[]{:S(2)}, u32[]{:S(2)}) collective-permute-start(bf16[3,96,576]{2,1,0:T(8,128)(2,1)S(1)} %get-tuple-element.268), channel_id=1, source_target_pairs={{8,0},{16,8},{24,16},{28,24},{20,28},{12,20},{4,12},{0,4},{9,1},{1... | collective-permute-start | bytes 995336 | tf_op jit(solution)/shard_map/ppermute | solution.py:533
  122.8 13.1 %collective-permute-start.35 = (bf16[3,96,576]{2,1,0:T(8,128)(2,1)S(1)}, bf16[3,96,576]{2,1,0:T(8,128)(2,1)S(1)}, u32[]{:S(2)}, u32[]{:S(2)}) collective-permute-start(bf16[3,96,576]{2,1,0:T(8,128)(2,1)S(1)} %get-tuple-element.269), channel_id=1, source_target_pairs={{0,8},{8,16},{16,24},{24,28},{28,20},{20,12},{12,4},{4,0},{1,9},{9... | collective-permute-start | bytes 995336 | tf_op jit(solution)/shard_map/ppermute | solution.py:533
  140.6 29.4 %collective-permute-start.41 = (bf16[1152,768]{1,0:T(8,128)(2,1)S(1)}, bf16[1152,768]{1,0:T(8,128)(2,1)S(1)}, u32[]{:S(2)}, u32[]{:S(2)}) collective-permute-start(bf16[1152,768]{1,0:T(8,128)(2,1)S(1)} %first_grad.1.own), channel_id=1, source_target_pairs={{0,1},{1,0},{2,3},{3,2},{4,5},{5,4},{6,7},{7,6},{8,9},{9,8},{10,11... | collective-permute-start | bytes 5308424 | tf_op jit(solution)/shard_map/ppermute | solution.py:444
  146.5 7.9 %collective-permute-start.40 = (bf16[2,96,384]{2,1,0:T(8,128)(2,1)S(1)}, bf16[2,96,384]{2,1,0:T(8,128)(2,1)S(1)}, u32[]{:S(2)}, u32[]{:S(2)}) collective-permute-start(bf16[2,96,384]{2,1,0:T(8,128)(2,1)S(1)} %get-tuple-element.280), channel_id=1, source_target_pairs={{8,0},{16,8},{24,16},{28,24},{20,28},{12,20},{4,12},{0,4},{9,1},{1... | collective-permute-start | bytes 442376 | tf_op jit(solution)/shard_map/ppermute | solution.py:533
  151.3 10.6 %collective-permute-start.55 = (bf16[3,96,576]{2,1,0:T(8,128)(2,1)S(1)}, bf16[3,96,576]{2,1,0:T(8,128)(2,1)S(1)}, u32[]{:S(2)}, u32[]{:S(2)}) collective-permute-start(bf16[3,96,576]{2,1,0:T(8,128)(2,1)S(1)} %get-tuple-element.266), channel_id=1, source_target_pairs={{8,0},{16,8},{24,16},{28,24},{20,28},{12,20},{4,12},{0,4},{9,1},{1... | collective-permute-start | bytes 995336 | tf_op jit(solution)/shard_map/ppermute | solution.py:533
  152.3 9.9 %collective-permute-start.54 = (bf16[3,96,576]{2,1,0:T(8,128)(2,1)S(1)}, bf16[3,96,576]{2,1,0:T(8,128)(2,1)S(1)}, u32[]{:S(2)}, u32[]{:S(2)}) collective-permute-start(bf16[3,96,576]{2,1,0:T(8,128)(2,1)S(1)} %get-tuple-element.267), channel_id=1, source_target_pairs={{0,8},{8,16},{16,24},{24,28},{28,20},{20,12},{12,4},{4,0},{1,9},{9... | collective-permute-start | bytes 995336 | tf_op jit(solution)/shard_map/ppermute | solution.py:533
  154.4 24.3 %collective-permute-start.43 = (bf16[1024,768]{1,0:T(8,128)(2,1)S(1)}, bf16[1024,768]{1,0:T(8,128)(2,1)S(1)}, u32[]{:S(2)}, u32[]{:S(2)}) collective-permute-start(bf16[1024,768]{1,0:T(8,128)(2,1)S(1)} %feed_out.1.feed_own), channel_id=1, source_target_pairs={{0,1},{1,0},{2,3},{3,2},{4,5},{5,4},{6,7},{7,6},{8,9},{9,8},{10,11... | collective-permute-start | bytes 4718600 | tf_op jit(solution)/shard_map/ppermute | solution.py:444
  155.3 9.5 %collective-permute-start.47 = (bf16[2,96,384]{2,1,0:T(8,128)(2,1)S(1)}, bf16[2,96,384]{2,1,0:T(8,128)(2,1)S(1)}, u32[]{:S(2)}, u32[]{:S(2)}) collective-permute-start(bf16[2,96,384]{2,1,0:T(8,128)(2,1)S(1)} %get-tuple-element.276), channel_id=1, source_target_pairs={{8,0},{16,8},{24,16},{28,24},{20,28},{12,20},{4,12},{0,4},{9,1},{1... | collective-permute-start | bytes 442376 | tf_op jit(solution)/shard_map/ppermute | solution.py:533
  175.7 8.9 %collective-permute-start.51 = (bf16[2,96,384]{2,1,0:T(8,128)(2,1)S(1)}, bf16[2,96,384]{2,1,0:T(8,128)(2,1)S(1)}, u32[]{:S(2)}, u32[]{:S(2)}) collective-permute-start(bf16[2,96,384]{2,1,0:T(8,128)(2,1)S(1)} %get-tuple-element.272), channel_id=1, source_target_pairs={{8,0},{16,8},{24,16},{28,24},{20,28},{12,20},{4,12},{0,4},{9,1},{1... | collective-permute-start | bytes 442376 | tf_op jit(solution)/shard_map/ppermute | solution.py:533
  (54 other events, 317.2 us)

commit v10 on v9

--- a/solution.py
+++ b/solution.py
@@ -135,10 +135,9 @@
     pairs = local // LANES
     groups = slots.shape[0]
     depth = width // groups
-    half = piece_plan(groups, [depth] * 2, 1)
-    later = piece_plan(groups, [depth] * 2 + [PAD], 1)
-    shift = groups + 1
-    plan = [one + tuple((piece + shift, row) for piece, row in two) for one, two in zip(half, later)]
+    half = piece_plan(groups, [depth] * 2, -1)
+    later = piece_plan(groups, [depth] * 2 + [PAD], -1)
+    plan = [one + tuple((piece + groups, row) for piece, row in two) for one, two in zip(half, later)]
     lane = lax.broadcasted_iota(jnp.int32, (LANES, width), 1) - lax.broadcasted_iota(jnp.int32, (LANES, width), 0)
     gain_sum = jnp.zeros((PAD, width), f32)
     for number, sources in enumerate(plan):
@@ -477,9 +476,10 @@
 
 
 class RingGather:
-    def __init__(self, block, cut):
+    def __init__(self, block, cut=0, way=None):
         self.count, self.ahead, self.back, _ = ring()
         self.cut = cut
+        self.way = way
         self.pieces = {0: (block,)}
         self.state = (block, block)
         self.hops = 0
@@ -488,6 +488,13 @@
     def hop(self):
         one, two = self.state
         middle = self.count // 2
+        if self.hops + 1 == middle and self.way is not None:
+            got = lax.ppermute((one, two)[self.way], "dp", (self.ahead, self.back)[self.way])
+            self.hops += 1
+            self.state = (got,)
+            self.past.append(self.state)
+            self.pieces[middle] = (got,)
+            return
         if self.hops + 1 == middle:
             one, two = one[: self.cut], two[self.cut :]
         one, two = lax.ppermute(one, "dp", self.ahead), lax.ppermute(two, "dp", self.back)
@@ -505,10 +512,11 @@
 
 
 class RingScatter:
-    def __init__(self, parts, axis):
+    def __init__(self, parts, axis=0, way=None):
         self.count, self.ahead, self.back, _ = ring()
         self.parts = parts
         self.axis = axis
+        self.way = way
         self.hops = 0
         self.state = ()
         self.past = []
@@ -520,16 +528,25 @@
         return total
 
     def hop(self):
+        if self.hops == 0 and self.way is not None:
+            got = lax.ppermute(self.part(0), "dp", (self.ahead, self.back)[self.way])
+            self.state = (got,)
+            self.past.append(self.state)
+            self.hops += 1
+            return
         if self.hops == 0:
             one, two = jnp.split(self.part(0), 2, axis=self.axis)
         else:
-            one, two = self.state
-            if self.hops == 1:
+            sides = [self.part(2 * self.hops - 1), self.part(2 * self.hops)]
+            if self.hops == 1 and self.way is not None:
+                sides[self.way] = sides[self.way] + self.state[0]
+            one, two = sides if self.hops == 1 and self.way is not None else self.state
+            if self.hops == 1 and self.way is None:
                 none = jnp.zeros_like(one)
                 one = jnp.concatenate([one, none], axis=self.axis)
                 two = jnp.concatenate([none, two], axis=self.axis)
-            at = 2 * self.hops - 1
-            one, two = self.part(at) + one, self.part(at + 1) + two
+            if self.hops > 1 or self.way is None:
+                one, two = sides[0] + one, sides[1] + two
         one, two = lax.ppermute(one, "dp", self.ahead), lax.ppermute(two, "dp", self.back)
         self.state = lax.optimization_barrier((one, two))
         self.past.append(self.state)
@@ -570,21 +587,23 @@
     gains = jnp.pad(jnp.stack([gain_one, gain_two]), ((0, PAD - 2), (0, local - depth)))
     middle_hop = groups // 2
     now = [
-        RingGather(w_qkv[:2].reshape(2 * depth, local), depth),
-        RingGather(jnp.concatenate([w_qkv[2], w_out.T, gains]), depth),
+        RingGather(w_qkv[:2].reshape(2 * depth, local), way=0),
+        RingGather(jnp.concatenate([w_qkv[2], w_out.T, gains]), way=1),
     ]
     alternate(*now)
     before, after = exchange(tokens[:HALF], tokens[rows - HALF :])
     slots = ring()[-1]
     cosine, sine, bounds = tables(lengths, rows)
+    hat, = call(
+        norm_kernel, [shape((extent, width), f32)], (tokens, before, after), rows * width * 2000, "first_norm"
+    )
+    alternate(*now)
+    now[1].after([hat])
     while now[0].hops < middle_hop:
         alternate(*now)
     mine_two = jnp.concatenate([w_in.reshape(2 * depth, units), w_down.T])
-    later = RingGather(tied([mine_two], [*now[0].state, *now[1].past[-2]])[0], depth)
+    later = RingGather(tied([mine_two], [*now[0].state, *now[1].state])[0], depth)
     later.hop()
-    hat, = call(
-        norm_kernel, [shape((extent, width), f32)], (tokens, before, after), rows * width * 2000, "first_norm"
-    )
     pieces = [piece for chain in now for slot in range(groups) for piece in chain.pieces[slot]]
     wide, gain, first, query, key, value = call(
         project_kernel,
@@ -698,6 +717,11 @@
         "first_grad",
     )
     first_other = swap(first_part)
+    def edge_sum(at):
+        here = slice(at, at + HALF)
+        return (first_part[here].astype(f32) + first_other[here].astype(f32)).astype(bf16)
+
+    from_before, from_after = exchange(edge_sum(0), edge_sum(rows + HALF))
     low_mid, grad_value_proj = tied([low_mid, grad_proj], [first_part, *sums_two.state])
     grads_b, = call(
         grad_kernel_two,
@@ -712,25 +736,21 @@
     feed, = call(
         feed_out_kernel,
         [shape((rows, width), bf16)],
-        (tied([hidden], grads_one)[0], whole),
+        (tied([hidden], [from_before, from_after])[0], whole),
         2 * rows * width * units,
         "feed_out",
     )
     feed_other = swap(feed)
-    sums_one = [RingScatter([part], 0) for part in grads_one]
+    sums_one = [RingScatter([part], way=way) for way, part in enumerate(grads_one)]
     alternate(*sums_one)
     sums_two.after(sums_one[0].state)
     while sums_two.hops < middle_hop:
         sums_two.hop()
 
-    def edge_sum(at):
-        here = slice(at, at + HALF)
-        return (first_part[here].astype(f32) + first_other[here].astype(f32)).astype(bf16)
-
-    from_before, from_after = exchange(edge_sum(0), edge_sum(rows + HALF))
     while sums_one[0].hops < middle_hop - 1:
+        if sums_one[0].hops == 2:
+            sums_one[1].after(sums_two.state)
         alternate(*sums_one)
-    sums_one[1].after([from_before, from_after])
     tokens, = tied([tokens], sums_one[0].state)
     alternate(*sums_one)
     mixed, token_grad = call(
@@ -741,8 +761,8 @@
         "token_grad",
     )
     two = over_ctx(sums_two.total())
-    one = tied([chain.total() for chain in sums_one], [mixed, token_grad])
-    one = jnp.concatenate([over_ctx(part) for part in one])
+    one = over_ctx(tied([sums_one[0].total()], [mixed, token_grad])[0])
+    one = jnp.concatenate([one, over_ctx(sums_one[1].total())])
     gain_one_grad = jnp.sum(one[:3] * w_qkv.astype(f32), axis=(0, 2)) / gain_one.astype(f32)
     gain_two_grad = jnp.sum(two[:2] * w_in.astype(f32), axis=(0, 2)) / gain_two.astype(f32)
     both = jnp.stack([gain_one_grad, gain_two_grad])

time: 195 us -> 211 us (1.082)
  local copies, waits for them, and re-layouts: 9.02 us -> 25 us
  waiting for transfers between devices: 46.5 us -> 49.9 us
  starting transfers between devices: 55 us -> 51.8 us
    unnamed x40 -> x74, local copies, waits for them, and re-layouts: 3.36 us -> 21.1 us
    ppermute x24 -> x20, starting transfers between devices: 31.2 us -> 14.4 us  [hop(): lax.ppermute(two, 'dp', self.back)]
    ppermute x24 -> x20, waiting for transfers between devices: 18 us -> 7.59 us  [hop(): lax.ppermute(one, 'dp', self.ahead)]
    ppermute x24 -> x20, starting transfers between devices: 18.5 us -> 28.1 us  [hop(): lax.ppermute(one, 'dp', self.ahead)]
    ppermute x0 -> x4, waiting for transfers between devices: none -> 9.22 us  [the longest x2 4.69 us: hop(): got = lax.ppermute(self.part(0), 'dp', (self.ahead, self.back)[self.way])]
    ppermute x24 -> x20, waiting for transfers between devices: 19.2 us -> 23.2 us  [hop(): lax.ppermute(two, 'dp', self.back)]
    ppermute x0 -> x4, starting transfers between devices: none -> 3.83 us  [the longest x2 2.25 us: hop(): got = lax.ppermute(self.part(0), 'dp', (self.ahead, self.back)[self.way])]
  transfers between devices with their start and end apart: 58 -> 54, of which waited for: 30 -> 24; matrix products, arithmetic and copies ran while one was open for 8% -> 6% of each run, Pallas kernels for 31% -> 27%
where the time goes in v10:
time: 211 us; the launch traced here: 210 us
  Pallas kernels  71.2 us (34%)
  starting transfers between devices  51.8 us (25%)
  waiting for transfers between devices  49.9 us (24%)
  local copies, waits for them, and re-layouts  25 us (12%)
  other arithmetic  11.2 us (5%)
    pallas_call x13, Pallas kernels, call(): pl.pallas_call(kernel, out_shape=out_shape, in_specs=[smem] * len(scalars...  71.2 us
    ppermute x20, starting transfers between devices, hop(): lax.ppermute(one, 'dp', self.ahead)  28.1 us
    ppermute x20, waiting for transfers between devices, hop(): lax.ppermute(two, 'dp', self.back)  23.2 us
    unnamed x74, local copies, waits for them, and re-layouts  21.1 us
    ppermute x20, starting transfers between devices, hop(): lax.ppermute(two, 'dp', self.back)  14.4 us
    ppermute x8, waiting for transfers between devices, swap(): return lax.ppermute(array, axis, [(0, 1), (1, 0)])  7.93 us
    ppermute x20, waiting for transfers between devices, hop(): lax.ppermute(one, 'dp', self.ahead)  7.59 us
    ppermute x2, waiting for transfers between devices, hop(): got = lax.ppermute(self.part(0), 'dp', (self.ahead, self.back)[self.way])  4.69 us
  transfers between devices with their start and end apart: 54, of which 24 were waited for; matrix products, arithmetic and copies ran while one was open for 6% of the time, Pallas kernels for 27%

profile of v10, /device:TPU:0, one launch (start us, length us, event | category | flops | bytes accessed | tf_op | source)
XLA Modules:
  0.0 210.3 jit_solution(9517516885009871007)
XLA Ops:
  1.6 3.0 %collective-permute-start.2 = (bf16[192,384]{1,0:T(8,128)(2,1)S(1)}, bf16[192,384]{1,0:T(8,128)(2,1)}, u32[]{:S(2)}, u32[]{:S(2)}) collective-permute-start(bf16[192,384]{1,0:T(8,128)(2,1)S(1)} %bitcast.96), channel_id=1, source_target_pairs={{8,0},{16,8},{24,16},{28,24},{20,28},{12,20},{4,12},{0,4},{9,1},{1... | collective-permute-start | bytes 442376 | tf_op jit(solution)/shard_map/ppermute | solution.py:500
  35.9 4.4 %collective-permute-done.14.rest_12_ = bf16[208,384]{1,0:T(8,128)(2,1)S(1)} collective-permute-done((bf16[208,384]{1,0:T(8,128)(2,1)S(1)}, bf16[208,384]{1,0:T(8,128)(2,1)S(1)}, u32[]{:S(2)}, u32[]{:S(2)}) %collective-permute-start.14) | collective-permute-done | bytes 159776 | tf_op jit(solution)/shard_map/ppermute | solution.py:492
  43.0 3.3 %negate_select_fusion = (f32[1152,128]{1,0:T(8,128)}, f32[1152,128]{1,0:T(8,128)}) fusion(f32[128]{0:T(128)S(1)} %fusion.20, f32[1152]{0:T(1024)S(1)} %subtract_convert_fusion, pred[128]{0:T(512)(128)(4,1)S(1)} %fusion.21), kind=kLoop, calls=%fused_computation | loop fusion | flops 442368 | bytes 1184896 | tf_op jit(solution)/shard_map/jit(_where)/select_n | solution.py:575
  59.4 6.4 %project.1 = (bf16[768,1536]{1,0:T(8,128)(2,1)S(1)}, f32[16,768]{1,0:T(8,128)S(1)}, bf16[1152,768]{1,0:T(8,128)(2,1)S(1)}, bf16[1024,384]{1,0:T(8,128)(2,1)S(1)}...) custom-call(s32[8]{0:T(128)S(1)} %compare_select_fusion.2.slots, f32[1152,768]{1,0:T(8,128)S(1)} %first_norm.1.hat, ...), custom_call_target="tpu_custom_call" | custom-call | flops 603979776 | bytes 1738752 | tf_op jit(solution)/shard_map/project/pallas_call | solution.py:49
  68.0 7.7 %attend.2 = (bf16[16,256,256]{2,1,0:T(8,128)(2,1)S(1)}, bf16[1024,384]{1,0:T(8,128)(2,1)S(1)}) custom-call(s32[5]{0:T(128)S(1)} %pad_add_fusion.bounds, bf16[1024,384]{1,0:T(8,128)(2,1)S(1)} %get-tuple-element.154.query, bf16[1152,384]{1,0:T(8,128)(2,1)S(1)} %get-tuple-element.155.key, bf16[1152,384]{1,0:T(8,128)(2,1)S(1)} %get-tuple-element.156.value), custom_call_target="tpu_custom_call" | custom-call | flops 754974720 | bytes 679936 | tf_op jit(solution)/shard_map/attend/pallas_call | solution.py:49
  79.9 6.6 %attend.3 = (bf16[8,256,256]{2,1,0:T(8,128)(2,1)S(1)}, bf16[1024,384]{1,0:T(8,128)(2,1)S(1)}, bf16[1024,768]{1,0:T(8,128)(2,1)S(1)}) custom-call(s32[5]{0:T(128)S(1)} %pad_add_fusion.bounds, bf16[1024,384]{1,0:T(8,128)(2,1)S(1)} %get-tuple-element.154.query, bf16[1152,384]{1,0:T(8,128)(2,1)S(1)} %get-tuple-element.155.key, ...), custom_call_target="tpu_custom_call" | custom-call | flops 528482304 | bytes 1138688 | tf_op jit(solution)/shard_map/attend/pallas_call | solution.py:49
  89.3 3.9 %collective-permute-done.22.rest_4_ = bf16[96,576]{1,0:T(8,128)(2,1)S(1)} collective-permute-done((bf16[96,576]{1,0:T(8,128)(2,1)S(1)}, bf16[96,576]{1,0:T(8,128)(2,1)S(1)}, u32[]{:S(2)}, u32[]{:S(2)}) %collective-permute-start.22) | collective-permute-done | bytes 110624 | tf_op jit(solution)/shard_map/ppermute | solution.py:500
  93.2 2.2 %collective-permute-done.23.rest_5_ = bf16[192,576]{1,0:T(8,128)(2,1)S(1)} collective-permute-done((bf16[192,576]{1,0:T(8,128)(2,1)S(1)}, bf16[192,576]{1,0:T(8,128)(2,1)S(1)}, u32[]{:S(2)}, u32[]{:S(2)}) %collective-permute-start.23) | collective-permute-done | bytes 221216 | tf_op jit(solution)/shard_map/ppermute | solution.py:500
  95.4 11.2 %feed_forward_and_back.1 = (f32[1024,768]{1,0:T(8,128)S(1)}, bf16[1024,768]{1,0:T(8,128)(2,1)S(1)}, bf16[1024,576]{1,0:T(8,128)(2,1)S(1)}, bf16[1024,576]{1,0:T(...) custom-call(s32[8]{0:T(128)S(1)} %compare_select_fusion.2.slots, ...), custom_call_target="tpu_custom_call" | custom-call | flops 905969664 | bytes 2684928 | tf_op jit(solution)/shard_map/feed_forward_and_back/pallas_call | solution.py:49
  106.7 4.7 %feed_weight_grads.1 = bf16[8,3,96,576]{3,2,1,0:T(8,128)(2,1)S(1)} custom-call(s32[8]{0:T(128)S(1)} %compare_select_fusion.2.slots, bf16[1024,768]{1,0:T(8,128)(2,1)S(1)} %get-tuple-element.178.second, bf16[1024,576]{1,0:T(8,128)(2,1)S(1)} %get-tuple-element.216.hidden, bf16[1024,576]{1,0:T(8,128)(2,1)S(1)} %get-tuple-element.180.grad_gate, ...), custom_call_target="tpu_custom_call" | custom-call | flops 566231040 | bytes 1167360 | tf_op jit(solution)/shard_map/feed_weight_grads/pallas_call | solution.py:49
  113.6 3.6 %middle_grad.1 = (f32[1024,768]{1,0:T(8,128)S(1)}, bf16[1024,768]{1,0:T(8,128)(2,1)S(1)}, bf16[1024,384]{1,0:T(8,128)(2,1)S(1)}) custom-call(f32[1024,768]{1,0:T(8,128)S(1)} %get-tuple-element.175.middle, bf16[1024,768]{1,0:T(8,128)(2,1)S(1)} %get-tuple-element.176.own, bf16[1024,768]{1,0:T(8,128)(2,1)S(1)} %collective-permute-done.24.other, ...), custom_call_target="tpu_custom_call" | custom-call | flops 301989888 | bytes 1972224 | tf_op jit(solution)/shard_map/middle_grad/pallas_call | solution.py:49
  121.0 12.3 %attention_back.1 = (bf16[1152,384]{1,0:T(8,128)(2,1)S(1)}, bf16[1152,384]{1,0:T(8,128)(2,1)S(1)}, bf16[1152,384]{1,0:T(8,128)(2,1)S(1)}) custom-call(bf16[1024,384]{1,0:T(8,128)(2,1)S(1)} %get-tuple-element.154.query, bf16[1152,384]{1,0:T(8,128)(2,1)S(1)} %get-tuple-element.155.key, bf16[1152,384]{1,0:T(8,128)(2,1)S(1)} %get-tuple-element.156.value, ...), custom_call_target="tpu_custom_call" | custom-call | flops 1132462080 | bytes 1290240 | tf_op jit(solution)/shard_map/attention_back/pallas_call | solution.py:49
  133.3 3.0 %query_key_grads.1 = (bf16[1152,1152]{1,0:T(8,128)(2,1)S(1)}, bf16[8,2,96,384]{3,2,1,0:T(8,128)(2,1)S(1)}) custom-call(s32[8]{0:T(128)S(1)} %compare_select_fusion.2.slots, bf16[1152,768]{1,0:T(8,128)(2,1)S(1)} %get-tuple-element.147.first, bf16[1152,384]{1,0:T(8,128)(2,1)S(1)} %get-tuple-element.195.rest_0_, ...), custom_call_target="tpu_custom_call" | custom-call | flops 226492416 | bytes 1032192 | tf_op jit(solution)/shard_map/query_key_grads/pallas_call | solution.py:49
  140.2 2.9 %first_grad.1.own = bf16[1152,768]{1,0:T(8,128)(2,1)S(1)} custom-call(bf16[1152,1152]{1,0:T(8,128)(2,1)S(1)} %get-tuple-element.207.grad_proj, bf16[768,1536]{1,0:T(8,128)(2,1)S(1)} %get-tuple-element.157.rest_0_.wide), custom_call_target="tpu_custom_call" | custom-call | flops 226492416 | bytes 847872 | tf_op jit(solution)/shard_map/first_grad/pallas_call | solution.py:49
  145.4 2.8 %collective-permute-done.33 = bf16[3,96,576]{2,1,0:T(8,128)(2,1)S(1)} collective-permute-done((bf16[3,96,576]{2,1,0:T(8,128)(2,1)S(1)}, bf16[3,96,576]{2,1,0:T(8,128)(2,1)S(1)}, u32[]{:S(2)}, u32[]{:S(2)}) %collective-permute-start.33) | collective-permute-done | bytes 331808 | tf_op jit(solution)/shard_map/ppermute | solution.py:550
  148.1 2.6 %collective-permute-done.32 = bf16[3,96,576]{2,1,0:T(8,128)(2,1)S(1)} collective-permute-done((bf16[3,96,576]{2,1,0:T(8,128)(2,1)S(1)}, bf16[3,96,576]{2,1,0:T(8,128)(2,1)S(1)}, u32[]{:S(2)}, u32[]{:S(2)}) %collective-permute-start.32) | collective-permute-done | bytes 331808 | tf_op jit(solution)/shard_map/ppermute | solution.py:550
  150.7 2.7 %value_out_grads.1 = bf16[8,2,96,384]{3,2,1,0:T(8,128)(2,1)S(1)} custom-call(s32[8]{0:T(128)S(1)} %compare_select_fusion.2.slots, bf16[1152,768]{1,0:T(8,128)(2,1)S(1)} %get-tuple-element.147.first, bf16[1152,1152]{1,0:T(8,128)(2,1)S(1)} %get-tuple-element.207.grad_proj, bf16[1024,768]{1,0:T(8,128)(2,1)S(1)} %get-tuple-element.208.low_mid, ...), custom_call_target="tpu_custom_call" | custom-call | flops 226492416 | bytes 995328 | tf_op jit(solution)/shard_map/value_out_grads/pallas_call | solution.py:49
  155.5 4.7 %collective-permute-done.34 = bf16[2,96,384]{2,1,0:T(8,128)(2,1)S(1)} collective-permute-done((bf16[2,96,384]{2,1,0:T(8,128)(2,1)S(1)}, bf16[2,96,384]{2,1,0:T(8,128)(2,1)S(1)}, u32[]{:S(2)}, u32[]{:S(2)}) %collective-permute-start.34) | collective-permute-done | bytes 147488 | tf_op jit(solution)/shard_map/ppermute | solution.py:532
  163.4 3.6 %collective-permute-done.41 = bf16[2,96,384]{2,1,0:T(8,128)(2,1)S(1)} collective-permute-done((bf16[2,96,384]{2,1,0:T(8,128)(2,1)S(1)}, bf16[2,96,384]{2,1,0:T(8,128)(2,1)S(1)}, u32[]{:S(2)}, u32[]{:S(2)}) %collective-permute-start.41) | collective-permute-done | bytes 147488 | tf_op jit(solution)/shard_map/ppermute | solution.py:550
  172.3 3.4 %collective-permute-done.46 = bf16[3,96,576]{2,1,0:T(8,128)(2,1)S(1)} collective-permute-done((bf16[3,96,576]{2,1,0:T(8,128)(2,1)S(1)}, bf16[3,96,576]{2,1,0:T(8,128)(2,1)S(1)}, u32[]{:S(2)}, u32[]{:S(2)}) %collective-permute-start.46) | collective-permute-done | bytes 331808 | tf_op jit(solution)/shard_map/ppermute | solution.py:550
  186.0 3.9 %collective-permute-done.50 = bf16[2,96,384]{2,1,0:T(8,128)(2,1)S(1)} collective-permute-done((bf16[2,96,384]{2,1,0:T(8,128)(2,1)S(1)}, bf16[2,96,384]{2,1,0:T(8,128)(2,1)S(1)}, u32[]{:S(2)}, u32[]{:S(2)}) %collective-permute-start.50) | collective-permute-done | bytes 147488 | tf_op jit(solution)/shard_map/ppermute | solution.py:550
  191.8 2.9 %collective-permute-done.52 = bf16[3,96,576]{2,1,0:T(8,128)(2,1)S(1)} collective-permute-done((bf16[3,96,576]{2,1,0:T(8,128)(2,1)S(1)}, bf16[3,96,576]{2,1,0:T(8,128)(2,1)S(1)}, u32[]{:S(2)}, u32[]{:S(2)}) %collective-permute-start.52) | collective-permute-done | bytes 331808 | tf_op jit(solution)/shard_map/ppermute | solution.py:443
  196.4 6.1 %token_grad.1 = (bf16[1024,768]{1,0:T(8,128)(2,1)}, f32[1024,768]{1,0:T(8,128)}) custom-call(bf16[1024,768]{1,0:T(8,128)(2,1)S(1)} %copy-done.1, f32[16,768]{1,0:T(8,128)S(1)} %get-tuple-element.170.gain, f32[1024,768]{1,0:T(8,128)S(1)} %get-tuple-element.215.grad_middle, bf16[1152,768]{1,0:T(8,128)(2,1)S(1)} %first_grad.1.own, ...), custom_call_target="tpu_custom_call" | custom-call | flops 196608000 | bytes 2439168 | tf_op jit(solution)/shard_map/token_grad/pallas_call | solution.py:49
  203.0 4.6 %collective-permute-done.44 = bf16[2,96,384]{2,1,0:T(8,128)(2,1)S(1)} collective-permute-done((bf16[2,96,384]{2,1,0:T(8,128)(2,1)S(1)}, bf16[2,96,384]{2,1,0:T(8,128)(2,1)S(1)}, u32[]{:S(2)}, u32[]{:S(2)}) %collective-permute-start.44) | collective-permute-done | bytes 147488 | tf_op jit(solution)/shard_map/ppermute | solution.py:443
  (219 shorter events, 96.9 us)
Async XLA Ops:
  1.6 12.2 %collective-permute-start.2 = (bf16[192,384]{1,0:T(8,128)(2,1)S(1)}, bf16[192,384]{1,0:T(8,128)(2,1)}, u32[]{:S(2)}, u32[]{:S(2)}) collective-permute-start(bf16[192,384]{1,0:T(8,128)(2,1)S(1)} %bitcast.96), channel_id=1, source_target_pairs={{8,0},{16,8},{24,16},{28,24},{20,28},{12,20},{4,12},{0,4},{9,1},{1... | collective-permute-start | bytes 442376 | tf_op jit(solution)/shard_map/ppermute | solution.py:500
  4.6 9.2 %collective-permute-start.1 = (bf16[192,384]{1,0:T(8,128)(2,1)S(1)}, bf16[192,384]{1,0:T(8,128)(2,1)}, u32[]{:S(2)}, u32[]{:S(2)}) collective-permute-start(bf16[192,384]{1,0:T(8,128)(2,1)S(1)} %bitcast.97), channel_id=1, source_target_pairs={{0,8},{8,16},{16,24},{24,28},{28,20},{20,12},{12,4},{4,0},{1,9},{9... | collective-permute-start | bytes 442376 | tf_op jit(solution)/shard_map/ppermute | solution.py:500
  15.9 8.9 %collective-permute-start.9 = (bf16[208,384]{1,0:T(8,128)(2,1)}, bf16[208,384]{1,0:T(8,128)(2,1)S(1)}, u32[]{:S(2)}, u32[]{:S(2)}) collective-permute-start(bf16[208,384]{1,0:T(8,128)(2,1)} %collective-permute-done.5.rest_15_), channel_id=1, source_target_pairs={{0,8},{8,16},{16,24},{24,28},{28,20},{20,12},{12,4},{4,0},{1,9},{9... | collective-permute-start | bytes 479240 | tf_op jit(solution)/shard_map/ppermute | solution.py:500
  41.0 24.8 %collective-permute-start.16 = (bf16[288,576]{1,0:T(8,128)(2,1)}, bf16[288,576]{1,0:T(8,128)(2,1)}, u32[]{:S(2)}, u32[]{:S(2)}) collective-permute-start(bf16[288,576]{1,0:T(8,128)(2,1)} %pad_maximum_fusion.1.rest_0_), channel_id=1, source_target_pairs={{8,0},{16,8},{24,16},{28,24},{20,28},{12,20},{4,12},{0,4},{9,1},{1... | collective-permute-start | bytes 995336 | tf_op jit(solution)/shard_map/ppermute | solution.py:500
  41.0 24.8 %collective-permute-start.15 = (bf16[288,576]{1,0:T(8,128)(2,1)}, bf16[288,576]{1,0:T(8,128)(2,1)}, u32[]{:S(2)}, u32[]{:S(2)}) collective-permute-start(bf16[288,576]{1,0:T(8,128)(2,1)} %pad_maximum_fusion.1.rest_0_), channel_id=1, source_target_pairs={{0,8},{8,16},{16,24},{24,28},{28,20},{20,12},{12,4},{4,0},{1,9},{9... | collective-permute-start | bytes 995336 | tf_op jit(solution)/shard_map/ppermute | solution.py:500
  65.8 10.2 %collective-permute-start.17 = (bf16[288,576]{1,0:T(8,128)(2,1)}, bf16[288,576]{1,0:T(8,128)(2,1)S(1)}, u32[]{:S(2)}, u32[]{:S(2)}) collective-permute-start(bf16[288,576]{1,0:T(8,128)(2,1)} %collective-permute-done.15.rest_8_), channel_id=1, source_target_pairs={{0,8},{8,16},{16,24},{24,28},{28,20},{20,12},{12,4},{4,0},{1,9},{9... | collective-permute-start | bytes 995336 | tf_op jit(solution)/shard_map/ppermute | solution.py:500
  67.4 10.4 %collective-permute-start.18 = (bf16[288,576]{1,0:T(8,128)(2,1)}, bf16[288,576]{1,0:T(8,128)(2,1)S(1)}, u32[]{:S(2)}, u32[]{:S(2)}) collective-permute-start(bf16[288,576]{1,0:T(8,128)(2,1)} %collective-permute-done.16.rest_1_), channel_id=1, source_target_pairs={{8,0},{16,8},{24,16},{28,24},{20,28},{12,20},{4,12},{0,4},{9,1},{1... | collective-permute-start | bytes 995336 | tf_op jit(solution)/shard_map/ppermute | solution.py:500
  118.9 14.4 %collective-permute-start.28 = (bf16[3,96,576]{2,1,0:T(8,128)(2,1)S(1)}, bf16[3,96,576]{2,1,0:T(8,128)(2,1)S(1)}, u32[]{:S(2)}, u32[]{:S(2)}) collective-permute-start(bf16[3,96,576]{2,1,0:T(8,128)(2,1)S(1)} %get-tuple-element.250), channel_id=1, source_target_pairs={{8,0},{16,8},{24,16},{28,24},{20,28},{12,20},{4,12},{0,4},{9,1},{1... | collective-permute-start | bytes 995336 | tf_op jit(solution)/shard_map/ppermute | solution.py:550
  119.4 13.9 %collective-permute-start.27 = (bf16[3,96,576]{2,1,0:T(8,128)(2,1)S(1)}, bf16[3,96,576]{2,1,0:T(8,128)(2,1)S(1)}, u32[]{:S(2)}, u32[]{:S(2)}) collective-permute-start(bf16[3,96,576]{2,1,0:T(8,128)(2,1)S(1)} %get-tuple-element.251), channel_id=1, source_target_pairs={{0,8},{8,16},{16,24},{24,28},{28,20},{20,12},{12,4},{4,0},{1,9},{9... | collective-permute-start | bytes 995336 | tf_op jit(solution)/shard_map/ppermute | solution.py:550
  138.1 10.0 %collective-permute-start.33 = (bf16[3,96,576]{2,1,0:T(8,128)(2,1)S(1)}, bf16[3,96,576]{2,1,0:T(8,128)(2,1)S(1)}, u32[]{:S(2)}, u32[]{:S(2)}) collective-permute-start(bf16[3,96,576]{2,1,0:T(8,128)(2,1)S(1)} %get-tuple-element.248), channel_id=1, source_target_pairs={{8,0},{16,8},{24,16},{28,24},{20,28},{12,20},{4,12},{0,4},{9,1},{1... | collective-permute-start | bytes 995336 | tf_op jit(solution)/shard_map/ppermute | solution.py:550
  138.6 12.1 %collective-permute-start.32 = (bf16[3,96,576]{2,1,0:T(8,128)(2,1)S(1)}, bf16[3,96,576]{2,1,0:T(8,128)(2,1)S(1)}, u32[]{:S(2)}, u32[]{:S(2)}) collective-permute-start(bf16[3,96,576]{2,1,0:T(8,128)(2,1)S(1)} %get-tuple-element.249), channel_id=1, source_target_pairs={{0,8},{8,16},{16,24},{24,28},{28,20},{20,12},{12,4},{4,0},{1,9},{9... | collective-permute-start | bytes 995336 | tf_op jit(solution)/shard_map/ppermute | solution.py:550
  143.1 33.0 %collective-permute-start.37 = (bf16[1152,768]{1,0:T(8,128)(2,1)S(1)}, bf16[1152,768]{1,0:T(8,128)(2,1)S(1)}, u32[]{:S(2)}, u32[]{:S(2)}) collective-permute-start(bf16[1152,768]{1,0:T(8,128)(2,1)S(1)} %first_grad.1.own), channel_id=1, source_target_pairs={{0,1},{1,0},{2,3},{3,2},{4,5},{5,4},{6,7},{7,6},{8,9},{9,8},{10,11... | collective-permute-start | bytes 5308424 | tf_op jit(solution)/shard_map/ppermute | solution.py:443
  143.2 10.8 %collective-permute-start.31 = (bf16[2,96,384]{2,1,0:T(8,128)(2,1)S(1)}, bf16[2,96,384]{2,1,0:T(8,128)(2,1)S(1)}, u32[]{:S(2)}, u32[]{:S(2)}) collective-permute-start(bf16[2,96,384]{2,1,0:T(8,128)(2,1)S(1)} %get-tuple-element.262), channel_id=1, source_target_pairs={{8,0},{16,8},{24,16},{28,24},{20,28},{12,20},{4,12},{0,4},{9,1},{1... | collective-permute-start | bytes 442376 | tf_op jit(solution)/shard_map/ppermute | solution.py:550
  143.7 10.3 %collective-permute-start.30 = (bf16[2,96,384]{2,1,0:T(8,128)(2,1)S(1)}, bf16[2,96,384]{2,1,0:T(8,128)(2,1)S(1)}, u32[]{:S(2)}, u32[]{:S(2)}) collective-permute-start(bf16[2,96,384]{2,1,0:T(8,128)(2,1)S(1)} %bitcast_add_fusion.9), channel_id=1, source_target_pairs={{0,8},{8,16},{16,24},{24,28},{28,20},{20,12},{12,4},{4,0},{1,9},{9... | collective-permute-start | bytes 442376 | tf_op jit(solution)/shard_map/ppermute | solution.py:550
  154.0 9.0 %collective-permute-start.40 = (bf16[2,96,384]{2,1,0:T(8,128)(2,1)S(1)}, bf16[2,96,384]{2,1,0:T(8,128)(2,1)S(1)}, u32[]{:S(2)}, u32[]{:S(2)}) collective-permute-start(bf16[2,96,384]{2,1,0:T(8,128)(2,1)S(1)} %get-tuple-element.258), channel_id=1, source_target_pairs={{0,8},{8,16},{16,24},{24,28},{28,20},{20,12},{12,4},{4,0},{1,9},{9... | collective-permute-start | bytes 442376 | tf_op jit(solution)/shard_map/ppermute | solution.py:550
  160.9 9.3 %collective-permute-start.36 = (bf16[2,96,384]{2,1,0:T(8,128)(2,1)S(1)}, bf16[2,96,384]{2,1,0:T(8,128)(2,1)S(1)}, u32[]{:S(2)}, u32[]{:S(2)}) collective-permute-start(bf16[2,96,384]{2,1,0:T(8,128)(2,1)S(1)} %get-tuple-element.260), channel_id=1, source_target_pairs={{8,0},{16,8},{24,16},{28,24},{20,28},{12,20},{4,12},{0,4},{9,1},{1... | collective-permute-start | bytes 442376 | tf_op jit(solution)/shard_map/ppermute | solution.py:550
  161.2 8.9 %collective-permute-start.35 = (bf16[2,96,384]{2,1,0:T(8,128)(2,1)S(1)}, bf16[2,96,384]{2,1,0:T(8,128)(2,1)S(1)}, u32[]{:S(2)}, u32[]{:S(2)}) collective-permute-start(bf16[2,96,384]{2,1,0:T(8,128)(2,1)S(1)} %get-tuple-element.261), channel_id=1, source_target_pairs={{0,8},{8,16},{16,24},{24,28},{28,20},{20,12},{12,4},{4,0},{1,9},{9... | collective-permute-start | bytes 442376 | tf_op jit(solution)/shard_map/ppermute | solution.py:550
  163.1 12.6 %collective-permute-start.46 = (bf16[3,96,576]{2,1,0:T(8,128)(2,1)S(1)}, bf16[3,96,576]{2,1,0:T(8,128)(2,1)S(1)}, u32[]{:S(2)}, u32[]{:S(2)}) collective-permute-start(bf16[3,96,576]{2,1,0:T(8,128)(2,1)S(1)} %get-tuple-element.246), channel_id=1, source_target_pairs={{8,0},{16,8},{24,16},{28,24},{20,28},{12,20},{4,12},{0,4},{9,1},{1... | collective-permute-start | bytes 995336 | tf_op jit(solution)/shard_map/ppermute | solution.py:550
  167.0 9.1 %collective-permute-start.45 = (bf16[3,96,576]{2,1,0:T(8,128)(2,1)S(1)}, bf16[3,96,576]{2,1,0:T(8,128)(2,1)S(1)}, u32[]{:S(2)}, u32[]{:S(2)}) collective-permute-start(bf16[3,96,576]{2,1,0:T(8,128)(2,1)S(1)} %get-tuple-element.247), channel_id=1, source_target_pairs={{0,8},{8,16},{16,24},{24,28},{28,20},{20,12},{12,4},{4,0},{1,9},{9... | collective-permute-start | bytes 995336 | tf_op jit(solution)/shard_map/ppermute | solution.py:550
  170.2 13.0 %collective-permute-start.43 = (bf16[2,96,384]{2,1,0:T(8,128)(2,1)S(1)}, bf16[2,96,384]{2,1,0:T(8,128)(2,1)S(1)}, u32[]{:S(2)}, u32[]{:S(2)}) collective-permute-start(bf16[2,96,384]{2,1,0:T(8,128)(2,1)S(1)} %get-tuple-element.252), channel_id=1, source_target_pairs={{8,0},{16,8},{24,16},{28,24},{20,28},{12,20},{4,12},{0,4},{9,1},{1... | collective-permute-start | bytes 442376 | tf_op jit(solution)/shard_map/ppermute | solution.py:550
  170.9 12.9 %collective-permute-start.42 = (bf16[2,96,384]{2,1,0:T(8,128)(2,1)S(1)}, bf16[2,96,384]{2,1,0:T(8,128)(2,1)S(1)}, u32[]{:S(2)}, u32[]{:S(2)}) collective-permute-start(bf16[2,96,384]{2,1,0:T(8,128)(2,1)S(1)} %get-tuple-element.253), channel_id=1, source_target_pairs={{0,8},{8,16},{16,24},{24,28},{28,20},{20,12},{12,4},{4,0},{1,9},{9... | collective-permute-start | bytes 442376 | tf_op jit(solution)/shard_map/ppermute | solution.py:550
  183.0 13.4 %collective-permute-start.39 = (bf16[1024,768]{1,0:T(8,128)(2,1)S(1)}, bf16[1024,768]{1,0:T(8,128)(2,1)S(1)}, u32[]{:S(2)}, u32[]{:S(2)}) collective-permute-start(bf16[1024,768]{1,0:T(8,128)(2,1)S(1)} %feed_out.1.feed_own), channel_id=1, source_target_pairs={{0,1},{1,0},{2,3},{3,2},{4,5},{5,4},{6,7},{7,6},{8,9},{9,8},{10,11... | collective-permute-start | bytes 4718600 | tf_op jit(solution)/shard_map/ppermute | solution.py:443
  183.2 11.4 %collective-permute-start.52 = (bf16[3,96,576]{2,1,0:T(8,128)(2,1)S(1)}, bf16[3,96,576]{2,1,0:T(8,128)(2,1)S(1)}, u32[]{:S(2)}, u32[]{:S(2)}) collective-permute-start(bf16[3,96,576]{2,1,0:T(8,128)(2,1)S(1)} %fusion.1), channel_id=1, source_target_pairs={{0,2},{2,0},{1,3},{3,1},{4,6},{6,4},{5,7},{7,5},{8,10},{10,8},{9,1... | collective-permute-start | bytes 995336 | tf_op jit(solution)/shard_map/ppermute | solution.py:443
  190.2 12.8 %collective-permute-start.51 = (bf16[2,96,384]{2,1,0:T(8,128)(2,1)S(1)}, bf16[2,96,384]{2,1,0:T(8,128)(2,1)S(1)}, u32[]{:S(2)}, u32[]{:S(2)}) collective-permute-start(bf16[2,96,384]{2,1,0:T(8,128)(2,1)S(1)} %fusion.3), channel_id=1, source_target_pairs={{0,2},{2,0},{1,3},{3,1},{4,6},{6,4},{5,7},{7,5},{8,10},{10,8},{9,1... | collective-permute-start | bytes 442376 | tf_op jit(solution)/shard_map/ppermute | solution.py:443
  (67 other events, 348.8 us)

commit v11 on v10

--- a/solution.py
+++ b/solution.py
@@ -3,6 +3,7 @@
 
 import jax
 import jax.numpy as jnp
+import numpy as np
 from jax import lax
 from jax.experimental import pallas as pl
 from jax.experimental.pallas import tpu as pltpu
@@ -448,11 +449,10 @@
     order = [2 * i for i in range(count // 2)] + [2 * i + 1 for i in reversed(range(count // 2))]
     ahead = [(order[i], order[(i + 1) % count]) for i in range(count)]
     back = [(j, i) for i, j in ahead]
-    index = lax.axis_index("dp")
-    spot = jnp.where(index % 2 == 0, index // 2, count - 1 - index // 2)
-    place = (spot + jnp.arange(count, dtype=jnp.int32)) % count
-    slots = jnp.where(place < count // 2, 2 * place, 2 * (count - 1 - place) + 1)
-    return count, ahead, back, slots.astype(jnp.int32)
+    places = {group: at for at, group in enumerate(order)}
+    table = np.array([[order[(places[i] + j) % count] for j in range(count)] for i in range(count)], np.int32)
+    slots = lax.dynamic_index_in_dim(jnp.asarray(table), lax.axis_index("dp"), keepdims=False)
+    return count, ahead, back, slots
 
 
 def tied(values, others):
@@ -562,7 +562,8 @@
 
 def tables(lengths, rows):
     place = lax.axis_index("ctx") * rows
-    ends = jnp.cumsum(lengths[0])
+    spots = jnp.arange(NSEQ, dtype=jnp.int32)
+    ends = jnp.sum(jnp.where(spots[None, :] <= spots[:, None], lengths[0][None, :], 0), axis=1)
     starts = ends - lengths[0]
     span = place + jnp.arange(-HALF, rows + HALF, dtype=jnp.int32)
     inside = (span[:, None] >= starts[None, :]) & (span[:, None] < ends[None, :])
@@ -594,6 +595,8 @@
     before, after = exchange(tokens[:HALF], tokens[rows - HALF :])
     slots = ring()[-1]
     cosine, sine, bounds = tables(lengths, rows)
+    for chain in now:
+        chain.after([cosine, sine, bounds, slots, before, after])
     hat, = call(
         norm_kernel, [shape((extent, width), f32)], (tokens, before, after), rows * width * 2000, "first_norm"
     )
@@ -687,7 +690,15 @@
         2 * rows * width * local * 4,
         "middle_grad",
     )
-    grad_att, = locked([grad_att], sums_two)
+    feed, = call(
+        feed_out_kernel,
+        [shape((rows, width), bf16)],
+        (tied([hidden], [grads_two])[0], whole),
+        2 * rows * width * units,
+        "feed_out",
+    )
+    grad_att, feed = locked([grad_att, feed], sums_two)
+    feed_other = swap(feed)
     sums_two.hop()
     grad_parts = call(
         functools.partial(back_kernel, (early, late)),
@@ -716,41 +727,32 @@
         2 * rows * width * local * 3,
         "first_grad",
     )
+    grads_b, = call(
+        grad_kernel_two,
+        [shape((groups, 2, depth, local), bf16)],
+        (first, grad_proj, low_mid, attended),
+        2 * rows * width * local * 3,
+        "value_out_grads",
+        (slots,),
+        [pltpu.VMEM((2, width, local), bf16)],
+    )
+    *grads_one, first_part = locked([grads_a, grads_b, first_part], sums_two)
     first_other = swap(first_part)
     def edge_sum(at):
         here = slice(at, at + HALF)
         return (first_part[here].astype(f32) + first_other[here].astype(f32)).astype(bf16)
 
     from_before, from_after = exchange(edge_sum(0), edge_sum(rows + HALF))
-    low_mid, grad_value_proj = tied([low_mid, grad_proj], [first_part, *sums_two.state])
-    grads_b, = call(
-        grad_kernel_two,
-        [shape((groups, 2, depth, local), bf16)],
-        (first, grad_value_proj, low_mid, attended),
-        2 * rows * width * local * 3,
-        "value_out_grads",
-        (slots,),
-        [pltpu.VMEM((2, width, local), bf16)],
-    )
-    grads_one = [grads_a, grads_b]
-    feed, = call(
-        feed_out_kernel,
-        [shape((rows, width), bf16)],
-        (tied([hidden], [from_before, from_after])[0], whole),
-        2 * rows * width * units,
-        "feed_out",
-    )
-    feed_other = swap(feed)
     sums_one = [RingScatter([part], way=way) for way, part in enumerate(grads_one)]
     alternate(*sums_one)
     sums_two.after(sums_one[0].state)
     while sums_two.hops < middle_hop:
         sums_two.hop()
 
-    while sums_one[0].hops < middle_hop - 1:
-        if sums_one[0].hops == 2:
-            sums_one[1].after(sums_two.state)
+    sums_one[1].after([from_before, from_after])
+    while sums_one[0].hops < middle_hop - 2:
         alternate(*sums_one)
+    sums_one[1].after(sums_two.state)
     tokens, = tied([tokens], sums_one[0].state)
     alternate(*sums_one)
     mixed, token_grad = call(
@@ -760,8 +762,10 @@
         rows * width * 2000,
         "token_grad",
     )
+    sums_one[0].after([mixed, token_grad])
+    alternate(*sums_one)
     two = over_ctx(sums_two.total())
-    one = over_ctx(tied([sums_one[0].total()], [mixed, token_grad])[0])
+    one = over_ctx(sums_one[0].total())
     one = jnp.concatenate([one, over_ctx(sums_one[1].total())])
     gain_one_grad = jnp.sum(one[:3] * w_qkv.astype(f32), axis=(0, 2)) / gain_one.astype(f32)
     gain_two_grad = jnp.sum(two[:2] * w_in.astype(f32), axis=(0, 2)) / gain_two.astype(f32)

time: 211 us -> 197 us (0.934)
  local copies, waits for them, and re-layouts: 25 us -> 4.74 us
  waiting for transfers between devices: 49.9 us -> 60.3 us
    unnamed x74 -> x14, local copies, waits for them, and re-layouts: 21.1 us -> 0.04 us
    ppermute x20, waiting for transfers between devices: 7.59 us -> 20.9 us  [hop(): lax.ppermute(one, 'dp', self.ahead)]
    ppermute x20, starting transfers between devices: 14.4 us -> 17.2 us  [hop(): lax.ppermute(two, 'dp', self.back)]
    ppermute x20, starting transfers between devices: 28.1 us -> 25.3 us  [hop(): lax.ppermute(one, 'dp', self.ahead)]
    ppermute x20, waiting for transfers between devices: 23.2 us -> 20.6 us  [hop(): lax.ppermute(two, 'dp', self.back)]
  transfers between devices with their start and end apart: 54 -> 54, of which waited for: 24 -> 26; matrix products, arithmetic and copies ran while one was open for 6% -> 6% of each run, Pallas kernels for 27% -> 30%
where the time goes in v11:
time: 197 us
  Pallas kernels  70 us (36%)
  waiting for transfers between devices  60.3 us (31%)
  starting transfers between devices  51.2 us (26%)
  other arithmetic  9.24 us (5%)
  local copies, waits for them, and re-layouts  4.74 us (2%)
    pallas_call x13, Pallas kernels, call(): pl.pallas_call(kernel, out_shape=out_shape, in_specs=[smem] * len(scalars...  70 us
    ppermute x20, starting transfers between devices, hop(): lax.ppermute(one, 'dp', self.ahead)  25.3 us
    ppermute x20, waiting for transfers between devices, hop(): lax.ppermute(one, 'dp', self.ahead)  20.9 us
    ppermute x20, waiting for transfers between devices, hop(): lax.ppermute(two, 'dp', self.back)  20.6 us
    ppermute x20, starting transfers between devices, hop(): lax.ppermute(two, 'dp', self.back)  17.2 us
    ppermute x8, waiting for transfers between devices, swap(): return lax.ppermute(array, axis, [(0, 1), (1, 0)])  8.85 us
    ppermute x2, waiting for transfers between devices, hop(): lax.ppermute((one, two)[self.way], 'dp', (self.ahead, self.back)[self.way])  5.12 us
  transfers between devices with their start and end apart: 54, of which 26 were waited for; matrix products, arithmetic and copies ran while one was open for 6% of the time, Pallas kernels for 30%

profile of v11, /device:TPU:0, one launch (start us, length us, event | category | flops | bytes accessed | tf_op | source)
XLA Modules:
  0.0 196.5 jit_solution(4822223187946399062)
XLA Ops:
  1.7 3.0 %collective-permute-start.2 = (bf16[192,384]{1,0:T(8,128)(2,1)S(1)}, bf16[192,384]{1,0:T(8,128)(2,1)S(1)}, u32[]{:S(2)}, u32[]{:S(2)}) collective-permute-start(bf16[192,384]{1,0:T(8,128)(2,1)S(1)} %bitcast.85), channel_id=1, source_target_pairs={{8,0},{16,8},{24,16},{28,24},{20,28},{12,20},{4,12},{0,4},{9,1},{1... | collective-permute-start | bytes 442376 | tf_op jit(solution)/shard_map/ppermute | solution.py:500
  29.9 3.1 %collective-permute-done.7.rest_5_ = bf16[192,384]{1,0:T(8,128)(2,1)S(1)} collective-permute-done((bf16[192,384]{1,0:T(8,128)(2,1)S(1)}, bf16[192,384]{1,0:T(8,128)(2,1)S(1)}, u32[]{:S(2)}, u32[]{:S(2)}) %collective-permute-start.7) | collective-permute-done | bytes 147488 | tf_op jit(solution)/shard_map/ppermute | solution.py:500
  33.0 3.2 %collective-permute-done.8.rest_3_ = bf16[192,384]{1,0:T(8,128)(2,1)S(1)} collective-permute-done((bf16[192,384]{1,0:T(8,128)(2,1)S(1)}, bf16[192,384]{1,0:T(8,128)(2,1)S(1)}, u32[]{:S(2)}, u32[]{:S(2)}) %collective-permute-start.8) | collective-permute-done | bytes 147488 | tf_op jit(solution)/shard_map/ppermute | solution.py:500
  38.3 5.1 %collective-permute-done.11.rest_4_ = bf16[192,384]{1,0:T(8,128)(2,1)S(1)} collective-permute-done((bf16[192,384]{1,0:T(8,128)(2,1)S(1)}, bf16[192,384]{1,0:T(8,128)(2,1)S(1)}, u32[]{:S(2)}, u32[]{:S(2)}) %collective-permute-start.11) | collective-permute-done | bytes 147488 | tf_op jit(solution)/shard_map/ppermute | solution.py:492
  45.4 5.7 %project.1 = (bf16[768,1536]{1,0:T(8,128)(2,1)S(1)}, f32[16,768]{1,0:T(8,128)S(1)}, bf16[1152,768]{1,0:T(8,128)(2,1)S(1)}, bf16[1024,384]{1,0:T(8,128)(2,1)S(1)}...) custom-call(s32[8]{0:T(128)S(1)} %dynamic-slice_bitcast_fusion.slots, f32[1152,768]{1,0:T(8,128)S(1)} %first_norm.1.hat, ...), custom_call_target="tpu_custom_call" | custom-call | flops 603979776 | bytes 1738752 | tf_op jit(solution)/shard_map/project/pallas_call | solution.py:50
  51.2 2.3 %collective-permute-done.16.rest_1_ = bf16[288,576]{1,0:T(8,128)(2,1)S(1)} collective-permute-done((bf16[288,576]{1,0:T(8,128)(2,1)S(1)}, bf16[288,576]{1,0:T(8,128)(2,1)S(1)}, u32[]{:S(2)}, u32[]{:S(2)}) %collective-permute-start.16) | collective-permute-done | bytes 331808 | tf_op jit(solution)/shard_map/ppermute | solution.py:500
  56.9 7.7 %attend.2 = (bf16[16,256,256]{2,1,0:T(8,128)(2,1)S(1)}, bf16[1024,384]{1,0:T(8,128)(2,1)S(1)}) custom-call(s32[5]{0:T(128)S(1)} %pad_add_fusion.bounds, bf16[1024,384]{1,0:T(8,128)(2,1)S(1)} %get-tuple-element.168.query, bf16[1152,384]{1,0:T(8,128)(2,1)S(1)} %get-tuple-element.169.key, bf16[1152,384]{1,0:T(8,128)(2,1)S(1)} %get-tuple-element.170.value), custom_call_target="tpu_custom_call" | custom-call | flops 754974720 | bytes 679936 | tf_op jit(solution)/shard_map/attend/pallas_call | solution.py:50
  68.8 6.6 %attend.3 = (bf16[8,256,256]{2,1,0:T(8,128)(2,1)S(1)}, bf16[1024,384]{1,0:T(8,128)(2,1)S(1)}, bf16[1024,768]{1,0:T(8,128)(2,1)S(1)}) custom-call(s32[5]{0:T(128)S(1)} %pad_add_fusion.bounds, bf16[1024,384]{1,0:T(8,128)(2,1)S(1)} %get-tuple-element.168.query, bf16[1152,384]{1,0:T(8,128)(2,1)S(1)} %get-tuple-element.169.key, ...), custom_call_target="tpu_custom_call" | custom-call | flops 528482304 | bytes 1138688 | tf_op jit(solution)/shard_map/attend/pallas_call | solution.py:50
  78.2 3.9 %collective-permute-done.22.rest_4_ = bf16[96,576]{1,0:T(8,128)(2,1)S(1)} collective-permute-done((bf16[96,576]{1,0:T(8,128)(2,1)S(1)}, bf16[96,576]{1,0:T(8,128)(2,1)S(1)}, u32[]{:S(2)}, u32[]{:S(2)}) %collective-permute-start.22) | collective-permute-done | bytes 110624 | tf_op jit(solution)/shard_map/ppermute | solution.py:500
  84.3 10.6 %feed_forward_and_back.1 = (f32[1024,768]{1,0:T(8,128)S(1)}, bf16[1024,768]{1,0:T(8,128)(2,1)S(1)}, bf16[1024,576]{1,0:T(8,128)(2,1)S(1)}, bf16[1024,576]{1,0:T(...) custom-call(s32[8]{0:T(128)S(1)} %dynamic-slice_bitcast_fusion.slots, ...), custom_call_target="tpu_custom_call" | custom-call | flops 905969664 | bytes 2684928 | tf_op jit(solution)/shard_map/feed_forward_and_back/pallas_call | solution.py:50
  95.0 4.7 %feed_weight_grads.1 = bf16[8,3,96,576]{3,2,1,0:T(8,128)(2,1)S(1)} custom-call(s32[8]{0:T(128)S(1)} %dynamic-slice_bitcast_fusion.slots, bf16[1024,768]{1,0:T(8,128)(2,1)S(1)} %get-tuple-element.193.second, bf16[1024,576]{1,0:T(8,128)(2,1)S(1)} %get-tuple-element.197.hidden, bf16[1024,576]{1,0:T(8,128)(2,1)S(1)} %get-tuple-element.194.grad_gate, ...), custom_call_target="tpu_custom_call" | custom-call | flops 566231040 | bytes 1167360 | tf_op jit(solution)/shard_map/feed_weight_grads/pallas_call | solution.py:50
  103.9 3.6 %middle_grad.1 = (f32[1024,768]{1,0:T(8,128)S(1)}, bf16[1024,768]{1,0:T(8,128)(2,1)S(1)}, bf16[1024,384]{1,0:T(8,128)(2,1)S(1)}) custom-call(f32[1024,768]{1,0:T(8,128)S(1)} %get-tuple-element.189.middle, bf16[1024,768]{1,0:T(8,128)(2,1)S(1)} %get-tuple-element.190.own, bf16[1024,768]{1,0:T(8,128)(2,1)S(1)} %collective-permute-done.24.other, ...), custom_call_target="tpu_custom_call" | custom-call | flops 301989888 | bytes 1972224 | tf_op jit(solution)/shard_map/middle_grad/pallas_call | solution.py:50
  109.7 12.3 %attention_back.1 = (bf16[1152,384]{1,0:T(8,128)(2,1)S(1)}, bf16[1152,384]{1,0:T(8,128)(2,1)S(1)}, bf16[1152,384]{1,0:T(8,128)(2,1)S(1)}) custom-call(bf16[1024,384]{1,0:T(8,128)(2,1)S(1)} %get-tuple-element.168.query, bf16[1152,384]{1,0:T(8,128)(2,1)S(1)} %get-tuple-element.169.key, bf16[1152,384]{1,0:T(8,128)(2,1)S(1)} %get-tuple-element.170.value, ...), custom_call_target="tpu_custom_call" | custom-call | flops 1132462080 | bytes 1290240 | tf_op jit(solution)/shard_map/attention_back/pallas_call | solution.py:50
  124.2 3.0 %query_key_grads.1 = (bf16[1152,1152]{1,0:T(8,128)(2,1)S(1)}, bf16[8,2,96,384]{3,2,1,0:T(8,128)(2,1)S(1)}) custom-call(s32[8]{0:T(128)S(1)} %dynamic-slice_bitcast_fusion.slots, bf16[1152,768]{1,0:T(8,128)(2,1)S(1)} %get-tuple-element.161.first, bf16[1152,384]{1,0:T(8,128)(2,1)S(1)} %get-tuple-element.211.rest_0_, ...), custom_call_target="tpu_custom_call" | custom-call | flops 226492416 | bytes 1032192 | tf_op jit(solution)/shard_map/query_key_grads/pallas_call | solution.py:50
  127.2 2.9 %first_grad.1.own = bf16[1152,768]{1,0:T(8,128)(2,1)S(1)} custom-call(bf16[1152,1152]{1,0:T(8,128)(2,1)S(1)} %get-tuple-element.215.grad_proj, bf16[768,1536]{1,0:T(8,128)(2,1)S(1)} %get-tuple-element.171.rest_0_.wide), custom_call_target="tpu_custom_call" | custom-call | flops 226492416 | bytes 847872 | tf_op jit(solution)/shard_map/first_grad/pallas_call | solution.py:50
  130.2 2.7 %value_out_grads.1 = bf16[8,2,96,384]{3,2,1,0:T(8,128)(2,1)S(1)} custom-call(s32[8]{0:T(128)S(1)} %dynamic-slice_bitcast_fusion.slots, bf16[1152,768]{1,0:T(8,128)(2,1)S(1)} %get-tuple-element.161.first, bf16[1152,1152]{1,0:T(8,128)(2,1)S(1)} %get-tuple-element.215.grad_proj, bf16[1024,768]{1,0:T(8,128)(2,1)S(1)} %get-tuple-element.216.low_mid, ...), custom_call_target="tpu_custom_call" | custom-call | flops 226492416 | bytes 995328 | tf_op jit(solution)/shard_map/value_out_grads/pallas_call | solution.py:50
  135.6 3.9 %collective-permute-done.31 = bf16[2,96,384]{2,1,0:T(8,128)(2,1)S(1)} collective-permute-done((bf16[2,96,384]{2,1,0:T(8,128)(2,1)S(1)}, bf16[2,96,384]{2,1,0:T(8,128)(2,1)S(1)}, u32[]{:S(2)}, u32[]{:S(2)}) %collective-permute-start.31) | collective-permute-done | bytes 147488 | tf_op jit(solution)/shard_map/ppermute | solution.py:532
  143.3 2.9 %collective-permute-done.32 = bf16[2,96,384]{2,1,0:T(8,128)(2,1)S(1)} collective-permute-done((bf16[2,96,384]{2,1,0:T(8,128)(2,1)S(1)}, bf16[2,96,384]{2,1,0:T(8,128)(2,1)S(1)}, u32[]{:S(2)}, u32[]{:S(2)}) %collective-permute-start.32) | collective-permute-done | bytes 147488 | tf_op jit(solution)/shard_map/ppermute | solution.py:550
  146.9 5.3 %collective-permute-done.46 = bf16[3,96,576]{2,1,0:T(8,128)(2,1)S(1)} collective-permute-done((bf16[3,96,576]{2,1,0:T(8,128)(2,1)S(1)}, bf16[3,96,576]{2,1,0:T(8,128)(2,1)S(1)}, u32[]{:S(2)}, u32[]{:S(2)}) %collective-permute-start.46) | collective-permute-done | bytes 331808 | tf_op jit(solution)/shard_map/ppermute | solution.py:550
  155.8 2.7 %collective-permute-done.38 = bf16[2,96,384]{2,1,0:T(8,128)(2,1)S(1)} collective-permute-done((bf16[2,96,384]{2,1,0:T(8,128)(2,1)S(1)}, bf16[2,96,384]{2,1,0:T(8,128)(2,1)S(1)}, u32[]{:S(2)}, u32[]{:S(2)}) %collective-permute-start.38) | collective-permute-done | bytes 147488 | tf_op jit(solution)/shard_map/ppermute | solution.py:550
  159.1 3.8 %collective-permute-done.52 = bf16[3,96,576]{2,1,0:T(8,128)(2,1)S(1)} collective-permute-done((bf16[3,96,576]{2,1,0:T(8,128)(2,1)S(1)}, bf16[3,96,576]{2,1,0:T(8,128)(2,1)S(1)}, u32[]{:S(2)}, u32[]{:S(2)}) %collective-permute-start.52) | collective-permute-done | bytes 331808 | tf_op jit(solution)/shard_map/ppermute | solution.py:444
  165.6 6.0 %token_grad.1 = (bf16[1024,768]{1,0:T(8,128)(2,1)}, f32[1024,768]{1,0:T(8,128)}) custom-call(bf16[1024,768]{1,0:T(8,128)(2,1)S(1)} %copy-done, f32[16,768]{1,0:T(8,128)S(1)} %get-tuple-element.184.gain, f32[1024,768]{1,0:T(8,128)S(1)} %get-tuple-element.226.grad_middle, bf16[1152,768]{1,0:T(8,128)(2,1)S(1)} %first_grad.1.own, ...), custom_call_target="tpu_custom_call" | custom-call | flops 196608000 | bytes 2439168 | tf_op jit(solution)/shard_map/token_grad/pallas_call | solution.py:50
  184.5 2.5 %collective-permute-done.50 = bf16[2,96,384]{2,1,0:T(8,128)(2,1)S(1)} collective-permute-done((bf16[2,96,384]{2,1,0:T(8,128)(2,1)S(1)}, bf16[2,96,384]{2,1,0:T(8,128)(2,1)S(1)}, u32[]{:S(2)}, u32[]{:S(2)}) %collective-permute-start.50) | collective-permute-done | bytes 147488 | tf_op jit(solution)/shard_map/ppermute | solution.py:550
  189.2 4.6 %collective-permute-done.51 = bf16[2,96,384]{2,1,0:T(8,128)(2,1)S(1)} collective-permute-done((bf16[2,96,384]{2,1,0:T(8,128)(2,1)S(1)}, bf16[2,96,384]{2,1,0:T(8,128)(2,1)S(1)}, u32[]{:S(2)}, u32[]{:S(2)}) %collective-permute-start.51) | collective-permute-done | bytes 147488 | tf_op jit(solution)/shard_map/ppermute | solution.py:444
  (159 shorter events, 83.4 us)
Async XLA Ops:
  1.7 15.1 %collective-permute-start.2 = (bf16[192,384]{1,0:T(8,128)(2,1)S(1)}, bf16[192,384]{1,0:T(8,128)(2,1)S(1)}, u32[]{:S(2)}, u32[]{:S(2)}) collective-permute-start(bf16[192,384]{1,0:T(8,128)(2,1)S(1)} %bitcast.85), channel_id=1, source_target_pairs={{8,0},{16,8},{24,16},{28,24},{20,28},{12,20},{4,12},{0,4},{9,1},{1... | collective-permute-start | bytes 442376 | tf_op jit(solution)/shard_map/ppermute | solution.py:500
  4.7 12.2 %collective-permute-start.1 = (bf16[192,384]{1,0:T(8,128)(2,1)S(1)}, bf16[192,384]{1,0:T(8,128)(2,1)S(1)}, u32[]{:S(2)}, u32[]{:S(2)}) collective-permute-start(bf16[192,384]{1,0:T(8,128)(2,1)S(1)} %bitcast.86), channel_id=1, source_target_pairs={{0,8},{8,16},{16,24},{24,28},{28,20},{20,12},{12,4},{4,0},{1,9},{9... | collective-permute-start | bytes 442376 | tf_op jit(solution)/shard_map/ppermute | solution.py:500
  7.3 9.5 %collective-permute-start.6 = (bf16[208,384]{1,0:T(8,128)(2,1)S(1)}, bf16[208,384]{1,0:T(8,128)(2,1)S(1)}, u32[]{:S(2)}, u32[]{:S(2)}) collective-permute-start(bf16[208,384]{1,0:T(8,128)(2,1)S(1)} %pad_maximum_fusion.2.rest_8_), channel_id=1, source_target_pairs={{8,0},{16,8},{24,16},{28,24},{20,28},{12,20},{4,12},{0,4},{9,1},{1... | collective-permute-start | bytes 479240 | tf_op jit(solution)/shard_map/ppermute | solution.py:500
  16.9 9.0 %collective-permute-start.9 = (bf16[208,384]{1,0:T(8,128)(2,1)S(1)}, bf16[208,384]{1,0:T(8,128)(2,1)S(1)}, u32[]{:S(2)}, u32[]{:S(2)}) collective-permute-start(bf16[208,384]{1,0:T(8,128)(2,1)S(1)} %collective-permute-done.5.rest_15_), channel_id=1, source_target_pairs={{0,8},{8,16},{16,24},{24,28},{28,20},{20,12},{12,4},{4,0},{1,9},{9... | collective-permute-start | bytes 479240 | tf_op jit(solution)/shard_map/ppermute | solution.py:500
  25.9 10.3 %collective-permute-start.12 = (bf16[208,384]{1,0:T(8,128)(2,1)S(1)}, bf16[208,384]{1,0:T(8,128)(2,1)S(1)}, u32[]{:S(2)}, u32[]{:S(2)}) collective-permute-start(bf16[208,384]{1,0:T(8,128)(2,1)S(1)} %collective-permute-done.9.rest_14_), channel_id=1, source_target_pairs={{0,8},{8,16},{16,24},{24,28},{28,20},{20,12},{12,4},{4,0},{1,9},{9... | collective-permute-start | bytes 479240 | tf_op jit(solution)/shard_map/ppermute | solution.py:500
  27.5 8.8 %collective-permute-start.13 = (bf16[208,384]{1,0:T(8,128)(2,1)S(1)}, bf16[208,384]{1,0:T(8,128)(2,1)S(1)}, u32[]{:S(2)}, u32[]{:S(2)}) collective-permute-start(bf16[208,384]{1,0:T(8,128)(2,1)S(1)} %collective-permute-done.10.rest_10_), channel_id=1, source_target_pairs={{8,0},{16,8},{24,16},{28,24},{20,28},{12,20},{4,12},{0,4},{9,1},{1... | collective-permute-start | bytes 479240 | tf_op jit(solution)/shard_map/ppermute | solution.py:500
  43.4 10.1 %collective-permute-start.16 = (bf16[288,576]{1,0:T(8,128)(2,1)S(1)}, bf16[288,576]{1,0:T(8,128)(2,1)S(1)}, u32[]{:S(2)}, u32[]{:S(2)}) collective-permute-start(bf16[288,576]{1,0:T(8,128)(2,1)S(1)} %pad_maximum_fusion.1.rest_0_), channel_id=1, source_target_pairs={{8,0},{16,8},{24,16},{28,24},{20,28},{12,20},{4,12},{0,4},{9,1},{1... | collective-permute-start | bytes 995336 | tf_op jit(solution)/shard_map/ppermute | solution.py:500
  43.8 11.1 %collective-permute-start.15 = (bf16[288,576]{1,0:T(8,128)(2,1)S(1)}, bf16[288,576]{1,0:T(8,128)(2,1)S(1)}, u32[]{:S(2)}, u32[]{:S(2)}) collective-permute-start(bf16[288,576]{1,0:T(8,128)(2,1)S(1)} %pad_maximum_fusion.1.rest_0_), channel_id=1, source_target_pairs={{0,8},{8,16},{16,24},{24,28},{28,20},{20,12},{12,4},{4,0},{1,9},{9... | collective-permute-start | bytes 995336 | tf_op jit(solution)/shard_map/ppermute | solution.py:500
  54.9 10.6 %collective-permute-start.17 = (bf16[288,576]{1,0:T(8,128)(2,1)S(1)}, bf16[288,576]{1,0:T(8,128)(2,1)S(1)}, u32[]{:S(2)}, u32[]{:S(2)}) collective-permute-start(bf16[288,576]{1,0:T(8,128)(2,1)S(1)} %collective-permute-done.15.rest_8_), channel_id=1, source_target_pairs={{0,8},{8,16},{16,24},{24,28},{28,20},{20,12},{12,4},{4,0},{1,9},{9... | collective-permute-start | bytes 995336 | tf_op jit(solution)/shard_map/ppermute | solution.py:500
  56.5 10.3 %collective-permute-start.18 = (bf16[288,576]{1,0:T(8,128)(2,1)S(1)}, bf16[288,576]{1,0:T(8,128)(2,1)S(1)}, u32[]{:S(2)}, u32[]{:S(2)}) collective-permute-start(bf16[288,576]{1,0:T(8,128)(2,1)S(1)} %collective-permute-done.16.rest_1_), channel_id=1, source_target_pairs={{8,0},{16,8},{24,16},{28,24},{20,28},{12,20},{4,12},{0,4},{9,1},{1... | collective-permute-start | bytes 995336 | tf_op jit(solution)/shard_map/ppermute | solution.py:500
  66.8 8.7 %collective-permute-start.19 = (bf16[288,576]{1,0:T(8,128)(2,1)S(1)}, bf16[288,576]{1,0:T(8,128)(2,1)S(1)}, u32[]{:S(2)}, u32[]{:S(2)}) collective-permute-start(bf16[288,576]{1,0:T(8,128)(2,1)S(1)} %collective-permute-done.17.rest_7_), channel_id=1, source_target_pairs={{0,8},{8,16},{16,24},{24,28},{28,20},{20,12},{12,4},{4,0},{1,9},{9... | collective-permute-start | bytes 995336 | tf_op jit(solution)/shard_map/ppermute | solution.py:500
  75.9 8.5 %collective-permute-start.21 = (bf16[1024,768]{1,0:T(8,128)(2,1)S(1)}, bf16[1024,768]{1,0:T(8,128)(2,1)S(1)}, u32[]{:S(2)}, u32[]{:S(2)}) collective-permute-start(bf16[1024,768]{1,0:T(8,128)(2,1)S(1)} %get-tuple-element.183.own), channel_id=1, source_target_pairs={{0,1},{1,0},{2,3},{3,2},{4,5},{5,4},{6,7},{7,6},{8,9},{9,8},{10,11... | collective-permute-start | bytes 4718600 | tf_op jit(solution)/shard_map/ppermute | solution.py:444
  107.7 14.4 %collective-permute-start.28 = (bf16[3,96,576]{2,1,0:T(8,128)(2,1)S(1)}, bf16[3,96,576]{2,1,0:T(8,128)(2,1)S(1)}, u32[]{:S(2)}, u32[]{:S(2)}) collective-permute-start(bf16[3,96,576]{2,1,0:T(8,128)(2,1)S(1)} %get-tuple-element.270), channel_id=1, source_target_pairs={{8,0},{16,8},{24,16},{28,24},{20,28},{12,20},{4,12},{0,4},{9,1},{1... | collective-permute-start | bytes 995336 | tf_op jit(solution)/shard_map/ppermute | solution.py:550
  108.1 13.9 %collective-permute-start.27 = (bf16[3,96,576]{2,1,0:T(8,128)(2,1)S(1)}, bf16[3,96,576]{2,1,0:T(8,128)(2,1)S(1)}, u32[]{:S(2)}, u32[]{:S(2)}) collective-permute-start(bf16[3,96,576]{2,1,0:T(8,128)(2,1)S(1)} %get-tuple-element.271), channel_id=1, source_target_pairs={{0,8},{8,16},{16,24},{24,28},{28,20},{20,12},{12,4},{4,0},{1,9},{9... | collective-permute-start | bytes 995336 | tf_op jit(solution)/shard_map/ppermute | solution.py:550
  122.2 10.7 %collective-permute-start.30 = (bf16[3,96,576]{2,1,0:T(8,128)(2,1)S(1)}, bf16[3,96,576]{2,1,0:T(8,128)(2,1)S(1)}, u32[]{:S(2)}, u32[]{:S(2)}) collective-permute-start(bf16[3,96,576]{2,1,0:T(8,128)(2,1)S(1)} %get-tuple-element.268), channel_id=1, source_target_pairs={{8,0},{16,8},{24,16},{28,24},{20,28},{12,20},{4,12},{0,4},{9,1},{1... | collective-permute-start | bytes 995336 | tf_op jit(solution)/shard_map/ppermute | solution.py:550
  122.7 10.2 %collective-permute-start.29 = (bf16[3,96,576]{2,1,0:T(8,128)(2,1)S(1)}, bf16[3,96,576]{2,1,0:T(8,128)(2,1)S(1)}, u32[]{:S(2)}, u32[]{:S(2)}) collective-permute-start(bf16[3,96,576]{2,1,0:T(8,128)(2,1)S(1)} %get-tuple-element.269), channel_id=1, source_target_pairs={{0,8},{8,16},{16,24},{24,28},{28,20},{20,12},{12,4},{4,0},{1,9},{9... | collective-permute-start | bytes 995336 | tf_op jit(solution)/shard_map/ppermute | solution.py:550
  132.9 25.6 %collective-permute-start.34 = (bf16[1152,768]{1,0:T(8,128)(2,1)S(1)}, bf16[1152,768]{1,0:T(8,128)(2,1)S(1)}, u32[]{:S(2)}, u32[]{:S(2)}) collective-permute-start(bf16[1152,768]{1,0:T(8,128)(2,1)S(1)} %first_grad.1.own), channel_id=1, source_target_pairs={{0,1},{1,0},{2,3},{3,2},{4,5},{5,4},{6,7},{7,6},{8,9},{9,8},{10,11... | collective-permute-start | bytes 5308424 | tf_op jit(solution)/shard_map/ppermute | solution.py:444
  133.0 8.7 %collective-permute-start.33 = (bf16[2,96,384]{2,1,0:T(8,128)(2,1)S(1)}, bf16[2,96,384]{2,1,0:T(8,128)(2,1)S(1)}, u32[]{:S(2)}, u32[]{:S(2)}) collective-permute-start(bf16[2,96,384]{2,1,0:T(8,128)(2,1)S(1)} %get-tuple-element.282), channel_id=1, source_target_pairs={{8,0},{16,8},{24,16},{28,24},{20,28},{12,20},{4,12},{0,4},{9,1},{1... | collective-permute-start | bytes 442376 | tf_op jit(solution)/shard_map/ppermute | solution.py:550
  135.1 11.1 %collective-permute-start.37 = (bf16[2,96,384]{2,1,0:T(8,128)(2,1)S(1)}, bf16[2,96,384]{2,1,0:T(8,128)(2,1)S(1)}, u32[]{:S(2)}, u32[]{:S(2)}) collective-permute-start(bf16[2,96,384]{2,1,0:T(8,128)(2,1)S(1)} %get-tuple-element.280), channel_id=1, source_target_pairs={{8,0},{16,8},{24,16},{28,24},{20,28},{12,20},{4,12},{0,4},{9,1},{1... | collective-permute-start | bytes 442376 | tf_op jit(solution)/shard_map/ppermute | solution.py:532
  141.2 11.0 %collective-permute-start.46 = (bf16[3,96,576]{2,1,0:T(8,128)(2,1)S(1)}, bf16[3,96,576]{2,1,0:T(8,128)(2,1)S(1)}, u32[]{:S(2)}, u32[]{:S(2)}) collective-permute-start(bf16[3,96,576]{2,1,0:T(8,128)(2,1)S(1)} %get-tuple-element.266), channel_id=1, source_target_pairs={{8,0},{16,8},{24,16},{28,24},{20,28},{12,20},{4,12},{0,4},{9,1},{1... | collective-permute-start | bytes 995336 | tf_op jit(solution)/shard_map/ppermute | solution.py:550
  141.7 11.9 %collective-permute-start.45 = (bf16[3,96,576]{2,1,0:T(8,128)(2,1)S(1)}, bf16[3,96,576]{2,1,0:T(8,128)(2,1)S(1)}, u32[]{:S(2)}, u32[]{:S(2)}) collective-permute-start(bf16[3,96,576]{2,1,0:T(8,128)(2,1)S(1)} %get-tuple-element.267), channel_id=1, source_target_pairs={{0,8},{8,16},{16,24},{24,28},{28,20},{20,12},{12,4},{4,0},{1,9},{9... | collective-permute-start | bytes 995336 | tf_op jit(solution)/shard_map/ppermute | solution.py:550
  146.2 19.4 %collective-permute-start.36 = (bf16[1024,768]{1,0:T(8,128)(2,1)S(1)}, bf16[1024,768]{1,0:T(8,128)(2,1)S(1)}, u32[]{:S(2)}, u32[]{:S(2)}) collective-permute-start(bf16[1024,768]{1,0:T(8,128)(2,1)S(1)} %feed_out.1.feed_own), channel_id=1, source_target_pairs={{0,1},{1,0},{2,3},{3,2},{4,5},{5,4},{6,7},{7,6},{8,9},{9,8},{10,11... | collective-permute-start | bytes 4718600 | tf_op jit(solution)/shard_map/ppermute | solution.py:444
  153.8 9.1 %collective-permute-start.52 = (bf16[3,96,576]{2,1,0:T(8,128)(2,1)S(1)}, bf16[3,96,576]{2,1,0:T(8,128)(2,1)S(1)}, u32[]{:S(2)}, u32[]{:S(2)}) collective-permute-start(bf16[3,96,576]{2,1,0:T(8,128)(2,1)S(1)} %fusion.1), channel_id=1, source_target_pairs={{0,2},{2,0},{1,3},{3,1},{4,6},{6,4},{5,7},{7,5},{8,10},{10,8},{9,1... | collective-permute-start | bytes 995336 | tf_op jit(solution)/shard_map/ppermute | solution.py:444
  154.4 17.3 %collective-permute-start.40 = (bf16[2,96,384]{2,1,0:T(8,128)(2,1)S(1)}, bf16[2,96,384]{2,1,0:T(8,128)(2,1)S(1)}, u32[]{:S(2)}, u32[]{:S(2)}) collective-permute-start(bf16[2,96,384]{2,1,0:T(8,128)(2,1)S(1)} %get-tuple-element.281), channel_id=1, source_target_pairs={{0,8},{8,16},{16,24},{24,28},{28,20},{20,12},{12,4},{4,0},{1,9},{9... | collective-permute-start | bytes 442376 | tf_op jit(solution)/shard_map/ppermute | solution.py:550
  (37 other events, 302.1 us)

commit v12 on v11

--- a/solution.py
+++ b/solution.py
@@ -136,9 +136,7 @@
     pairs = local // LANES
     groups = slots.shape[0]
     depth = width // groups
-    half = piece_plan(groups, [depth] * 2, -1)
-    later = piece_plan(groups, [depth] * 2 + [PAD], -1)
-    plan = [one + tuple((piece + groups, row) for piece, row in two) for one, two in zip(half, later)]
+    plan = piece_plan(groups, [depth] * 4 + [PAD], 2)
     lane = lax.broadcasted_iota(jnp.int32, (LANES, width), 1) - lax.broadcasted_iota(jnp.int32, (LANES, width), 0)
     gain_sum = jnp.zeros((PAD, width), f32)
     for number, sources in enumerate(plan):
@@ -363,13 +361,17 @@
     loop(extent // BLOCK, turn_step)
 
 
-def grad_kernel_one(slots, first, *rest):
-    parts, (grad_proj, grads, total) = rest[:-3], rest[-3:]
+def grad_kernel_one(slots, first, wide, *rest):
+    parts, (grad_proj, grads, edges, total) = rest[:-4], rest[-4:]
     local = len(parts) * LANES
     for pair, part in enumerate(parts):
         for number in range(3):
             lanes = slice(number * local + pair * LANES, number * local + (pair + 1) * LANES)
             grad_proj[:, lanes] = part[:, number * LANES : (number + 1) * LANES]
+    extent = first.shape[0]
+    for side, start in enumerate((0, extent - HALF)):
+        outer = grad_proj[start : start + HALF, :]
+        edges[side] = dot(outer, wide[:, : 3 * local], NT).astype(bf16)
     weight_grads([(first, grad_proj.at[:, at * local : (at + 1) * local]) for at in range(2)], slots, grads, total)
 
 
@@ -391,17 +393,19 @@
 
 
 def first_kernel(grad_proj, wide, partial):
-    extent, inner = grad_proj.shape
-    size = step_of(extent, 384)
+    rows = partial.shape[0]
+    inner = grad_proj.shape[1]
+    size = step_of(rows, 256)
 
     def step(index):
-        here = pl.ds(pl.multiple_of(index * size, size), size)
-        partial[here, :] = dot(grad_proj[here, :], wide[:, :inner], NT).astype(bf16)
-
-    loop(extent // size, step)
-
-
-def final_kernel(tokens, gain, grad_middle, own, other, before, after, middle, feed_own, feed_other, mixed, token_grad):
+        at = pl.multiple_of(index * size, size)
+        wider = pl.ds(pl.multiple_of(at + HALF, HALF), size)
+        partial[pl.ds(at, size), :] = dot(grad_proj[wider, :], wide[:, :inner], NT).astype(bf16)
+
+    loop(rows // size, step)
+
+
+def token_kernel(tokens, gain, grad_middle, own, other, one, two, token_grad):
     rows, width = tokens.shape
     gains = gain[:1, :]
     size = BLOCK
@@ -411,17 +415,44 @@
         return norm_back(grad, gains, hat, scale)
 
     def step(index):
-        at = pl.multiple_of(index * size, size)
-        here, wider = pl.ds(at, size), pl.ds(pl.multiple_of(at + HALF, HALF), size)
-        grad = own[wider, :].astype(f32) + other[wider, :].astype(f32)
+        here = pl.ds(pl.multiple_of(index * size, size), size)
+        grad = own[here, :].astype(f32) + other[here, :].astype(f32)
         token_grad[here, :] = grad_middle[here, :] + back(here, grad)
-        feed = feed_own[here, :].astype(f32) + feed_other[here, :].astype(f32)
-        mixed[here, :] = (middle[here, :] + feed).astype(bf16)
 
     loop(rows // size, step)
-    for start, edge in ((0, before), (rows - HALF, after)):
+    for side, start in enumerate((0, rows - HALF)):
         here = pl.ds(start, HALF)
-        token_grad[here, :] += back(here, edge[...].astype(f32))
+        token_grad[here, :] += back(here, one[side].astype(f32) + two[side].astype(f32))
+
+
+def mixed_kernel(middle, own, other, mixed):
+    rows = middle.shape[0]
+
+    def step(index):
+        here = pl.ds(pl.multiple_of(index * BLOCK, BLOCK), BLOCK)
+        mixed[here, :] = (middle[here, :] + (own[here, :].astype(f32) + other[here, :].astype(f32))).astype(bf16)
+
+    loop(rows // BLOCK, step)
+
+
+def traded(edges, cross):
+    devices, cores = lax.axis_size("ctx"), lax.axis_size("tensor")
+    spot = lax.axis_index("ctx")
+
+    def pairs(by, start, stop):
+        return [(i * cores + c, (i + by) * cores + (c + cross) % cores) for i in range(start, stop) for c in range(cores)]
+
+    axes = ("ctx", "tensor")
+    if devices == 2:
+        got = lax.ppermute(jnp.where(spot == 0, edges[1], edges[0]), axes, pairs(1, 0, 1) + pairs(-1, 1, 2))
+        none = jnp.zeros_like(got)
+        return jnp.stack([jnp.where(spot == 1, got, none), jnp.where(spot == 0, got, none)])
+    return jnp.stack(
+        [
+            lax.ppermute(edges[1], axes, pairs(1, 0, devices - 1)),
+            lax.ppermute(edges[0], axes, pairs(-1, 1, devices)),
+        ]
+    )
 
 
 def exchange(initial, last):
@@ -587,27 +618,24 @@
     middle_hop = groups // 2
     gains = jnp.pad(jnp.stack([gain_one, gain_two]), ((0, PAD - 2), (0, local - depth)))
     middle_hop = groups // 2
-    now = [
-        RingGather(w_qkv[:2].reshape(2 * depth, local), way=0),
-        RingGather(jnp.concatenate([w_qkv[2], w_out.T, gains]), way=1),
-    ]
-    alternate(*now)
+    now = RingGather(jnp.concatenate([w_qkv.reshape(3 * depth, local), w_out.T, gains]), 2 * depth)
+    now.hop()
     before, after = exchange(tokens[:HALF], tokens[rows - HALF :])
     slots = ring()[-1]
     cosine, sine, bounds = tables(lengths, rows)
-    for chain in now:
-        chain.after([cosine, sine, bounds, slots, before, after])
+    now.hop()
+    now.after([cosine, sine, bounds, slots, before, after])
     hat, = call(
         norm_kernel, [shape((extent, width), f32)], (tokens, before, after), rows * width * 2000, "first_norm"
     )
-    alternate(*now)
-    now[1].after([hat])
-    while now[0].hops < middle_hop:
-        alternate(*now)
+    while now.hops < middle_hop:
+        if now.hops + 1 == middle_hop:
+            now.after([hat])
+        now.hop()
     mine_two = jnp.concatenate([w_in.reshape(2 * depth, units), w_down.T])
-    later = RingGather(tied([mine_two], [*now[0].state, *now[1].state])[0], depth)
+    later = RingGather(tied([mine_two], now.state)[0], depth)
     later.hop()
-    pieces = [piece for chain in now for slot in range(groups) for piece in chain.pieces[slot]]
+    pieces = [piece for slot in range(groups) for piece in now.pieces[slot]]
     wide, gain, first, query, key, value = call(
         project_kernel,
         [
@@ -711,10 +739,14 @@
     )
     grad_parts = locked(grad_parts, sums_two)
     sums_two.hop()
-    grad_proj, grads_a = call(
+    grad_proj, grads_a, edges = call(
         grad_kernel_one,
-        [shape((extent, 3 * local), bf16), shape((groups, 2, depth, local), bf16)],
-        (first, *grad_parts),
+        [
+            shape((extent, 3 * local), bf16),
+            shape((groups, 2, depth, local), bf16),
+            shape((2, HALF, width), bf16),
+        ],
+        (first, wide, *grad_parts),
         2 * rows * width * local * 3,
         "query_key_grads",
         (slots,),
@@ -722,7 +754,7 @@
     )
     first_part, = call(
         first_kernel,
-        [shape((extent, width), bf16)],
+        [shape((rows, width), bf16)],
         (grad_proj, wide),
         2 * rows * width * local * 3,
         "first_grad",
@@ -736,37 +768,44 @@
         (slots,),
         [pltpu.VMEM((2, width, local), bf16)],
     )
-    *grads_one, first_part = locked([grads_a, grads_b, first_part], sums_two)
+    sent = [traded(edges, 0), traded(edges, 1)]
+    *grads_one, first_part, same, cross = locked([grads_a, grads_b, first_part, *sent], sums_two)
     first_other = swap(first_part)
-    def edge_sum(at):
-        here = slice(at, at + HALF)
-        return (first_part[here].astype(f32) + first_other[here].astype(f32)).astype(bf16)
-
-    from_before, from_after = exchange(edge_sum(0), edge_sum(rows + HALF))
     sums_one = [RingScatter([part], way=way) for way, part in enumerate(grads_one)]
     alternate(*sums_one)
     sums_two.after(sums_one[0].state)
     while sums_two.hops < middle_hop:
         sums_two.hop()
 
-    sums_one[1].after([from_before, from_after])
     while sums_one[0].hops < middle_hop - 2:
         alternate(*sums_one)
     sums_one[1].after(sums_two.state)
-    tokens, = tied([tokens], sums_one[0].state)
     alternate(*sums_one)
-    mixed, token_grad = call(
-        final_kernel,
-        [shape((rows, width), bf16), shape((rows, width), f32)],
-        (tokens, gain, grad_middle, first_part, first_other, from_before, from_after, middle, feed, feed_other),
-        rows * width * 2000,
+    alternate(*sums_one)
+    tokens, middle = tied([tokens, middle], sums_one[1].past[-2])
+    token_grad, = call(
+        token_kernel,
+        [shape((rows, width), f32)],
+        (tokens, gain, grad_middle, first_part, first_other, same, cross),
+        rows * width * 200,
         "token_grad",
     )
-    sums_one[0].after([mixed, token_grad])
-    alternate(*sums_one)
     two = over_ctx(sums_two.total())
-    one = over_ctx(sums_one[0].total())
-    one = jnp.concatenate([one, over_ctx(sums_one[1].total())])
+    two, = locked([two], sums_one[1])
+    mixed, = call(
+        mixed_kernel,
+        [shape((rows, width), bf16)],
+        (middle, feed, feed_other),
+        rows * width * 100,
+        "mixed",
+    )
+    one = [chain.total() for chain in sums_one]
+    if lax.axis_size("ctx") == 2:
+        mixed, token_grad, *got = lax.optimization_barrier((mixed, token_grad, *[swap(part, "ctx") for part in one]))
+        one = [part.astype(f32) + more.astype(f32) for part, more in zip(one, got)]
+    else:
+        one = [lax.psum(part, "ctx").astype(f32) for part in one]
+    one = jnp.concatenate(one)
     gain_one_grad = jnp.sum(one[:3] * w_qkv.astype(f32), axis=(0, 2)) / gain_one.astype(f32)
     gain_two_grad = jnp.sum(two[:2] * w_in.astype(f32), axis=(0, 2)) / gain_two.astype(f32)
     both = jnp.stack([gain_one_grad, gain_two_grad])

time: 197 us -> 192 us (0.975)
  waiting for transfers between devices: 60.3 us -> 55.3 us
    ppermute x20 -> x18, starting transfers between devices: 25.3 us -> 8.8 us  [hop(): lax.ppermute(one, 'dp', self.ahead)]
    ppermute x20 -> x18, starting transfers between devices: 17.2 us -> 29.9 us  [hop(): lax.ppermute(two, 'dp', self.back)]
    ppermute x8, waiting for transfers between devices: 8.85 us -> 1.58 us  [swap(): return lax.ppermute(array, axis, [(0, 1), (1, 0)])]
    ppermute x2, waiting for transfers between devices: 5.12 us -> 0.01 us  [traded(): lax.ppermute(jnp.where(spot == 0, edges[1], edges[0]), axes, pairs(1, 0,...]
    ppermute x8, starting transfers between devices: 1.99 us -> 7 us  [swap(): return lax.ppermute(array, axis, [(0, 1), (1, 0)])]
    ppermute x20 -> x18, waiting for transfers between devices: 20.9 us -> 25.9 us  [hop(): lax.ppermute(one, 'dp', self.ahead)]
    ppermute x20 -> x18, waiting for transfers between devices: 20.6 us -> 25 us  [hop(): lax.ppermute(two, 'dp', self.back)]
    pallas_call x13 -> x14, Pallas kernels: 70 us -> 71.5 us  [call(): pl.pallas_call(kernel, out_shape=out_shape, in_specs=[smem] * len(scalars...]
  transfers between devices with their start and end apart: 54 -> 49, of which waited for: 26 -> 29; matrix products, arithmetic and copies ran while one was open for 6% -> 5% of each run, Pallas kernels for 30% -> 30%
where the time goes in v12:
time: 192 us
  Pallas kernels  71.5 us (37%)
  waiting for transfers between devices  55.3 us (29%)
  starting transfers between devices  51.5 us (27%)
  other arithmetic  9.51 us (5%)
  local copies, waits for them, and re-layouts  2.82 us (1%)
    pallas_call x14, Pallas kernels, call(): pl.pallas_call(kernel, out_shape=out_shape, in_specs=[smem] * len(scalars...  71.5 us
    ppermute x18, starting transfers between devices, hop(): lax.ppermute(two, 'dp', self.back)  29.9 us
    ppermute x18, waiting for transfers between devices, hop(): lax.ppermute(one, 'dp', self.ahead)  25.9 us
    ppermute x18, waiting for transfers between devices, hop(): lax.ppermute(two, 'dp', self.back)  25 us
    ppermute x18, starting transfers between devices, hop(): lax.ppermute(one, 'dp', self.ahead)  8.8 us
    ppermute x8, starting transfers between devices, swap(): return lax.ppermute(array, axis, [(0, 1), (1, 0)])  7 us
  transfers between devices with their start and end apart: 49, of which 29 were waited for; matrix products, arithmetic and copies ran while one was open for 5% of the time, Pallas kernels for 30%

profile of v12, /device:TPU:0, one launch (start us, length us, event | category | flops | bytes accessed | tf_op | source)
XLA Modules:
  0.0 191.7 jit_solution(5653888981871126131)
XLA Ops:
  2.5 3.0 %collective-permute-start.2 = (bf16[400,384]{1,0:T(8,128)(2,1)S(1)}, bf16[400,384]{1,0:T(8,128)(2,1)S(1)}, u32[]{:S(2)}, u32[]{:S(2)}) collective-permute-start(bf16[400,384]{1,0:T(8,128)(2,1)S(1)} %pad_maximum_fusion.2.rest_0_), channel_id=1, source_target_pairs={{8,0},{16,8},{24,16},{28,24},{20,28},{12,20},{4,12},{0,4},{9,1},{1... | collective-permute-start | bytes 921608 | tf_op jit(solution)/shard_map/ppermute | solution.py:531
  16.9 5.1 %collective-permute-done.4.rest_2_ = bf16[400,384]{1,0:T(8,128)(2,1)S(1)} collective-permute-done((bf16[400,384]{1,0:T(8,128)(2,1)S(1)}, bf16[400,384]{1,0:T(8,128)(2,1)S(1)}, u32[]{:S(2)}, u32[]{:S(2)}) %collective-permute-start.4) | collective-permute-done | bytes 307232 | tf_op jit(solution)/shard_map/ppermute | solution.py:531
  27.4 2.8 %collective-permute-done.5.rest_6_ = bf16[400,384]{1,0:T(8,128)(2,1)S(1)} collective-permute-done((bf16[400,384]{1,0:T(8,128)(2,1)S(1)}, bf16[400,384]{1,0:T(8,128)(2,1)S(1)}, u32[]{:S(2)}, u32[]{:S(2)}) %collective-permute-start.5) | collective-permute-done | bytes 307232 | tf_op jit(solution)/shard_map/ppermute | solution.py:531
  34.1 6.2 %collective-permute-done.7.rest_4_ = bf16[192,384]{1,0:T(8,128)(2,1)S(1)} collective-permute-done((bf16[192,384]{1,0:T(8,128)(2,1)S(1)}, bf16[192,384]{1,0:T(8,128)(2,1)S(1)}, u32[]{:S(2)}, u32[]{:S(2)}) %collective-permute-start.7) | collective-permute-done | bytes 147488 | tf_op jit(solution)/shard_map/ppermute | solution.py:531
  42.3 5.7 %project.1 = (bf16[768,1536]{1,0:T(8,128)(2,1)S(1)}, f32[16,768]{1,0:T(8,128)S(1)}, bf16[1152,768]{1,0:T(8,128)(2,1)S(1)}, bf16[1024,384]{1,0:T(8,128)(2,1)S(1)}...) custom-call(s32[8]{0:T(128)S(1)} %dynamic-slice_bitcast_fusion.slots, f32[1152,768]{1,0:T(8,128)S(1)} %first_norm.1.hat, ...), custom_call_target="tpu_custom_call" | custom-call | flops 603979776 | bytes 1738752 | tf_op jit(solution)/shard_map/project/pallas_call | solution.py:50
  48.1 3.4 %collective-permute-done.10.rest_1_ = bf16[288,576]{1,0:T(8,128)(2,1)S(1)} collective-permute-done((bf16[288,576]{1,0:T(8,128)(2,1)S(1)}, bf16[288,576]{1,0:T(8,128)(2,1)S(1)}, u32[]{:S(2)}, u32[]{:S(2)}) %collective-permute-start.10) | collective-permute-done | bytes 331808 | tf_op jit(solution)/shard_map/ppermute | solution.py:531
  54.0 7.7 %attend.2 = (bf16[16,256,256]{2,1,0:T(8,128)(2,1)S(1)}, bf16[1024,384]{1,0:T(8,128)(2,1)S(1)}) custom-call(s32[5]{0:T(128)S(1)} %pad_add_fusion.bounds, bf16[1024,384]{1,0:T(8,128)(2,1)S(1)} %get-tuple-element.145.query, bf16[1152,384]{1,0:T(8,128)(2,1)S(1)} %get-tuple-element.146.key, bf16[1152,384]{1,0:T(8,128)(2,1)S(1)} %get-tuple-element.147.value), custom_call_target="tpu_custom_call" | custom-call | flops 754974720 | bytes 679936 | tf_op jit(solution)/shard_map/attend/pallas_call | solution.py:50
  64.6 6.6 %attend.3 = (bf16[8,256,256]{2,1,0:T(8,128)(2,1)S(1)}, bf16[1024,384]{1,0:T(8,128)(2,1)S(1)}, bf16[1024,768]{1,0:T(8,128)(2,1)S(1)}) custom-call(s32[5]{0:T(128)S(1)} %pad_add_fusion.bounds, bf16[1024,384]{1,0:T(8,128)(2,1)S(1)} %get-tuple-element.145.query, bf16[1152,384]{1,0:T(8,128)(2,1)S(1)} %get-tuple-element.146.key, ...), custom_call_target="tpu_custom_call" | custom-call | flops 528482304 | bytes 1138688 | tf_op jit(solution)/shard_map/attend/pallas_call | solution.py:50
  73.7 5.0 %collective-permute-done.16.rest_4_ = bf16[96,576]{1,0:T(8,128)(2,1)S(1)} collective-permute-done((bf16[96,576]{1,0:T(8,128)(2,1)S(1)}, bf16[96,576]{1,0:T(8,128)(2,1)S(1)}, u32[]{:S(2)}, u32[]{:S(2)}) %collective-permute-start.16) | collective-permute-done | bytes 110624 | tf_op jit(solution)/shard_map/ppermute | solution.py:531
  79.8 10.6 %feed_forward_and_back.1 = (f32[1024,768]{1,0:T(8,128)S(1)}, bf16[1024,768]{1,0:T(8,128)(2,1)S(1)}, bf16[1024,576]{1,0:T(8,128)(2,1)S(1)}, bf16[1024,576]{1,0:T(...) custom-call(s32[8]{0:T(128)S(1)} %dynamic-slice_bitcast_fusion.slots, ...), custom_call_target="tpu_custom_call" | custom-call | flops 905969664 | bytes 2684928 | tf_op jit(solution)/shard_map/feed_forward_and_back/pallas_call | solution.py:50
  90.4 4.7 %feed_weight_grads.1 = bf16[8,3,96,576]{3,2,1,0:T(8,128)(2,1)S(1)} custom-call(s32[8]{0:T(128)S(1)} %dynamic-slice_bitcast_fusion.slots, bf16[1024,768]{1,0:T(8,128)(2,1)S(1)} %get-tuple-element.171.second, bf16[1024,576]{1,0:T(8,128)(2,1)S(1)} %get-tuple-element.175.hidden, bf16[1024,576]{1,0:T(8,128)(2,1)S(1)} %get-tuple-element.172.grad_gate, ...), custom_call_target="tpu_custom_call" | custom-call | flops 566231040 | bytes 1167360 | tf_op jit(solution)/shard_map/feed_weight_grads/pallas_call | solution.py:50
  99.4 3.6 %middle_grad.1 = (f32[1024,768]{1,0:T(8,128)S(1)}, bf16[1024,768]{1,0:T(8,128)(2,1)S(1)}, bf16[1024,384]{1,0:T(8,128)(2,1)S(1)}) custom-call(f32[1024,768]{1,0:T(8,128)S(1)} %get-tuple-element.220.middle, bf16[1024,768]{1,0:T(8,128)(2,1)S(1)} %get-tuple-element.168.own, bf16[1024,768]{1,0:T(8,128)(2,1)S(1)} %collective-permute-done.18.other, ...), custom_call_target="tpu_custom_call" | custom-call | flops 301989888 | bytes 1972224 | tf_op jit(solution)/shard_map/middle_grad/pallas_call | solution.py:50
  105.8 12.3 %attention_back.1 = (bf16[1152,384]{1,0:T(8,128)(2,1)S(1)}, bf16[1152,384]{1,0:T(8,128)(2,1)S(1)}, bf16[1152,384]{1,0:T(8,128)(2,1)S(1)}) custom-call(bf16[1024,384]{1,0:T(8,128)(2,1)S(1)} %get-tuple-element.145.query, bf16[1152,384]{1,0:T(8,128)(2,1)S(1)} %get-tuple-element.146.key, bf16[1152,384]{1,0:T(8,128)(2,1)S(1)} %get-tuple-element.147.value, ...), custom_call_target="tpu_custom_call" | custom-call | flops 1132462080 | bytes 1290240 | tf_op jit(solution)/shard_map/attention_back/pallas_call | solution.py:50
  118.2 4.0 %query_key_grads.1 = (bf16[1152,1152]{1,0:T(8,128)(2,1)S(1)}, bf16[8,2,96,384]{3,2,1,0:T(8,128)(2,1)S(1)}, bf16[2,64,768]{2,1,0:T(8,128)(2,1)S(1)}) custom-call(s32[8]{0:T(128)S(1)} %dynamic-slice_bitcast_fusion.slots, bf16[1152,768]{1,0:T(8,128)(2,1)S(1)} %get-tuple-element.167.first, bf16[768,1536]{1,0:T(8,128)(2,1)S(1)} %get-tuple-element.148.rest_0_.wide, ...), custom_call_target="tpu_custom_call" | custom-call | flops 226492416 | bytes 1351680 | tf_op jit(solution)/shard_map/query_key_grads/pallas_call | solution.py:50
  126.3 2.9 %first_grad.1.own = bf16[1024,768]{1,0:T(8,128)(2,1)S(1)} custom-call(bf16[1152,1152]{1,0:T(8,128)(2,1)S(1)} %get-tuple-element.193.grad_proj, bf16[768,1536]{1,0:T(8,128)(2,1)S(1)} %get-tuple-element.148.rest_0_.wide), custom_call_target="tpu_custom_call" | custom-call | flops 226492416 | bytes 823296 | tf_op jit(solution)/shard_map/first_grad/pallas_call | solution.py:50
  129.2 2.7 %value_out_grads.1 = bf16[8,2,96,384]{3,2,1,0:T(8,128)(2,1)S(1)} custom-call(s32[8]{0:T(128)S(1)} %dynamic-slice_bitcast_fusion.slots, bf16[1152,768]{1,0:T(8,128)(2,1)S(1)} %get-tuple-element.167.first, bf16[1152,1152]{1,0:T(8,128)(2,1)S(1)} %get-tuple-element.193.grad_proj, bf16[1024,768]{1,0:T(8,128)(2,1)S(1)} %get-tuple-element.194.low_mid, ...), custom_call_target="tpu_custom_call" | custom-call | flops 226492416 | bytes 995328 | tf_op jit(solution)/shard_map/value_out_grads/pallas_call | solution.py:50
  132.0 3.0 %collective-permute-done.26 = bf16[3,96,576]{2,1,0:T(8,128)(2,1)S(1)} collective-permute-done((bf16[3,96,576]{2,1,0:T(8,128)(2,1)S(1)}, bf16[3,96,576]{2,1,0:T(8,128)(2,1)S(1)}, u32[]{:S(2)}, u32[]{:S(2)}) %collective-permute-start.26) | collective-permute-done | bytes 331808 | tf_op jit(solution)/shard_map/ppermute | solution.py:581
  140.5 2.6 %collective-permute-done.29 = bf16[2,96,384]{2,1,0:T(8,128)(2,1)S(1)} collective-permute-done((bf16[2,96,384]{2,1,0:T(8,128)(2,1)S(1)}, bf16[2,96,384]{2,1,0:T(8,128)(2,1)S(1)}, u32[]{:S(2)}, u32[]{:S(2)}) %collective-permute-start.29) | collective-permute-done | bytes 147488 | tf_op jit(solution)/shard_map/ppermute | solution.py:563
  146.3 2.3 %collective-permute-done.33 = bf16[2,96,384]{2,1,0:T(8,128)(2,1)S(1)} collective-permute-done((bf16[2,96,384]{2,1,0:T(8,128)(2,1)S(1)}, bf16[2,96,384]{2,1,0:T(8,128)(2,1)S(1)}, u32[]{:S(2)}, u32[]{:S(2)}) %collective-permute-start.33) | collective-permute-done | bytes 147488 | tf_op jit(solution)/shard_map/ppermute | solution.py:581
  152.9 2.6 %collective-permute-done.40 = bf16[2,96,384]{2,1,0:T(8,128)(2,1)S(1)} collective-permute-done((bf16[2,96,384]{2,1,0:T(8,128)(2,1)S(1)}, bf16[2,96,384]{2,1,0:T(8,128)(2,1)S(1)}, u32[]{:S(2)}, u32[]{:S(2)}) %collective-permute-start.40) | collective-permute-done | bytes 147488 | tf_op jit(solution)/shard_map/ppermute | solution.py:581
  159.2 3.5 %collective-permute-done.32 = bf16[3,96,576]{2,1,0:T(8,128)(2,1)S(1)} collective-permute-done((bf16[3,96,576]{2,1,0:T(8,128)(2,1)S(1)}, bf16[3,96,576]{2,1,0:T(8,128)(2,1)S(1)}, u32[]{:S(2)}, u32[]{:S(2)}) %collective-permute-start.32) | collective-permute-done | bytes 331808 | tf_op jit(solution)/shard_map/ppermute | solution.py:581
  166.4 2.7 %collective-permute-start.44 = (bf16[3,96,576]{2,1,0:T(8,128)(2,1)S(1)}, bf16[3,96,576]{2,1,0:T(8,128)(2,1)S(1)}, u32[]{:S(2)}, u32[]{:S(2)}) collective-permute-start(bf16[3,96,576]{2,1,0:T(8,128)(2,1)S(1)} %fusion.1), channel_id=1, source_target_pairs={{0,2},{2,0},{1,3},{3,1},{4,6},{6,4},{5,7},{7,5},{8,10},{10,8},{9,1... | collective-permute-start | bytes 995336 | tf_op jit(solution)/shard_map/ppermute | solution.py:475
  172.4 3.0 %collective-permute-done.46 = bf16[2,96,384]{2,1,0:T(8,128)(2,1)S(1)} collective-permute-done((bf16[2,96,384]{2,1,0:T(8,128)(2,1)S(1)}, bf16[2,96,384]{2,1,0:T(8,128)(2,1)S(1)}, u32[]{:S(2)}, u32[]{:S(2)}) %collective-permute-start.46) | collective-permute-done | bytes 147488 | tf_op jit(solution)/shard_map/ppermute | solution.py:581
  184.0 4.9 %token_grad.1 = f32[1024,768]{1,0:T(8,128)} custom-call(bf16[1024,768]{1,0:T(8,128)(2,1)S(1)} %copy-done, f32[16,768]{1,0:T(8,128)S(1)} %get-tuple-element.161.gain, f32[1024,768]{1,0:T(8,128)S(1)} %get-tuple-element.223.grad_middle, bf16[1024,768]{1,0:T(8,128)(2,1)S(1)} %first_grad.1.own, bf16[1024,768]{1,0:T(8,128)(2,1)S(1)} %collective-permute-done.38.other, ...), custom_call_target="tpu_custom_call" | custom-call | flops 19660800 | bytes 1431552 | tf_op jit(solution)/shard_map/token_grad/pallas_call | solution.py:50
  (153 shorter events, 79.6 us)
Async XLA Ops:
  2.5 10.3 %collective-permute-start.2 = (bf16[400,384]{1,0:T(8,128)(2,1)S(1)}, bf16[400,384]{1,0:T(8,128)(2,1)S(1)}, u32[]{:S(2)}, u32[]{:S(2)}) collective-permute-start(bf16[400,384]{1,0:T(8,128)(2,1)S(1)} %pad_maximum_fusion.2.rest_0_), channel_id=1, source_target_pairs={{8,0},{16,8},{24,16},{28,24},{20,28},{12,20},{4,12},{0,4},{9,1},{1... | collective-permute-start | bytes 921608 | tf_op jit(solution)/shard_map/ppermute | solution.py:531
  5.4 8.7 %collective-permute-start.1 = (bf16[400,384]{1,0:T(8,128)(2,1)S(1)}, bf16[400,384]{1,0:T(8,128)(2,1)S(1)}, u32[]{:S(2)}, u32[]{:S(2)}) collective-permute-start(bf16[400,384]{1,0:T(8,128)(2,1)S(1)} %pad_maximum_fusion.2.rest_0_), channel_id=1, source_target_pairs={{0,8},{8,16},{16,24},{24,28},{28,20},{20,12},{12,4},{4,0},{1,9},{9... | collective-permute-start | bytes 921608 | tf_op jit(solution)/shard_map/ppermute | solution.py:531
  6.6 10.3 %collective-permute-start = (bf16[64,768]{1,0:T(8,128)(2,1)S(1)}, bf16[64,768]{1,0:T(8,128)(2,1)S(1)}, u32[]{:S(2)}, u32[]{:S(2)}) collective-permute-start(bf16[64,768]{1,0:T(8,128)(2,1)S(1)} %slice_select_fusion), channel_id=1, source_target_pairs={{0,2},{2,0},{1,3},{3,1},{4,6},{6,4},{5,7},{7,5},{8,10},{10,8},{9,1... | collective-permute-start | bytes 294920 | tf_op jit(solution)/shard_map/ppermute | solution.py:461
  40.3 11.2 %collective-permute-start.10 = (bf16[288,576]{1,0:T(8,128)(2,1)S(1)}, bf16[288,576]{1,0:T(8,128)(2,1)S(1)}, u32[]{:S(2)}, u32[]{:S(2)}) collective-permute-start(bf16[288,576]{1,0:T(8,128)(2,1)S(1)} %pad_maximum_fusion.1.rest_0_), channel_id=1, source_target_pairs={{8,0},{16,8},{24,16},{28,24},{20,28},{12,20},{4,12},{0,4},{9,1},{1... | collective-permute-start | bytes 995336 | tf_op jit(solution)/shard_map/ppermute | solution.py:531
  41.9 10.1 %collective-permute-start.9 = (bf16[288,576]{1,0:T(8,128)(2,1)S(1)}, bf16[288,576]{1,0:T(8,128)(2,1)S(1)}, u32[]{:S(2)}, u32[]{:S(2)}) collective-permute-start(bf16[288,576]{1,0:T(8,128)(2,1)S(1)} %pad_maximum_fusion.1.rest_0_), channel_id=1, source_target_pairs={{0,8},{8,16},{16,24},{24,28},{28,20},{20,12},{12,4},{4,0},{1,9},{9... | collective-permute-start | bytes 995336 | tf_op jit(solution)/shard_map/ppermute | solution.py:531
  51.9 10.4 %collective-permute-start.11 = (bf16[288,576]{1,0:T(8,128)(2,1)S(1)}, bf16[288,576]{1,0:T(8,128)(2,1)S(1)}, u32[]{:S(2)}, u32[]{:S(2)}) collective-permute-start(bf16[288,576]{1,0:T(8,128)(2,1)S(1)} %collective-permute-done.9.rest_8_), channel_id=1, source_target_pairs={{0,8},{8,16},{16,24},{24,28},{28,20},{20,12},{12,4},{4,0},{1,9},{9... | collective-permute-start | bytes 995336 | tf_op jit(solution)/shard_map/ppermute | solution.py:531
  52.3 10.2 %collective-permute-start.12 = (bf16[288,576]{1,0:T(8,128)(2,1)S(1)}, bf16[288,576]{1,0:T(8,128)(2,1)S(1)}, u32[]{:S(2)}, u32[]{:S(2)}) collective-permute-start(bf16[288,576]{1,0:T(8,128)(2,1)S(1)} %collective-permute-done.10.rest_1_), channel_id=1, source_target_pairs={{8,0},{16,8},{24,16},{28,24},{20,28},{12,20},{4,12},{0,4},{9,1},{1... | collective-permute-start | bytes 995336 | tf_op jit(solution)/shard_map/ppermute | solution.py:531
  62.6 8.7 %collective-permute-start.13 = (bf16[288,576]{1,0:T(8,128)(2,1)S(1)}, bf16[288,576]{1,0:T(8,128)(2,1)S(1)}, u32[]{:S(2)}, u32[]{:S(2)}) collective-permute-start(bf16[288,576]{1,0:T(8,128)(2,1)S(1)} %collective-permute-done.11.rest_7_), channel_id=1, source_target_pairs={{0,8},{8,16},{16,24},{24,28},{28,20},{20,12},{12,4},{4,0},{1,9},{9... | collective-permute-start | bytes 995336 | tf_op jit(solution)/shard_map/ppermute | solution.py:531
  103.7 14.4 %collective-permute-start.22 = (bf16[3,96,576]{2,1,0:T(8,128)(2,1)S(1)}, bf16[3,96,576]{2,1,0:T(8,128)(2,1)S(1)}, u32[]{:S(2)}, u32[]{:S(2)}) collective-permute-start(bf16[3,96,576]{2,1,0:T(8,128)(2,1)S(1)} %get-tuple-element.254), channel_id=1, source_target_pairs={{8,0},{16,8},{24,16},{28,24},{20,28},{12,20},{4,12},{0,4},{9,1},{1... | collective-permute-start | bytes 995336 | tf_op jit(solution)/shard_map/ppermute | solution.py:581
  105.3 12.8 %collective-permute-start.21 = (bf16[3,96,576]{2,1,0:T(8,128)(2,1)S(1)}, bf16[3,96,576]{2,1,0:T(8,128)(2,1)S(1)}, u32[]{:S(2)}, u32[]{:S(2)}) collective-permute-start(bf16[3,96,576]{2,1,0:T(8,128)(2,1)S(1)} %get-tuple-element.255), channel_id=1, source_target_pairs={{0,8},{8,16},{16,24},{24,28},{28,20},{20,12},{12,4},{4,0},{1,9},{9... | collective-permute-start | bytes 995336 | tf_op jit(solution)/shard_map/ppermute | solution.py:581
  122.2 9.7 %collective-permute-start.24 = (bf16[64,768]{1,0:T(8,128)(2,1)S(1)}, bf16[64,768]{1,0:T(8,128)(2,1)S(1)}, u32[]{:S(2)}, u32[]{:S(2)}) collective-permute-start(bf16[64,768]{1,0:T(8,128)(2,1)S(1)} %select_bitcast_fusion.4), channel_id=1, source_target_pairs={{0,3},{1,2},{2,1},{3,0},{4,7},{5,6},{6,5},{7,4},{8,11},{9,10},{10,... | collective-permute-start | bytes 294920 | tf_op jit(solution)/shard_map/ppermute | solution.py:447
  122.3 9.6 %collective-permute-start.23 = (bf16[64,768]{1,0:T(8,128)(2,1)S(1)}, bf16[64,768]{1,0:T(8,128)(2,1)S(1)}, u32[]{:S(2)}, u32[]{:S(2)}) collective-permute-start(bf16[64,768]{1,0:T(8,128)(2,1)S(1)} %select_bitcast_fusion.4), channel_id=1, source_target_pairs={{0,2},{1,3},{2,0},{3,1},{4,6},{5,7},{6,4},{7,5},{8,10},{9,11},{10,... | collective-permute-start | bytes 294920 | tf_op jit(solution)/shard_map/ppermute | solution.py:447
  124.0 11.0 %collective-permute-start.26 = (bf16[3,96,576]{2,1,0:T(8,128)(2,1)S(1)}, bf16[3,96,576]{2,1,0:T(8,128)(2,1)S(1)}, u32[]{:S(2)}, u32[]{:S(2)}) collective-permute-start(bf16[3,96,576]{2,1,0:T(8,128)(2,1)S(1)} %get-tuple-element.252), channel_id=1, source_target_pairs={{8,0},{16,8},{24,16},{28,24},{20,28},{12,20},{4,12},{0,4},{9,1},{1... | collective-permute-start | bytes 995336 | tf_op jit(solution)/shard_map/ppermute | solution.py:581
  125.8 10.5 %collective-permute-start.25 = (bf16[3,96,576]{2,1,0:T(8,128)(2,1)S(1)}, bf16[3,96,576]{2,1,0:T(8,128)(2,1)S(1)}, u32[]{:S(2)}, u32[]{:S(2)}) collective-permute-start(bf16[3,96,576]{2,1,0:T(8,128)(2,1)S(1)} %get-tuple-element.253), channel_id=1, source_target_pairs={{0,8},{8,16},{16,24},{24,28},{28,20},{20,12},{12,4},{4,0},{1,9},{9... | collective-permute-start | bytes 995336 | tf_op jit(solution)/shard_map/ppermute | solution.py:581
  138.5 14.0 %collective-permute-start.27 = (bf16[2,96,384]{2,1,0:T(8,128)(2,1)S(1)}, bf16[2,96,384]{2,1,0:T(8,128)(2,1)S(1)}, u32[]{:S(2)}, u32[]{:S(2)}) collective-permute-start(bf16[2,96,384]{2,1,0:T(8,128)(2,1)S(1)} %get-tuple-element.267), channel_id=1, source_target_pairs={{0,8},{8,16},{16,24},{24,28},{28,20},{20,12},{12,4},{4,0},{1,9},{9... | collective-permute-start | bytes 442376 | tf_op jit(solution)/shard_map/ppermute | solution.py:581
  143.7 9.2 %collective-permute-start.30 = (bf16[2,96,384]{2,1,0:T(8,128)(2,1)S(1)}, bf16[2,96,384]{2,1,0:T(8,128)(2,1)S(1)}, u32[]{:S(2)}, u32[]{:S(2)}) collective-permute-start(bf16[2,96,384]{2,1,0:T(8,128)(2,1)S(1)} %bitcast_add_fusion.14), channel_id=1, source_target_pairs={{8,0},{16,8},{24,16},{28,24},{20,28},{12,20},{4,12},{0,4},{9,1},{1... | collective-permute-start | bytes 442376 | tf_op jit(solution)/shard_map/ppermute | solution.py:581
  150.8 11.9 %collective-permute-start.32 = (bf16[3,96,576]{2,1,0:T(8,128)(2,1)S(1)}, bf16[3,96,576]{2,1,0:T(8,128)(2,1)S(1)}, u32[]{:S(2)}, u32[]{:S(2)}) collective-permute-start(bf16[3,96,576]{2,1,0:T(8,128)(2,1)S(1)} %get-tuple-element.250), channel_id=1, source_target_pairs={{8,0},{16,8},{24,16},{28,24},{20,28},{12,20},{4,12},{0,4},{9,1},{1... | collective-permute-start | bytes 995336 | tf_op jit(solution)/shard_map/ppermute | solution.py:581
  152.5 11.5 %collective-permute-start.31 = (bf16[3,96,576]{2,1,0:T(8,128)(2,1)S(1)}, bf16[3,96,576]{2,1,0:T(8,128)(2,1)S(1)}, u32[]{:S(2)}, u32[]{:S(2)}) collective-permute-start(bf16[3,96,576]{2,1,0:T(8,128)(2,1)S(1)} %get-tuple-element.251), channel_id=1, source_target_pairs={{0,8},{8,16},{16,24},{24,28},{28,20},{20,12},{12,4},{4,0},{1,9},{9... | collective-permute-start | bytes 995336 | tf_op jit(solution)/shard_map/ppermute | solution.py:581
  152.9 29.5 %collective-permute-start.37 = (bf16[1024,768]{1,0:T(8,128)(2,1)S(1)}, bf16[1024,768]{1,0:T(8,128)(2,1)S(1)}, u32[]{:S(2)}, u32[]{:S(2)}) collective-permute-start(bf16[1024,768]{1,0:T(8,128)(2,1)S(1)} %feed_out.1.own), channel_id=1, source_target_pairs={{0,1},{1,0},{2,3},{3,2},{4,5},{5,4},{6,7},{7,6},{8,9},{9,8},{10,11... | collective-permute-start | bytes 4718600 | tf_op jit(solution)/shard_map/ppermute | solution.py:475
  157.1 9.2 %collective-permute-start.42 = (bf16[2,96,384]{2,1,0:T(8,128)(2,1)S(1)}, bf16[2,96,384]{2,1,0:T(8,128)(2,1)S(1)}, u32[]{:S(2)}, u32[]{:S(2)}) collective-permute-start(bf16[2,96,384]{2,1,0:T(8,128)(2,1)S(1)} %get-tuple-element.258), channel_id=1, source_target_pairs={{8,0},{16,8},{24,16},{28,24},{20,28},{12,20},{4,12},{0,4},{9,1},{1... | collective-permute-start | bytes 442376 | tf_op jit(solution)/shard_map/ppermute | solution.py:581
  166.3 17.7 %collective-permute-start.38 = (bf16[1024,768]{1,0:T(8,128)(2,1)S(1)}, bf16[1024,768]{1,0:T(8,128)(2,1)S(1)}, u32[]{:S(2)}, u32[]{:S(2)}) collective-permute-start(bf16[1024,768]{1,0:T(8,128)(2,1)S(1)} %first_grad.1.own), channel_id=1, source_target_pairs={{0,1},{1,0},{2,3},{3,2},{4,5},{5,4},{6,7},{7,6},{8,9},{9,8},{10,11... | collective-permute-start | bytes 4718600 | tf_op jit(solution)/shard_map/ppermute | solution.py:475
  166.4 12.1 %collective-permute-start.44 = (bf16[3,96,576]{2,1,0:T(8,128)(2,1)S(1)}, bf16[3,96,576]{2,1,0:T(8,128)(2,1)S(1)}, u32[]{:S(2)}, u32[]{:S(2)}) collective-permute-start(bf16[3,96,576]{2,1,0:T(8,128)(2,1)S(1)} %fusion.1), channel_id=1, source_target_pairs={{0,2},{2,0},{1,3},{3,1},{4,6},{6,4},{5,7},{7,5},{8,10},{10,8},{9,1... | collective-permute-start | bytes 995336 | tf_op jit(solution)/shard_map/ppermute | solution.py:475
  175.4 13.5 %collective-permute-start.43 = (bf16[2,96,384]{2,1,0:T(8,128)(2,1)S(1)}, bf16[2,96,384]{2,1,0:T(8,128)(2,1)S(1)}, u32[]{:S(2)}, u32[]{:S(2)}) collective-permute-start(bf16[2,96,384]{2,1,0:T(8,128)(2,1)S(1)} %fusion.5), channel_id=1, source_target_pairs={{0,2},{2,0},{1,3},{3,1},{4,6},{6,4},{5,7},{7,5},{8,10},{10,8},{9,1... | collective-permute-start | bytes 442376 | tf_op jit(solution)/shard_map/ppermute | solution.py:475
  178.7 10.2 %collective-permute-start.47 = (bf16[2,96,384]{2,1,0:T(8,128)(2,1)S(1)}, bf16[2,96,384]{2,1,0:T(8,128)(2,1)S(1)}, u32[]{:S(2)}, u32[]{:S(2)}) collective-permute-start(bf16[2,96,384]{2,1,0:T(8,128)(2,1)S(1)} %fusion.3), channel_id=1, source_target_pairs={{0,2},{2,0},{1,3},{3,1},{4,6},{6,4},{5,7},{7,5},{8,10},{10,8},{9,1... | collective-permute-start | bytes 442376 | tf_op jit(solution)/shard_map/ppermute | solution.py:475
  (32 other events, 242.9 us)

commit v13 on v12

--- a/solution.py
+++ b/solution.py
@@ -182,8 +182,7 @@
 
 def attend_kernel(chosen, last, bounds, query, key, value, *rest):
     if last:
-        wide, done, shares, attended, branch = rest
-        attended[...] = done[...]
+        wide, shares, attended, branch = rest
     else:
         shares, attended = rest
     rows, local = query.shape
@@ -361,17 +360,13 @@
     loop(extent // BLOCK, turn_step)
 
 
-def grad_kernel_one(slots, first, wide, *rest):
-    parts, (grad_proj, grads, edges, total) = rest[:-4], rest[-4:]
+def grad_kernel_one(slots, first, *rest):
+    parts, (grad_proj, grads, total) = rest[:-3], rest[-3:]
     local = len(parts) * LANES
     for pair, part in enumerate(parts):
         for number in range(3):
             lanes = slice(number * local + pair * LANES, number * local + (pair + 1) * LANES)
             grad_proj[:, lanes] = part[:, number * LANES : (number + 1) * LANES]
-    extent = first.shape[0]
-    for side, start in enumerate((0, extent - HALF)):
-        outer = grad_proj[start : start + HALF, :]
-        edges[side] = dot(outer, wide[:, : 3 * local], NT).astype(bf16)
     weight_grads([(first, grad_proj.at[:, at * local : (at + 1) * local]) for at in range(2)], slots, grads, total)
 
 
@@ -392,8 +387,11 @@
         grads[number] = total[:, pl.ds(pl.multiple_of(slots[slot] * depth, depth), depth), :]
 
 
-def first_kernel(grad_proj, wide, partial):
+def first_kernel(grad_proj, wide, partial, edges):
     rows = partial.shape[0]
+    for side, start in enumerate((0, rows + HALF)):
+        outer = grad_proj[start : start + HALF, :]
+        edges[side] = dot(outer, wide[:, : outer.shape[1]], NT).astype(bf16)
     inner = grad_proj.shape[1]
     size = step_of(rows, 256)
 
@@ -623,7 +621,10 @@
     before, after = exchange(tokens[:HALF], tokens[rows - HALF :])
     slots = ring()[-1]
     cosine, sine, bounds = tables(lengths, rows)
+    mine_two = jnp.concatenate([w_in.reshape(2 * depth, units), w_down.T])
+    later = RingGather(tied([mine_two], now.state)[0], depth)
     now.hop()
+    later.hop()
     now.after([cosine, sine, bounds, slots, before, after])
     hat, = call(
         norm_kernel, [shape((extent, width), f32)], (tokens, before, after), rows * width * 2000, "first_norm"
@@ -632,9 +633,11 @@
         if now.hops + 1 == middle_hop:
             now.after([hat])
         now.hop()
-    mine_two = jnp.concatenate([w_in.reshape(2 * depth, units), w_down.T])
-    later = RingGather(tied([mine_two], now.state)[0], depth)
-    later.hop()
+        later.after(now.past[-2])
+        later.hop()
+    later.after(now.state)
+    while later.hops < middle_hop:
+        later.hop()
     pieces = [piece for slot in range(groups) for piece in now.pieces[slot]]
     wide, gain, first, query, key, value = call(
         project_kernel,
@@ -651,36 +654,21 @@
         "project",
         (slots,),
     )
-    early, late = tuple(range(pairs - 1)), (pairs - 1,)
-
-    query, key, value = locked([query, key, value], later)
-    later.hop()
-    shares_early, attended = call(
-        functools.partial(attend_kernel, early, False),
-        [shape((blocks * len(early), KEYS, KEYS), bf16), shape((rows, local), bf16)],
-        (query, key, value),
-        2 * rows * width * local * 10,
-        "attend",
-        (bounds,),
-    )
-    attended, = locked([attended], later)
-    later.hop()
-    shares_late, attended, branch = call(
-        functools.partial(attend_kernel, late, True),
+    query, key, value = tied([query, key, value], later.state)
+    everything = tuple(range(pairs))
+    shares, attended, branch = call(
+        functools.partial(attend_kernel, everything, True),
         [
-            shape((blocks * len(late), KEYS, KEYS), bf16),
+            shape((blocks * pairs, KEYS, KEYS), bf16),
             shape((rows, local), bf16),
             shape((rows, width), bf16),
         ],
-        (query, key, value, wide, attended),
-        2 * rows * width * local * 7,
+        (query, key, value, wide),
+        2 * rows * width * local * 16,
         "attend",
         (bounds,),
     )
-    branch, = locked([branch], later)
     branch_other = swap(branch)
-    while later.hops < middle_hop:
-        later.hop()
     pieces = [piece for slot in range(groups) for piece in later.pieces[slot]]
     middle, second, hidden, grad_gate, grad_upper, partial, whole = call(
         feed_kernel,
@@ -729,9 +717,9 @@
     feed_other = swap(feed)
     sums_two.hop()
     grad_parts = call(
-        functools.partial(back_kernel, (early, late)),
+        functools.partial(back_kernel, (everything,)),
         [shape((extent, 3 * LANES), bf16)] * pairs,
-        (query, key, value, grad_att, cosine, sine, shares_early, shares_late),
+        (query, key, value, grad_att, cosine, sine, shares),
         2 * rows * width * local * 15,
         "attention_back",
         (),
@@ -739,22 +727,21 @@
     )
     grad_parts = locked(grad_parts, sums_two)
     sums_two.hop()
-    grad_proj, grads_a, edges = call(
+    grad_proj, grads_a = call(
         grad_kernel_one,
         [
             shape((extent, 3 * local), bf16),
             shape((groups, 2, depth, local), bf16),
-            shape((2, HALF, width), bf16),
         ],
-        (first, wide, *grad_parts),
+        (first, *grad_parts),
         2 * rows * width * local * 3,
         "query_key_grads",
         (slots,),
         [pltpu.VMEM((2, width, local), bf16)],
     )
-    first_part, = call(
+    first_part, edges = call(
         first_kernel,
-        [shape((rows, width), bf16)],
+        [shape((rows, width), bf16), shape((2, HALF, width), bf16)],
         (grad_proj, wide),
         2 * rows * width * local * 3,
         "first_grad",
@@ -768,21 +755,33 @@
         (slots,),
         [pltpu.VMEM((2, width, local), bf16)],
     )
-    sent = [traded(edges, 0), traded(edges, 1)]
-    *grads_one, first_part, same, cross = locked([grads_a, grads_b, first_part, *sent], sums_two)
+    *grads_one, first_part, edges = locked([grads_a, grads_b, first_part, edges], sums_two)
+    same, cross = traded(edges, 0), traded(edges, 1)
     first_other = swap(first_part)
     sums_one = [RingScatter([part], way=way) for way, part in enumerate(grads_one)]
     alternate(*sums_one)
-    sums_two.after(sums_one[0].state)
     while sums_two.hops < middle_hop:
         sums_two.hop()
 
+    for chain in sums_one:
+        chain.after(sums_two.state)
     while sums_one[0].hops < middle_hop - 2:
         alternate(*sums_one)
-    sums_one[1].after(sums_two.state)
+    mixed, = call(
+        mixed_kernel,
+        [shape((rows, width), bf16)],
+        (middle, feed, feed_other),
+        rows * width * 100,
+        "mixed",
+    )
+    sums_one[1].after([mixed])
     alternate(*sums_one)
     alternate(*sums_one)
     tokens, middle = tied([tokens, middle], sums_one[1].past[-2])
+    two = sums_two.total()
+    gain_two_grad = jnp.sum(two[:2].astype(f32) * w_in.astype(f32), axis=(0, 2)) / gain_two.astype(f32)
+    two = over_ctx(two)
+    two, gain_two_grad, same, cross = locked([two, gain_two_grad, same, cross], sums_one[1])
     token_grad, = call(
         token_kernel,
         [shape((rows, width), f32)],
@@ -790,26 +789,20 @@
         rows * width * 200,
         "token_grad",
     )
-    two = over_ctx(sums_two.total())
-    two, = locked([two], sums_one[1])
-    mixed, = call(
-        mixed_kernel,
-        [shape((rows, width), bf16)],
-        (middle, feed, feed_other),
-        rows * width * 100,
-        "mixed",
-    )
     one = [chain.total() for chain in sums_one]
+    weights = w_qkv.astype(f32)
+    gain_one_grad = jnp.sum(one[0].astype(f32) * weights[:2], axis=(0, 2)) + jnp.sum(one[1][0].astype(f32) * weights[2], axis=1)
+    both = jnp.stack([gain_one_grad / gain_one.astype(f32), gain_two_grad])
+    both = both + swap(both)
     if lax.axis_size("ctx") == 2:
-        mixed, token_grad, *got = lax.optimization_barrier((mixed, token_grad, *[swap(part, "ctx") for part in one]))
+        both = both + swap(both, "ctx")
+        got = [swap(part, "ctx") for part in one]
+        token_grad, both, *got = lax.optimization_barrier((token_grad, both, *got))
         one = [part.astype(f32) + more.astype(f32) for part, more in zip(one, got)]
     else:
+        both = lax.psum(both, "ctx")
         one = [lax.psum(part, "ctx").astype(f32) for part in one]
     one = jnp.concatenate(one)
-    gain_one_grad = jnp.sum(one[:3] * w_qkv.astype(f32), axis=(0, 2)) / gain_one.astype(f32)
-    gain_two_grad = jnp.sum(two[:2] * w_in.astype(f32), axis=(0, 2)) / gain_two.astype(f32)
-    both = jnp.stack([gain_one_grad, gain_two_grad])
-    both = both + swap(both)
     return (mixed, token_grad, both[0], one[:3], one[3].T, both[1], two[:2], two[2].T)
 
 

time: 192 us -> 200 us (1.042)
  waiting for transfers between devices: 55.3 us -> 64.9 us
  starting transfers between devices: 51.5 us -> 49.3 us
    ppermute x18, starting transfers between devices: 29.9 us -> 12.5 us  [hop(): lax.ppermute(two, 'dp', self.back)]
    ppermute x18, starting transfers between devices: 8.8 us -> 25 us  [hop(): lax.ppermute(one, 'dp', self.ahead)]
    ppermute x8 -> x9, waiting for transfers between devices: 1.58 us -> 10.1 us  [swap(): return lax.ppermute(array, axis, [(0, 1), (1, 0)])]
    ppermute x18, waiting for transfers between devices: 25 us -> 20.3 us  [hop(): lax.ppermute(two, 'dp', self.back)]
    ppermute x18, waiting for transfers between devices: 25.9 us -> 29.9 us  [hop(): lax.ppermute(one, 'dp', self.ahead)]
    ppermute x8 -> x9, starting transfers between devices: 7 us -> 5.68 us  [swap(): return lax.ppermute(array, axis, [(0, 1), (1, 0)])]
    pallas_call x14 -> x13, Pallas kernels: 71.5 us -> 70.4 us  [call(): pl.pallas_call(kernel, out_shape=out_shape, in_specs=[smem] * len(scalars...]
  transfers between devices with their start and end apart: 49 -> 50, of which waited for: 29 -> 26; matrix products, arithmetic and copies ran while one was open for 5% -> 5% of each run, Pallas kernels for 30% -> 24%
where the time goes in v13:
time: 200 us
  Pallas kernels  70.4 us (35%)
  waiting for transfers between devices  64.9 us (32%)
  starting transfers between devices  49.3 us (25%)
  other arithmetic  10.5 us (5%)
  local copies, waits for them, and re-layouts  3.64 us (2%)
    pallas_call x13, Pallas kernels, call(): pl.pallas_call(kernel, out_shape=out_shape, in_specs=[smem] * len(scalars...  70.4 us
    ppermute x18, waiting for transfers between devices, hop(): lax.ppermute(one, 'dp', self.ahead)  29.9 us
    ppermute x18, starting transfers between devices, hop(): lax.ppermute(one, 'dp', self.ahead)  25 us
    ppermute x18, waiting for transfers between devices, hop(): lax.ppermute(two, 'dp', self.back)  20.3 us
    ppermute x18, starting transfers between devices, hop(): lax.ppermute(two, 'dp', self.back)  12.5 us
    ppermute x9, waiting for transfers between devices, swap(): return lax.ppermute(array, axis, [(0, 1), (1, 0)])  10.1 us
    ppermute x9, starting transfers between devices, swap(): return lax.ppermute(array, axis, [(0, 1), (1, 0)])  5.68 us
  transfers between devices with their start and end apart: 50, of which 26 were waited for; matrix products, arithmetic and copies ran while one was open for 5% of the time, Pallas kernels for 24%

profile of v13, /device:TPU:0, one launch (start us, length us, event | category | flops | bytes accessed | tf_op | source)
XLA Modules:
  0.0 199.9 jit_solution(18023677872210327972)
XLA Ops:
  2.5 3.1 %collective-permute-start.1 = (bf16[400,384]{1,0:T(8,128)(2,1)S(1)}, bf16[400,384]{1,0:T(8,128)(2,1)}, u32[]{:S(2)}, u32[]{:S(2)}) collective-permute-start(bf16[400,384]{1,0:T(8,128)(2,1)S(1)} %pad_maximum_fusion.2.rest_0_), channel_id=1, source_target_pairs={{0,8},{8,16},{16,24},{24,28},{28,20},{20,12},{12,4},{4,0},{1,9},{9... | collective-permute-start | bytes 921608 | tf_op jit(solution)/shard_map/ppermute | solution.py:529
  18.4 2.1 %negate_select_fusion = (f32[1152,128]{1,0:T(8,128)S(1)}, f32[1152,128]{1,0:T(8,128)S(1)}) fusion(f32[128]{0:T(128)S(1)} %fusion.16, f32[1152]{0:T(1024)S(1)} %subtract_convert_fusion, pred[128]{0:T(512)(128)(4,1)S(1)} %fusion.17), kind=kLoop, calls=%fused_computation | loop fusion | flops 442368 | bytes 1184896 | tf_op jit(solution)/shard_map/jit(_where)/select_n | solution.py:605
  21.4 3.5 %collective-permute-done.3.rest_7_ = bf16[400,384]{1,0:T(8,128)(2,1)} collective-permute-done((bf16[400,384]{1,0:T(8,128)(2,1)}, bf16[400,384]{1,0:T(8,128)(2,1)}, u32[]{:S(2)}, u32[]{:S(2)}) %collective-permute-start.3) | collective-permute-done | bytes 307232 | tf_op jit(solution)/shard_map/ppermute | solution.py:529
  26.5 5.2 %collective-permute-done.10.rest_1_ = bf16[288,576]{1,0:T(8,128)(2,1)} collective-permute-done((bf16[288,576]{1,0:T(8,128)(2,1)S(1)}, bf16[288,576]{1,0:T(8,128)(2,1)}, u32[]{:S(2)}, u32[]{:S(2)}) %collective-permute-start.10) | collective-permute-done | bytes 331808 | tf_op jit(solution)/shard_map/ppermute | solution.py:529
  35.8 10.6 %collective-permute-done.5.rest_6_ = bf16[400,384]{1,0:T(8,128)(2,1)S(1)} collective-permute-done((bf16[400,384]{1,0:T(8,128)(2,1)}, bf16[400,384]{1,0:T(8,128)(2,1)S(1)}, u32[]{:S(2)}, u32[]{:S(2)}) %collective-permute-start.5) | collective-permute-done | bytes 307232 | tf_op jit(solution)/shard_map/ppermute | solution.py:529
  54.0 3.9 %collective-permute-done.7.rest_4_ = bf16[192,384]{1,0:T(8,128)(2,1)S(1)} collective-permute-done((bf16[192,384]{1,0:T(8,128)(2,1)S(1)}, bf16[192,384]{1,0:T(8,128)(2,1)S(1)}, u32[]{:S(2)}, u32[]{:S(2)}) %collective-permute-start.7) | collective-permute-done | bytes 147488 | tf_op jit(solution)/shard_map/ppermute | solution.py:529
  57.9 3.6 %collective-permute-done.8.rest_5_ = bf16[208,384]{1,0:T(8,128)(2,1)S(1)} collective-permute-done((bf16[208,384]{1,0:T(8,128)(2,1)S(1)}, bf16[208,384]{1,0:T(8,128)(2,1)S(1)}, u32[]{:S(2)}, u32[]{:S(2)}) %collective-permute-start.8) | collective-permute-done | bytes 159776 | tf_op jit(solution)/shard_map/ppermute | solution.py:529
  63.8 6.4 %project.1 = (bf16[768,1536]{1,0:T(8,128)(2,1)S(1)}, f32[16,768]{1,0:T(8,128)S(1)}, bf16[1152,768]{1,0:T(8,128)(2,1)S(1)}, bf16[1024,384]{1,0:T(8,128)(2,1)S(1)}...) custom-call(s32[8]{0:T(128)S(1)} %dynamic-slice_bitcast_fusion.slots, f32[1152,768]{1,0:T(8,128)S(1)} %first_norm.1.hat, ...), custom_call_target="tpu_custom_call" | custom-call | flops 603979776 | bytes 1738752 | tf_op jit(solution)/shard_map/project/pallas_call | solution.py:50
  70.3 11.9 %attend.1 = (bf16[24,256,256]{2,1,0:T(8,128)(2,1)S(1)}, bf16[1024,384]{1,0:T(8,128)(2,1)S(1)}, bf16[1024,768]{1,0:T(8,128)(2,1)S(1)}) custom-call(s32[5]{0:T(128)S(1)} %pad_add_fusion.bounds, bf16[1024,384]{1,0:T(8,128)(2,1)S(1)} %get-tuple-element.155.query, bf16[1152,384]{1,0:T(8,128)(2,1)S(1)} %get-tuple-element.156.key, ...), custom_call_target="tpu_custom_call" | custom-call | flops 1207959552 | bytes 1302528 | tf_op jit(solution)/shard_map/attend/pallas_call | solution.py:50
  82.3 3.4 %collective-permute-done.17.other = bf16[1024,768]{1,0:T(8,128)(2,1)S(1)} collective-permute-done((bf16[1024,768]{1,0:T(8,128)(2,1)S(1)}, bf16[1024,768]{1,0:T(8,128)(2,1)S(1)}, u32[]{:S(2)}, u32[]{:S(2)}) %collective-permute-start.17) | collective-permute-done | bytes 1572896 | tf_op jit(solution)/shard_map/ppermute | solution.py:473
  85.7 11.2 %feed_forward_and_back.1 = (f32[1024,768]{1,0:T(8,128)S(1)}, bf16[1024,768]{1,0:T(8,128)(2,1)S(1)}, bf16[1024,576]{1,0:T(8,128)(2,1)S(1)}, bf16[1024,576]{1,0:T(...) custom-call(s32[8]{0:T(128)S(1)} %dynamic-slice_bitcast_fusion.slots, ...), custom_call_target="tpu_custom_call" | custom-call | flops 905969664 | bytes 2684928 | tf_op jit(solution)/shard_map/feed_forward_and_back/pallas_call | solution.py:50
  97.1 4.7 %feed_weight_grads.1 = bf16[8,3,96,576]{3,2,1,0:T(8,128)(2,1)S(1)} custom-call(s32[8]{0:T(128)S(1)} %dynamic-slice_bitcast_fusion.slots, bf16[1024,768]{1,0:T(8,128)(2,1)S(1)} %get-tuple-element.165.second, bf16[1024,576]{1,0:T(8,128)(2,1)S(1)} %get-tuple-element.169.hidden, bf16[1024,576]{1,0:T(8,128)(2,1)S(1)} %get-tuple-element.166.grad_gate, ...), custom_call_target="tpu_custom_call" | custom-call | flops 566231040 | bytes 1167360 | tf_op jit(solution)/shard_map/feed_weight_grads/pallas_call | solution.py:50
  104.0 2.0 %feed_out.1.own = bf16[1024,768]{1,0:T(8,128)(2,1)S(1)} custom-call(bf16[1024,576]{1,0:T(8,128)(2,1)S(1)} %get-tuple-element.169.hidden, bf16[3,768,576]{2,1,0:T(8,128)(2,1)S(1)} %get-tuple-element.170.whole), custom_call_target="tpu_custom_call" | custom-call | flops 113246208 | bytes 675840 | tf_op jit(solution)/shard_map/feed_out/pallas_call | solution.py:50
  106.0 3.6 %middle_grad.1 = (f32[1024,768]{1,0:T(8,128)S(1)}, bf16[1024,768]{1,0:T(8,128)(2,1)S(1)}, bf16[1024,384]{1,0:T(8,128)(2,1)S(1)}) custom-call(f32[1024,768]{1,0:T(8,128)S(1)} %get-tuple-element.161.middle, bf16[1024,768]{1,0:T(8,128)(2,1)S(1)} %get-tuple-element.162.own, bf16[1024,768]{1,0:T(8,128)(2,1)S(1)} %collective-permute-done.18.other, ...), custom_call_target="tpu_custom_call" | custom-call | flops 301989888 | bytes 1972224 | tf_op jit(solution)/shard_map/middle_grad/pallas_call | solution.py:50
  112.0 12.3 %attention_back.1 = (bf16[1152,384]{1,0:T(8,128)(2,1)S(1)}, bf16[1152,384]{1,0:T(8,128)(2,1)S(1)}, bf16[1152,384]{1,0:T(8,128)(2,1)S(1)}) custom-call(bf16[1024,384]{1,0:T(8,128)(2,1)S(1)} %get-tuple-element.155.query, bf16[1152,384]{1,0:T(8,128)(2,1)S(1)} %get-tuple-element.156.key, bf16[1152,384]{1,0:T(8,128)(2,1)S(1)} %get-tuple-element.157.value, ...), custom_call_target="tpu_custom_call" | custom-call | flops 1132462080 | bytes 1290240 | tf_op jit(solution)/shard_map/attention_back/pallas_call | solution.py:50
  126.6 3.0 %query_key_grads.1 = (bf16[1152,1152]{1,0:T(8,128)(2,1)S(1)}, bf16[8,2,96,384]{3,2,1,0:T(8,128)(2,1)S(1)}) custom-call(s32[8]{0:T(128)S(1)} %dynamic-slice_bitcast_fusion.slots, bf16[1152,768]{1,0:T(8,128)(2,1)S(1)} %get-tuple-element.174.first, bf16[1152,384]{1,0:T(8,128)(2,1)S(1)} %get-tuple-element.184.rest_0_, ...), custom_call_target="tpu_custom_call" | custom-call | flops 226492416 | bytes 1032192 | tf_op jit(solution)/shard_map/query_key_grads/pallas_call | solution.py:50
  129.6 4.1 %first_grad.1 = (bf16[1024,768]{1,0:T(8,128)(2,1)S(1)}, bf16[2,64,768]{2,1,0:T(8,128)(2,1)S(1)}) custom-call(bf16[1152,1152]{1,0:T(8,128)(2,1)S(1)} %get-tuple-element.188.grad_proj, bf16[768,1536]{1,0:T(8,128)(2,1)S(1)} %get-tuple-element.158.rest_0_.wide), custom_call_target="tpu_custom_call" | custom-call | flops 226492416 | bytes 847872 | tf_op jit(solution)/shard_map/first_grad/pallas_call | solution.py:50
  133.7 2.7 %value_out_grads.1 = bf16[8,2,96,384]{3,2,1,0:T(8,128)(2,1)S(1)} custom-call(s32[8]{0:T(128)S(1)} %dynamic-slice_bitcast_fusion.slots, bf16[1152,768]{1,0:T(8,128)(2,1)S(1)} %get-tuple-element.174.first, bf16[1152,1152]{1,0:T(8,128)(2,1)S(1)} %get-tuple-element.188.grad_proj, bf16[1024,768]{1,0:T(8,128)(2,1)S(1)} %get-tuple-element.189.low_mid, ...), custom_call_target="tpu_custom_call" | custom-call | flops 226492416 | bytes 995328 | tf_op jit(solution)/shard_map/value_out_grads/pallas_call | solution.py:50
  144.6 5.7 %collective-permute-done.28 = bf16[3,96,576]{2,1,0:T(8,128)(2,1)S(1)} collective-permute-done((bf16[3,96,576]{2,1,0:T(8,128)(2,1)S(1)}, bf16[3,96,576]{2,1,0:T(8,128)(2,1)S(1)}, u32[]{:S(2)}, u32[]{:S(2)}) %collective-permute-start.28) | collective-permute-done | bytes 331808 | tf_op jit(solution)/shard_map/ppermute | solution.py:579
  169.2 2.5 %collective-permute-done.37 = bf16[3,96,576]{2,1,0:T(8,128)(2,1)S(1)} collective-permute-done((bf16[3,96,576]{2,1,0:T(8,128)(2,1)S(1)}, bf16[3,96,576]{2,1,0:T(8,128)(2,1)S(1)}, u32[]{:S(2)}, u32[]{:S(2)}) %collective-permute-start.37) | collective-permute-done | bytes 331808 | tf_op jit(solution)/shard_map/ppermute | solution.py:473
  173.8 3.0 %collective-permute-done.35 = bf16[2,96,384]{2,1,0:T(8,128)(2,1)S(1)} collective-permute-done((bf16[2,96,384]{2,1,0:T(8,128)(2,1)S(1)}, bf16[2,96,384]{2,1,0:T(8,128)(2,1)S(1)}, u32[]{:S(2)}, u32[]{:S(2)}) %collective-permute-start.35) | collective-permute-done | bytes 147488 | tf_op jit(solution)/shard_map/ppermute | solution.py:579
  179.1 2.9 %collective-permute-done.42 = bf16[2,96,384]{2,1,0:T(8,128)(2,1)S(1)} collective-permute-done((bf16[2,96,384]{2,1,0:T(8,128)(2,1)S(1)}, bf16[2,96,384]{2,1,0:T(8,128)(2,1)S(1)}, u32[]{:S(2)}, u32[]{:S(2)}) %collective-permute-start.42) | collective-permute-done | bytes 147488 | tf_op jit(solution)/shard_map/ppermute | solution.py:579
  188.6 4.3 %collective-permute-done.47 = f32[2,96]{1,0:T(2,128)S(1)} collective-permute-done((f32[2,96]{1,0:T(2,128)S(1)}, f32[2,96]{1,0:T(2,128)S(1)}, u32[]{:S(2)}, u32[]{:S(2)}) %collective-permute-start.47) | collective-permute-done | bytes 800 | tf_op jit(solution)/shard_map/ppermute | solution.py:473
  192.9 4.9 %token_grad.1 = f32[1024,768]{1,0:T(8,128)} custom-call(bf16[1024,768]{1,0:T(8,128)(2,1)S(1)} %copy-done, f32[16,768]{1,0:T(8,128)S(1)} %get-tuple-element.160.gain, f32[1024,768]{1,0:T(8,128)S(1)} %get-tuple-element.217.grad_middle, bf16[1024,768]{1,0:T(8,128)(2,1)S(1)} %get-tuple-element.218.own, bf16[1024,768]{1,0:T(8,128)(2,1)S(1)} %collective-permute-done.36.other, ...), custom_call_target="tpu_custom_call" | custom-call | flops 19660800 | bytes 1431552 | tf_op jit(solution)/shard_map/token_grad/pallas_call | solution.py:50
  (156 shorter events, 78.2 us)
Async XLA Ops:
  2.5 10.4 %collective-permute-start.1 = (bf16[400,384]{1,0:T(8,128)(2,1)S(1)}, bf16[400,384]{1,0:T(8,128)(2,1)}, u32[]{:S(2)}, u32[]{:S(2)}) collective-permute-start(bf16[400,384]{1,0:T(8,128)(2,1)S(1)} %pad_maximum_fusion.2.rest_0_), channel_id=1, source_target_pairs={{0,8},{8,16},{16,24},{24,28},{28,20},{20,12},{12,4},{4,0},{1,9},{9... | collective-permute-start | bytes 921608 | tf_op jit(solution)/shard_map/ppermute | solution.py:529
  7.1 26.6 %collective-permute-start = (bf16[64,768]{1,0:T(8,128)(2,1)}, bf16[64,768]{1,0:T(8,128)(2,1)S(1)}, u32[]{:S(2)}, u32[]{:S(2)}) collective-permute-start(bf16[64,768]{1,0:T(8,128)(2,1)} %slice_select_fusion), channel_id=1, source_target_pairs={{0,2},{2,0},{1,3},{3,1},{4,6},{6,4},{5,7},{7,5},{8,10},{10,8},{9,1... | collective-permute-start | bytes 294920 | tf_op jit(solution)/shard_map/ppermute | solution.py:459
  14.4 10.5 %collective-permute-start.3 = (bf16[400,384]{1,0:T(8,128)(2,1)}, bf16[400,384]{1,0:T(8,128)(2,1)}, u32[]{:S(2)}, u32[]{:S(2)}) collective-permute-start(bf16[400,384]{1,0:T(8,128)(2,1)} %collective-permute-done.1.rest_8_), channel_id=1, source_target_pairs={{0,8},{8,16},{16,24},{24,28},{28,20},{20,12},{12,4},{4,0},{1,9},{9... | collective-permute-start | bytes 921608 | tf_op jit(solution)/shard_map/ppermute | solution.py:529
  15.9 10.5 %collective-permute-start.4 = (bf16[400,384]{1,0:T(8,128)(2,1)}, bf16[400,384]{1,0:T(8,128)(2,1)}, u32[]{:S(2)}, u32[]{:S(2)}) collective-permute-start(bf16[400,384]{1,0:T(8,128)(2,1)} %collective-permute-done.2.rest_1_), channel_id=1, source_target_pairs={{8,0},{16,8},{24,16},{28,24},{20,28},{12,20},{4,12},{0,4},{9,1},{1... | collective-permute-start | bytes 921608 | tf_op jit(solution)/shard_map/ppermute | solution.py:529
  16.4 15.3 %collective-permute-start.10 = (bf16[288,576]{1,0:T(8,128)(2,1)S(1)}, bf16[288,576]{1,0:T(8,128)(2,1)}, u32[]{:S(2)}, u32[]{:S(2)}) collective-permute-start(bf16[288,576]{1,0:T(8,128)(2,1)S(1)} %pad_maximum_fusion.1.rest_0_), channel_id=1, source_target_pairs={{8,0},{16,8},{24,16},{28,24},{20,28},{12,20},{4,12},{0,4},{9,1},{1... | collective-permute-start | bytes 995336 | tf_op jit(solution)/shard_map/ppermute | solution.py:529
  16.7 15.0 %collective-permute-start.9 = (bf16[288,576]{1,0:T(8,128)(2,1)S(1)}, bf16[288,576]{1,0:T(8,128)(2,1)}, u32[]{:S(2)}, u32[]{:S(2)}) collective-permute-start(bf16[288,576]{1,0:T(8,128)(2,1)S(1)} %pad_maximum_fusion.1.rest_0_), channel_id=1, source_target_pairs={{0,8},{8,16},{16,24},{24,28},{28,20},{20,12},{12,4},{4,0},{1,9},{9... | collective-permute-start | bytes 995336 | tf_op jit(solution)/shard_map/ppermute | solution.py:529
  31.7 16.0 %collective-permute-start.11 = (bf16[288,576]{1,0:T(8,128)(2,1)}, bf16[288,576]{1,0:T(8,128)(2,1)S(1)}, u32[]{:S(2)}, u32[]{:S(2)}) collective-permute-start(bf16[288,576]{1,0:T(8,128)(2,1)} %collective-permute-done.9.rest_8_), channel_id=1, source_target_pairs={{0,8},{8,16},{16,24},{24,28},{28,20},{20,12},{12,4},{4,0},{1,9},{9... | collective-permute-start | bytes 995336 | tf_op jit(solution)/shard_map/ppermute | solution.py:529
  33.3 14.5 %collective-permute-start.12 = (bf16[288,576]{1,0:T(8,128)(2,1)}, bf16[288,576]{1,0:T(8,128)(2,1)S(1)}, u32[]{:S(2)}, u32[]{:S(2)}) collective-permute-start(bf16[288,576]{1,0:T(8,128)(2,1)} %collective-permute-done.10.rest_1_), channel_id=1, source_target_pairs={{8,0},{16,8},{24,16},{28,24},{20,28},{12,20},{4,12},{0,4},{9,1},{1... | collective-permute-start | bytes 995336 | tf_op jit(solution)/shard_map/ppermute | solution.py:529
  33.8 12.7 %collective-permute-start.5 = (bf16[400,384]{1,0:T(8,128)(2,1)}, bf16[400,384]{1,0:T(8,128)(2,1)S(1)}, u32[]{:S(2)}, u32[]{:S(2)}) collective-permute-start(bf16[400,384]{1,0:T(8,128)(2,1)} %collective-permute-done.3.rest_7_), channel_id=1, source_target_pairs={{0,8},{8,16},{16,24},{24,28},{28,20},{20,12},{12,4},{4,0},{1,9},{9... | collective-permute-start | bytes 921608 | tf_op jit(solution)/shard_map/ppermute | solution.py:529
  35.4 12.3 %collective-permute-start.6 = (bf16[400,384]{1,0:T(8,128)(2,1)}, bf16[400,384]{1,0:T(8,128)(2,1)S(1)}, u32[]{:S(2)}, u32[]{:S(2)}) collective-permute-start(bf16[400,384]{1,0:T(8,128)(2,1)} %collective-permute-done.4.rest_2_), channel_id=1, source_target_pairs={{8,0},{16,8},{24,16},{28,24},{20,28},{12,20},{4,12},{0,4},{9,1},{1... | collective-permute-start | bytes 921608 | tf_op jit(solution)/shard_map/ppermute | solution.py:529
  47.7 13.7 %collective-permute-start.13 = (bf16[288,576]{1,0:T(8,128)(2,1)S(1)}, bf16[288,576]{1,0:T(8,128)(2,1)S(1)}, u32[]{:S(2)}, u32[]{:S(2)}) collective-permute-start(bf16[288,576]{1,0:T(8,128)(2,1)S(1)} %collective-permute-done.11.rest_7_), channel_id=1, source_target_pairs={{0,8},{8,16},{16,24},{24,28},{28,20},{20,12},{12,4},{4,0},{1,9},{9... | collective-permute-start | bytes 995336 | tf_op jit(solution)/shard_map/ppermute | solution.py:529
  49.7 11.8 %collective-permute-start.14 = (bf16[288,576]{1,0:T(8,128)(2,1)S(1)}, bf16[288,576]{1,0:T(8,128)(2,1)S(1)}, u32[]{:S(2)}, u32[]{:S(2)}) collective-permute-start(bf16[288,576]{1,0:T(8,128)(2,1)S(1)} %collective-permute-done.12.rest_2_), channel_id=1, source_target_pairs={{8,0},{16,8},{24,16},{28,24},{20,28},{12,20},{4,12},{0,4},{9,1},{1... | collective-permute-start | bytes 995336 | tf_op jit(solution)/shard_map/ppermute | solution.py:529
  109.9 14.4 %collective-permute-start.22 = (bf16[3,96,576]{2,1,0:T(8,128)(2,1)S(1)}, bf16[3,96,576]{2,1,0:T(8,128)(2,1)S(1)}, u32[]{:S(2)}, u32[]{:S(2)}) collective-permute-start(bf16[3,96,576]{2,1,0:T(8,128)(2,1)S(1)} %get-tuple-element.249), channel_id=1, source_target_pairs={{0,8},{8,16},{16,24},{24,28},{28,20},{20,12},{12,4},{4,0},{1,9},{9... | collective-permute-start | bytes 995336 | tf_op jit(solution)/shard_map/ppermute | solution.py:579
  111.0 13.3 %collective-permute-start.23 = (bf16[3,96,576]{2,1,0:T(8,128)(2,1)S(1)}, bf16[3,96,576]{2,1,0:T(8,128)(2,1)S(1)}, u32[]{:S(2)}, u32[]{:S(2)}) collective-permute-start(bf16[3,96,576]{2,1,0:T(8,128)(2,1)S(1)} %get-tuple-element.248), channel_id=1, source_target_pairs={{8,0},{16,8},{24,16},{28,24},{20,28},{12,20},{4,12},{0,4},{9,1},{1... | collective-permute-start | bytes 995336 | tf_op jit(solution)/shard_map/ppermute | solution.py:579
  124.4 12.0 %collective-permute-start.24 = (bf16[3,96,576]{2,1,0:T(8,128)(2,1)S(1)}, bf16[3,96,576]{2,1,0:T(8,128)(2,1)S(1)}, u32[]{:S(2)}, u32[]{:S(2)}) collective-permute-start(bf16[3,96,576]{2,1,0:T(8,128)(2,1)S(1)} %get-tuple-element.247), channel_id=1, source_target_pairs={{0,8},{8,16},{16,24},{24,28},{28,20},{20,12},{12,4},{4,0},{1,9},{9... | collective-permute-start | bytes 995336 | tf_op jit(solution)/shard_map/ppermute | solution.py:579
  125.5 10.9 %collective-permute-start.25 = (bf16[3,96,576]{2,1,0:T(8,128)(2,1)S(1)}, bf16[3,96,576]{2,1,0:T(8,128)(2,1)S(1)}, u32[]{:S(2)}, u32[]{:S(2)}) collective-permute-start(bf16[3,96,576]{2,1,0:T(8,128)(2,1)S(1)} %get-tuple-element.246), channel_id=1, source_target_pairs={{8,0},{16,8},{24,16},{28,24},{20,28},{12,20},{4,12},{0,4},{9,1},{1... | collective-permute-start | bytes 995336 | tf_op jit(solution)/shard_map/ppermute | solution.py:579
  126.5 40.4 %collective-permute-start.21 = (bf16[1024,768]{1,0:T(8,128)(2,1)S(1)}, bf16[1024,768]{1,0:T(8,128)(2,1)S(1)}, u32[]{:S(2)}, u32[]{:S(2)}) collective-permute-start(bf16[1024,768]{1,0:T(8,128)(2,1)S(1)} %feed_out.1.own), channel_id=1, source_target_pairs={{0,1},{1,0},{2,3},{3,2},{4,5},{5,4},{6,7},{7,6},{8,9},{9,8},{10,11... | collective-permute-start | bytes 4718600 | tf_op jit(solution)/shard_map/ppermute | solution.py:473
  138.7 11.5 %collective-permute-start.28 = (bf16[3,96,576]{2,1,0:T(8,128)(2,1)S(1)}, bf16[3,96,576]{2,1,0:T(8,128)(2,1)S(1)}, u32[]{:S(2)}, u32[]{:S(2)}) collective-permute-start(bf16[3,96,576]{2,1,0:T(8,128)(2,1)S(1)} %get-tuple-element.245), channel_id=1, source_target_pairs={{0,8},{8,16},{16,24},{24,28},{28,20},{20,12},{12,4},{4,0},{1,9},{9... | collective-permute-start | bytes 995336 | tf_op jit(solution)/shard_map/ppermute | solution.py:579
  139.8 11.5 %collective-permute-start.29 = (bf16[3,96,576]{2,1,0:T(8,128)(2,1)S(1)}, bf16[3,96,576]{2,1,0:T(8,128)(2,1)S(1)}, u32[]{:S(2)}, u32[]{:S(2)}) collective-permute-start(bf16[3,96,576]{2,1,0:T(8,128)(2,1)S(1)} %get-tuple-element.244), channel_id=1, source_target_pairs={{8,0},{16,8},{24,16},{28,24},{20,28},{12,20},{4,12},{0,4},{9,1},{1... | collective-permute-start | bytes 995336 | tf_op jit(solution)/shard_map/ppermute | solution.py:579
  141.2 12.0 %collective-permute-start.30 = (bf16[2,96,384]{2,1,0:T(8,128)(2,1)S(1)}, bf16[2,96,384]{2,1,0:T(8,128)(2,1)S(1)}, u32[]{:S(2)}, u32[]{:S(2)}) collective-permute-start(bf16[2,96,384]{2,1,0:T(8,128)(2,1)S(1)} %get-tuple-element.259), channel_id=1, source_target_pairs={{0,8},{8,16},{16,24},{24,28},{28,20},{20,12},{12,4},{4,0},{1,9},{9... | collective-permute-start | bytes 442376 | tf_op jit(solution)/shard_map/ppermute | solution.py:561
  143.7 13.8 %collective-permute-start.33 = (bf16[2,96,384]{2,1,0:T(8,128)(2,1)S(1)}, bf16[2,96,384]{2,1,0:T(8,128)(2,1)S(1)}, u32[]{:S(2)}, u32[]{:S(2)}) collective-permute-start(bf16[2,96,384]{2,1,0:T(8,128)(2,1)S(1)} %get-tuple-element.258), channel_id=1, source_target_pairs={{8,0},{16,8},{24,16},{28,24},{20,28},{12,20},{4,12},{0,4},{9,1},{1... | collective-permute-start | bytes 442376 | tf_op jit(solution)/shard_map/ppermute | solution.py:579
  160.6 32.3 %collective-permute-start.36 = (bf16[1024,768]{1,0:T(8,128)(2,1)S(1)}, bf16[1024,768]{1,0:T(8,128)(2,1)S(1)}, u32[]{:S(2)}, u32[]{:S(2)}) collective-permute-start(bf16[1024,768]{1,0:T(8,128)(2,1)S(1)} %get-tuple-element.218.own), channel_id=1, source_target_pairs={{0,1},{1,0},{2,3},{3,2},{4,5},{5,4},{6,7},{7,6},{8,9},{9,8},{10,11... | collective-permute-start | bytes 4718600 | tf_op jit(solution)/shard_map/ppermute | solution.py:473
  183.4 14.4 %collective-permute-start.48 = (bf16[2,96,384]{2,1,0:T(8,128)(2,1)S(1)}, bf16[2,96,384]{2,1,0:T(8,128)(2,1)S(1)}, u32[]{:S(2)}, u32[]{:S(2)}) collective-permute-start(bf16[2,96,384]{2,1,0:T(8,128)(2,1)S(1)} %get-tuple-element.243), channel_id=1, source_target_pairs={{0,2},{2,0},{1,3},{3,1},{4,6},{6,4},{5,7},{7,5},{8,10},{10,8},{9,1... | collective-permute-start | bytes 442376 | tf_op jit(solution)/shard_map/ppermute | solution.py:473
  185.0 12.8 %collective-permute-start.49 = (bf16[2,96,384]{2,1,0:T(8,128)(2,1)S(1)}, bf16[2,96,384]{2,1,0:T(8,128)(2,1)S(1)}, u32[]{:S(2)}, u32[]{:S(2)}) collective-permute-start(bf16[2,96,384]{2,1,0:T(8,128)(2,1)S(1)} %fusion.4), channel_id=1, source_target_pairs={{0,2},{2,0},{1,3},{3,1},{4,6},{6,4},{5,7},{7,5},{8,10},{10,8},{9,1... | collective-permute-start | bytes 442376 | tf_op jit(solution)/shard_map/ppermute | solution.py:473
  (32 other events, 262.7 us)

commit v14 on v12

--- a/solution.py
+++ b/solution.py
@@ -361,17 +361,13 @@
     loop(extent // BLOCK, turn_step)
 
 
-def grad_kernel_one(slots, first, wide, *rest):
-    parts, (grad_proj, grads, edges, total) = rest[:-4], rest[-4:]
+def grad_kernel_one(slots, first, *rest):
+    parts, (grad_proj, grads, total) = rest[:-3], rest[-3:]
     local = len(parts) * LANES
     for pair, part in enumerate(parts):
         for number in range(3):
             lanes = slice(number * local + pair * LANES, number * local + (pair + 1) * LANES)
             grad_proj[:, lanes] = part[:, number * LANES : (number + 1) * LANES]
-    extent = first.shape[0]
-    for side, start in enumerate((0, extent - HALF)):
-        outer = grad_proj[start : start + HALF, :]
-        edges[side] = dot(outer, wide[:, : 3 * local], NT).astype(bf16)
     weight_grads([(first, grad_proj.at[:, at * local : (at + 1) * local]) for at in range(2)], slots, grads, total)
 
 
@@ -392,8 +388,11 @@
         grads[number] = total[:, pl.ds(pl.multiple_of(slots[slot] * depth, depth), depth), :]
 
 
-def first_kernel(grad_proj, wide, partial):
+def first_kernel(grad_proj, wide, partial, edges):
     rows = partial.shape[0]
+    for side, start in enumerate((0, rows + HALF)):
+        outer = grad_proj[start : start + HALF, :]
+        edges[side] = dot(outer, wide[:, : outer.shape[1]], NT).astype(bf16)
     inner = grad_proj.shape[1]
     size = step_of(rows, 256)
 
@@ -739,22 +738,21 @@
     )
     grad_parts = locked(grad_parts, sums_two)
     sums_two.hop()
-    grad_proj, grads_a, edges = call(
+    grad_proj, grads_a = call(
         grad_kernel_one,
         [
             shape((extent, 3 * local), bf16),
             shape((groups, 2, depth, local), bf16),
-            shape((2, HALF, width), bf16),
         ],
-        (first, wide, *grad_parts),
+        (first, *grad_parts),
         2 * rows * width * local * 3,
         "query_key_grads",
         (slots,),
         [pltpu.VMEM((2, width, local), bf16)],
     )
-    first_part, = call(
+    first_part, edges = call(
         first_kernel,
-        [shape((rows, width), bf16)],
+        [shape((rows, width), bf16), shape((2, HALF, width), bf16)],
         (grad_proj, wide),
         2 * rows * width * local * 3,
         "first_grad",
@@ -768,8 +766,7 @@
         (slots,),
         [pltpu.VMEM((2, width, local), bf16)],
     )
-    sent = [traded(edges, 0), traded(edges, 1)]
-    *grads_one, first_part, same, cross = locked([grads_a, grads_b, first_part, *sent], sums_two)
+    *grads_one, first_part, edges = locked([grads_a, grads_b, first_part, edges], sums_two)
     first_other = swap(first_part)
     sums_one = [RingScatter([part], way=way) for way, part in enumerate(grads_one)]
     alternate(*sums_one)
@@ -779,7 +776,9 @@
 
     while sums_one[0].hops < middle_hop - 2:
         alternate(*sums_one)
-    sums_one[1].after(sums_two.state)
+    edges, = tied([edges], sums_one[0].past[0])
+    same, cross = traded(edges, 0), traded(edges, 1)
+    sums_one[1].after([*sums_two.state, same, cross])
     alternate(*sums_one)
     alternate(*sums_one)
     tokens, middle = tied([tokens, middle], sums_one[1].past[-2])

time: 192 us -> 189 us (0.984)
  starting transfers between devices: 51.5 us -> 45.3 us
  waiting for transfers between devices: 55.3 us -> 58.2 us
    ppermute x8, starting transfers between devices: 7 us -> 0.75 us  [swap(): return lax.ppermute(array, axis, [(0, 1), (1, 0)])]
    ppermute x18, waiting for transfers between devices: 25.9 us -> 22.1 us  [hop(): lax.ppermute(one, 'dp', self.ahead)]
    ppermute x18, waiting for transfers between devices: 25 us -> 28.6 us  [hop(): lax.ppermute(two, 'dp', self.back)]
    ppermute x2, waiting for transfers between devices: 0.01 us -> 2.39 us  [traded(): lax.ppermute(jnp.where(spot == 0, edges[1], edges[0]), axes, pairs(1, 0,...]
    ppermute x8, waiting for transfers between devices: 1.58 us -> 3.58 us  [swap(): return lax.ppermute(array, axis, [(0, 1), (1, 0)])]
  transfers between devices with their start and end apart: 49 -> 49, of which waited for: 29 -> 26; matrix products, arithmetic and copies ran while one was open for 5% -> 5% of each run, Pallas kernels for 30% -> 32%
where the time goes in v14:
time: 189 us
  Pallas kernels  71.6 us (38%)
  waiting for transfers between devices  58.2 us (31%)
  starting transfers between devices  45.3 us (24%)
  other arithmetic  9.51 us (5%)
  local copies, waits for them, and re-layouts  2.82 us (1%)
    pallas_call x14, Pallas kernels, call(): pl.pallas_call(kernel, out_shape=out_shape, in_specs=[smem] * len(scalars...  71.6 us
    ppermute x18, starting transfers between devices, hop(): lax.ppermute(two, 'dp', self.back)  30.3 us
    ppermute x18, waiting for transfers between devices, hop(): lax.ppermute(two, 'dp', self.back)  28.6 us
    ppermute x18, waiting for transfers between devices, hop(): lax.ppermute(one, 'dp', self.ahead)  22.1 us
    ppermute x18, starting transfers between devices, hop(): lax.ppermute(one, 'dp', self.ahead)  8.51 us
  transfers between devices with their start and end apart: 49, of which 26 were waited for; matrix products, arithmetic and copies ran while one was open for 5% of the time, Pallas kernels for 32%

profile of v14, /device:TPU:0, one launch (start us, length us, event | category | flops | bytes accessed | tf_op | source)
XLA Modules:
  0.0 188.6 jit_solution(15743357612603515591)
XLA Ops:
  2.5 3.0 %collective-permute-start.2 = (bf16[400,384]{1,0:T(8,128)(2,1)S(1)}, bf16[400,384]{1,0:T(8,128)(2,1)S(1)}, u32[]{:S(2)}, u32[]{:S(2)}) collective-permute-start(bf16[400,384]{1,0:T(8,128)(2,1)S(1)} %pad_maximum_fusion.2.rest_0_), channel_id=1, source_target_pairs={{8,0},{16,8},{24,16},{28,24},{20,28},{12,20},{4,12},{0,4},{9,1},{1... | collective-permute-start | bytes 921608 | tf_op jit(solution)/shard_map/ppermute | solution.py:530
  10.2 2.1 %negate_select_fusion = (f32[1152,128]{1,0:T(8,128)S(1)}, f32[1152,128]{1,0:T(8,128)S(1)}) fusion(f32[128]{0:T(128)S(1)} %fusion.14, f32[1152]{0:T(1024)S(1)} %subtract_convert_fusion, pred[128]{0:T(512)(128)(4,1)S(1)} %fusion.15), kind=kLoop, calls=%fused_computation | loop fusion | flops 442368 | bytes 1184896 | tf_op jit(solution)/shard_map/jit(_where)/select_n | solution.py:606
  16.9 5.1 %collective-permute-done.4.rest_2_ = bf16[400,384]{1,0:T(8,128)(2,1)S(1)} collective-permute-done((bf16[400,384]{1,0:T(8,128)(2,1)S(1)}, bf16[400,384]{1,0:T(8,128)(2,1)S(1)}, u32[]{:S(2)}, u32[]{:S(2)}) %collective-permute-start.4) | collective-permute-done | bytes 307232 | tf_op jit(solution)/shard_map/ppermute | solution.py:530
  27.4 2.8 %collective-permute-done.5.rest_6_ = bf16[400,384]{1,0:T(8,128)(2,1)S(1)} collective-permute-done((bf16[400,384]{1,0:T(8,128)(2,1)S(1)}, bf16[400,384]{1,0:T(8,128)(2,1)S(1)}, u32[]{:S(2)}, u32[]{:S(2)}) %collective-permute-start.5) | collective-permute-done | bytes 307232 | tf_op jit(solution)/shard_map/ppermute | solution.py:530
  34.1 6.2 %collective-permute-done.7.rest_4_ = bf16[192,384]{1,0:T(8,128)(2,1)S(1)} collective-permute-done((bf16[192,384]{1,0:T(8,128)(2,1)S(1)}, bf16[192,384]{1,0:T(8,128)(2,1)S(1)}, u32[]{:S(2)}, u32[]{:S(2)}) %collective-permute-start.7) | collective-permute-done | bytes 147488 | tf_op jit(solution)/shard_map/ppermute | solution.py:530
  42.3 5.7 %project.1 = (bf16[768,1536]{1,0:T(8,128)(2,1)S(1)}, f32[16,768]{1,0:T(8,128)S(1)}, bf16[1152,768]{1,0:T(8,128)(2,1)S(1)}, bf16[1024,384]{1,0:T(8,128)(2,1)S(1)}...) custom-call(s32[8]{0:T(128)S(1)} %dynamic-slice_bitcast_fusion.slots, f32[1152,768]{1,0:T(8,128)S(1)} %first_norm.1.hat, ...), custom_call_target="tpu_custom_call" | custom-call | flops 603979776 | bytes 1738752 | tf_op jit(solution)/shard_map/project/pallas_call | solution.py:50
  48.1 3.4 %collective-permute-done.10.rest_1_ = bf16[288,576]{1,0:T(8,128)(2,1)S(1)} collective-permute-done((bf16[288,576]{1,0:T(8,128)(2,1)S(1)}, bf16[288,576]{1,0:T(8,128)(2,1)S(1)}, u32[]{:S(2)}, u32[]{:S(2)}) %collective-permute-start.10) | collective-permute-done | bytes 331808 | tf_op jit(solution)/shard_map/ppermute | solution.py:530
  54.0 7.7 %attend.2 = (bf16[16,256,256]{2,1,0:T(8,128)(2,1)S(1)}, bf16[1024,384]{1,0:T(8,128)(2,1)S(1)}) custom-call(s32[5]{0:T(128)S(1)} %pad_add_fusion.bounds, bf16[1024,384]{1,0:T(8,128)(2,1)S(1)} %get-tuple-element.146.query, bf16[1152,384]{1,0:T(8,128)(2,1)S(1)} %get-tuple-element.147.key, bf16[1152,384]{1,0:T(8,128)(2,1)S(1)} %get-tuple-element.148.value), custom_call_target="tpu_custom_call" | custom-call | flops 754974720 | bytes 679936 | tf_op jit(solution)/shard_map/attend/pallas_call | solution.py:50
  64.6 6.6 %attend.3 = (bf16[8,256,256]{2,1,0:T(8,128)(2,1)S(1)}, bf16[1024,384]{1,0:T(8,128)(2,1)S(1)}, bf16[1024,768]{1,0:T(8,128)(2,1)S(1)}) custom-call(s32[5]{0:T(128)S(1)} %pad_add_fusion.bounds, bf16[1024,384]{1,0:T(8,128)(2,1)S(1)} %get-tuple-element.146.query, bf16[1152,384]{1,0:T(8,128)(2,1)S(1)} %get-tuple-element.147.key, ...), custom_call_target="tpu_custom_call" | custom-call | flops 528482304 | bytes 1138688 | tf_op jit(solution)/shard_map/attend/pallas_call | solution.py:50
  73.7 5.0 %collective-permute-done.16.rest_4_ = bf16[96,576]{1,0:T(8,128)(2,1)S(1)} collective-permute-done((bf16[96,576]{1,0:T(8,128)(2,1)S(1)}, bf16[96,576]{1,0:T(8,128)(2,1)S(1)}, u32[]{:S(2)}, u32[]{:S(2)}) %collective-permute-start.16) | collective-permute-done | bytes 110624 | tf_op jit(solution)/shard_map/ppermute | solution.py:530
  79.8 10.6 %feed_forward_and_back.1 = (f32[1024,768]{1,0:T(8,128)S(1)}, bf16[1024,768]{1,0:T(8,128)(2,1)S(1)}, bf16[1024,576]{1,0:T(8,128)(2,1)S(1)}, bf16[1024,576]{1,0:T(...) custom-call(s32[8]{0:T(128)S(1)} %dynamic-slice_bitcast_fusion.slots, ...), custom_call_target="tpu_custom_call" | custom-call | flops 905969664 | bytes 2684928 | tf_op jit(solution)/shard_map/feed_forward_and_back/pallas_call | solution.py:50
  90.4 4.7 %feed_weight_grads.1 = bf16[8,3,96,576]{3,2,1,0:T(8,128)(2,1)S(1)} custom-call(s32[8]{0:T(128)S(1)} %dynamic-slice_bitcast_fusion.slots, bf16[1024,768]{1,0:T(8,128)(2,1)S(1)} %get-tuple-element.172.second, bf16[1024,576]{1,0:T(8,128)(2,1)S(1)} %get-tuple-element.176.hidden, bf16[1024,576]{1,0:T(8,128)(2,1)S(1)} %get-tuple-element.173.grad_gate, ...), custom_call_target="tpu_custom_call" | custom-call | flops 566231040 | bytes 1167360 | tf_op jit(solution)/shard_map/feed_weight_grads/pallas_call | solution.py:50
  97.3 2.0 %feed_out.1.own = bf16[1024,768]{1,0:T(8,128)(2,1)S(1)} custom-call(bf16[1024,576]{1,0:T(8,128)(2,1)S(1)} %get-tuple-element.176.hidden, bf16[3,768,576]{2,1,0:T(8,128)(2,1)S(1)} %get-tuple-element.177.whole), custom_call_target="tpu_custom_call" | custom-call | flops 113246208 | bytes 675840 | tf_op jit(solution)/shard_map/feed_out/pallas_call | solution.py:50
  99.4 3.6 %middle_grad.1 = (f32[1024,768]{1,0:T(8,128)S(1)}, bf16[1024,768]{1,0:T(8,128)(2,1)S(1)}, bf16[1024,384]{1,0:T(8,128)(2,1)S(1)}) custom-call(f32[1024,768]{1,0:T(8,128)S(1)} %get-tuple-element.224.middle, bf16[1024,768]{1,0:T(8,128)(2,1)S(1)} %get-tuple-element.169.own, bf16[1024,768]{1,0:T(8,128)(2,1)S(1)} %collective-permute-done.18.other, ...), custom_call_target="tpu_custom_call" | custom-call | flops 301989888 | bytes 1972224 | tf_op jit(solution)/shard_map/middle_grad/pallas_call | solution.py:50
  105.8 12.3 %attention_back.1 = (bf16[1152,384]{1,0:T(8,128)(2,1)S(1)}, bf16[1152,384]{1,0:T(8,128)(2,1)S(1)}, bf16[1152,384]{1,0:T(8,128)(2,1)S(1)}) custom-call(bf16[1024,384]{1,0:T(8,128)(2,1)S(1)} %get-tuple-element.146.query, bf16[1152,384]{1,0:T(8,128)(2,1)S(1)} %get-tuple-element.147.key, bf16[1152,384]{1,0:T(8,128)(2,1)S(1)} %get-tuple-element.148.value, ...), custom_call_target="tpu_custom_call" | custom-call | flops 1132462080 | bytes 1290240 | tf_op jit(solution)/shard_map/attention_back/pallas_call | solution.py:50
  120.3 3.0 %query_key_grads.1 = (bf16[1152,1152]{1,0:T(8,128)(2,1)S(1)}, bf16[8,2,96,384]{3,2,1,0:T(8,128)(2,1)S(1)}) custom-call(s32[8]{0:T(128)S(1)} %dynamic-slice_bitcast_fusion.slots, bf16[1152,768]{1,0:T(8,128)(2,1)S(1)} %get-tuple-element.168.first, bf16[1152,384]{1,0:T(8,128)(2,1)S(1)} %get-tuple-element.190.rest_0_, ...), custom_call_target="tpu_custom_call" | custom-call | flops 226492416 | bytes 1032192 | tf_op jit(solution)/shard_map/query_key_grads/pallas_call | solution.py:50
  123.3 4.1 %first_grad.1 = (bf16[1024,768]{1,0:T(8,128)(2,1)S(1)}, bf16[2,64,768]{2,1,0:T(8,128)(2,1)S(1)}) custom-call(bf16[1152,1152]{1,0:T(8,128)(2,1)S(1)} %get-tuple-element.194.grad_proj, bf16[768,1536]{1,0:T(8,128)(2,1)S(1)} %get-tuple-element.149.rest_0_.wide), custom_call_target="tpu_custom_call" | custom-call | flops 226492416 | bytes 847872 | tf_op jit(solution)/shard_map/first_grad/pallas_call | solution.py:50
  127.5 2.7 %value_out_grads.1 = bf16[8,2,96,384]{3,2,1,0:T(8,128)(2,1)S(1)} custom-call(s32[8]{0:T(128)S(1)} %dynamic-slice_bitcast_fusion.slots, bf16[1152,768]{1,0:T(8,128)(2,1)S(1)} %get-tuple-element.168.first, bf16[1152,1152]{1,0:T(8,128)(2,1)S(1)} %get-tuple-element.194.grad_proj, bf16[1024,768]{1,0:T(8,128)(2,1)S(1)} %get-tuple-element.195.low_mid, ...), custom_call_target="tpu_custom_call" | custom-call | flops 226492416 | bytes 995328 | tf_op jit(solution)/shard_map/value_out_grads/pallas_call | solution.py:50
  138.6 2.4 %collective-permute-done.32 = bf16[64,768]{1,0:T(8,128)(2,1)S(1)} collective-permute-done((bf16[64,768]{1,0:T(8,128)(2,1)S(1)}, bf16[64,768]{1,0:T(8,128)(2,1)S(1)}, u32[]{:S(2)}, u32[]{:S(2)}) %collective-permute-start.32) | collective-permute-done | bytes 98336 | tf_op jit(solution)/shard_map/ppermute | solution.py:446
  147.7 10.2 %collective-permute-done.40 = bf16[2,96,384]{2,1,0:T(8,128)(2,1)S(1)} collective-permute-done((bf16[2,96,384]{2,1,0:T(8,128)(2,1)S(1)}, bf16[2,96,384]{2,1,0:T(8,128)(2,1)S(1)}, u32[]{:S(2)}, u32[]{:S(2)}) %collective-permute-start.40) | collective-permute-done | bytes 147488 | tf_op jit(solution)/shard_map/ppermute | solution.py:580
  162.3 2.3 %collective-permute-done.42 = bf16[2,96,384]{2,1,0:T(8,128)(2,1)S(1)} collective-permute-done((bf16[2,96,384]{2,1,0:T(8,128)(2,1)S(1)}, bf16[2,96,384]{2,1,0:T(8,128)(2,1)S(1)}, u32[]{:S(2)}, u32[]{:S(2)}) %collective-permute-start.42) | collective-permute-done | bytes 147488 | tf_op jit(solution)/shard_map/ppermute | solution.py:580
  169.7 3.0 %collective-permute-done.46 = bf16[2,96,384]{2,1,0:T(8,128)(2,1)S(1)} collective-permute-done((bf16[2,96,384]{2,1,0:T(8,128)(2,1)S(1)}, bf16[2,96,384]{2,1,0:T(8,128)(2,1)S(1)}, u32[]{:S(2)}, u32[]{:S(2)}) %collective-permute-start.46) | collective-permute-done | bytes 147488 | tf_op jit(solution)/shard_map/ppermute | solution.py:580
  174.3 3.1 %collective-permute-done.44 = bf16[3,96,576]{2,1,0:T(8,128)(2,1)S(1)} collective-permute-done((bf16[3,96,576]{2,1,0:T(8,128)(2,1)S(1)}, bf16[3,96,576]{2,1,0:T(8,128)(2,1)S(1)}, u32[]{:S(2)}, u32[]{:S(2)}) %collective-permute-start.44) | collective-permute-done | bytes 331808 | tf_op jit(solution)/shard_map/ppermute | solution.py:474
  181.0 4.9 %token_grad.1 = f32[1024,768]{1,0:T(8,128)} custom-call(bf16[1024,768]{1,0:T(8,128)(2,1)S(1)} %copy-done, f32[16,768]{1,0:T(8,128)S(1)} %get-tuple-element.162.gain, f32[1024,768]{1,0:T(8,128)S(1)} %get-tuple-element.227.grad_middle, bf16[1024,768]{1,0:T(8,128)(2,1)S(1)} %get-tuple-element.228.own, bf16[1024,768]{1,0:T(8,128)(2,1)S(1)} %collective-permute-done.38.other, ...), custom_call_target="tpu_custom_call" | custom-call | flops 19660800 | bytes 1431552 | tf_op jit(solution)/shard_map/token_grad/pallas_call | solution.py:50
  (153 shorter events, 70.9 us)
Async XLA Ops:
  2.5 10.3 %collective-permute-start.2 = (bf16[400,384]{1,0:T(8,128)(2,1)S(1)}, bf16[400,384]{1,0:T(8,128)(2,1)S(1)}, u32[]{:S(2)}, u32[]{:S(2)}) collective-permute-start(bf16[400,384]{1,0:T(8,128)(2,1)S(1)} %pad_maximum_fusion.2.rest_0_), channel_id=1, source_target_pairs={{8,0},{16,8},{24,16},{28,24},{20,28},{12,20},{4,12},{0,4},{9,1},{1... | collective-permute-start | bytes 921608 | tf_op jit(solution)/shard_map/ppermute | solution.py:530
  5.4 8.7 %collective-permute-start.1 = (bf16[400,384]{1,0:T(8,128)(2,1)S(1)}, bf16[400,384]{1,0:T(8,128)(2,1)S(1)}, u32[]{:S(2)}, u32[]{:S(2)}) collective-permute-start(bf16[400,384]{1,0:T(8,128)(2,1)S(1)} %pad_maximum_fusion.2.rest_0_), channel_id=1, source_target_pairs={{0,8},{8,16},{16,24},{24,28},{28,20},{20,12},{12,4},{4,0},{1,9},{9... | collective-permute-start | bytes 921608 | tf_op jit(solution)/shard_map/ppermute | solution.py:530
  6.6 10.3 %collective-permute-start = (bf16[64,768]{1,0:T(8,128)(2,1)S(1)}, bf16[64,768]{1,0:T(8,128)(2,1)S(1)}, u32[]{:S(2)}, u32[]{:S(2)}) collective-permute-start(bf16[64,768]{1,0:T(8,128)(2,1)S(1)} %slice_select_fusion), channel_id=1, source_target_pairs={{0,2},{2,0},{1,3},{3,1},{4,6},{6,4},{5,7},{7,5},{8,10},{10,8},{9,1... | collective-permute-start | bytes 294920 | tf_op jit(solution)/shard_map/ppermute | solution.py:460
  40.3 11.2 %collective-permute-start.10 = (bf16[288,576]{1,0:T(8,128)(2,1)S(1)}, bf16[288,576]{1,0:T(8,128)(2,1)S(1)}, u32[]{:S(2)}, u32[]{:S(2)}) collective-permute-start(bf16[288,576]{1,0:T(8,128)(2,1)S(1)} %pad_maximum_fusion.1.rest_0_), channel_id=1, source_target_pairs={{8,0},{16,8},{24,16},{28,24},{20,28},{12,20},{4,12},{0,4},{9,1},{1... | collective-permute-start | bytes 995336 | tf_op jit(solution)/shard_map/ppermute | solution.py:530
  41.9 10.1 %collective-permute-start.9 = (bf16[288,576]{1,0:T(8,128)(2,1)S(1)}, bf16[288,576]{1,0:T(8,128)(2,1)S(1)}, u32[]{:S(2)}, u32[]{:S(2)}) collective-permute-start(bf16[288,576]{1,0:T(8,128)(2,1)S(1)} %pad_maximum_fusion.1.rest_0_), channel_id=1, source_target_pairs={{0,8},{8,16},{16,24},{24,28},{28,20},{20,12},{12,4},{4,0},{1,9},{9... | collective-permute-start | bytes 995336 | tf_op jit(solution)/shard_map/ppermute | solution.py:530
  51.9 10.4 %collective-permute-start.11 = (bf16[288,576]{1,0:T(8,128)(2,1)S(1)}, bf16[288,576]{1,0:T(8,128)(2,1)S(1)}, u32[]{:S(2)}, u32[]{:S(2)}) collective-permute-start(bf16[288,576]{1,0:T(8,128)(2,1)S(1)} %collective-permute-done.9.rest_8_), channel_id=1, source_target_pairs={{0,8},{8,16},{16,24},{24,28},{28,20},{20,12},{12,4},{4,0},{1,9},{9... | collective-permute-start | bytes 995336 | tf_op jit(solution)/shard_map/ppermute | solution.py:530
  52.3 10.2 %collective-permute-start.12 = (bf16[288,576]{1,0:T(8,128)(2,1)S(1)}, bf16[288,576]{1,0:T(8,128)(2,1)S(1)}, u32[]{:S(2)}, u32[]{:S(2)}) collective-permute-start(bf16[288,576]{1,0:T(8,128)(2,1)S(1)} %collective-permute-done.10.rest_1_), channel_id=1, source_target_pairs={{8,0},{16,8},{24,16},{28,24},{20,28},{12,20},{4,12},{0,4},{9,1},{1... | collective-permute-start | bytes 995336 | tf_op jit(solution)/shard_map/ppermute | solution.py:530
  62.6 8.7 %collective-permute-start.13 = (bf16[288,576]{1,0:T(8,128)(2,1)S(1)}, bf16[288,576]{1,0:T(8,128)(2,1)S(1)}, u32[]{:S(2)}, u32[]{:S(2)}) collective-permute-start(bf16[288,576]{1,0:T(8,128)(2,1)S(1)} %collective-permute-done.11.rest_7_), channel_id=1, source_target_pairs={{0,8},{8,16},{16,24},{24,28},{28,20},{20,12},{12,4},{4,0},{1,9},{9... | collective-permute-start | bytes 995336 | tf_op jit(solution)/shard_map/ppermute | solution.py:530
  71.2 8.5 %collective-permute-start.15 = (bf16[1024,768]{1,0:T(8,128)(2,1)S(1)}, bf16[1024,768]{1,0:T(8,128)(2,1)S(1)}, u32[]{:S(2)}, u32[]{:S(2)}) collective-permute-start(bf16[1024,768]{1,0:T(8,128)(2,1)S(1)} %get-tuple-element.161.own), channel_id=1, source_target_pairs={{0,1},{1,0},{2,3},{3,2},{4,5},{5,4},{6,7},{7,6},{8,9},{9,8},{10,11... | collective-permute-start | bytes 4718600 | tf_op jit(solution)/shard_map/ppermute | solution.py:474
  103.7 14.4 %collective-permute-start.22 = (bf16[3,96,576]{2,1,0:T(8,128)(2,1)S(1)}, bf16[3,96,576]{2,1,0:T(8,128)(2,1)S(1)}, u32[]{:S(2)}, u32[]{:S(2)}) collective-permute-start(bf16[3,96,576]{2,1,0:T(8,128)(2,1)S(1)} %get-tuple-element.256), channel_id=1, source_target_pairs={{8,0},{16,8},{24,16},{28,24},{20,28},{12,20},{4,12},{0,4},{9,1},{1... | collective-permute-start | bytes 995336 | tf_op jit(solution)/shard_map/ppermute | solution.py:580
  105.3 12.8 %collective-permute-start.21 = (bf16[3,96,576]{2,1,0:T(8,128)(2,1)S(1)}, bf16[3,96,576]{2,1,0:T(8,128)(2,1)S(1)}, u32[]{:S(2)}, u32[]{:S(2)}) collective-permute-start(bf16[3,96,576]{2,1,0:T(8,128)(2,1)S(1)} %get-tuple-element.257), channel_id=1, source_target_pairs={{0,8},{8,16},{16,24},{24,28},{28,20},{20,12},{12,4},{4,0},{1,9},{9... | collective-permute-start | bytes 995336 | tf_op jit(solution)/shard_map/ppermute | solution.py:580
  118.3 11.9 %collective-permute-start.24 = (bf16[3,96,576]{2,1,0:T(8,128)(2,1)S(1)}, bf16[3,96,576]{2,1,0:T(8,128)(2,1)S(1)}, u32[]{:S(2)}, u32[]{:S(2)}) collective-permute-start(bf16[3,96,576]{2,1,0:T(8,128)(2,1)S(1)} %get-tuple-element.254), channel_id=1, source_target_pairs={{8,0},{16,8},{24,16},{28,24},{20,28},{12,20},{4,12},{0,4},{9,1},{1... | collective-permute-start | bytes 995336 | tf_op jit(solution)/shard_map/ppermute | solution.py:580
  119.9 10.3 %collective-permute-start.23 = (bf16[3,96,576]{2,1,0:T(8,128)(2,1)S(1)}, bf16[3,96,576]{2,1,0:T(8,128)(2,1)S(1)}, u32[]{:S(2)}, u32[]{:S(2)}) collective-permute-start(bf16[3,96,576]{2,1,0:T(8,128)(2,1)S(1)} %get-tuple-element.255), channel_id=1, source_target_pairs={{0,8},{8,16},{16,24},{24,28},{28,20},{20,12},{12,4},{4,0},{1,9},{9... | collective-permute-start | bytes 995336 | tf_op jit(solution)/shard_map/ppermute | solution.py:580
  132.4 14.0 %collective-permute-start.25 = (bf16[2,96,384]{2,1,0:T(8,128)(2,1)S(1)}, bf16[2,96,384]{2,1,0:T(8,128)(2,1)S(1)}, u32[]{:S(2)}, u32[]{:S(2)}) collective-permute-start(bf16[2,96,384]{2,1,0:T(8,128)(2,1)S(1)} %get-tuple-element.269), channel_id=1, source_target_pairs={{0,8},{8,16},{16,24},{24,28},{28,20},{20,12},{12,4},{4,0},{1,9},{9... | collective-permute-start | bytes 442376 | tf_op jit(solution)/shard_map/ppermute | solution.py:580
  132.8 9.7 %collective-permute-start.34 = (bf16[2,96,384]{2,1,0:T(8,128)(2,1)S(1)}, bf16[2,96,384]{2,1,0:T(8,128)(2,1)S(1)}, u32[]{:S(2)}, u32[]{:S(2)}) collective-permute-start(bf16[2,96,384]{2,1,0:T(8,128)(2,1)S(1)} %get-tuple-element.266), channel_id=1, source_target_pairs={{8,0},{16,8},{24,16},{28,24},{20,28},{12,20},{4,12},{0,4},{9,1},{1... | collective-permute-start | bytes 442376 | tf_op jit(solution)/shard_map/ppermute | solution.py:580
  136.0 9.8 %collective-permute-start.31 = (bf16[64,768]{1,0:T(8,128)(2,1)S(1)}, bf16[64,768]{1,0:T(8,128)(2,1)S(1)}, u32[]{:S(2)}, u32[]{:S(2)}) collective-permute-start(bf16[64,768]{1,0:T(8,128)(2,1)S(1)} %select_bitcast_fusion.4), channel_id=1, source_target_pairs={{0,2},{1,3},{2,0},{3,1},{4,6},{5,7},{6,4},{7,5},{8,10},{9,11},{10,... | collective-permute-start | bytes 294920 | tf_op jit(solution)/shard_map/ppermute | solution.py:446
  142.6 17.5 %collective-permute-start.30 = (bf16[3,96,576]{2,1,0:T(8,128)(2,1)S(1)}, bf16[3,96,576]{2,1,0:T(8,128)(2,1)S(1)}, u32[]{:S(2)}, u32[]{:S(2)}) collective-permute-start(bf16[3,96,576]{2,1,0:T(8,128)(2,1)S(1)} %get-tuple-element.252), channel_id=1, source_target_pairs={{8,0},{16,8},{24,16},{28,24},{20,28},{12,20},{4,12},{0,4},{9,1},{1... | collective-permute-start | bytes 995336 | tf_op jit(solution)/shard_map/ppermute | solution.py:580
  144.3 13.6 %collective-permute-start.40 = (bf16[2,96,384]{2,1,0:T(8,128)(2,1)S(1)}, bf16[2,96,384]{2,1,0:T(8,128)(2,1)S(1)}, u32[]{:S(2)}, u32[]{:S(2)}) collective-permute-start(bf16[2,96,384]{2,1,0:T(8,128)(2,1)S(1)} %get-tuple-element.262), channel_id=1, source_target_pairs={{8,0},{16,8},{24,16},{28,24},{20,28},{12,20},{4,12},{0,4},{9,1},{1... | collective-permute-start | bytes 442376 | tf_op jit(solution)/shard_map/ppermute | solution.py:580
  145.8 12.1 %collective-permute-start.39 = (bf16[2,96,384]{2,1,0:T(8,128)(2,1)S(1)}, bf16[2,96,384]{2,1,0:T(8,128)(2,1)S(1)}, u32[]{:S(2)}, u32[]{:S(2)}) collective-permute-start(bf16[2,96,384]{2,1,0:T(8,128)(2,1)S(1)} %get-tuple-element.263), channel_id=1, source_target_pairs={{0,8},{8,16},{16,24},{24,28},{28,20},{20,12},{12,4},{4,0},{1,9},{9... | collective-permute-start | bytes 442376 | tf_op jit(solution)/shard_map/ppermute | solution.py:580
  146.4 13.7 %collective-permute-start.29 = (bf16[3,96,576]{2,1,0:T(8,128)(2,1)S(1)}, bf16[3,96,576]{2,1,0:T(8,128)(2,1)S(1)}, u32[]{:S(2)}, u32[]{:S(2)}) collective-permute-start(bf16[3,96,576]{2,1,0:T(8,128)(2,1)S(1)} %get-tuple-element.253), channel_id=1, source_target_pairs={{0,8},{8,16},{16,24},{24,28},{28,20},{20,12},{12,4},{4,0},{1,9},{9... | collective-permute-start | bytes 995336 | tf_op jit(solution)/shard_map/ppermute | solution.py:580
  147.7 31.6 %collective-permute-start.37 = (bf16[1024,768]{1,0:T(8,128)(2,1)S(1)}, bf16[1024,768]{1,0:T(8,128)(2,1)S(1)}, u32[]{:S(2)}, u32[]{:S(2)}) collective-permute-start(bf16[1024,768]{1,0:T(8,128)(2,1)S(1)} %feed_out.1.own), channel_id=1, source_target_pairs={{0,1},{1,0},{2,3},{3,2},{4,5},{5,4},{6,7},{7,6},{8,9},{9,8},{10,11... | collective-permute-start | bytes 4718600 | tf_op jit(solution)/shard_map/ppermute | solution.py:474
  164.6 16.4 %collective-permute-start.38 = (bf16[1024,768]{1,0:T(8,128)(2,1)S(1)}, bf16[1024,768]{1,0:T(8,128)(2,1)S(1)}, u32[]{:S(2)}, u32[]{:S(2)}) collective-permute-start(bf16[1024,768]{1,0:T(8,128)(2,1)S(1)} %get-tuple-element.228.own), channel_id=1, source_target_pairs={{0,1},{1,0},{2,3},{3,2},{4,5},{5,4},{6,7},{7,6},{8,9},{9,8},{10,11... | collective-permute-start | bytes 4718600 | tf_op jit(solution)/shard_map/ppermute | solution.py:474
  165.9 11.5 %collective-permute-start.44 = (bf16[3,96,576]{2,1,0:T(8,128)(2,1)S(1)}, bf16[3,96,576]{2,1,0:T(8,128)(2,1)S(1)}, u32[]{:S(2)}, u32[]{:S(2)}) collective-permute-start(bf16[3,96,576]{2,1,0:T(8,128)(2,1)S(1)} %fusion.1), channel_id=1, source_target_pairs={{0,2},{2,0},{1,3},{3,1},{4,6},{6,4},{5,7},{7,5},{8,10},{10,8},{9,1... | collective-permute-start | bytes 995336 | tf_op jit(solution)/shard_map/ppermute | solution.py:474
  172.7 13.1 %collective-permute-start.43 = (bf16[2,96,384]{2,1,0:T(8,128)(2,1)S(1)}, bf16[2,96,384]{2,1,0:T(8,128)(2,1)S(1)}, u32[]{:S(2)}, u32[]{:S(2)}) collective-permute-start(bf16[2,96,384]{2,1,0:T(8,128)(2,1)S(1)} %fusion.5), channel_id=1, source_target_pairs={{0,2},{2,0},{1,3},{3,1},{4,6},{6,4},{5,7},{7,5},{8,10},{10,8},{9,1... | collective-permute-start | bytes 442376 | tf_op jit(solution)/shard_map/ppermute | solution.py:474
  (32 other events, 239.8 us)

commit v15 on v14

--- a/solution.py
+++ b/solution.py
@@ -789,8 +789,6 @@
         rows * width * 200,
         "token_grad",
     )
-    two = over_ctx(sums_two.total())
-    two, = locked([two], sums_one[1])
     mixed, = call(
         mixed_kernel,
         [shape((rows, width), bf16)],
@@ -799,11 +797,15 @@
         "mixed",
     )
     one = [chain.total() for chain in sums_one]
+    two = sums_two.total()
     if lax.axis_size("ctx") == 2:
+        got_two, = tied([swap(two, "ctx")], [one[1]])
         mixed, token_grad, *got = lax.optimization_barrier((mixed, token_grad, *[swap(part, "ctx") for part in one]))
         one = [part.astype(f32) + more.astype(f32) for part, more in zip(one, got)]
+        two = two.astype(f32) + got_two.astype(f32)
     else:
         one = [lax.psum(part, "ctx").astype(f32) for part in one]
+        two = lax.psum(two, "ctx").astype(f32)
     one = jnp.concatenate(one)
     gain_one_grad = jnp.sum(one[:3] * w_qkv.astype(f32), axis=(0, 2)) / gain_one.astype(f32)
     gain_two_grad = jnp.sum(two[:2] * w_in.astype(f32), axis=(0, 2)) / gain_two.astype(f32)

time: 189 us -> 189 us (level)
  no operation moved by 1% of the time
where the time goes in v15:
time: 189 us; the launch traced here: 188 us
  Pallas kernels  71.6 us (38%)
  waiting for transfers between devices  57.6 us (30%)
  starting transfers between devices  45.8 us (24%)
  other arithmetic  9.5 us (5%)
  local copies, waits for them, and re-layouts  2.82 us (1%)
    pallas_call x14, Pallas kernels, call(): pl.pallas_call(kernel, out_shape=out_shape, in_specs=[smem] * len(scalars...  71.6 us
    ppermute x18, starting transfers between devices, hop(): lax.ppermute(two, 'dp', self.back)  30.3 us
    ppermute x18, waiting for transfers between devices, hop(): lax.ppermute(two, 'dp', self.back)  28.6 us
    ppermute x18, waiting for transfers between devices, hop(): lax.ppermute(one, 'dp', self.ahead)  22.1 us
    ppermute x18, starting transfers between devices, hop(): lax.ppermute(one, 'dp', self.ahead)  8.51 us
  transfers between devices with their start and end apart: 49, of which 26 were waited for; matrix products, arithmetic and copies ran while one was open for 5% of the time, Pallas kernels for 32%

profile of v15, /device:TPU:0, one launch (start us, length us, event | category | flops | bytes accessed | tf_op | source)
XLA Modules:
  0.0 188.5 jit_solution(6217226802506108674)
XLA Ops:
  2.5 3.0 %collective-permute-start.2 = (bf16[400,384]{1,0:T(8,128)(2,1)S(1)}, bf16[400,384]{1,0:T(8,128)(2,1)S(1)}, u32[]{:S(2)}, u32[]{:S(2)}) collective-permute-start(bf16[400,384]{1,0:T(8,128)(2,1)S(1)} %pad_maximum_fusion.2.rest_0_), channel_id=1, source_target_pairs={{8,0},{16,8},{24,16},{28,24},{20,28},{12,20},{4,12},{0,4},{9,1},{1... | collective-permute-start | bytes 921608 | tf_op jit(solution)/shard_map/ppermute | solution.py:530
  10.2 2.1 %negate_select_fusion = (f32[1152,128]{1,0:T(8,128)S(1)}, f32[1152,128]{1,0:T(8,128)S(1)}) fusion(f32[128]{0:T(128)S(1)} %fusion.14, f32[1152]{0:T(1024)S(1)} %subtract_convert_fusion, pred[128]{0:T(512)(128)(4,1)S(1)} %fusion.15), kind=kLoop, calls=%fused_computation | loop fusion | flops 442368 | bytes 1184896 | tf_op jit(solution)/shard_map/jit(_where)/select_n | solution.py:606
  16.9 5.1 %collective-permute-done.4.rest_2_ = bf16[400,384]{1,0:T(8,128)(2,1)S(1)} collective-permute-done((bf16[400,384]{1,0:T(8,128)(2,1)S(1)}, bf16[400,384]{1,0:T(8,128)(2,1)S(1)}, u32[]{:S(2)}, u32[]{:S(2)}) %collective-permute-start.4) | collective-permute-done | bytes 307232 | tf_op jit(solution)/shard_map/ppermute | solution.py:530
  27.4 2.8 %collective-permute-done.5.rest_6_ = bf16[400,384]{1,0:T(8,128)(2,1)S(1)} collective-permute-done((bf16[400,384]{1,0:T(8,128)(2,1)S(1)}, bf16[400,384]{1,0:T(8,128)(2,1)S(1)}, u32[]{:S(2)}, u32[]{:S(2)}) %collective-permute-start.5) | collective-permute-done | bytes 307232 | tf_op jit(solution)/shard_map/ppermute | solution.py:530
  34.1 6.2 %collective-permute-done.7.rest_4_ = bf16[192,384]{1,0:T(8,128)(2,1)S(1)} collective-permute-done((bf16[192,384]{1,0:T(8,128)(2,1)S(1)}, bf16[192,384]{1,0:T(8,128)(2,1)S(1)}, u32[]{:S(2)}, u32[]{:S(2)}) %collective-permute-start.7) | collective-permute-done | bytes 147488 | tf_op jit(solution)/shard_map/ppermute | solution.py:530
  42.3 5.7 %project.1 = (bf16[768,1536]{1,0:T(8,128)(2,1)S(1)}, f32[16,768]{1,0:T(8,128)S(1)}, bf16[1152,768]{1,0:T(8,128)(2,1)S(1)}, bf16[1024,384]{1,0:T(8,128)(2,1)S(1)}...) custom-call(s32[8]{0:T(128)S(1)} %dynamic-slice_bitcast_fusion.slots, f32[1152,768]{1,0:T(8,128)S(1)} %first_norm.1.hat, ...), custom_call_target="tpu_custom_call" | custom-call | flops 603979776 | bytes 1738752 | tf_op jit(solution)/shard_map/project/pallas_call | solution.py:50
  48.1 3.4 %collective-permute-done.10.rest_1_ = bf16[288,576]{1,0:T(8,128)(2,1)S(1)} collective-permute-done((bf16[288,576]{1,0:T(8,128)(2,1)S(1)}, bf16[288,576]{1,0:T(8,128)(2,1)S(1)}, u32[]{:S(2)}, u32[]{:S(2)}) %collective-permute-start.10) | collective-permute-done | bytes 331808 | tf_op jit(solution)/shard_map/ppermute | solution.py:530
  54.0 7.7 %attend.2 = (bf16[16,256,256]{2,1,0:T(8,128)(2,1)S(1)}, bf16[1024,384]{1,0:T(8,128)(2,1)S(1)}) custom-call(s32[5]{0:T(128)S(1)} %pad_add_fusion.bounds, bf16[1024,384]{1,0:T(8,128)(2,1)S(1)} %get-tuple-element.144.query, bf16[1152,384]{1,0:T(8,128)(2,1)S(1)} %get-tuple-element.145.key, bf16[1152,384]{1,0:T(8,128)(2,1)S(1)} %get-tuple-element.146.value), custom_call_target="tpu_custom_call" | custom-call | flops 754974720 | bytes 679936 | tf_op jit(solution)/shard_map/attend/pallas_call | solution.py:50
  64.6 6.6 %attend.3 = (bf16[8,256,256]{2,1,0:T(8,128)(2,1)S(1)}, bf16[1024,384]{1,0:T(8,128)(2,1)S(1)}, bf16[1024,768]{1,0:T(8,128)(2,1)S(1)}) custom-call(s32[5]{0:T(128)S(1)} %pad_add_fusion.bounds, bf16[1024,384]{1,0:T(8,128)(2,1)S(1)} %get-tuple-element.144.query, bf16[1152,384]{1,0:T(8,128)(2,1)S(1)} %get-tuple-element.145.key, ...), custom_call_target="tpu_custom_call" | custom-call | flops 528482304 | bytes 1138688 | tf_op jit(solution)/shard_map/attend/pallas_call | solution.py:50
  73.7 5.0 %collective-permute-done.16.rest_4_ = bf16[96,576]{1,0:T(8,128)(2,1)S(1)} collective-permute-done((bf16[96,576]{1,0:T(8,128)(2,1)S(1)}, bf16[96,576]{1,0:T(8,128)(2,1)S(1)}, u32[]{:S(2)}, u32[]{:S(2)}) %collective-permute-start.16) | collective-permute-done | bytes 110624 | tf_op jit(solution)/shard_map/ppermute | solution.py:530
  79.8 10.6 %feed_forward_and_back.1 = (f32[1024,768]{1,0:T(8,128)S(1)}, bf16[1024,768]{1,0:T(8,128)(2,1)S(1)}, bf16[1024,576]{1,0:T(8,128)(2,1)S(1)}, bf16[1024,576]{1,0:T(...) custom-call(s32[8]{0:T(128)S(1)} %dynamic-slice_bitcast_fusion.slots, ...), custom_call_target="tpu_custom_call" | custom-call | flops 905969664 | bytes 2684928 | tf_op jit(solution)/shard_map/feed_forward_and_back/pallas_call | solution.py:50
  90.4 4.7 %feed_weight_grads.1 = bf16[8,3,96,576]{3,2,1,0:T(8,128)(2,1)S(1)} custom-call(s32[8]{0:T(128)S(1)} %dynamic-slice_bitcast_fusion.slots, bf16[1024,768]{1,0:T(8,128)(2,1)S(1)} %get-tuple-element.170.second, bf16[1024,576]{1,0:T(8,128)(2,1)S(1)} %get-tuple-element.174.hidden, bf16[1024,576]{1,0:T(8,128)(2,1)S(1)} %get-tuple-element.171.grad_gate, ...), custom_call_target="tpu_custom_call" | custom-call | flops 566231040 | bytes 1167360 | tf_op jit(solution)/shard_map/feed_weight_grads/pallas_call | solution.py:50
  97.3 2.0 %feed_out.1.own = bf16[1024,768]{1,0:T(8,128)(2,1)S(1)} custom-call(bf16[1024,576]{1,0:T(8,128)(2,1)S(1)} %get-tuple-element.174.hidden, bf16[3,768,576]{2,1,0:T(8,128)(2,1)S(1)} %get-tuple-element.175.whole), custom_call_target="tpu_custom_call" | custom-call | flops 113246208 | bytes 675840 | tf_op jit(solution)/shard_map/feed_out/pallas_call | solution.py:50
  99.4 3.6 %middle_grad.1 = (f32[1024,768]{1,0:T(8,128)S(1)}, bf16[1024,768]{1,0:T(8,128)(2,1)S(1)}, bf16[1024,384]{1,0:T(8,128)(2,1)S(1)}) custom-call(f32[1024,768]{1,0:T(8,128)S(1)} %get-tuple-element.222.middle, bf16[1024,768]{1,0:T(8,128)(2,1)S(1)} %get-tuple-element.167.own, bf16[1024,768]{1,0:T(8,128)(2,1)S(1)} %collective-permute-done.18.other, ...), custom_call_target="tpu_custom_call" | custom-call | flops 301989888 | bytes 1972224 | tf_op jit(solution)/shard_map/middle_grad/pallas_call | solution.py:50
  105.8 12.3 %attention_back.1 = (bf16[1152,384]{1,0:T(8,128)(2,1)S(1)}, bf16[1152,384]{1,0:T(8,128)(2,1)S(1)}, bf16[1152,384]{1,0:T(8,128)(2,1)S(1)}) custom-call(bf16[1024,384]{1,0:T(8,128)(2,1)S(1)} %get-tuple-element.144.query, bf16[1152,384]{1,0:T(8,128)(2,1)S(1)} %get-tuple-element.145.key, bf16[1152,384]{1,0:T(8,128)(2,1)S(1)} %get-tuple-element.146.value, ...), custom_call_target="tpu_custom_call" | custom-call | flops 1132462080 | bytes 1290240 | tf_op jit(solution)/shard_map/attention_back/pallas_call | solution.py:50
  120.3 3.0 %query_key_grads.1 = (bf16[1152,1152]{1,0:T(8,128)(2,1)S(1)}, bf16[8,2,96,384]{3,2,1,0:T(8,128)(2,1)S(1)}) custom-call(s32[8]{0:T(128)S(1)} %dynamic-slice_bitcast_fusion.slots, bf16[1152,768]{1,0:T(8,128)(2,1)S(1)} %get-tuple-element.166.first, bf16[1152,384]{1,0:T(8,128)(2,1)S(1)} %get-tuple-element.188.rest_0_, ...), custom_call_target="tpu_custom_call" | custom-call | flops 226492416 | bytes 1032192 | tf_op jit(solution)/shard_map/query_key_grads/pallas_call | solution.py:50
  123.3 4.1 %first_grad.1 = (bf16[1024,768]{1,0:T(8,128)(2,1)S(1)}, bf16[2,64,768]{2,1,0:T(8,128)(2,1)S(1)}) custom-call(bf16[1152,1152]{1,0:T(8,128)(2,1)S(1)} %get-tuple-element.192.grad_proj, bf16[768,1536]{1,0:T(8,128)(2,1)S(1)} %get-tuple-element.147.rest_0_.wide), custom_call_target="tpu_custom_call" | custom-call | flops 226492416 | bytes 847872 | tf_op jit(solution)/shard_map/first_grad/pallas_call | solution.py:50
  127.5 2.7 %value_out_grads.1 = bf16[8,2,96,384]{3,2,1,0:T(8,128)(2,1)S(1)} custom-call(s32[8]{0:T(128)S(1)} %dynamic-slice_bitcast_fusion.slots, bf16[1152,768]{1,0:T(8,128)(2,1)S(1)} %get-tuple-element.166.first, bf16[1152,1152]{1,0:T(8,128)(2,1)S(1)} %get-tuple-element.192.grad_proj, bf16[1024,768]{1,0:T(8,128)(2,1)S(1)} %get-tuple-element.193.low_mid, ...), custom_call_target="tpu_custom_call" | custom-call | flops 226492416 | bytes 995328 | tf_op jit(solution)/shard_map/value_out_grads/pallas_call | solution.py:50
  138.6 2.4 %collective-permute-done.32 = bf16[64,768]{1,0:T(8,128)(2,1)S(1)} collective-permute-done((bf16[64,768]{1,0:T(8,128)(2,1)S(1)}, bf16[64,768]{1,0:T(8,128)(2,1)S(1)}, u32[]{:S(2)}, u32[]{:S(2)}) %collective-permute-start.32) | collective-permute-done | bytes 98336 | tf_op jit(solution)/shard_map/ppermute | solution.py:446
  147.7 10.2 %collective-permute-done.40 = bf16[2,96,384]{2,1,0:T(8,128)(2,1)S(1)} collective-permute-done((bf16[2,96,384]{2,1,0:T(8,128)(2,1)S(1)}, bf16[2,96,384]{2,1,0:T(8,128)(2,1)S(1)}, u32[]{:S(2)}, u32[]{:S(2)}) %collective-permute-start.40) | collective-permute-done | bytes 147488 | tf_op jit(solution)/shard_map/ppermute | solution.py:580
  162.3 2.3 %collective-permute-done.42 = bf16[2,96,384]{2,1,0:T(8,128)(2,1)S(1)} collective-permute-done((bf16[2,96,384]{2,1,0:T(8,128)(2,1)S(1)}, bf16[2,96,384]{2,1,0:T(8,128)(2,1)S(1)}, u32[]{:S(2)}, u32[]{:S(2)}) %collective-permute-start.42) | collective-permute-done | bytes 147488 | tf_op jit(solution)/shard_map/ppermute | solution.py:580
  169.6 3.1 %collective-permute-done.45 = bf16[2,96,384]{2,1,0:T(8,128)(2,1)S(1)} collective-permute-done((bf16[2,96,384]{2,1,0:T(8,128)(2,1)S(1)}, bf16[2,96,384]{2,1,0:T(8,128)(2,1)S(1)}, u32[]{:S(2)}, u32[]{:S(2)}) %collective-permute-start.45) | collective-permute-done | bytes 147488 | tf_op jit(solution)/shard_map/ppermute | solution.py:580
  174.9 2.5 %collective-permute-done.47 = bf16[3,96,576]{2,1,0:T(8,128)(2,1)S(1)} collective-permute-done((bf16[3,96,576]{2,1,0:T(8,128)(2,1)S(1)}, bf16[3,96,576]{2,1,0:T(8,128)(2,1)S(1)}, u32[]{:S(2)}, u32[]{:S(2)}) %collective-permute-start.47) | collective-permute-done | bytes 331808 | tf_op jit(solution)/shard_map/ppermute | solution.py:474
  180.8 4.9 %token_grad.1 = f32[1024,768]{1,0:T(8,128)} custom-call(bf16[1024,768]{1,0:T(8,128)(2,1)S(1)} %copy-done, f32[16,768]{1,0:T(8,128)S(1)} %get-tuple-element.160.gain, f32[1024,768]{1,0:T(8,128)S(1)} %get-tuple-element.225.grad_middle, bf16[1024,768]{1,0:T(8,128)(2,1)S(1)} %get-tuple-element.226.own, bf16[1024,768]{1,0:T(8,128)(2,1)S(1)} %collective-permute-done.38.other, ...), custom_call_target="tpu_custom_call" | custom-call | flops 19660800 | bytes 1431552 | tf_op jit(solution)/shard_map/token_grad/pallas_call | solution.py:50
  (153 shorter events, 71.3 us)
Async XLA Ops:
  2.5 10.3 %collective-permute-start.2 = (bf16[400,384]{1,0:T(8,128)(2,1)S(1)}, bf16[400,384]{1,0:T(8,128)(2,1)S(1)}, u32[]{:S(2)}, u32[]{:S(2)}) collective-permute-start(bf16[400,384]{1,0:T(8,128)(2,1)S(1)} %pad_maximum_fusion.2.rest_0_), channel_id=1, source_target_pairs={{8,0},{16,8},{24,16},{28,24},{20,28},{12,20},{4,12},{0,4},{9,1},{1... | collective-permute-start | bytes 921608 | tf_op jit(solution)/shard_map/ppermute | solution.py:530
  5.4 8.7 %collective-permute-start.1 = (bf16[400,384]{1,0:T(8,128)(2,1)S(1)}, bf16[400,384]{1,0:T(8,128)(2,1)S(1)}, u32[]{:S(2)}, u32[]{:S(2)}) collective-permute-start(bf16[400,384]{1,0:T(8,128)(2,1)S(1)} %pad_maximum_fusion.2.rest_0_), channel_id=1, source_target_pairs={{0,8},{8,16},{16,24},{24,28},{28,20},{20,12},{12,4},{4,0},{1,9},{9... | collective-permute-start | bytes 921608 | tf_op jit(solution)/shard_map/ppermute | solution.py:530
  6.6 10.3 %collective-permute-start = (bf16[64,768]{1,0:T(8,128)(2,1)S(1)}, bf16[64,768]{1,0:T(8,128)(2,1)S(1)}, u32[]{:S(2)}, u32[]{:S(2)}) collective-permute-start(bf16[64,768]{1,0:T(8,128)(2,1)S(1)} %slice_select_fusion), channel_id=1, source_target_pairs={{0,2},{2,0},{1,3},{3,1},{4,6},{6,4},{5,7},{7,5},{8,10},{10,8},{9,1... | collective-permute-start | bytes 294920 | tf_op jit(solution)/shard_map/ppermute | solution.py:460
  40.3 11.2 %collective-permute-start.10 = (bf16[288,576]{1,0:T(8,128)(2,1)S(1)}, bf16[288,576]{1,0:T(8,128)(2,1)S(1)}, u32[]{:S(2)}, u32[]{:S(2)}) collective-permute-start(bf16[288,576]{1,0:T(8,128)(2,1)S(1)} %pad_maximum_fusion.1.rest_0_), channel_id=1, source_target_pairs={{8,0},{16,8},{24,16},{28,24},{20,28},{12,20},{4,12},{0,4},{9,1},{1... | collective-permute-start | bytes 995336 | tf_op jit(solution)/shard_map/ppermute | solution.py:530
  41.9 10.1 %collective-permute-start.9 = (bf16[288,576]{1,0:T(8,128)(2,1)S(1)}, bf16[288,576]{1,0:T(8,128)(2,1)S(1)}, u32[]{:S(2)}, u32[]{:S(2)}) collective-permute-start(bf16[288,576]{1,0:T(8,128)(2,1)S(1)} %pad_maximum_fusion.1.rest_0_), channel_id=1, source_target_pairs={{0,8},{8,16},{16,24},{24,28},{28,20},{20,12},{12,4},{4,0},{1,9},{9... | collective-permute-start | bytes 995336 | tf_op jit(solution)/shard_map/ppermute | solution.py:530
  51.9 10.4 %collective-permute-start.11 = (bf16[288,576]{1,0:T(8,128)(2,1)S(1)}, bf16[288,576]{1,0:T(8,128)(2,1)S(1)}, u32[]{:S(2)}, u32[]{:S(2)}) collective-permute-start(bf16[288,576]{1,0:T(8,128)(2,1)S(1)} %collective-permute-done.9.rest_8_), channel_id=1, source_target_pairs={{0,8},{8,16},{16,24},{24,28},{28,20},{20,12},{12,4},{4,0},{1,9},{9... | collective-permute-start | bytes 995336 | tf_op jit(solution)/shard_map/ppermute | solution.py:530
  52.3 10.2 %collective-permute-start.12 = (bf16[288,576]{1,0:T(8,128)(2,1)S(1)}, bf16[288,576]{1,0:T(8,128)(2,1)S(1)}, u32[]{:S(2)}, u32[]{:S(2)}) collective-permute-start(bf16[288,576]{1,0:T(8,128)(2,1)S(1)} %collective-permute-done.10.rest_1_), channel_id=1, source_target_pairs={{8,0},{16,8},{24,16},{28,24},{20,28},{12,20},{4,12},{0,4},{9,1},{1... | collective-permute-start | bytes 995336 | tf_op jit(solution)/shard_map/ppermute | solution.py:530
  62.6 8.7 %collective-permute-start.13 = (bf16[288,576]{1,0:T(8,128)(2,1)S(1)}, bf16[288,576]{1,0:T(8,128)(2,1)S(1)}, u32[]{:S(2)}, u32[]{:S(2)}) collective-permute-start(bf16[288,576]{1,0:T(8,128)(2,1)S(1)} %collective-permute-done.11.rest_7_), channel_id=1, source_target_pairs={{0,8},{8,16},{16,24},{24,28},{28,20},{20,12},{12,4},{4,0},{1,9},{9... | collective-permute-start | bytes 995336 | tf_op jit(solution)/shard_map/ppermute | solution.py:530
  103.7 14.4 %collective-permute-start.22 = (bf16[3,96,576]{2,1,0:T(8,128)(2,1)S(1)}, bf16[3,96,576]{2,1,0:T(8,128)(2,1)S(1)}, u32[]{:S(2)}, u32[]{:S(2)}) collective-permute-start(bf16[3,96,576]{2,1,0:T(8,128)(2,1)S(1)} %get-tuple-element.252), channel_id=1, source_target_pairs={{8,0},{16,8},{24,16},{28,24},{20,28},{12,20},{4,12},{0,4},{9,1},{1... | collective-permute-start | bytes 995336 | tf_op jit(solution)/shard_map/ppermute | solution.py:580
  105.3 12.8 %collective-permute-start.21 = (bf16[3,96,576]{2,1,0:T(8,128)(2,1)S(1)}, bf16[3,96,576]{2,1,0:T(8,128)(2,1)S(1)}, u32[]{:S(2)}, u32[]{:S(2)}) collective-permute-start(bf16[3,96,576]{2,1,0:T(8,128)(2,1)S(1)} %get-tuple-element.253), channel_id=1, source_target_pairs={{0,8},{8,16},{16,24},{24,28},{28,20},{20,12},{12,4},{4,0},{1,9},{9... | collective-permute-start | bytes 995336 | tf_op jit(solution)/shard_map/ppermute | solution.py:580
  118.3 11.9 %collective-permute-start.24 = (bf16[3,96,576]{2,1,0:T(8,128)(2,1)S(1)}, bf16[3,96,576]{2,1,0:T(8,128)(2,1)S(1)}, u32[]{:S(2)}, u32[]{:S(2)}) collective-permute-start(bf16[3,96,576]{2,1,0:T(8,128)(2,1)S(1)} %get-tuple-element.250), channel_id=1, source_target_pairs={{8,0},{16,8},{24,16},{28,24},{20,28},{12,20},{4,12},{0,4},{9,1},{1... | collective-permute-start | bytes 995336 | tf_op jit(solution)/shard_map/ppermute | solution.py:580
  119.9 10.3 %collective-permute-start.23 = (bf16[3,96,576]{2,1,0:T(8,128)(2,1)S(1)}, bf16[3,96,576]{2,1,0:T(8,128)(2,1)S(1)}, u32[]{:S(2)}, u32[]{:S(2)}) collective-permute-start(bf16[3,96,576]{2,1,0:T(8,128)(2,1)S(1)} %get-tuple-element.251), channel_id=1, source_target_pairs={{0,8},{8,16},{16,24},{24,28},{28,20},{20,12},{12,4},{4,0},{1,9},{9... | collective-permute-start | bytes 995336 | tf_op jit(solution)/shard_map/ppermute | solution.py:580
  132.4 14.0 %collective-permute-start.25 = (bf16[2,96,384]{2,1,0:T(8,128)(2,1)S(1)}, bf16[2,96,384]{2,1,0:T(8,128)(2,1)S(1)}, u32[]{:S(2)}, u32[]{:S(2)}) collective-permute-start(bf16[2,96,384]{2,1,0:T(8,128)(2,1)S(1)} %get-tuple-element.265), channel_id=1, source_target_pairs={{0,8},{8,16},{16,24},{24,28},{28,20},{20,12},{12,4},{4,0},{1,9},{9... | collective-permute-start | bytes 442376 | tf_op jit(solution)/shard_map/ppermute | solution.py:580
  132.8 9.7 %collective-permute-start.34 = (bf16[2,96,384]{2,1,0:T(8,128)(2,1)S(1)}, bf16[2,96,384]{2,1,0:T(8,128)(2,1)S(1)}, u32[]{:S(2)}, u32[]{:S(2)}) collective-permute-start(bf16[2,96,384]{2,1,0:T(8,128)(2,1)S(1)} %get-tuple-element.262), channel_id=1, source_target_pairs={{8,0},{16,8},{24,16},{28,24},{20,28},{12,20},{4,12},{0,4},{9,1},{1... | collective-permute-start | bytes 442376 | tf_op jit(solution)/shard_map/ppermute | solution.py:580
  136.0 9.8 %collective-permute-start.31 = (bf16[64,768]{1,0:T(8,128)(2,1)S(1)}, bf16[64,768]{1,0:T(8,128)(2,1)S(1)}, u32[]{:S(2)}, u32[]{:S(2)}) collective-permute-start(bf16[64,768]{1,0:T(8,128)(2,1)S(1)} %select_bitcast_fusion.4), channel_id=1, source_target_pairs={{0,2},{1,3},{2,0},{3,1},{4,6},{5,7},{6,4},{7,5},{8,10},{9,11},{10,... | collective-permute-start | bytes 294920 | tf_op jit(solution)/shard_map/ppermute | solution.py:446
  142.6 17.5 %collective-permute-start.30 = (bf16[3,96,576]{2,1,0:T(8,128)(2,1)S(1)}, bf16[3,96,576]{2,1,0:T(8,128)(2,1)S(1)}, u32[]{:S(2)}, u32[]{:S(2)}) collective-permute-start(bf16[3,96,576]{2,1,0:T(8,128)(2,1)S(1)} %get-tuple-element.248), channel_id=1, source_target_pairs={{8,0},{16,8},{24,16},{28,24},{20,28},{12,20},{4,12},{0,4},{9,1},{1... | collective-permute-start | bytes 995336 | tf_op jit(solution)/shard_map/ppermute | solution.py:580
  144.3 13.6 %collective-permute-start.40 = (bf16[2,96,384]{2,1,0:T(8,128)(2,1)S(1)}, bf16[2,96,384]{2,1,0:T(8,128)(2,1)S(1)}, u32[]{:S(2)}, u32[]{:S(2)}) collective-permute-start(bf16[2,96,384]{2,1,0:T(8,128)(2,1)S(1)} %get-tuple-element.258), channel_id=1, source_target_pairs={{8,0},{16,8},{24,16},{28,24},{20,28},{12,20},{4,12},{0,4},{9,1},{1... | collective-permute-start | bytes 442376 | tf_op jit(solution)/shard_map/ppermute | solution.py:580
  145.8 12.1 %collective-permute-start.39 = (bf16[2,96,384]{2,1,0:T(8,128)(2,1)S(1)}, bf16[2,96,384]{2,1,0:T(8,128)(2,1)S(1)}, u32[]{:S(2)}, u32[]{:S(2)}) collective-permute-start(bf16[2,96,384]{2,1,0:T(8,128)(2,1)S(1)} %get-tuple-element.259), channel_id=1, source_target_pairs={{0,8},{8,16},{16,24},{24,28},{28,20},{20,12},{12,4},{4,0},{1,9},{9... | collective-permute-start | bytes 442376 | tf_op jit(solution)/shard_map/ppermute | solution.py:580
  146.4 13.7 %collective-permute-start.29 = (bf16[3,96,576]{2,1,0:T(8,128)(2,1)S(1)}, bf16[3,96,576]{2,1,0:T(8,128)(2,1)S(1)}, u32[]{:S(2)}, u32[]{:S(2)}) collective-permute-start(bf16[3,96,576]{2,1,0:T(8,128)(2,1)S(1)} %get-tuple-element.249), channel_id=1, source_target_pairs={{0,8},{8,16},{16,24},{24,28},{28,20},{20,12},{12,4},{4,0},{1,9},{9... | collective-permute-start | bytes 995336 | tf_op jit(solution)/shard_map/ppermute | solution.py:580
  147.7 31.5 %collective-permute-start.37 = (bf16[1024,768]{1,0:T(8,128)(2,1)S(1)}, bf16[1024,768]{1,0:T(8,128)(2,1)S(1)}, u32[]{:S(2)}, u32[]{:S(2)}) collective-permute-start(bf16[1024,768]{1,0:T(8,128)(2,1)S(1)} %feed_out.1.own), channel_id=1, source_target_pairs={{0,1},{1,0},{2,3},{3,2},{4,5},{5,4},{6,7},{7,6},{8,9},{9,8},{10,11... | collective-permute-start | bytes 4718600 | tf_op jit(solution)/shard_map/ppermute | solution.py:474
  164.6 16.2 %collective-permute-start.38 = (bf16[1024,768]{1,0:T(8,128)(2,1)S(1)}, bf16[1024,768]{1,0:T(8,128)(2,1)S(1)}, u32[]{:S(2)}, u32[]{:S(2)}) collective-permute-start(bf16[1024,768]{1,0:T(8,128)(2,1)S(1)} %get-tuple-element.226.own), channel_id=1, source_target_pairs={{0,1},{1,0},{2,3},{3,2},{4,5},{5,4},{6,7},{7,6},{8,9},{9,8},{10,11... | collective-permute-start | bytes 4718600 | tf_op jit(solution)/shard_map/ppermute | solution.py:474
  165.9 11.5 %collective-permute-start.47 = (bf16[3,96,576]{2,1,0:T(8,128)(2,1)S(1)}, bf16[3,96,576]{2,1,0:T(8,128)(2,1)S(1)}, u32[]{:S(2)}, u32[]{:S(2)}) collective-permute-start(bf16[3,96,576]{2,1,0:T(8,128)(2,1)S(1)} %fusion.1), channel_id=1, source_target_pairs={{0,2},{2,0},{1,3},{3,1},{4,6},{6,4},{5,7},{7,5},{8,10},{10,8},{9,1... | collective-permute-start | bytes 995336 | tf_op jit(solution)/shard_map/ppermute | solution.py:474
  172.7 13.0 %collective-permute-start.43 = (bf16[2,96,384]{2,1,0:T(8,128)(2,1)S(1)}, bf16[2,96,384]{2,1,0:T(8,128)(2,1)S(1)}, u32[]{:S(2)}, u32[]{:S(2)}) collective-permute-start(bf16[2,96,384]{2,1,0:T(8,128)(2,1)S(1)} %fusion.5), channel_id=1, source_target_pairs={{0,2},{2,0},{1,3},{3,1},{4,6},{6,4},{5,7},{7,5},{8,10},{10,8},{9,1... | collective-permute-start | bytes 442376 | tf_op jit(solution)/shard_map/ppermute | solution.py:474
  174.4 11.3 %collective-permute-start.46 = (bf16[2,96,384]{2,1,0:T(8,128)(2,1)S(1)}, bf16[2,96,384]{2,1,0:T(8,128)(2,1)S(1)}, u32[]{:S(2)}, u32[]{:S(2)}) collective-permute-start(bf16[2,96,384]{2,1,0:T(8,128)(2,1)S(1)} %fusion.3), channel_id=1, source_target_pairs={{0,2},{2,0},{1,3},{3,1},{4,6},{6,4},{5,7},{7,5},{8,10},{10,8},{9,1... | collective-permute-start | bytes 442376 | tf_op jit(solution)/shard_map/ppermute | solution.py:474
  (32 other events, 235.2 us)

commit v16 on v15

--- a/solution.py
+++ b/solution.py
@@ -799,7 +799,7 @@
     one = [chain.total() for chain in sums_one]
     two = sums_two.total()
     if lax.axis_size("ctx") == 2:
-        got_two, = tied([swap(two, "ctx")], [one[1]])
+        got_two, = tied([swap(two, "ctx")], [one[1], mixed, token_grad])
         mixed, token_grad, *got = lax.optimization_barrier((mixed, token_grad, *[swap(part, "ctx") for part in one]))
         one = [part.astype(f32) + more.astype(f32) for part, more in zip(one, got)]
         two = two.astype(f32) + got_two.astype(f32)

time: 189 us -> 189 us (level)
    ppermute x18, waiting for transfers between devices: 22.1 us -> 28.8 us  [hop(): lax.ppermute(one, 'dp', self.ahead)]
    ppermute x18, waiting for transfers between devices: 28.6 us -> 22.1 us  [hop(): lax.ppermute(two, 'dp', self.back)]
    ppermute x8, waiting for transfers between devices: 2.98 us -> 0.47 us  [swap(): return lax.ppermute(array, axis, [(0, 1), (1, 0)])]
  transfers between devices with their start and end apart: 49 -> 49, of which waited for: 26 -> 28; matrix products, arithmetic and copies ran while one was open for 5% -> 5% of each run, Pallas kernels for 32% -> 32%
where the time goes in v16:
time: 189 us
  Pallas kernels  71.6 us (38%)
  waiting for transfers between devices  56.7 us (30%)
  starting transfers between devices  46.9 us (25%)
  other arithmetic  9.53 us (5%)
  local copies, waits for them, and re-layouts  2.83 us (1%)
    pallas_call x14, Pallas kernels, call(): pl.pallas_call(kernel, out_shape=out_shape, in_specs=[smem] * len(scalars...  71.6 us
    ppermute x18, starting transfers between devices, hop(): lax.ppermute(two, 'dp', self.back)  30.5 us
    ppermute x18, waiting for transfers between devices, hop(): lax.ppermute(one, 'dp', self.ahead)  28.8 us
    ppermute x18, waiting for transfers between devices, hop(): lax.ppermute(two, 'dp', self.back)  22.1 us
    ppermute x18, starting transfers between devices, hop(): lax.ppermute(one, 'dp', self.ahead)  7.51 us
  transfers between devices with their start and end apart: 49, of which 28 were waited for; matrix products, arithmetic and copies ran while one was open for 5% of the time, Pallas kernels for 32%

profile of v16, /device:TPU:0, one launch (start us, length us, event | category | flops | bytes accessed | tf_op | source)
XLA Modules:
  0.0 188.7 jit_solution(5561147744602719876)
XLA Ops:
  2.5 3.0 %collective-permute-start.2 = (bf16[400,384]{1,0:T(8,128)(2,1)S(1)}, bf16[400,384]{1,0:T(8,128)(2,1)S(1)}, u32[]{:S(2)}, u32[]{:S(2)}) collective-permute-start(bf16[400,384]{1,0:T(8,128)(2,1)S(1)} %pad_maximum_fusion.2.rest_0_), channel_id=1, source_target_pairs={{8,0},{16,8},{24,16},{28,24},{20,28},{12,20},{4,12},{0,4},{9,1},{1... | collective-permute-start | bytes 921608 | tf_op jit(solution)/shard_map/ppermute | solution.py:530
  10.2 2.1 %negate_select_fusion = (f32[1152,128]{1,0:T(8,128)S(1)}, f32[1152,128]{1,0:T(8,128)S(1)}) fusion(f32[128]{0:T(128)S(1)} %fusion.14, f32[1152]{0:T(1024)S(1)} %subtract_convert_fusion, pred[128]{0:T(512)(128)(4,1)S(1)} %fusion.15), kind=kLoop, calls=%fused_computation | loop fusion | flops 442368 | bytes 1184896 | tf_op jit(solution)/shard_map/jit(_where)/select_n | solution.py:606
  16.9 5.1 %collective-permute-done.4.rest_2_ = bf16[400,384]{1,0:T(8,128)(2,1)S(1)} collective-permute-done((bf16[400,384]{1,0:T(8,128)(2,1)S(1)}, bf16[400,384]{1,0:T(8,128)(2,1)S(1)}, u32[]{:S(2)}, u32[]{:S(2)}) %collective-permute-start.4) | collective-permute-done | bytes 307232 | tf_op jit(solution)/shard_map/ppermute | solution.py:530
  27.4 2.8 %collective-permute-done.5.rest_6_ = bf16[400,384]{1,0:T(8,128)(2,1)S(1)} collective-permute-done((bf16[400,384]{1,0:T(8,128)(2,1)S(1)}, bf16[400,384]{1,0:T(8,128)(2,1)S(1)}, u32[]{:S(2)}, u32[]{:S(2)}) %collective-permute-start.5) | collective-permute-done | bytes 307232 | tf_op jit(solution)/shard_map/ppermute | solution.py:530
  34.1 6.2 %collective-permute-done.7.rest_4_ = bf16[192,384]{1,0:T(8,128)(2,1)S(1)} collective-permute-done((bf16[192,384]{1,0:T(8,128)(2,1)S(1)}, bf16[192,384]{1,0:T(8,128)(2,1)S(1)}, u32[]{:S(2)}, u32[]{:S(2)}) %collective-permute-start.7) | collective-permute-done | bytes 147488 | tf_op jit(solution)/shard_map/ppermute | solution.py:530
  42.3 5.7 %project.1 = (bf16[768,1536]{1,0:T(8,128)(2,1)S(1)}, f32[16,768]{1,0:T(8,128)S(1)}, bf16[1152,768]{1,0:T(8,128)(2,1)S(1)}, bf16[1024,384]{1,0:T(8,128)(2,1)S(1)}...) custom-call(s32[8]{0:T(128)S(1)} %dynamic-slice_bitcast_fusion.slots, f32[1152,768]{1,0:T(8,128)S(1)} %first_norm.1.hat, ...), custom_call_target="tpu_custom_call" | custom-call | flops 603979776 | bytes 1738752 | tf_op jit(solution)/shard_map/project/pallas_call | solution.py:50
  48.1 3.4 %collective-permute-done.10.rest_1_ = bf16[288,576]{1,0:T(8,128)(2,1)S(1)} collective-permute-done((bf16[288,576]{1,0:T(8,128)(2,1)S(1)}, bf16[288,576]{1,0:T(8,128)(2,1)S(1)}, u32[]{:S(2)}, u32[]{:S(2)}) %collective-permute-start.10) | collective-permute-done | bytes 331808 | tf_op jit(solution)/shard_map/ppermute | solution.py:530
  54.0 7.7 %attend.2 = (bf16[16,256,256]{2,1,0:T(8,128)(2,1)S(1)}, bf16[1024,384]{1,0:T(8,128)(2,1)S(1)}) custom-call(s32[5]{0:T(128)S(1)} %pad_add_fusion.bounds, bf16[1024,384]{1,0:T(8,128)(2,1)S(1)} %get-tuple-element.144.query, bf16[1152,384]{1,0:T(8,128)(2,1)S(1)} %get-tuple-element.145.key, bf16[1152,384]{1,0:T(8,128)(2,1)S(1)} %get-tuple-element.146.value), custom_call_target="tpu_custom_call" | custom-call | flops 754974720 | bytes 679936 | tf_op jit(solution)/shard_map/attend/pallas_call | solution.py:50
  64.6 6.6 %attend.3 = (bf16[8,256,256]{2,1,0:T(8,128)(2,1)S(1)}, bf16[1024,384]{1,0:T(8,128)(2,1)S(1)}, bf16[1024,768]{1,0:T(8,128)(2,1)S(1)}) custom-call(s32[5]{0:T(128)S(1)} %pad_add_fusion.bounds, bf16[1024,384]{1,0:T(8,128)(2,1)S(1)} %get-tuple-element.144.query, bf16[1152,384]{1,0:T(8,128)(2,1)S(1)} %get-tuple-element.145.key, ...), custom_call_target="tpu_custom_call" | custom-call | flops 528482304 | bytes 1138688 | tf_op jit(solution)/shard_map/attend/pallas_call | solution.py:50
  73.7 5.0 %collective-permute-done.16.rest_4_ = bf16[96,576]{1,0:T(8,128)(2,1)S(1)} collective-permute-done((bf16[96,576]{1,0:T(8,128)(2,1)S(1)}, bf16[96,576]{1,0:T(8,128)(2,1)S(1)}, u32[]{:S(2)}, u32[]{:S(2)}) %collective-permute-start.16) | collective-permute-done | bytes 110624 | tf_op jit(solution)/shard_map/ppermute | solution.py:530
  79.8 10.6 %feed_forward_and_back.1 = (f32[1024,768]{1,0:T(8,128)S(1)}, bf16[1024,768]{1,0:T(8,128)(2,1)S(1)}, bf16[1024,576]{1,0:T(8,128)(2,1)S(1)}, bf16[1024,576]{1,0:T(...) custom-call(s32[8]{0:T(128)S(1)} %dynamic-slice_bitcast_fusion.slots, ...), custom_call_target="tpu_custom_call" | custom-call | flops 905969664 | bytes 2684928 | tf_op jit(solution)/shard_map/feed_forward_and_back/pallas_call | solution.py:50
  90.4 4.7 %feed_weight_grads.1 = bf16[8,3,96,576]{3,2,1,0:T(8,128)(2,1)S(1)} custom-call(s32[8]{0:T(128)S(1)} %dynamic-slice_bitcast_fusion.slots, bf16[1024,768]{1,0:T(8,128)(2,1)S(1)} %get-tuple-element.170.second, bf16[1024,576]{1,0:T(8,128)(2,1)S(1)} %get-tuple-element.174.hidden, bf16[1024,576]{1,0:T(8,128)(2,1)S(1)} %get-tuple-element.171.grad_gate, ...), custom_call_target="tpu_custom_call" | custom-call | flops 566231040 | bytes 1167360 | tf_op jit(solution)/shard_map/feed_weight_grads/pallas_call | solution.py:50
  99.4 3.6 %middle_grad.1 = (f32[1024,768]{1,0:T(8,128)S(1)}, bf16[1024,768]{1,0:T(8,128)(2,1)S(1)}, bf16[1024,384]{1,0:T(8,128)(2,1)S(1)}) custom-call(f32[1024,768]{1,0:T(8,128)S(1)} %get-tuple-element.222.middle, bf16[1024,768]{1,0:T(8,128)(2,1)S(1)} %get-tuple-element.167.own, bf16[1024,768]{1,0:T(8,128)(2,1)S(1)} %collective-permute-done.18.other, ...), custom_call_target="tpu_custom_call" | custom-call | flops 301989888 | bytes 1972224 | tf_op jit(solution)/shard_map/middle_grad/pallas_call | solution.py:50
  105.8 12.3 %attention_back.1 = (bf16[1152,384]{1,0:T(8,128)(2,1)S(1)}, bf16[1152,384]{1,0:T(8,128)(2,1)S(1)}, bf16[1152,384]{1,0:T(8,128)(2,1)S(1)}) custom-call(bf16[1024,384]{1,0:T(8,128)(2,1)S(1)} %get-tuple-element.144.query, bf16[1152,384]{1,0:T(8,128)(2,1)S(1)} %get-tuple-element.145.key, bf16[1152,384]{1,0:T(8,128)(2,1)S(1)} %get-tuple-element.146.value, ...), custom_call_target="tpu_custom_call" | custom-call | flops 1132462080 | bytes 1290240 | tf_op jit(solution)/shard_map/attention_back/pallas_call | solution.py:50
  120.4 3.0 %query_key_grads.1 = (bf16[1152,1152]{1,0:T(8,128)(2,1)S(1)}, bf16[8,2,96,384]{3,2,1,0:T(8,128)(2,1)S(1)}) custom-call(s32[8]{0:T(128)S(1)} %dynamic-slice_bitcast_fusion.slots, bf16[1152,768]{1,0:T(8,128)(2,1)S(1)} %get-tuple-element.166.first, bf16[1152,384]{1,0:T(8,128)(2,1)S(1)} %get-tuple-element.188.rest_0_, ...), custom_call_target="tpu_custom_call" | custom-call | flops 226492416 | bytes 1032192 | tf_op jit(solution)/shard_map/query_key_grads/pallas_call | solution.py:50
  123.3 4.1 %first_grad.1 = (bf16[1024,768]{1,0:T(8,128)(2,1)S(1)}, bf16[2,64,768]{2,1,0:T(8,128)(2,1)S(1)}) custom-call(bf16[1152,1152]{1,0:T(8,128)(2,1)S(1)} %get-tuple-element.192.grad_proj, bf16[768,1536]{1,0:T(8,128)(2,1)S(1)} %get-tuple-element.147.rest_0_.wide), custom_call_target="tpu_custom_call" | custom-call | flops 226492416 | bytes 847872 | tf_op jit(solution)/shard_map/first_grad/pallas_call | solution.py:50
  127.5 2.7 %value_out_grads.1 = bf16[8,2,96,384]{3,2,1,0:T(8,128)(2,1)S(1)} custom-call(s32[8]{0:T(128)S(1)} %dynamic-slice_bitcast_fusion.slots, bf16[1152,768]{1,0:T(8,128)(2,1)S(1)} %get-tuple-element.166.first, bf16[1152,1152]{1,0:T(8,128)(2,1)S(1)} %get-tuple-element.192.grad_proj, bf16[1024,768]{1,0:T(8,128)(2,1)S(1)} %get-tuple-element.193.low_mid, ...), custom_call_target="tpu_custom_call" | custom-call | flops 226492416 | bytes 995328 | tf_op jit(solution)/shard_map/value_out_grads/pallas_call | solution.py:50
  134.4 2.5 %collective-permute-done.27 = bf16[2,96,384]{2,1,0:T(8,128)(2,1)S(1)} collective-permute-done((bf16[2,96,384]{2,1,0:T(8,128)(2,1)S(1)}, bf16[2,96,384]{2,1,0:T(8,128)(2,1)S(1)}, u32[]{:S(2)}, u32[]{:S(2)}) %collective-permute-start.27) | collective-permute-done | bytes 147488 | tf_op jit(solution)/shard_map/ppermute | solution.py:562
  139.2 2.8 %collective-permute-done.32 = bf16[64,768]{1,0:T(8,128)(2,1)S(1)} collective-permute-done((bf16[64,768]{1,0:T(8,128)(2,1)S(1)}, bf16[64,768]{1,0:T(8,128)(2,1)S(1)}, u32[]{:S(2)}, u32[]{:S(2)}) %collective-permute-start.32) | collective-permute-done | bytes 98336 | tf_op jit(solution)/shard_map/ppermute | solution.py:446
  144.1 3.8 %collective-permute-done.33 = bf16[2,96,384]{2,1,0:T(8,128)(2,1)S(1)} collective-permute-done((bf16[2,96,384]{2,1,0:T(8,128)(2,1)S(1)}, bf16[2,96,384]{2,1,0:T(8,128)(2,1)S(1)}, u32[]{:S(2)}, u32[]{:S(2)}) %collective-permute-start.33) | collective-permute-done | bytes 147488 | tf_op jit(solution)/shard_map/ppermute | solution.py:580
  156.5 5.1 %collective-permute-done.30 = bf16[3,96,576]{2,1,0:T(8,128)(2,1)S(1)} collective-permute-done((bf16[3,96,576]{2,1,0:T(8,128)(2,1)S(1)}, bf16[3,96,576]{2,1,0:T(8,128)(2,1)S(1)}, u32[]{:S(2)}, u32[]{:S(2)}) %collective-permute-start.30) | collective-permute-done | bytes 331808 | tf_op jit(solution)/shard_map/ppermute | solution.py:580
  167.8 2.1 %collective-permute-done.35 = bf16[2,96,384]{2,1,0:T(8,128)(2,1)S(1)} collective-permute-done((bf16[2,96,384]{2,1,0:T(8,128)(2,1)S(1)}, bf16[2,96,384]{2,1,0:T(8,128)(2,1)S(1)}, u32[]{:S(2)}, u32[]{:S(2)}) %collective-permute-start.35) | collective-permute-done | bytes 147488 | tf_op jit(solution)/shard_map/ppermute | solution.py:580
  172.1 3.1 %collective-permute-done.45 = bf16[2,96,384]{2,1,0:T(8,128)(2,1)S(1)} collective-permute-done((bf16[2,96,384]{2,1,0:T(8,128)(2,1)S(1)}, bf16[2,96,384]{2,1,0:T(8,128)(2,1)S(1)}, u32[]{:S(2)}, u32[]{:S(2)}) %collective-permute-start.45) | collective-permute-done | bytes 147488 | tf_op jit(solution)/shard_map/ppermute | solution.py:580
  179.3 4.9 %token_grad.1 = f32[1024,768]{1,0:T(8,128)} custom-call(bf16[1024,768]{1,0:T(8,128)(2,1)S(1)} %copy-done, f32[16,768]{1,0:T(8,128)S(1)} %get-tuple-element.160.gain, f32[1024,768]{1,0:T(8,128)S(1)} %get-tuple-element.225.grad_middle, bf16[1024,768]{1,0:T(8,128)(2,1)S(1)} %get-tuple-element.226.own, bf16[1024,768]{1,0:T(8,128)(2,1)S(1)} %collective-permute-done.38.other, ...), custom_call_target="tpu_custom_call" | custom-call | flops 19660800 | bytes 1431552 | tf_op jit(solution)/shard_map/token_grad/pallas_call | solution.py:50
  (153 shorter events, 74.8 us)
Async XLA Ops:
  2.5 10.3 %collective-permute-start.2 = (bf16[400,384]{1,0:T(8,128)(2,1)S(1)}, bf16[400,384]{1,0:T(8,128)(2,1)S(1)}, u32[]{:S(2)}, u32[]{:S(2)}) collective-permute-start(bf16[400,384]{1,0:T(8,128)(2,1)S(1)} %pad_maximum_fusion.2.rest_0_), channel_id=1, source_target_pairs={{8,0},{16,8},{24,16},{28,24},{20,28},{12,20},{4,12},{0,4},{9,1},{1... | collective-permute-start | bytes 921608 | tf_op jit(solution)/shard_map/ppermute | solution.py:530
  5.4 8.7 %collective-permute-start.1 = (bf16[400,384]{1,0:T(8,128)(2,1)S(1)}, bf16[400,384]{1,0:T(8,128)(2,1)S(1)}, u32[]{:S(2)}, u32[]{:S(2)}) collective-permute-start(bf16[400,384]{1,0:T(8,128)(2,1)S(1)} %pad_maximum_fusion.2.rest_0_), channel_id=1, source_target_pairs={{0,8},{8,16},{16,24},{24,28},{28,20},{20,12},{12,4},{4,0},{1,9},{9... | collective-permute-start | bytes 921608 | tf_op jit(solution)/shard_map/ppermute | solution.py:530
  6.6 10.3 %collective-permute-start = (bf16[64,768]{1,0:T(8,128)(2,1)S(1)}, bf16[64,768]{1,0:T(8,128)(2,1)S(1)}, u32[]{:S(2)}, u32[]{:S(2)}) collective-permute-start(bf16[64,768]{1,0:T(8,128)(2,1)S(1)} %slice_select_fusion), channel_id=1, source_target_pairs={{0,2},{2,0},{1,3},{3,1},{4,6},{6,4},{5,7},{7,5},{8,10},{10,8},{9,1... | collective-permute-start | bytes 294920 | tf_op jit(solution)/shard_map/ppermute | solution.py:460
  40.3 11.2 %collective-permute-start.10 = (bf16[288,576]{1,0:T(8,128)(2,1)S(1)}, bf16[288,576]{1,0:T(8,128)(2,1)S(1)}, u32[]{:S(2)}, u32[]{:S(2)}) collective-permute-start(bf16[288,576]{1,0:T(8,128)(2,1)S(1)} %pad_maximum_fusion.1.rest_0_), channel_id=1, source_target_pairs={{8,0},{16,8},{24,16},{28,24},{20,28},{12,20},{4,12},{0,4},{9,1},{1... | collective-permute-start | bytes 995336 | tf_op jit(solution)/shard_map/ppermute | solution.py:530
  41.9 10.1 %collective-permute-start.9 = (bf16[288,576]{1,0:T(8,128)(2,1)S(1)}, bf16[288,576]{1,0:T(8,128)(2,1)S(1)}, u32[]{:S(2)}, u32[]{:S(2)}) collective-permute-start(bf16[288,576]{1,0:T(8,128)(2,1)S(1)} %pad_maximum_fusion.1.rest_0_), channel_id=1, source_target_pairs={{0,8},{8,16},{16,24},{24,28},{28,20},{20,12},{12,4},{4,0},{1,9},{9... | collective-permute-start | bytes 995336 | tf_op jit(solution)/shard_map/ppermute | solution.py:530
  51.9 10.4 %collective-permute-start.11 = (bf16[288,576]{1,0:T(8,128)(2,1)S(1)}, bf16[288,576]{1,0:T(8,128)(2,1)S(1)}, u32[]{:S(2)}, u32[]{:S(2)}) collective-permute-start(bf16[288,576]{1,0:T(8,128)(2,1)S(1)} %collective-permute-done.9.rest_8_), channel_id=1, source_target_pairs={{0,8},{8,16},{16,24},{24,28},{28,20},{20,12},{12,4},{4,0},{1,9},{9... | collective-permute-start | bytes 995336 | tf_op jit(solution)/shard_map/ppermute | solution.py:530
  52.3 10.2 %collective-permute-start.12 = (bf16[288,576]{1,0:T(8,128)(2,1)S(1)}, bf16[288,576]{1,0:T(8,128)(2,1)S(1)}, u32[]{:S(2)}, u32[]{:S(2)}) collective-permute-start(bf16[288,576]{1,0:T(8,128)(2,1)S(1)} %collective-permute-done.10.rest_1_), channel_id=1, source_target_pairs={{8,0},{16,8},{24,16},{28,24},{20,28},{12,20},{4,12},{0,4},{9,1},{1... | collective-permute-start | bytes 995336 | tf_op jit(solution)/shard_map/ppermute | solution.py:530
  62.6 8.7 %collective-permute-start.13 = (bf16[288,576]{1,0:T(8,128)(2,1)S(1)}, bf16[288,576]{1,0:T(8,128)(2,1)S(1)}, u32[]{:S(2)}, u32[]{:S(2)}) collective-permute-start(bf16[288,576]{1,0:T(8,128)(2,1)S(1)} %collective-permute-done.11.rest_7_), channel_id=1, source_target_pairs={{0,8},{8,16},{16,24},{24,28},{28,20},{20,12},{12,4},{4,0},{1,9},{9... | collective-permute-start | bytes 995336 | tf_op jit(solution)/shard_map/ppermute | solution.py:530
  71.2 8.5 %collective-permute-start.15 = (bf16[1024,768]{1,0:T(8,128)(2,1)S(1)}, bf16[1024,768]{1,0:T(8,128)(2,1)S(1)}, u32[]{:S(2)}, u32[]{:S(2)}) collective-permute-start(bf16[1024,768]{1,0:T(8,128)(2,1)S(1)} %get-tuple-element.159.own), channel_id=1, source_target_pairs={{0,1},{1,0},{2,3},{3,2},{4,5},{5,4},{6,7},{7,6},{8,9},{9,8},{10,11... | collective-permute-start | bytes 4718600 | tf_op jit(solution)/shard_map/ppermute | solution.py:474
  103.7 14.4 %collective-permute-start.22 = (bf16[3,96,576]{2,1,0:T(8,128)(2,1)S(1)}, bf16[3,96,576]{2,1,0:T(8,128)(2,1)S(1)}, u32[]{:S(2)}, u32[]{:S(2)}) collective-permute-start(bf16[3,96,576]{2,1,0:T(8,128)(2,1)S(1)} %get-tuple-element.252), channel_id=1, source_target_pairs={{8,0},{16,8},{24,16},{28,24},{20,28},{12,20},{4,12},{0,4},{9,1},{1... | collective-permute-start | bytes 995336 | tf_op jit(solution)/shard_map/ppermute | solution.py:580
  105.3 12.8 %collective-permute-start.21 = (bf16[3,96,576]{2,1,0:T(8,128)(2,1)S(1)}, bf16[3,96,576]{2,1,0:T(8,128)(2,1)S(1)}, u32[]{:S(2)}, u32[]{:S(2)}) collective-permute-start(bf16[3,96,576]{2,1,0:T(8,128)(2,1)S(1)} %get-tuple-element.253), channel_id=1, source_target_pairs={{0,8},{8,16},{16,24},{24,28},{28,20},{20,12},{12,4},{4,0},{1,9},{9... | collective-permute-start | bytes 995336 | tf_op jit(solution)/shard_map/ppermute | solution.py:580
  118.3 11.9 %collective-permute-start.24 = (bf16[3,96,576]{2,1,0:T(8,128)(2,1)S(1)}, bf16[3,96,576]{2,1,0:T(8,128)(2,1)S(1)}, u32[]{:S(2)}, u32[]{:S(2)}) collective-permute-start(bf16[3,96,576]{2,1,0:T(8,128)(2,1)S(1)} %get-tuple-element.250), channel_id=1, source_target_pairs={{8,0},{16,8},{24,16},{28,24},{20,28},{12,20},{4,12},{0,4},{9,1},{1... | collective-permute-start | bytes 995336 | tf_op jit(solution)/shard_map/ppermute | solution.py:580
  119.9 10.3 %collective-permute-start.23 = (bf16[3,96,576]{2,1,0:T(8,128)(2,1)S(1)}, bf16[3,96,576]{2,1,0:T(8,128)(2,1)S(1)}, u32[]{:S(2)}, u32[]{:S(2)}) collective-permute-start(bf16[3,96,576]{2,1,0:T(8,128)(2,1)S(1)} %get-tuple-element.251), channel_id=1, source_target_pairs={{0,8},{8,16},{16,24},{24,28},{28,20},{20,12},{12,4},{4,0},{1,9},{9... | collective-permute-start | bytes 995336 | tf_op jit(solution)/shard_map/ppermute | solution.py:580
  120.4 57.2 %collective-permute-start.37 = (bf16[1024,768]{1,0:T(8,128)(2,1)S(1)}, bf16[1024,768]{1,0:T(8,128)(2,1)S(1)}, u32[]{:S(2)}, u32[]{:S(2)}) collective-permute-start(bf16[1024,768]{1,0:T(8,128)(2,1)S(1)} %feed_out.1.own), channel_id=1, source_target_pairs={{0,1},{1,0},{2,3},{3,2},{4,5},{5,4},{6,7},{7,6},{8,9},{9,8},{10,11... | collective-permute-start | bytes 4718600 | tf_op jit(solution)/shard_map/ppermute | solution.py:474
  132.4 17.7 %collective-permute-start.25 = (bf16[2,96,384]{2,1,0:T(8,128)(2,1)S(1)}, bf16[2,96,384]{2,1,0:T(8,128)(2,1)S(1)}, u32[]{:S(2)}, u32[]{:S(2)}) collective-permute-start(bf16[2,96,384]{2,1,0:T(8,128)(2,1)S(1)} %get-tuple-element.265), channel_id=1, source_target_pairs={{0,8},{8,16},{16,24},{24,28},{28,20},{20,12},{12,4},{4,0},{1,9},{9... | collective-permute-start | bytes 442376 | tf_op jit(solution)/shard_map/ppermute | solution.py:580
  132.8 9.7 %collective-permute-start.34 = (bf16[2,96,384]{2,1,0:T(8,128)(2,1)S(1)}, bf16[2,96,384]{2,1,0:T(8,128)(2,1)S(1)}, u32[]{:S(2)}, u32[]{:S(2)}) collective-permute-start(bf16[2,96,384]{2,1,0:T(8,128)(2,1)S(1)} %get-tuple-element.262), channel_id=1, source_target_pairs={{8,0},{16,8},{24,16},{28,24},{20,28},{12,20},{4,12},{0,4},{9,1},{1... | collective-permute-start | bytes 442376 | tf_op jit(solution)/shard_map/ppermute | solution.py:580
  137.5 12.1 %collective-permute-start.31 = (bf16[64,768]{1,0:T(8,128)(2,1)S(1)}, bf16[64,768]{1,0:T(8,128)(2,1)S(1)}, u32[]{:S(2)}, u32[]{:S(2)}) collective-permute-start(bf16[64,768]{1,0:T(8,128)(2,1)S(1)} %select_bitcast_fusion.4), channel_id=1, source_target_pairs={{0,2},{1,3},{2,0},{3,1},{4,6},{5,7},{6,4},{7,5},{8,10},{9,11},{10,... | collective-permute-start | bytes 294920 | tf_op jit(solution)/shard_map/ppermute | solution.py:446
  150.0 29.2 %collective-permute-start.38 = (bf16[1024,768]{1,0:T(8,128)(2,1)S(1)}, bf16[1024,768]{1,0:T(8,128)(2,1)S(1)}, u32[]{:S(2)}, u32[]{:S(2)}) collective-permute-start(bf16[1024,768]{1,0:T(8,128)(2,1)S(1)} %get-tuple-element.226.own), channel_id=1, source_target_pairs={{0,1},{1,0},{2,3},{3,2},{4,5},{5,4},{6,7},{7,6},{8,9},{9,8},{10,11... | collective-permute-start | bytes 4718600 | tf_op jit(solution)/shard_map/ppermute | solution.py:474
  150.1 11.4 %collective-permute-start.30 = (bf16[3,96,576]{2,1,0:T(8,128)(2,1)S(1)}, bf16[3,96,576]{2,1,0:T(8,128)(2,1)S(1)}, u32[]{:S(2)}, u32[]{:S(2)}) collective-permute-start(bf16[3,96,576]{2,1,0:T(8,128)(2,1)S(1)} %get-tuple-element.248), channel_id=1, source_target_pairs={{8,0},{16,8},{24,16},{28,24},{20,28},{12,20},{4,12},{0,4},{9,1},{1... | collective-permute-start | bytes 995336 | tf_op jit(solution)/shard_map/ppermute | solution.py:580
  153.1 9.5 %collective-permute-start.29 = (bf16[3,96,576]{2,1,0:T(8,128)(2,1)S(1)}, bf16[3,96,576]{2,1,0:T(8,128)(2,1)S(1)}, u32[]{:S(2)}, u32[]{:S(2)}) collective-permute-start(bf16[3,96,576]{2,1,0:T(8,128)(2,1)S(1)} %get-tuple-element.249), channel_id=1, source_target_pairs={{0,8},{8,16},{16,24},{24,28},{28,20},{20,12},{12,4},{4,0},{1,9},{9... | collective-permute-start | bytes 995336 | tf_op jit(solution)/shard_map/ppermute | solution.py:580
  154.9 9.9 %collective-permute-start.42 = (bf16[2,96,384]{2,1,0:T(8,128)(2,1)S(1)}, bf16[2,96,384]{2,1,0:T(8,128)(2,1)S(1)}, u32[]{:S(2)}, u32[]{:S(2)}) collective-permute-start(bf16[2,96,384]{2,1,0:T(8,128)(2,1)S(1)} %get-tuple-element.256), channel_id=1, source_target_pairs={{8,0},{16,8},{24,16},{28,24},{20,28},{12,20},{4,12},{0,4},{9,1},{1... | collective-permute-start | bytes 442376 | tf_op jit(solution)/shard_map/ppermute | solution.py:580
  166.9 17.2 %collective-permute-start.47 = (bf16[3,96,576]{2,1,0:T(8,128)(2,1)S(1)}, bf16[3,96,576]{2,1,0:T(8,128)(2,1)S(1)}, u32[]{:S(2)}, u32[]{:S(2)}) collective-permute-start(bf16[3,96,576]{2,1,0:T(8,128)(2,1)S(1)} %fusion.1), channel_id=1, source_target_pairs={{0,2},{2,0},{1,3},{3,1},{4,6},{6,4},{5,7},{7,5},{8,10},{10,8},{9,1... | collective-permute-start | bytes 995336 | tf_op jit(solution)/shard_map/ppermute | solution.py:474
  175.1 10.8 %collective-permute-start.43 = (bf16[2,96,384]{2,1,0:T(8,128)(2,1)S(1)}, bf16[2,96,384]{2,1,0:T(8,128)(2,1)S(1)}, u32[]{:S(2)}, u32[]{:S(2)}) collective-permute-start(bf16[2,96,384]{2,1,0:T(8,128)(2,1)S(1)} %fusion.5), channel_id=1, source_target_pairs={{0,2},{2,0},{1,3},{3,1},{4,6},{6,4},{5,7},{7,5},{8,10},{10,8},{9,1... | collective-permute-start | bytes 442376 | tf_op jit(solution)/shard_map/ppermute | solution.py:474
  176.7 9.1 %collective-permute-start.46 = (bf16[2,96,384]{2,1,0:T(8,128)(2,1)S(1)}, bf16[2,96,384]{2,1,0:T(8,128)(2,1)S(1)}, u32[]{:S(2)}, u32[]{:S(2)}) collective-permute-start(bf16[2,96,384]{2,1,0:T(8,128)(2,1)S(1)} %fusion.3), channel_id=1, source_target_pairs={{0,2},{2,0},{1,3},{3,1},{4,6},{6,4},{5,7},{7,5},{8,10},{10,8},{9,1... | collective-permute-start | bytes 442376 | tf_op jit(solution)/shard_map/ppermute | solution.py:474
  (32 other events, 223.5 us)
